TPU v7x, 768 devices: a whole 4x8x12 slice. The times are simulated.
768 devices in a mesh: dp: 48 (over x, z_lo, core), expert: 2 (over z_hi), tensor: 8 (over y).
Axes of the slice: x: 4, y: 8, z: 12 (z_hi: 2, z_lo: 6; z = z_hi * 6 + z_lo), core: 2. Of those that a mesh axis runs over, the one named last changes fastest.
Arguments:
- routes: int32 [98304, 2], P(('dp', 'expert', 'tensor')), may hold values from 0 to 7, as said below
- upgrad: bfloat16 [48, 2, 8, 2, 40, 8192], P('dp', 'expert', None, None, None, 'tensor'), may hold values from -6 to 6
- weight: bfloat16 [2, 3072, 8192], P('expert', 'dp', 'tensor'), may hold values from -0.0625 to 0.0625
Outputs:
- input_grad: bfloat16 [98304, 3072], P(('dp', 'expert', 'tensor'))
Inputs may be any that keep to these rules, and one draw needn't show every extreme that they name: `routes`: each row names two different experts. In the rows of one device, each expert whose number is below the size of the expert axis is named by at most 40 rows, and in every group of devices with one dp index one such expert is named by exactly 40 rows on each of its devices.
All inputs are finite; a program needn't handle non-finite values.
Results may differ from a plain program's by a relative error of at most 0.018.
Values may be sent and summed in bfloat16 or wider, within the bound.
No kernel may reach another device: no remote copies, remote signals or barrier semaphores. Data moves between devices by JAX's collectives and lax.ppermute only.
A program may use at most 32 MiB of HBM per device.

v0:
```python
import jax
import jax.numpy as jnp
from jax import lax
from jax.sharding import PartitionSpec as P


def shards(routes, upgrad, weight):
    tensor_count = upgrad.shape[2]
    owners = upgrad.shape[3]
    capacity = upgrad.shape[4]
    hidden = upgrad.shape[5]
    grad_rows = upgrad.reshape(tensor_count, owners, capacity, hidden)
    weight_slab = weight[0]
    feature_count = weight_slab.shape[0] * lax.axis_size("dp")
    contract = (((1,), (1,)), ((), ()))
    flat_rows = grad_rows.reshape(tensor_count * owners * capacity, hidden)
    partials = lax.dot_general(
        flat_rows,
        lax.all_gather(weight_slab, "dp", axis=0, tiled=True),
        contract,
        preferred_element_type=jnp.float32,
    )
    partials = partials.reshape(tensor_count, owners, capacity, feature_count)
    summed = lax.psum_scatter(
        partials.astype(jnp.bfloat16), "tensor", scatter_dimension=0, tiled=True
    ).astype(jnp.float32)
    summed_rows = summed[0].astype(jnp.bfloat16)
    returned = lax.all_to_all(summed_rows, "expert", split_axis=0, concat_axis=0, tiled=True)
    tokens = routes.shape[0]
    owner_ids = lax.iota(jnp.int32, owners)
    is_routed = jnp.any(routes[:, :, None] == owner_ids[None, None, :], axis=1)
    slot_index = jnp.cumsum(is_routed.astype(jnp.int32), axis=0) - 1
    positions = lax.iota(jnp.int32, capacity)
    onehot = is_routed[:, :, None] & (slot_index[:, :, None] == positions[None, None, :])
    onehot = onehot.reshape(tokens, owners * capacity).astype(jnp.bfloat16)
    gathered = jnp.dot(
        onehot,
        returned.reshape(owners * capacity, feature_count),
        preferred_element_type=jnp.float32,
    )
    return gathered.astype(jnp.bfloat16)


def solution(mesh):
    return jax.shard_map(
        shards,
        mesh=mesh,
        in_specs=(
            P(("dp", "expert", "tensor"), None),
            P("dp", "expert", None, None, None, "tensor"),
            P("expert", "dp", "tensor"),
        ),
        out_specs=P(("dp", "expert", "tensor"), None),
        check_vma=False,
    )
```

profile of v0, /device:TPU:64, one launch (start us, length us, event | category | flops | bytes accessed | tf_op | source)
XLA Modules:
  0.0 223.5 jit_solution(12647610316148671534)
XLA Ops:
  6.5 0.0 copy-start
  6.5 0.0 all-gather.3.cloned.1.call-start
  6.5 0.7 all-gather.3.cloned.1.call-update
  7.3 0.0 reduce-scatter.2.cloned.1.call-start
  7.3 109.3 %all-gather.3.cloned.1.call-done = bf16[1,3072,1024]{2,1,0:T(8,128)(2,1)} async-done(((bf16[1,64,1024]{2,1,0:T(8,128)(2,1)}), bf16[1,3072,1024]{2,1,0:T(8,128)(2,1)}) %all-gather.3.cloned.1.call-update) | async-done | bytes 6291472 | tf_op jit(solution)/shard_map/all_gather | solution.py:19
  116.6 0.0 copy-done
  116.6 8.6 %fusion.2 = bf16[8,2,40,3072]{3,2,1,0:T(8,128)(2,1)} fusion(bf16[1,3072,1024]{2,1,0:T(8,128)(2,1)} %all-gather.3.cloned.1.call-done, bf16[1,1,8,2,40,1024]{5,4,3,2,1,0:T(8,128)(2,1)S(1)} %copy-done), kind=kOutput, calls=%fused_computation.2 | convolution fusion | flops 4028497920 | bytes 11534336 | tf_op jit(solution)/shard_map/dot_general | solution.py:17
  125.2 0.0 copy-start.1
  125.2 0.0 reduce-scatter.2.cloned.1.call-update
  125.3 56.4 %reduce-scatter.2.cloned.1.call-done = bf16[1,2,40,3072]{3,2,1,0:T(8,128)(2,1)} async-done(((bf16[8,2,40,3072]{3,2,1,0:T(8,128)(2,1)}), bf16[1,2,40,3072]{3,2,1,0:T(8,128)(2,1)}) %reduce-scatter.2.cloned.1.call-update) | async-done | bytes 491536 | tf_op jit(solution)/shard_map/reduce_scatter | solution.py:24
  181.7 9.2 %all-to-all-start = ((bf16[2,40,3072]{2,1,0:T(8,128)(2,1)}), bf16[2,40,3072]{2,1,0:T(8,128)(2,1)S(1)}, u32[]{:S(2)}, u32[]{:S(2)}) async-start(bf16[2,40,3072]{2,1,0:T(8,128)(2,1)} %bitcast.18), calls=%async_computation.1 | async-start | bytes 983040 | tf_op jit(solution)/shard_map/all_to_all | solution.py:28
  190.9 0.0 copy-done.1
  190.9 0.1 copy.7
  191.0 0.2 reduce_window_sum.11
  191.2 0.1 copy.8
  191.2 24.2 %all-to-all-done = bf16[2,40,3072]{2,1,0:T(8,128)(2,1)S(1)} async-done(((bf16[2,40,3072]{2,1,0:T(8,128)(2,1)}), bf16[2,40,3072]{2,1,0:T(8,128)(2,1)S(1)}, u32[]{:S(2)}, u32[]{:S(2)}) %all-to-all-start) | async-done | bytes 491552 | tf_op jit(solution)/shard_map/all_to_all | solution.py:28
  215.4 1.3 fusion.5
  (3 shorter events, 0.0 us)
Async XLA Ops:
  6.5 110.1 %copy-start = (bf16[1,1,8,2,40,1024]{5,4,3,2,1,0:T(8,128)(2,1)S(1)}, bf16[1,1,8,2,40,1024]{5,4,3,2,1,0:T(8,128)(2,1)}, u32[]{:S(2)}) copy-start(bf16[1,1,8,2,40,1024]{5,4,3,2,1,0:T(8,128)(2,1)} %param.4) | copy-start | bytes 3932164
  6.5 110.1 %all-gather.3.cloned.1.call-start = ((), (), s32[]{:S(2)}) async-start(), calls=%async_computation.3 | async-start | bytes 6422528 | tf_op jit(solution)/shard_map/all_gather | solution.py:19
  7.3 174.4 %reduce-scatter.2.cloned.1.call-start = ((), (), s32[]{:S(2)}) async-start(), calls=%async_computation.2 | async-start | bytes 4423680 | tf_op jit(solution)/shard_map/reduce_scatter | solution.py:24
  125.2 65.6 %copy-start.1 = (s32[128,2]{0,1:T(2,128)S(1)}, s32[128,2]{0,1:T(2,128)}, u32[]{:S(2)}) copy-start(s32[128,2]{0,1:T(2,128)} %param.3) | copy-start | bytes 3076
  181.7 33.7 %all-to-all-start = ((bf16[2,40,3072]{2,1,0:T(8,128)(2,1)}), bf16[2,40,3072]{2,1,0:T(8,128)(2,1)S(1)}, u32[]{:S(2)}, u32[]{:S(2)}) async-start(bf16[2,40,3072]{2,1,0:T(8,128)(2,1)} %bitcast.18), calls=%async_computation.1 | async-start | bytes 983040 | tf_op jit(solution)/shard_map/all_to_all | solution.py:28
Sparse Core Ops, SparseCore 0:
  9.9 106.6 all-gather.2
  125.4 56.2 reduce-scatter.1
where the time goes:
time: 224 us
  waiting for transfers between devices  191 us (85%)
  between operations  13.4 us (6%)
  matrix products  9.94 us (4%)
  starting transfers between devices  9.26 us (4%)
    all_gather x1, waiting for transfers between devices, shards(): lax.all_gather(weight_slab, 'dp', axis=0, tiled=True)  109 us
    reduce_scatter x1, waiting for transfers between devices, shards(): lax.psum_scatter(partials.astype(jnp.bfloat16), 'tensor', scatter_dimensi...  56.4 us
    all_to_all x1, waiting for transfers between devices, shards(): lax.all_to_all(summed_rows, 'expert', split_axis=0, concat_axis=0, tiled=...  24.2 us
    all_to_all x1, starting transfers between devices, shards(): lax.all_to_all(summed_rows, 'expert', split_axis=0, concat_axis=0, tiled=...  9.22 us
    dot_general x1, matrix products, shards(): lax.dot_general(flat_rows, lax.all_gather(weight_slab, 'dp', axis=0, tile...  8.65 us
  transfers between devices with their start and end apart: 3, of which 3 were waited for; matrix products, arithmetic and copies ran while one was open for 0% of the time, Pallas kernels for 0%

commit v1 on v0

v1 whole, which is shorter than its diff:
```python
import jax
import jax.numpy as jnp
from jax import lax
from jax.experimental import pallas as pl
from jax.experimental.pallas import tpu as pltpu
from jax.sharding import PartitionSpec as P

NX, NZ, NC = 4, 6, 2
HALF = NZ // 2


def dp_index(x, z, c):
    return (x * NZ + z) * NC + c


def dp_perm(move):
    return [
        (dp_index(x, z, c), dp_index(*move(x, z, c)))
        for x in range(NX)
        for z in range(NZ)
        for c in range(NC)
    ]


SWAP_CORE = dp_perm(lambda x, z, c: (x, z, 1 - c))
SWAP_HALF = dp_perm(lambda x, z, c: (x, (z + HALF) % NZ, c))
TURN_UP = dp_perm(lambda x, z, c: (x, HALF * (z // HALF) + (z % HALF + 1) % HALF, c))
TURN_DOWN = dp_perm(lambda x, z, c: (x, HALF * (z // HALF) + (z % HALF - 1) % HALF, c))
X_UP = dp_perm(lambda x, z, c: ((x + 1) % NX, z, c))
X_DOWN = dp_perm(lambda x, z, c: ((x - 1) % NX, z, c))


def gather_weight(slab):
    move = lambda value, perm: lax.ppermute(value, "dp", perm)
    pair = jnp.stack([slab, move(slab, SWAP_HALF)])
    own = jnp.concatenate([pair, move(pair, TURN_UP), move(pair, TURN_DOWN)])
    below = move(own, X_UP)
    above = move(own, X_DOWN)
    far_first = move(below[:HALF], X_UP)
    far_last = move(above[HALF:], X_DOWN)
    return own, jnp.concatenate([below, above]), jnp.concatenate([far_first, far_last])


def block_places():
    dp = lax.axis_index("dp")
    z = (dp // NC) % NZ
    x = dp // (NC * NZ)
    half, m = z // HALF, z % HALF
    zs = []
    for turn in (0, -1, 1):
        at = (m + turn + HALF) % HALF
        zs += [half * HALF + at, (1 - half) * HALF + at]
    xs = [x, (x - 1 + NX) % NX, (x + 1) % NX, (x + 2) % NX]
    return jnp.stack([xi * NZ + zi for xi in xs for zi in zs]).astype(jnp.int32)


def sum_over_tensor(partial):
    n = partial.shape[0]
    mid = n // 2
    half_rows = partial.shape[1] // 2
    up = [(i, (i + 1) % n) for i in range(n)]
    down = [(i, (i - 1) % n) for i in range(n)]
    first = lax.ppermute(partial[mid, :half_rows], "tensor", up)
    last = lax.ppermute(partial[mid, half_rows:], "tensor", down)
    add = lambda a, b: (a.astype(jnp.float32) + b.astype(jnp.float32)).astype(jnp.bfloat16)
    going_up = jnp.concatenate([add(partial[mid - 1, :half_rows], first), partial[mid - 1, half_rows:]])
    going_down = jnp.concatenate([partial[mid + 1, :half_rows], add(partial[mid + 1, half_rows:], last)])
    for step in range(1, mid):
        from_below = lax.ppermute(going_up, "tensor", up)
        from_above = lax.ppermute(going_down, "tensor", down)
        if step < mid - 1:
            going_up = add(partial[mid - 1 - step], from_below)
            going_down = add(partial[mid + 1 + step], from_above)
    total = partial[0].astype(jnp.float32) + from_below.astype(jnp.float32) + from_above.astype(jnp.float32)
    return total.astype(jnp.bfloat16)


def exchange(summed, owners, capacity):
    features = summed.shape[-1]
    me = lax.axis_index("expert")
    rows = summed.reshape(NC, owners, capacity, features)
    keep = lax.dynamic_index_in_dim(rows, me, 1, keepdims=False)
    give = lax.dynamic_index_in_dim(rows, 1 - me, 1, keepdims=False)
    got = lax.ppermute(give, "expert", [(0, 1), (1, 0)])
    first = jnp.where(me == 0, keep, got)
    second = jnp.where(me == 0, got, keep)
    both = jnp.stack([first, second], axis=1).reshape(NC, owners * capacity, features)
    return both[0], lax.ppermute(both[1], "dp", SWAP_CORE)


def place_kernel(groups, width, places, core, onehot, *refs):
    out = refs[-1]
    first_core = core[0] == 0
    at = 0
    for g in range(groups):
        mine = jnp.dot(onehot[...], refs[2 * g][...], preferred_element_type=jnp.float32).astype(jnp.bfloat16)
        theirs = jnp.dot(onehot[...], refs[2 * g + 1][...], preferred_element_type=jnp.float32).astype(jnp.bfloat16)
        low = jnp.where(first_core, mine, theirs)
        high = jnp.where(first_core, theirs, mine)
        for b in range(mine.shape[1] // width):
            block = jnp.concatenate([low[:, b * width:(b + 1) * width], high[:, b * width:(b + 1) * width]], axis=1)
            start = pl.multiple_of(places[at] * (NC * width), NC * width)
            out[:, pl.ds(start, NC * width)] = block
            at += 1


def shards(routes, upgrad, weight):
    _, _, tensor_count, owners, capacity, hidden = upgrad.shape
    slab = weight[0]
    width = slab.shape[0]
    rows = owners * capacity
    me = lax.axis_index("tensor")
    dp = lax.axis_index("dp")

    own_rows = upgrad.reshape(tensor_count, rows, hidden)
    other_rows = lax.ppermute(own_rows, "dp", SWAP_CORE)
    turned = jnp.concatenate([own_rows, other_rows], axis=1)
    turned = jnp.concatenate([turned, turned], axis=0)
    turned = lax.dynamic_slice_in_dim(turned, me, tensor_count, 0)
    flat = turned.reshape(tensor_count * NC * rows, hidden)

    parts = []
    for blocks in gather_weight(slab):
        features = blocks.shape[0] * width
        partial = lax.dot_general(
            flat,
            blocks.reshape(features, hidden),
            (((1,), (1,)), ((), ())),
            preferred_element_type=jnp.float32,
        ).astype(jnp.bfloat16)
        summed = sum_over_tensor(partial.reshape(tensor_count, NC * rows, features))
        parts += exchange(summed, owners, capacity)

    owner_ids = lax.iota(jnp.int32, owners)
    is_routed = jnp.any(routes[:, :, None] == owner_ids[None, None, :], axis=1)
    slot_index = jnp.cumsum(is_routed.astype(jnp.int32), axis=0) - 1
    onehot = is_routed[:, :, None] & (slot_index[:, :, None] == lax.iota(jnp.int32, capacity)[None, None, :])
    onehot = onehot.reshape(routes.shape[0], rows).astype(jnp.bfloat16)

    smem = pl.BlockSpec(memory_space=pltpu.SMEM)
    vmem = pl.BlockSpec(memory_space=pltpu.VMEM)
    groups = len(parts) // 2

    def body(*refs):
        place_kernel(groups, width, *refs)

    return pl.pallas_call(
        body,
        out_shape=jax.ShapeDtypeStruct((routes.shape[0], NX * NZ * NC * width), jnp.bfloat16),
        in_specs=[smem, smem] + [vmem] * (1 + len(parts)),
        out_specs=vmem,
        compiler_params=pltpu.CompilerParams(vmem_limit_bytes=32 * 1024 * 1024),
    )(block_places(), (dp % NC).astype(jnp.int32).reshape(1), onehot, *parts)


def solution(mesh):
    return jax.shard_map(
        shards,
        mesh=mesh,
        in_specs=(
            P(("dp", "expert", "tensor"), None),
            P("dp", "expert", None, None, None, "tensor"),
            P("expert", "dp", "tensor"),
        ),
        out_specs=P(("dp", "expert", "tensor"), None),
        check_vma=False,
    )
```

time: 224 us -> 210 us (0.938)
  the two profiles are of different devices: /device:TPU:64 before, /device:TPU:1 now
where the time goes in v1:
time: 210 us; the launch traced here: 207 us
  starting transfers between devices  151 us (72%)
  waiting for transfers between devices  36 us (17%)
  other arithmetic  9 us (4%)
  matrix products  6.51 us (3%)
    ppermute x9, starting transfers between devices, sum_over_tensor(): from_above = lax.ppermute(going_down, 'tensor', down)  34.9 us
    ppermute x7, starting transfers between devices, gather_weight(): move = lambda value, perm: lax.ppermute(value, 'dp', perm)  34.6 us
    ppermute x7, waiting for transfers between devices, gather_weight(): move = lambda value, perm: lax.ppermute(value, 'dp', perm)  21.9 us
    ppermute x3, starting transfers between devices, exchange(): got = lax.ppermute(give, 'expert', [(0, 1), (1, 0)])  21.4 us
    ppermute x9, starting transfers between devices, sum_over_tensor(): from_below = lax.ppermute(going_up, 'tensor', up)  19.9 us
    ppermute x3, starting transfers between devices, exchange(): return (both[0], lax.ppermute(both[1], 'dp', SWAP_CORE))  15.9 us
    ppermute x3, starting transfers between devices, sum_over_tensor(): last = lax.ppermute(partial[mid, half_rows:], 'tensor', down)  12.5 us
    ppermute x3, waiting for transfers between devices, exchange(): got = lax.ppermute(give, 'expert', [(0, 1), (1, 0)])  7.62 us
  transfers between devices with their start and end apart: 38, of which 8 were waited for; matrix products, arithmetic and copies ran while one was open for 7% of the time, Pallas kernels for 0%

profile of v1, /device:TPU:1, one launch (start us, length us, event | category | flops | bytes accessed | tf_op | source)
XLA Modules:
  0.0 206.6 jit_solution(10203046715102600073)
XLA Ops:
  0.0 8.4 %collective-permute-start.1 = (bf16[64,1024]{1,0:T(8,128)(2,1)}, bf16[64,1024]{1,0:T(8,128)(2,1)S(1)}, u32[]{:S(2)}, u32[]{:S(2)}) collective-permute-start(bf16[64,1024]{1,0:T(8,128)(2,1)} %bitcast.167), channel_id=1, source_target_pairs={{0,96},{16,112},{32,128},{48,144},{64,160},{80,176},{96,0},{112,16... | collective-permute-start | bytes 393224 | tf_op jit(solution)/shard_map/ppermute | solution.py:34
  8.4 2.6 %collective-permute-done.1 = bf16[64,1024]{1,0:T(8,128)(2,1)S(1)} collective-permute-done((bf16[64,1024]{1,0:T(8,128)(2,1)}, bf16[64,1024]{1,0:T(8,128)(2,1)S(1)}, u32[]{:S(2)}, u32[]{:S(2)}) %collective-permute-start.1) | collective-permute-done | bytes 131104 | tf_op jit(solution)/shard_map/ppermute | solution.py:34
  11.0 0.9 pad_maximum_fusion.3
  11.9 8.9 %collective-permute-start.2 = (bf16[2,64,1024]{2,1,0:T(8,128)(2,1)S(1)}, bf16[2,64,1024]{2,1,0:T(8,128)(2,1)S(1)}, u32[]{:S(2)}, u32[]{:S(2)}) collective-permute-start(bf16[2,64,1024]{2,1,0:T(8,128)(2,1)S(1)} %pad_maximum_fusion.3), channel_id=1, source_target_pairs={{0,32},{16,48},{32,64},{48,80},{64,0},{80,16},{96,128},{112,144},{... | collective-permute-start | bytes 786440 | tf_op jit(solution)/shard_map/ppermute | solution.py:34
  20.8 4.3 %collective-permute-start.3 = (bf16[2,64,1024]{2,1,0:T(8,128)(2,1)S(1)}, bf16[2,64,1024]{2,1,0:T(8,128)(2,1)S(1)}, u32[]{:S(2)}, u32[]{:S(2)}) collective-permute-start(bf16[2,64,1024]{2,1,0:T(8,128)(2,1)S(1)} %pad_maximum_fusion.3), channel_id=1, source_target_pairs={{0,64},{16,80},{32,0},{48,16},{64,32},{80,48},{96,160},{112,176},{... | collective-permute-start | bytes 786440 | tf_op jit(solution)/shard_map/ppermute | solution.py:34
  25.1 4.8 %collective-permute-start = (bf16[8,80,1024]{2,1,0:T(8,128)(2,1)}, bf16[8,80,1024]{2,1,0:T(8,128)(2,1)}, u32[]{:S(2)}, u32[]{:S(2)}) collective-permute-start(bf16[8,80,1024]{2,1,0:T(8,128)(2,1)} %bitcast.158), channel_id=1, source_target_pairs={{0,16},{16,0},{32,48},{48,32},{64,80},{80,64},{96,112},{112,96},{1... | collective-permute-start | bytes 3932168 | tf_op jit(solution)/shard_map/ppermute | solution.py:116
  29.9 5.5 %collective-permute-done.3 = bf16[2,64,1024]{2,1,0:T(8,128)(2,1)S(1)} collective-permute-done((bf16[2,64,1024]{2,1,0:T(8,128)(2,1)S(1)}, bf16[2,64,1024]{2,1,0:T(8,128)(2,1)S(1)}, u32[]{:S(2)}, u32[]{:S(2)}) %collective-permute-start.3) | collective-permute-done | bytes 262176 | tf_op jit(solution)/shard_map/ppermute | solution.py:34
  35.4 1.9 pad_maximum_fusion.1
  37.3 2.5 %collective-permute-start.14 = (bf16[6,64,1024]{2,1,0:T(8,128)(2,1)}, bf16[6,64,1024]{2,1,0:T(8,128)(2,1)S(1)}, u32[]{:S(2)}, u32[]{:S(2)}) collective-permute-start(bf16[6,64,1024]{2,1,0:T(8,128)(2,1)} %pad_maximum_fusion.1), channel_id=1, source_target_pairs={{0,192},{16,208},{32,224},{48,240},{64,256},{80,272},{96,288},{112... | collective-permute-start | bytes 2359304 | tf_op jit(solution)/shard_map/ppermute | solution.py:34
  39.9 3.9 %collective-permute-start.15 = (bf16[6,64,1024]{2,1,0:T(8,128)(2,1)}, bf16[6,64,1024]{2,1,0:T(8,128)(2,1)S(1)}, u32[]{:S(2)}, u32[]{:S(2)}) collective-permute-start(bf16[6,64,1024]{2,1,0:T(8,128)(2,1)} %pad_maximum_fusion.1), channel_id=1, source_target_pairs={{0,576},{16,592},{32,608},{48,624},{64,640},{80,656},{96,672},{112... | collective-permute-start | bytes 2359304 | tf_op jit(solution)/shard_map/ppermute | solution.py:34
  43.8 0.7 compare_reduce_fusion
  44.5 0.1 copy.20
  44.6 0.2 reduce_window_sum.11
  44.9 0.1 copy.22
  45.0 0.1 copy.24
  45.2 0.1 eq.57
  45.2 13.8 %collective-permute-done.14 = bf16[6,64,1024]{2,1,0:T(8,128)(2,1)S(1)} collective-permute-done((bf16[6,64,1024]{2,1,0:T(8,128)(2,1)}, bf16[6,64,1024]{2,1,0:T(8,128)(2,1)S(1)}, u32[]{:S(2)}, u32[]{:S(2)}) %collective-permute-start.14) | collective-permute-done | bytes 786464 | tf_op jit(solution)/shard_map/ppermute | solution.py:34
  59.1 1.9 collective-permute-start.26
  61.1 4.6 %collective-permute-start.27 = (bf16[3,64,1024]{2,1,0:T(8,128)(2,1)S(1)}, bf16[3,64,1024]{2,1,0:T(8,128)(2,1)S(1)}, u32[]{:S(2)}, u32[]{:S(2)}) collective-permute-start(bf16[3,64,1024]{2,1,0:T(8,128)(2,1)S(1)} %slice.212), channel_id=1, source_target_pairs={{0,576},{16,592},{32,608},{48,624},{64,640},{80,656},{96,672},{112... | collective-permute-start | bytes 1179656 | tf_op jit(solution)/shard_map/ppermute | solution.py:34
  65.7 0.1 pad_maximum_fusion
  65.8 4.0 %fusion.1 = bf16[8,160,1024]{2,1,0:T(8,128)(2,1)S(1)} fusion(s32[]{:T(128)S(6)} %select_n.109, bf16[8,80,1024]{2,1,0:T(8,128)(2,1)S(1)} %bitcast.159, bf16[8,80,1024]{2,1,0:T(8,128)(2,1)} %collective-permute-done), kind=kLoop, calls=%fused_computation.8 | loop fusion | flops 10485760 | bytes 5242884 | tf_op jit(solution)/shard_map/concatenate | solution.py:118
  69.8 2.3 %convolution_convert_fusion = bf16[1280,768]{1,0:T(8,128)(2,1)S(1)} fusion(bf16[1280,1024]{1,0:T(8,128)(2,1)S(1)} %bitcast.152, bf16[768,1024]{1,0:T(8,128)(2,1)S(1)} %bitcast.157), kind=kOutput, calls=%fused_computation.4 | convolution fusion | flops 2014248960 | bytes 6160384 | tf_op jit(solution)/shard_map/dot_general | solution.py:125
  72.1 2.7 %convolution_convert_fusion.2 = bf16[1280,384]{1,0:T(8,128)(2,1)S(1)} fusion(bf16[1280,1024]{1,0:T(8,128)(2,1)S(1)} %bitcast.153, bf16[384,1024]{1,0:T(8,128)(2,1)} %bitcast.31), kind=kOutput, calls=%fused_computation.6 | convolution fusion | flops 1007124480 | bytes 4390912 | tf_op jit(solution)/shard_map/dot_general | solution.py:125
  74.8 2.8 %collective-permute-start.4 = (bf16[80,384]{1,0:T(8,128)(2,1)S(1)}, bf16[80,384]{1,0:T(8,128)(2,1)S(1)}, u32[]{:S(2)}, u32[]{:S(2)}) collective-permute-start(bf16[80,384]{1,0:T(8,128)(2,1)S(1)} %get-tuple-element.25), channel_id=1, source_target_pairs={{0,1},{1,2},{2,3},{3,4},{4,5},{5,6},{6,7},{7,0},{8,9},{9,10},{10,1... | collective-permute-start | bytes 184328 | tf_op jit(solution)/shard_map/ppermute | solution.py:63
  77.6 3.8 %collective-permute-start.8 = (bf16[80,384]{1,0:T(8,128)(2,1)S(1)}, bf16[80,384]{1,0:T(8,128)(2,1)S(1)}, u32[]{:S(2)}, u32[]{:S(2)}) collective-permute-start(bf16[80,384]{1,0:T(8,128)(2,1)S(1)} %get-tuple-element.26), channel_id=1, source_target_pairs={{0,7},{1,0},{2,1},{3,2},{4,3},{5,4},{6,5},{7,6},{8,15},{9,8},{10,9... | collective-permute-start | bytes 184328 | tf_op jit(solution)/shard_map/ppermute | solution.py:64
  81.5 1.9 collective-permute-start.16
  83.5 4.6 %collective-permute-start.20 = (bf16[80,768]{1,0:T(8,128)(2,1)S(1)}, bf16[80,768]{1,0:T(8,128)(2,1)S(1)}, u32[]{:S(2)}, u32[]{:S(2)}) collective-permute-start(bf16[80,768]{1,0:T(8,128)(2,1)S(1)} %get-tuple-element.10), channel_id=1, source_target_pairs={{0,7},{1,0},{2,1},{3,2},{4,3},{5,4},{6,5},{7,6},{8,15},{9,8},{10,9... | collective-permute-start | bytes 368648 | tf_op jit(solution)/shard_map/ppermute | solution.py:64
  88.1 1.9 collective-permute-start.5
  90.1 4.6 %collective-permute-start.9 = (bf16[160,384]{1,0:T(8,128)(2,1)S(1)}, bf16[160,384]{1,0:T(8,128)(2,1)S(1)}, u32[]{:S(2)}, u32[]{:S(2)}) collective-permute-start(bf16[160,384]{1,0:T(8,128)(2,1)S(1)} %pad_maximum_fusion.8), channel_id=1, source_target_pairs={{0,7},{1,0},{2,1},{3,2},{4,3},{5,4},{6,5},{7,6},{8,15},{9,8},{10,9... | collective-permute-start | bytes 368648 | tf_op jit(solution)/shard_map/ppermute | solution.py:70
  94.8 1.9 collective-permute-start.17
  96.7 4.6 %collective-permute-start.21 = (bf16[160,768]{1,0:T(8,128)(2,1)S(1)}, bf16[160,768]{1,0:T(8,128)(2,1)S(1)}, u32[]{:S(2)}, u32[]{:S(2)}) collective-permute-start(bf16[160,768]{1,0:T(8,128)(2,1)S(1)} %pad_maximum_fusion.5), channel_id=1, source_target_pairs={{0,7},{1,0},{2,1},{3,2},{4,3},{5,4},{6,5},{7,6},{8,15},{9,8},{10,9... | collective-permute-start | bytes 737288 | tf_op jit(solution)/shard_map/ppermute | solution.py:70
  101.4 1.9 collective-permute-start.6
  103.4 1.6 convolution_convert_fusion.1
  105.0 2.4 %collective-permute-start.28 = (bf16[80,384]{1,0:T(8,128)(2,1)S(1)}, bf16[80,384]{1,0:T(8,128)(2,1)S(1)}, u32[]{:S(2)}, u32[]{:S(2)}) collective-permute-start(bf16[80,384]{1,0:T(8,128)(2,1)S(1)} %get-tuple-element.17), channel_id=1, source_target_pairs={{0,1},{1,2},{2,3},{3,4},{4,5},{5,6},{6,7},{7,0},{8,9},{9,10},{10,1... | collective-permute-start | bytes 184328 | tf_op jit(solution)/shard_map/ppermute | solution.py:63
  107.4 4.1 %collective-permute-start.32 = (bf16[80,384]{1,0:T(8,128)(2,1)S(1)}, bf16[80,384]{1,0:T(8,128)(2,1)S(1)}, u32[]{:S(2)}, u32[]{:S(2)}) collective-permute-start(bf16[80,384]{1,0:T(8,128)(2,1)S(1)} %get-tuple-element.18), channel_id=1, source_target_pairs={{0,7},{1,0},{2,1},{3,2},{4,3},{5,4},{6,5},{7,6},{8,15},{9,8},{10,9... | collective-permute-start | bytes 184328 | tf_op jit(solution)/shard_map/ppermute | solution.py:64
  111.5 0.1 add_convert_fusion.13
  111.6 3.4 %collective-permute-start.10 = (bf16[160,384]{1,0:T(8,128)(2,1)S(1)}, bf16[160,384]{1,0:T(8,128)(2,1)S(1)}, u32[]{:S(2)}, u32[]{:S(2)}) collective-permute-start(bf16[160,384]{1,0:T(8,128)(2,1)S(1)} %get-tuple-element.22), channel_id=1, source_target_pairs={{0,7},{1,0},{2,1},{3,2},{4,3},{5,4},{6,5},{7,6},{8,15},{9,8},{10,9... | collective-permute-start | bytes 368648 | tf_op jit(solution)/shard_map/ppermute | solution.py:70
  115.0 1.9 collective-permute-start.7
  117.0 3.6 %collective-permute-start.29 = (bf16[160,384]{1,0:T(8,128)(2,1)S(1)}, bf16[160,384]{1,0:T(8,128)(2,1)S(1)}, u32[]{:S(2)}, u32[]{:S(2)}) collective-permute-start(bf16[160,384]{1,0:T(8,128)(2,1)S(1)} %pad_maximum_fusion.9), channel_id=1, source_target_pairs={{0,1},{1,2},{2,3},{3,4},{4,5},{5,6},{6,7},{7,0},{8,9},{9,10},{10,1... | collective-permute-start | bytes 368648 | tf_op jit(solution)/shard_map/ppermute | solution.py:69
  120.6 2.9 %collective-permute-start.33 = (bf16[160,384]{1,0:T(8,128)(2,1)S(1)}, bf16[160,384]{1,0:T(8,128)(2,1)S(1)}, u32[]{:S(2)}, u32[]{:S(2)}) collective-permute-start(bf16[160,384]{1,0:T(8,128)(2,1)S(1)} %pad_maximum_fusion.10), channel_id=1, source_target_pairs={{0,7},{1,0},{2,1},{3,2},{4,3},{5,4},{6,5},{7,6},{8,15},{9,8},{10,9... | collective-permute-start | bytes 368648 | tf_op jit(solution)/shard_map/ppermute | solution.py:70
  123.6 2.4 %collective-permute-start.18 = (bf16[160,768]{1,0:T(8,128)(2,1)S(1)}, bf16[160,768]{1,0:T(8,128)(2,1)S(1)}, u32[]{:S(2)}, u32[]{:S(2)}) collective-permute-start(bf16[160,768]{1,0:T(8,128)(2,1)S(1)} %add_convert_fusion.4), channel_id=1, source_target_pairs={{0,1},{1,2},{2,3},{3,4},{4,5},{5,6},{6,7},{7,0},{8,9},{9,10},{10,1... | collective-permute-start | bytes 737288 | tf_op jit(solution)/shard_map/ppermute | solution.py:69
  126.1 4.1 %collective-permute-start.11 = (bf16[160,384]{1,0:T(8,128)(2,1)S(1)}, bf16[160,384]{1,0:T(8,128)(2,1)S(1)}, u32[]{:S(2)}, u32[]{:S(2)}) collective-permute-start(bf16[160,384]{1,0:T(8,128)(2,1)S(1)} %add_convert_fusion.11), channel_id=1, source_target_pairs={{0,7},{1,0},{2,1},{3,2},{4,3},{5,4},{6,5},{7,6},{8,15},{9,8},{10,9... | collective-permute-start | bytes 368648 | tf_op jit(solution)/shard_map/ppermute | solution.py:70
  130.2 2.4 %collective-permute-start.30 = (bf16[160,384]{1,0:T(8,128)(2,1)S(1)}, bf16[160,384]{1,0:T(8,128)(2,1)S(1)}, u32[]{:S(2)}, u32[]{:S(2)}) collective-permute-start(bf16[160,384]{1,0:T(8,128)(2,1)S(1)} %add_convert_fusion.9), channel_id=1, source_target_pairs={{0,1},{1,2},{2,3},{3,4},{4,5},{5,6},{6,7},{7,0},{8,9},{9,10},{10,1... | collective-permute-start | bytes 368648 | tf_op jit(solution)/shard_map/ppermute | solution.py:69
  132.6 0.7 collective-permute-done.11
  133.4 14.3 %collective-permute-start.12 = (bf16[2,40,384]{2,1,0:T(8,128)(2,1)S(1)}, bf16[2,40,384]{2,1,0:T(8,128)(2,1)S(1)}, u32[]{:S(2)}, u32[]{:S(2)}) collective-permute-start(bf16[2,40,384]{2,1,0:T(8,128)(2,1)S(1)} %dynamic-slice_bitcast_fusion.2), channel_id=1, source_target_pairs={{0,8},{8,0},{1,9},{9,1},{2,10},{10,2},{3,11},{11,3},{4,12},{12,4},... | collective-permute-start | bytes 184328 | tf_op jit(solution)/shard_map/ppermute | solution.py:84
  147.8 4.1 %collective-permute-start.34 = (bf16[160,384]{1,0:T(8,128)(2,1)S(1)}, bf16[160,384]{1,0:T(8,128)(2,1)S(1)}, u32[]{:S(2)}, u32[]{:S(2)}) collective-permute-start(bf16[160,384]{1,0:T(8,128)(2,1)S(1)} %get-tuple-element.14), channel_id=1, source_target_pairs={{0,7},{1,0},{2,1},{3,2},{4,3},{5,4},{6,5},{7,6},{8,15},{9,8},{10,9... | collective-permute-start | bytes 368648 | tf_op jit(solution)/shard_map/ppermute | solution.py:70
  151.9 1.9 collective-permute-start.31
  153.8 0.1 add_convert_fusion.3
  154.0 4.6 %collective-permute-start.22 = (bf16[160,768]{1,0:T(8,128)(2,1)S(1)}, bf16[160,768]{1,0:T(8,128)(2,1)S(1)}, u32[]{:S(2)}, u32[]{:S(2)}) collective-permute-start(bf16[160,768]{1,0:T(8,128)(2,1)S(1)} %get-tuple-element.6), channel_id=1, source_target_pairs={{0,7},{1,0},{2,1},{3,2},{4,3},{5,4},{6,5},{7,6},{8,15},{9,8},{10,9... | collective-permute-start | bytes 737288 | tf_op jit(solution)/shard_map/ppermute | solution.py:70
  158.6 1.9 collective-permute-start.19
  160.5 9.6 %collective-permute-start.13 = (bf16[80,384]{1,0:T(8,128)(2,1)S(1)}, bf16[80,384]{1,0:T(8,128)(2,1)S(1)}, u32[]{:S(2)}, u32[]{:S(2)}) collective-permute-start(bf16[80,384]{1,0:T(8,128)(2,1)S(1)} %bitcast.176), channel_id=1, source_target_pairs={{0,16},{16,0},{32,48},{48,32},{64,80},{80,64},{96,112},{112,96},{1... | collective-permute-start | bytes 184328 | tf_op jit(solution)/shard_map/ppermute | solution.py:88
  170.2 4.9 %collective-permute-start.35 = (bf16[160,384]{1,0:T(8,128)(2,1)S(1)}, bf16[160,384]{1,0:T(8,128)(2,1)S(1)}, u32[]{:S(2)}, u32[]{:S(2)}) collective-permute-start(bf16[160,384]{1,0:T(8,128)(2,1)S(1)} %add_convert_fusion.6), channel_id=1, source_target_pairs={{0,7},{1,0},{2,1},{3,2},{4,3},{5,4},{6,5},{7,6},{8,15},{9,8},{10,9... | collective-permute-start | bytes 368648 | tf_op jit(solution)/shard_map/ppermute | solution.py:70
  175.2 1.9 collective-permute-start.23
  177.1 0.7 collective-permute-done.35
  177.9 1.9 collective-permute-start.36
  179.8 4.5 %collective-permute-done.23 = bf16[160,768]{1,0:T(8,128)(2,1)S(1)} collective-permute-done((bf16[160,768]{1,0:T(8,128)(2,1)S(1)}, bf16[160,768]{1,0:T(8,128)(2,1)S(1)}, u32[]{:S(2)}, u32[]{:S(2)}) %collective-permute-start.23) | collective-permute-done | bytes 245792 | tf_op jit(solution)/shard_map/ppermute | solution.py:70
  184.3 0.1 add_convert_fusion
  184.4 5.2 %collective-permute-start.24 = (bf16[2,40,768]{2,1,0:T(8,128)(2,1)S(1)}, bf16[2,40,768]{2,1,0:T(8,128)(2,1)S(1)}, u32[]{:S(2)}, u32[]{:S(2)}) collective-permute-start(bf16[2,40,768]{2,1,0:T(8,128)(2,1)S(1)} %dynamic-slice_bitcast_fusion), channel_id=1, source_target_pairs={{0,8},{8,0},{1,9},{9,1},{2,10},{10,2},{3,11},{11,3},{4,12},{12,4},... | collective-permute-start | bytes 368648 | tf_op jit(solution)/shard_map/ppermute | solution.py:84
  189.7 3.9 %collective-permute-start.37 = (bf16[80,384]{1,0:T(8,128)(2,1)S(1)}, bf16[80,384]{1,0:T(8,128)(2,1)S(1)}, u32[]{:S(2)}, u32[]{:S(2)}) collective-permute-start(bf16[80,384]{1,0:T(8,128)(2,1)S(1)} %bitcast.177), channel_id=1, source_target_pairs={{0,16},{16,0},{32,48},{48,32},{64,80},{80,64},{96,112},{112,96},{1... | collective-permute-start | bytes 184328 | tf_op jit(solution)/shard_map/ppermute | solution.py:88
  193.6 7.6 %collective-permute-done.24 = bf16[2,40,768]{2,1,0:T(8,128)(2,1)S(1)} collective-permute-done((bf16[2,40,768]{2,1,0:T(8,128)(2,1)S(1)}, bf16[2,40,768]{2,1,0:T(8,128)(2,1)S(1)}, u32[]{:S(2)}, u32[]{:S(2)}) %collective-permute-start.24) | collective-permute-done | bytes 122912 | tf_op jit(solution)/shard_map/ppermute | solution.py:84
  201.3 2.4 %collective-permute-start.25 = (bf16[80,768]{1,0:T(8,128)(2,1)S(1)}, bf16[80,768]{1,0:T(8,128)(2,1)S(1)}, u32[]{:S(2)}, u32[]{:S(2)}) collective-permute-start(bf16[80,768]{1,0:T(8,128)(2,1)S(1)} %bitcast.175), channel_id=1, source_target_pairs={{0,16},{16,0},{32,48},{48,32},{64,80},{80,64},{96,112},{112,96},{1... | collective-permute-start | bytes 368648 | tf_op jit(solution)/shard_map/ppermute | solution.py:88
  203.9 0.1 stack.132.refs_0_
  204.1 0.6 collective-permute-done.25.refs_6_
  204.7 2.0 shard_map.37
  (72 shorter events, 1.3 us)
Async XLA Ops:
  0.0 11.0 %collective-permute-start.1 = (bf16[64,1024]{1,0:T(8,128)(2,1)}, bf16[64,1024]{1,0:T(8,128)(2,1)S(1)}, u32[]{:S(2)}, u32[]{:S(2)}) collective-permute-start(bf16[64,1024]{1,0:T(8,128)(2,1)} %bitcast.167), channel_id=1, source_target_pairs={{0,96},{16,112},{32,128},{48,144},{64,160},{80,176},{96,0},{112,16... | collective-permute-start | bytes 393224 | tf_op jit(solution)/shard_map/ppermute | solution.py:34
  11.9 18.0 %collective-permute-start.2 = (bf16[2,64,1024]{2,1,0:T(8,128)(2,1)S(1)}, bf16[2,64,1024]{2,1,0:T(8,128)(2,1)S(1)}, u32[]{:S(2)}, u32[]{:S(2)}) collective-permute-start(bf16[2,64,1024]{2,1,0:T(8,128)(2,1)S(1)} %pad_maximum_fusion.3), channel_id=1, source_target_pairs={{0,32},{16,48},{32,64},{48,80},{64,0},{80,16},{96,128},{112,144},{... | collective-permute-start | bytes 786440 | tf_op jit(solution)/shard_map/ppermute | solution.py:34
  20.8 14.6 %collective-permute-start.3 = (bf16[2,64,1024]{2,1,0:T(8,128)(2,1)S(1)}, bf16[2,64,1024]{2,1,0:T(8,128)(2,1)S(1)}, u32[]{:S(2)}, u32[]{:S(2)}) collective-permute-start(bf16[2,64,1024]{2,1,0:T(8,128)(2,1)S(1)} %pad_maximum_fusion.3), channel_id=1, source_target_pairs={{0,64},{16,80},{32,0},{48,16},{64,32},{80,48},{96,160},{112,176},{... | collective-permute-start | bytes 786440 | tf_op jit(solution)/shard_map/ppermute | solution.py:34
  25.1 40.7 %collective-permute-start = (bf16[8,80,1024]{2,1,0:T(8,128)(2,1)}, bf16[8,80,1024]{2,1,0:T(8,128)(2,1)}, u32[]{:S(2)}, u32[]{:S(2)}) collective-permute-start(bf16[8,80,1024]{2,1,0:T(8,128)(2,1)} %bitcast.158), channel_id=1, source_target_pairs={{0,16},{16,0},{32,48},{48,32},{64,80},{80,64},{96,112},{112,96},{1... | collective-permute-start | bytes 3932168 | tf_op jit(solution)/shard_map/ppermute | solution.py:116
  37.3 21.8 %collective-permute-start.14 = (bf16[6,64,1024]{2,1,0:T(8,128)(2,1)}, bf16[6,64,1024]{2,1,0:T(8,128)(2,1)S(1)}, u32[]{:S(2)}, u32[]{:S(2)}) collective-permute-start(bf16[6,64,1024]{2,1,0:T(8,128)(2,1)} %pad_maximum_fusion.1), channel_id=1, source_target_pairs={{0,192},{16,208},{32,224},{48,240},{64,256},{80,272},{96,288},{112... | collective-permute-start | bytes 2359304 | tf_op jit(solution)/shard_map/ppermute | solution.py:34
  39.9 21.2 %collective-permute-start.15 = (bf16[6,64,1024]{2,1,0:T(8,128)(2,1)}, bf16[6,64,1024]{2,1,0:T(8,128)(2,1)S(1)}, u32[]{:S(2)}, u32[]{:S(2)}) collective-permute-start(bf16[6,64,1024]{2,1,0:T(8,128)(2,1)} %pad_maximum_fusion.1), channel_id=1, source_target_pairs={{0,576},{16,592},{32,608},{48,624},{64,640},{80,656},{96,672},{112... | collective-permute-start | bytes 2359304 | tf_op jit(solution)/shard_map/ppermute | solution.py:34
  44.6 21.2 %copy-start = (bf16[1,1,8,2,40,1024]{5,4,3,2,1,0:T(8,128)(2,1)S(1)}, bf16[1,1,8,2,40,1024]{5,4,3,2,1,0:T(8,128)(2,1)}, u32[]{:S(2)}) copy-start(bf16[1,1,8,2,40,1024]{5,4,3,2,1,0:T(8,128)(2,1)} %param.4) | copy-start | bytes 3932164
  59.1 42.3 %collective-permute-start.26 = (bf16[3,64,1024]{2,1,0:T(8,128)(2,1)S(1)}, bf16[3,64,1024]{2,1,0:T(8,128)(2,1)S(1)}, u32[]{:S(2)}, u32[]{:S(2)}) collective-permute-start(bf16[3,64,1024]{2,1,0:T(8,128)(2,1)S(1)} %slice.211), channel_id=1, source_target_pairs={{0,192},{16,208},{32,224},{48,240},{64,256},{80,272},{96,288},{112... | collective-permute-start | bytes 1179656 | tf_op jit(solution)/shard_map/ppermute | solution.py:34
  61.1 42.2 %collective-permute-start.27 = (bf16[3,64,1024]{2,1,0:T(8,128)(2,1)S(1)}, bf16[3,64,1024]{2,1,0:T(8,128)(2,1)S(1)}, u32[]{:S(2)}, u32[]{:S(2)}) collective-permute-start(bf16[3,64,1024]{2,1,0:T(8,128)(2,1)S(1)} %slice.212), channel_id=1, source_target_pairs={{0,576},{16,592},{32,608},{48,624},{64,640},{80,656},{96,672},{112... | collective-permute-start | bytes 1179656 | tf_op jit(solution)/shard_map/ppermute | solution.py:34
  74.8 8.6 %collective-permute-start.4 = (bf16[80,384]{1,0:T(8,128)(2,1)S(1)}, bf16[80,384]{1,0:T(8,128)(2,1)S(1)}, u32[]{:S(2)}, u32[]{:S(2)}) collective-permute-start(bf16[80,384]{1,0:T(8,128)(2,1)S(1)} %get-tuple-element.25), channel_id=1, source_target_pairs={{0,1},{1,2},{2,3},{3,4},{4,5},{5,6},{6,7},{7,0},{8,9},{9,10},{10,1... | collective-permute-start | bytes 184328 | tf_op jit(solution)/shard_map/ppermute | solution.py:63
  77.6 10.4 %collective-permute-start.8 = (bf16[80,384]{1,0:T(8,128)(2,1)S(1)}, bf16[80,384]{1,0:T(8,128)(2,1)S(1)}, u32[]{:S(2)}, u32[]{:S(2)}) collective-permute-start(bf16[80,384]{1,0:T(8,128)(2,1)S(1)} %get-tuple-element.26), channel_id=1, source_target_pairs={{0,7},{1,0},{2,1},{3,2},{4,3},{5,4},{6,5},{7,6},{8,15},{9,8},{10,9... | collective-permute-start | bytes 184328 | tf_op jit(solution)/shard_map/ppermute | solution.py:64
  81.5 8.5 %collective-permute-start.16 = (bf16[80,768]{1,0:T(8,128)(2,1)S(1)}, bf16[80,768]{1,0:T(8,128)(2,1)S(1)}, u32[]{:S(2)}, u32[]{:S(2)}) collective-permute-start(bf16[80,768]{1,0:T(8,128)(2,1)S(1)} %get-tuple-element.9), channel_id=1, source_target_pairs={{0,1},{1,2},{2,3},{3,4},{4,5},{5,6},{6,7},{7,0},{8,9},{9,10},{10,1... | collective-permute-start | bytes 368648 | tf_op jit(solution)/shard_map/ppermute | solution.py:63
  83.5 11.2 %collective-permute-start.20 = (bf16[80,768]{1,0:T(8,128)(2,1)S(1)}, bf16[80,768]{1,0:T(8,128)(2,1)S(1)}, u32[]{:S(2)}, u32[]{:S(2)}) collective-permute-start(bf16[80,768]{1,0:T(8,128)(2,1)S(1)} %get-tuple-element.10), channel_id=1, source_target_pairs={{0,7},{1,0},{2,1},{3,2},{4,3},{5,4},{6,5},{7,6},{8,15},{9,8},{10,9... | collective-permute-start | bytes 368648 | tf_op jit(solution)/shard_map/ppermute | solution.py:64
  88.1 8.6 %collective-permute-start.5 = (bf16[160,384]{1,0:T(8,128)(2,1)S(1)}, bf16[160,384]{1,0:T(8,128)(2,1)S(1)}, u32[]{:S(2)}, u32[]{:S(2)}) collective-permute-start(bf16[160,384]{1,0:T(8,128)(2,1)S(1)} %pad_maximum_fusion.7), channel_id=1, source_target_pairs={{0,1},{1,2},{2,3},{3,4},{4,5},{5,6},{6,7},{7,0},{8,9},{9,10},{10,1... | collective-permute-start | bytes 368648 | tf_op jit(solution)/shard_map/ppermute | solution.py:69
  90.1 17.3 %collective-permute-start.9 = (bf16[160,384]{1,0:T(8,128)(2,1)S(1)}, bf16[160,384]{1,0:T(8,128)(2,1)S(1)}, u32[]{:S(2)}, u32[]{:S(2)}) collective-permute-start(bf16[160,384]{1,0:T(8,128)(2,1)S(1)} %pad_maximum_fusion.8), channel_id=1, source_target_pairs={{0,7},{1,0},{2,1},{3,2},{4,3},{5,4},{6,5},{7,6},{8,15},{9,8},{10,9... | collective-permute-start | bytes 368648 | tf_op jit(solution)/shard_map/ppermute | solution.py:70
  94.8 25.9 %collective-permute-start.17 = (bf16[160,768]{1,0:T(8,128)(2,1)S(1)}, bf16[160,768]{1,0:T(8,128)(2,1)S(1)}, u32[]{:S(2)}, u32[]{:S(2)}) collective-permute-start(bf16[160,768]{1,0:T(8,128)(2,1)S(1)} %pad_maximum_fusion.4), channel_id=1, source_target_pairs={{0,1},{1,2},{2,3},{3,4},{4,5},{5,6},{6,7},{7,0},{8,9},{9,10},{10,1... | collective-permute-start | bytes 737288 | tf_op jit(solution)/shard_map/ppermute | solution.py:69
  96.7 57.1 %collective-permute-start.21 = (bf16[160,768]{1,0:T(8,128)(2,1)S(1)}, bf16[160,768]{1,0:T(8,128)(2,1)S(1)}, u32[]{:S(2)}, u32[]{:S(2)}) collective-permute-start(bf16[160,768]{1,0:T(8,128)(2,1)S(1)} %pad_maximum_fusion.5), channel_id=1, source_target_pairs={{0,7},{1,0},{2,1},{3,2},{4,3},{5,4},{6,5},{7,6},{8,15},{9,8},{10,9... | collective-permute-start | bytes 737288 | tf_op jit(solution)/shard_map/ppermute | solution.py:70
  101.4 10.1 %collective-permute-start.6 = (bf16[160,384]{1,0:T(8,128)(2,1)S(1)}, bf16[160,384]{1,0:T(8,128)(2,1)S(1)}, u32[]{:S(2)}, u32[]{:S(2)}) collective-permute-start(bf16[160,384]{1,0:T(8,128)(2,1)S(1)} %add_convert_fusion.14), channel_id=1, source_target_pairs={{0,1},{1,2},{2,3},{3,4},{4,5},{5,6},{6,7},{7,0},{8,9},{9,10},{10,1... | collective-permute-start | bytes 368648 | tf_op jit(solution)/shard_map/ppermute | solution.py:69
  105.0 10.0 %collective-permute-start.28 = (bf16[80,384]{1,0:T(8,128)(2,1)S(1)}, bf16[80,384]{1,0:T(8,128)(2,1)S(1)}, u32[]{:S(2)}, u32[]{:S(2)}) collective-permute-start(bf16[80,384]{1,0:T(8,128)(2,1)S(1)} %get-tuple-element.17), channel_id=1, source_target_pairs={{0,1},{1,2},{2,3},{3,4},{4,5},{5,6},{6,7},{7,0},{8,9},{9,10},{10,1... | collective-permute-start | bytes 184328 | tf_op jit(solution)/shard_map/ppermute | solution.py:63
  107.4 9.5 %collective-permute-start.32 = (bf16[80,384]{1,0:T(8,128)(2,1)S(1)}, bf16[80,384]{1,0:T(8,128)(2,1)S(1)}, u32[]{:S(2)}, u32[]{:S(2)}) collective-permute-start(bf16[80,384]{1,0:T(8,128)(2,1)S(1)} %get-tuple-element.18), channel_id=1, source_target_pairs={{0,7},{1,0},{2,1},{3,2},{4,3},{5,4},{6,5},{7,6},{8,15},{9,8},{10,9... | collective-permute-start | bytes 184328 | tf_op jit(solution)/shard_map/ppermute | solution.py:64
  111.6 12.0 %collective-permute-start.10 = (bf16[160,384]{1,0:T(8,128)(2,1)S(1)}, bf16[160,384]{1,0:T(8,128)(2,1)S(1)}, u32[]{:S(2)}, u32[]{:S(2)}) collective-permute-start(bf16[160,384]{1,0:T(8,128)(2,1)S(1)} %get-tuple-element.22), channel_id=1, source_target_pairs={{0,7},{1,0},{2,1},{3,2},{4,3},{5,4},{6,5},{7,6},{8,15},{9,8},{10,9... | collective-permute-start | bytes 368648 | tf_op jit(solution)/shard_map/ppermute | solution.py:70
  115.0 15.2 %collective-permute-start.7 = (bf16[160,384]{1,0:T(8,128)(2,1)S(1)}, bf16[160,384]{1,0:T(8,128)(2,1)S(1)}, u32[]{:S(2)}, u32[]{:S(2)}) collective-permute-start(bf16[160,384]{1,0:T(8,128)(2,1)S(1)} %get-tuple-element.21), channel_id=1, source_target_pairs={{0,1},{1,2},{2,3},{3,4},{4,5},{5,6},{6,7},{7,0},{8,9},{9,10},{10,1... | collective-permute-start | bytes 368648 | tf_op jit(solution)/shard_map/ppermute | solution.py:69
  117.0 9.1 %collective-permute-start.29 = (bf16[160,384]{1,0:T(8,128)(2,1)S(1)}, bf16[160,384]{1,0:T(8,128)(2,1)S(1)}, u32[]{:S(2)}, u32[]{:S(2)}) collective-permute-start(bf16[160,384]{1,0:T(8,128)(2,1)S(1)} %pad_maximum_fusion.9), channel_id=1, source_target_pairs={{0,1},{1,2},{2,3},{3,4},{4,5},{5,6},{6,7},{7,0},{8,9},{9,10},{10,1... | collective-permute-start | bytes 368648 | tf_op jit(solution)/shard_map/ppermute | solution.py:69
  120.6 27.1 %collective-permute-start.33 = (bf16[160,384]{1,0:T(8,128)(2,1)S(1)}, bf16[160,384]{1,0:T(8,128)(2,1)S(1)}, u32[]{:S(2)}, u32[]{:S(2)}) collective-permute-start(bf16[160,384]{1,0:T(8,128)(2,1)S(1)} %pad_maximum_fusion.10), channel_id=1, source_target_pairs={{0,7},{1,0},{2,1},{3,2},{4,3},{5,4},{6,5},{7,6},{8,15},{9,8},{10,9... | collective-permute-start | bytes 368648 | tf_op jit(solution)/shard_map/ppermute | solution.py:70
  123.6 30.2 %collective-permute-start.18 = (bf16[160,768]{1,0:T(8,128)(2,1)S(1)}, bf16[160,768]{1,0:T(8,128)(2,1)S(1)}, u32[]{:S(2)}, u32[]{:S(2)}) collective-permute-start(bf16[160,768]{1,0:T(8,128)(2,1)S(1)} %add_convert_fusion.4), channel_id=1, source_target_pairs={{0,1},{1,2},{2,3},{3,4},{4,5},{5,6},{6,7},{7,0},{8,9},{9,10},{10,1... | collective-permute-start | bytes 737288 | tf_op jit(solution)/shard_map/ppermute | solution.py:69
  126.1 7.2 %collective-permute-start.11 = (bf16[160,384]{1,0:T(8,128)(2,1)S(1)}, bf16[160,384]{1,0:T(8,128)(2,1)S(1)}, u32[]{:S(2)}, u32[]{:S(2)}) collective-permute-start(bf16[160,384]{1,0:T(8,128)(2,1)S(1)} %add_convert_fusion.11), channel_id=1, source_target_pairs={{0,7},{1,0},{2,1},{3,2},{4,3},{5,4},{6,5},{7,6},{8,15},{9,8},{10,9... | collective-permute-start | bytes 368648 | tf_op jit(solution)/shard_map/ppermute | solution.py:70
  130.2 17.5 %collective-permute-start.30 = (bf16[160,384]{1,0:T(8,128)(2,1)S(1)}, bf16[160,384]{1,0:T(8,128)(2,1)S(1)}, u32[]{:S(2)}, u32[]{:S(2)}) collective-permute-start(bf16[160,384]{1,0:T(8,128)(2,1)S(1)} %add_convert_fusion.9), channel_id=1, source_target_pairs={{0,1},{1,2},{2,3},{3,4},{4,5},{5,6},{6,7},{7,0},{8,9},{9,10},{10,1... | collective-permute-start | bytes 368648 | tf_op jit(solution)/shard_map/ppermute | solution.py:69
  133.4 27.1 %collective-permute-start.12 = (bf16[2,40,384]{2,1,0:T(8,128)(2,1)S(1)}, bf16[2,40,384]{2,1,0:T(8,128)(2,1)S(1)}, u32[]{:S(2)}, u32[]{:S(2)}) collective-permute-start(bf16[2,40,384]{2,1,0:T(8,128)(2,1)S(1)} %dynamic-slice_bitcast_fusion.2), channel_id=1, source_target_pairs={{0,8},{8,0},{1,9},{9,1},{2,10},{10,2},{3,11},{11,3},{4,12},{12,4},... | collective-permute-start | bytes 184328 | tf_op jit(solution)/shard_map/ppermute | solution.py:84
  147.8 22.4 %collective-permute-start.34 = (bf16[160,384]{1,0:T(8,128)(2,1)S(1)}, bf16[160,384]{1,0:T(8,128)(2,1)S(1)}, u32[]{:S(2)}, u32[]{:S(2)}) collective-permute-start(bf16[160,384]{1,0:T(8,128)(2,1)S(1)} %get-tuple-element.14), channel_id=1, source_target_pairs={{0,7},{1,0},{2,1},{3,2},{4,3},{5,4},{6,5},{7,6},{8,15},{9,8},{10,9... | collective-permute-start | bytes 368648 | tf_op jit(solution)/shard_map/ppermute | solution.py:70
  151.9 25.2 %collective-permute-start.31 = (bf16[160,384]{1,0:T(8,128)(2,1)S(1)}, bf16[160,384]{1,0:T(8,128)(2,1)S(1)}, u32[]{:S(2)}, u32[]{:S(2)}) collective-permute-start(bf16[160,384]{1,0:T(8,128)(2,1)S(1)} %get-tuple-element.13), channel_id=1, source_target_pairs={{0,1},{1,2},{2,3},{3,4},{4,5},{5,6},{6,7},{7,0},{8,9},{9,10},{10,1... | collective-permute-start | bytes 368648 | tf_op jit(solution)/shard_map/ppermute | solution.py:69
  154.0 21.1 %collective-permute-start.22 = (bf16[160,768]{1,0:T(8,128)(2,1)S(1)}, bf16[160,768]{1,0:T(8,128)(2,1)S(1)}, u32[]{:S(2)}, u32[]{:S(2)}) collective-permute-start(bf16[160,768]{1,0:T(8,128)(2,1)S(1)} %get-tuple-element.6), channel_id=1, source_target_pairs={{0,7},{1,0},{2,1},{3,2},{4,3},{5,4},{6,5},{7,6},{8,15},{9,8},{10,9... | collective-permute-start | bytes 737288 | tf_op jit(solution)/shard_map/ppermute | solution.py:70
  158.6 21.2 %collective-permute-start.19 = (bf16[160,768]{1,0:T(8,128)(2,1)S(1)}, bf16[160,768]{1,0:T(8,128)(2,1)S(1)}, u32[]{:S(2)}, u32[]{:S(2)}) collective-permute-start(bf16[160,768]{1,0:T(8,128)(2,1)S(1)} %get-tuple-element.5), channel_id=1, source_target_pairs={{0,1},{1,2},{2,3},{3,4},{4,5},{5,6},{6,7},{7,0},{8,9},{9,10},{10,1... | collective-permute-start | bytes 737288 | tf_op jit(solution)/shard_map/ppermute | solution.py:69
  160.5 43.5 %collective-permute-start.13 = (bf16[80,384]{1,0:T(8,128)(2,1)S(1)}, bf16[80,384]{1,0:T(8,128)(2,1)S(1)}, u32[]{:S(2)}, u32[]{:S(2)}) collective-permute-start(bf16[80,384]{1,0:T(8,128)(2,1)S(1)} %bitcast.176), channel_id=1, source_target_pairs={{0,16},{16,0},{32,48},{48,32},{64,80},{80,64},{96,112},{112,96},{1... | collective-permute-start | bytes 184328 | tf_op jit(solution)/shard_map/ppermute | solution.py:88
  170.2 7.6 %collective-permute-start.35 = (bf16[160,384]{1,0:T(8,128)(2,1)S(1)}, bf16[160,384]{1,0:T(8,128)(2,1)S(1)}, u32[]{:S(2)}, u32[]{:S(2)}) collective-permute-start(bf16[160,384]{1,0:T(8,128)(2,1)S(1)} %add_convert_fusion.6), channel_id=1, source_target_pairs={{0,7},{1,0},{2,1},{3,2},{4,3},{5,4},{6,5},{7,6},{8,15},{9,8},{10,9... | collective-permute-start | bytes 368648 | tf_op jit(solution)/shard_map/ppermute | solution.py:70
  175.2 9.2 %collective-permute-start.23 = (bf16[160,768]{1,0:T(8,128)(2,1)S(1)}, bf16[160,768]{1,0:T(8,128)(2,1)S(1)}, u32[]{:S(2)}, u32[]{:S(2)}) collective-permute-start(bf16[160,768]{1,0:T(8,128)(2,1)S(1)} %add_convert_fusion.1), channel_id=1, source_target_pairs={{0,7},{1,0},{2,1},{3,2},{4,3},{5,4},{6,5},{7,6},{8,15},{9,8},{10,9... | collective-permute-start | bytes 737288 | tf_op jit(solution)/shard_map/ppermute | solution.py:70
  177.9 11.8 %collective-permute-start.36 = (bf16[2,40,384]{2,1,0:T(8,128)(2,1)S(1)}, bf16[2,40,384]{2,1,0:T(8,128)(2,1)S(1)}, u32[]{:S(2)}, u32[]{:S(2)}) collective-permute-start(bf16[2,40,384]{2,1,0:T(8,128)(2,1)S(1)} %dynamic-slice_bitcast_fusion.1), channel_id=1, source_target_pairs={{0,8},{8,0},{1,9},{9,1},{2,10},{10,2},{3,11},{11,3},{4,12},{12,4},... | collective-permute-start | bytes 184328 | tf_op jit(solution)/shard_map/ppermute | solution.py:84
  184.4 16.8 %collective-permute-start.24 = (bf16[2,40,768]{2,1,0:T(8,128)(2,1)S(1)}, bf16[2,40,768]{2,1,0:T(8,128)(2,1)S(1)}, u32[]{:S(2)}, u32[]{:S(2)}) collective-permute-start(bf16[2,40,768]{2,1,0:T(8,128)(2,1)S(1)} %dynamic-slice_bitcast_fusion), channel_id=1, source_target_pairs={{0,8},{8,0},{1,9},{9,1},{2,10},{10,2},{3,11},{11,3},{4,12},{12,4},... | collective-permute-start | bytes 368648 | tf_op jit(solution)/shard_map/ppermute | solution.py:84
  189.7 14.4 %collective-permute-start.37 = (bf16[80,384]{1,0:T(8,128)(2,1)S(1)}, bf16[80,384]{1,0:T(8,128)(2,1)S(1)}, u32[]{:S(2)}, u32[]{:S(2)}) collective-permute-start(bf16[80,384]{1,0:T(8,128)(2,1)S(1)} %bitcast.177), channel_id=1, source_target_pairs={{0,16},{16,0},{32,48},{48,32},{64,80},{80,64},{96,112},{112,96},{1... | collective-permute-start | bytes 184328 | tf_op jit(solution)/shard_map/ppermute | solution.py:88
  201.3 3.4 %collective-permute-start.25 = (bf16[80,768]{1,0:T(8,128)(2,1)S(1)}, bf16[80,768]{1,0:T(8,128)(2,1)S(1)}, u32[]{:S(2)}, u32[]{:S(2)}) collective-permute-start(bf16[80,768]{1,0:T(8,128)(2,1)S(1)} %bitcast.175), channel_id=1, source_target_pairs={{0,16},{16,0},{32,48},{48,32},{64,80},{80,64},{96,112},{112,96},{1... | collective-permute-start | bytes 368648 | tf_op jit(solution)/shard_map/ppermute | solution.py:88

commit v2 on v0

v2 whole, which is shorter than its diff:
```python
import jax
import jax.numpy as jnp
from jax import lax
from jax.experimental import pallas as pl
from jax.experimental.pallas import tpu as pltpu
from jax.sharding import Mesh, PartitionSpec as P

SIZES = {"x": 4, "h": 2, "m": 3, "c": 2, "e": 2, "q": 4, "p": 2}
GROUPS = ((0, 2), (2, 3))


def spread(value, axis):
    count = SIZES[axis]
    return lax.all_to_all(jnp.broadcast_to(value[None], (count,) + value.shape), axis, 0, 0)


def gather_weight(slab):
    width, hidden = slab.shape
    halves = slab.reshape(SIZES["p"], width // SIZES["p"], hidden)
    sent = jnp.broadcast_to(halves[None], (SIZES["h"],) + halves.shape)
    got = lax.all_to_all(sent.reshape((-1,) + halves.shape[1:]), ("h", "p"), 0, 0)
    got = got.reshape((SIZES["h"],) + halves.shape).transpose(0, 2, 1, 3)
    column = spread(got, "m")
    return [spread(column[low:high], "x") for low, high in GROUPS]


def gather_rows(own):
    def both(value, axis, at):
        other = lax.ppermute(value, axis, [(0, 1), (1, 0)])
        first = lax.axis_index(axis) == 0
        return jnp.stack([jnp.where(first, value, other), jnp.where(first, other, value)], axis=at)

    return both(both(own, "p", 2), "c", 1)


def place_kernel(out, onehot, pieces, width):
    columns = []
    count = SIZES["m"] * SIZES["h"]
    for x in range(SIZES["x"]):
        for z in range(count):
            h, m = z // SIZES["m"], z % SIZES["m"]
            for group, (low, high) in enumerate(GROUPS):
                if low <= m < high:
                    at = ((x * (high - low) + m - low) * SIZES["h"] + h) * width
                    for c in range(SIZES["c"]):
                        for p in range(SIZES["p"]):
                            columns.append(pieces[group][p * SIZES["c"] + c, :, at:at + width])
    tile = SIZES["c"] * SIZES["p"]
    for start in range(0, len(columns), tile):
        block = jnp.concatenate(columns[start:start + tile], axis=1)
        result = jnp.dot(onehot[...], block, preferred_element_type=jnp.float32)
        out[:, start * width:(start + tile) * width] = result.astype(out.dtype)


def shards(routes, upgrad, weight):
    _, _, tensor_count, owners, capacity, hidden = upgrad.shape
    slab = weight[0]
    width = slab.shape[0] // SIZES["p"]
    rows = owners * capacity

    weights = gather_weight(slab)
    grads = gather_rows(upgrad.reshape(tensor_count, rows, hidden))
    flat = grads.reshape(-1, SIZES["p"] * hidden)

    pieces = []
    for blocks in weights:
        blocks = blocks.reshape(-1, SIZES["p"] * hidden)
        features = blocks.shape[0]
        partial = lax.dot_general(
            flat, blocks, (((1,), (1,)), ((), ())), preferred_element_type=jnp.float32
        ).astype(jnp.bfloat16)
        parts = lax.all_to_all(partial.reshape(SIZES["q"], -1, features), "q", 0, 0)
        summed = jnp.sum(parts.astype(jnp.float32), axis=0).astype(jnp.bfloat16)
        returned = lax.all_to_all(summed.reshape(-1, capacity, features), ("p", "c", "e"), 0, 0)
        pieces.append(returned.reshape(-1, rows, features))

    owner_ids = lax.iota(jnp.int32, owners)
    is_routed = jnp.any(routes[:, :, None] == owner_ids[None, None, :], axis=1)
    slot_index = jnp.cumsum(is_routed.astype(jnp.int32), axis=0) - 1
    onehot = is_routed[:, :, None] & (slot_index[:, :, None] == lax.iota(jnp.int32, capacity)[None, None, :])
    onehot = onehot.reshape(routes.shape[0], rows).astype(jnp.bfloat16)

    def body(onehot_ref, *refs):
        place_kernel(refs[-1], onehot_ref, refs[:-1], width)

    vmem = pl.BlockSpec(memory_space=pltpu.VMEM)
    total = sum(piece.shape[0] * piece.shape[2] for piece in pieces)
    return pl.pallas_call(
        body,
        out_shape=jax.ShapeDtypeStruct((routes.shape[0], total), jnp.bfloat16),
        in_specs=[vmem] * (1 + len(pieces)),
        out_specs=vmem,
        compiler_params=pltpu.CompilerParams(vmem_limit_bytes=32 * 1024 * 1024),
    )(onehot, *pieces)


def solution(mesh):
    fine = Mesh(mesh.devices.reshape(tuple(SIZES.values())), tuple(SIZES))
    dp, tensor = ("x", "h", "m", "c"), ("q", "p")
    return jax.shard_map(
        shards,
        mesh=fine,
        in_specs=(
            P(dp + ("e",) + tensor, None),
            P(dp, "e", None, None, None, tensor),
            P("e", dp, tensor),
        ),
        out_specs=P(dp + ("e",) + tensor, None),
        check_vma=False,
    )
```

time: 224 us -> 216 us (0.964)
  the two profiles are of different devices: /device:TPU:64 before, /device:TPU:65 now
where the time goes in v2:
time: 216 us; the launch traced here: 215 us
  waiting for transfers between devices  98.1 us (45%)
  starting transfers between devices  63.3 us (29%)
  local copies, waits for them, and re-layouts  32.6 us (15%)
  other arithmetic  10.4 us (5%)
  matrix products  8.91 us (4%)
    all_to_all x2, waiting for transfers between devices, shards(): parts = lax.all_to_all(partial.reshape(SIZES['q'], -1, features), 'q', 0, 0)  32.3 us
    all_to_all x2, waiting for transfers between devices, shards(): lax.all_to_all(summed.reshape(-1, capacity, features), ('p', 'c', 'e'), 0...  29 us
    all_to_all x1, waiting for transfers between devices, gather_weight(): lax.all_to_all(sent.reshape((-1,) + halves.shape[1:]), ('h', 'p'), 0, 0)  21.6 us
    all_to_all x2, starting transfers between devices, shards(): lax.all_to_all(summed.reshape(-1, capacity, features), ('p', 'c', 'e'), 0...  21 us
    all_to_all x3, waiting for transfers between devices, spread(): lax.all_to_all(jnp.broadcast_to(value[None], (count,) + value.shape), axi...  15.2 us
    all_to_all x2, starting transfers between devices, shards(): parts = lax.all_to_all(partial.reshape(SIZES['q'], -1, features), 'q', 0, 0)  13.6 us
    all_to_all x3, starting transfers between devices, spread(): lax.all_to_all(jnp.broadcast_to(value[None], (count,) + value.shape), axi...  13.4 us
    unnamed x9, local copies, waits for them, and re-layouts  11.7 us
  transfers between devices with their start and end apart: 10, of which 7 were waited for; matrix products, arithmetic and copies ran while one was open for 23% of the time, Pallas kernels for 0%

profile of v2, /device:TPU:65, one launch (start us, length us, event | category | flops | bytes accessed | tf_op | source)
XLA Modules:
  0.0 215.0 jit_solution(1336750646287730842)
XLA Ops:
  0.0 3.2 %collective-permute-start = (bf16[8,80,1024]{2,1,0:T(8,128)(2,1)}, bf16[8,80,1024]{2,1,0:T(8,128)(2,1)}, u32[]{:S(2)}, u32[]{:S(2)}) collective-permute-start(bf16[8,80,1024]{2,1,0:T(8,128)(2,1)} %bitcast.43), channel_id=1, source_target_pairs={{0,1},{1,0},{2,3},{3,2},{4,5},{5,4},{6,7},{7,6},{8,9},{9,8},{10,11... | collective-permute-start | bytes 3932168 | tf_op jit(solution)/shard_map/ppermute | solution.py:29
  3.2 1.6 broadcast_in_dim.13
  4.8 8.2 %all-to-all-start = ((bf16[4,32,1024]{2,1,0:T(8,128)(2,1)}), bf16[4,32,1024]{2,1,0:T(8,128)(2,1)S(1)}, u32[]{:S(2)}, u32[]{:S(2)}) async-start(bf16[4,32,1024]{2,1,0:T(8,128)(2,1)} %bitcast.8), calls=%async_computation | async-start | bytes 524288 | tf_op jit(solution)/shard_map/all_to_all | solution.py:21
  13.0 21.6 %all-to-all-done = bf16[4,32,1024]{2,1,0:T(8,128)(2,1)S(1)} async-done(((bf16[4,32,1024]{2,1,0:T(8,128)(2,1)}), bf16[4,32,1024]{2,1,0:T(8,128)(2,1)S(1)}, u32[]{:S(2)}, u32[]{:S(2)}) %all-to-all-start) | async-done | bytes 262176 | tf_op jit(solution)/shard_map/all_to_all | solution.py:21
  34.7 0.3 copy.33
  34.9 1.3 broadcast_in_dim.14
  36.2 4.5 %all-to-all-start.1 = ((bf16[3,2,32,2,1024]{4,3,2,1,0:T(2,128)(2,1)}), bf16[3,2,32,2,1024]{4,3,2,1,0:T(2,128)(2,1)S(1)}, u32[]{:S(2)}, u32[]{:S(2)}) async-start(bf16[3,2,32,2,1024]{4,3,2,1,0:T(2,128)(2,1)} %broadcast_in_dim.14), calls=%async_computation.1 | async-start | bytes 1572864 | tf_op jit(solution)/shard_map/all_to_all | solution.py:14
  40.8 0.0 collective-permute-done
  40.8 1.9 select_bitcast_fusion.3
  42.6 1.7 pad_maximum_fusion.1
  44.4 3.9 %collective-permute-start.1 = (bf16[8,80,2,1024]{3,1,0,2:T(8,128)(2,1)}, bf16[8,80,2,1024]{3,1,0,2:T(8,128)(2,1)}, u32[]{:S(2)}, u32[]{:S(2)}) collective-permute-start(bf16[8,80,2,1024]{3,1,0,2:T(8,128)(2,1)} %pad_maximum_fusion.1), channel_id=1, source_target_pairs={{0,16},{16,0},{1,17},{17,1},{2,18},{18,2},{3,19},{19,3},{4,20},{20... | collective-permute-start | bytes 7864328 | tf_op jit(solution)/shard_map/ppermute | solution.py:29
  48.3 4.2 %all-to-all-done.1 = bf16[3,2,32,2,1024]{4,3,2,1,0:T(2,128)(2,1)S(1)} async-done(((bf16[3,2,32,2,1024]{4,3,2,1,0:T(2,128)(2,1)}), bf16[3,2,32,2,1024]{4,3,2,1,0:T(2,128)(2,1)S(1)}, u32[]{:S(2)}, u32[]{:S(2)}) %all-to-all-start.1) | async-done | bytes 786464 | tf_op jit(solution)/shard_map/all_to_all | solution.py:14
  52.5 0.2 slice_bitcast_fusion
  52.7 1.5 broadcast_in_dim.17
  54.2 4.2 %all-to-all-start.5 = ((bf16[4,1,2,32,2,1024]{5,4,3,2,1,0:T(2,128)(2,1)}), bf16[4,1,2,32,2,1024]{5,4,3,2,1,0:T(2,128)(2,1)}, u32[]{:S(2)}, u32[]{:S(2)}) async-start(bf16[4,1,2,32,2,1024]{5,4,3,2,1,0:T(2,128)(2,1)} %broadcast_in_dim.17), calls=%async_computation.5 | async-start | bytes 2097152 | tf_op jit(solution)/shard_map/all_to_all | solution.py:14
  58.5 1.2 slice.8
  59.6 11.1 %all-to-all-done.5 = bf16[4,1,2,32,2,1024]{5,4,3,2,1,0:T(2,128)(2,1)} async-done(((bf16[4,1,2,32,2,1024]{5,4,3,2,1,0:T(2,128)(2,1)}), bf16[4,1,2,32,2,1024]{5,4,3,2,1,0:T(2,128)(2,1)}, u32[]{:S(2)}, u32[]{:S(2)}) %all-to-all-start.5) | async-done | bytes 1048608 | tf_op jit(solution)/shard_map/all_to_all | solution.py:14
  70.7 4.1 %broadcast_in_dim.15 = bf16[4,2,2,32,2,1024]{5,4,3,2,1,0:T(2,128)(2,1)} broadcast(bf16[2,2,32,2,1024]{4,3,2,1,0:T(2,128)(2,1)} %slice.8), dimensions={1,2,3,4,5} | broadcast | bytes 2621440 | tf_op jit(solution)/shard_map/broadcast_in_dim | solution.py:14
  74.8 4.6 %all-to-all-start.2 = ((bf16[4,2,2,32,2,1024]{5,4,3,2,1,0:T(2,128)(2,1)}), bf16[4,2,2,32,2,1024]{5,4,3,2,1,0:T(2,128)(2,1)}, u32[]{:S(2)}, u32[]{:S(2)}) async-start(bf16[4,2,2,32,2,1024]{5,4,3,2,1,0:T(2,128)(2,1)} %broadcast_in_dim.15), calls=%async_computation.2 | async-start | bytes 4194304 | tf_op jit(solution)/shard_map/all_to_all | solution.py:14
  79.4 2.5 %copy.36 = bf16[32,8,2,1024]{3,1,2,0:T(8,128)(2,1)} copy(bf16[32,8,2,1024]{3,2,1,0:T(2,128)(2,1)} %bitcast.26) | data formatting | bytes 2097152
  81.9 0.0 collective-permute-done.1
  81.9 2.1 select_bitcast_fusion.1
  84.0 2.7 %pad_maximum_fusion = bf16[8,2,80,2,1024]{4,2,0,3,1:T(8,128)(2,1)} fusion(bf16[8,1,80,2,1024]{4,2,0,3,1:T(8,128)(2,1)S(1)} %get-tuple-element.6, bf16[8,1,80,2,1024]{4,2,0,3,1:T(8,128)(2,1)S(1)} %get-tuple-element.5), kind=kLoop, calls=%fused_computation | loop fusion | flops 2621440 | bytes 10485760 | tf_op jit(solution)/shard_map/stack | solution.py:31
  86.7 10.2 %copy.32 = bf16[8,2,80,2,1024]{4,3,2,1,0:T(2,128)(2,1)} copy(bf16[8,2,80,2,1024]{4,2,0,3,1:T(8,128)(2,1)} %pad_maximum_fusion) | data formatting | bytes 10485760 | tf_op jit(solution)/shard_map/stack | solution.py:31
  97.0 0.0 copy-start.1
  97.0 4.7 %copy.34 = bf16[160,8,2,1024]{3,1,2,0:T(8,128)(2,1)S(1)} copy(bf16[160,8,2,1024]{3,2,1,0:T(2,128)(2,1)} %bitcast.39) | data formatting | bytes 10485760
  101.7 0.0 copy-start
  101.7 2.3 %copy-done = bf16[160,8,2,1024]{3,1,2,0:T(8,128)(2,1)} copy-done((bf16[160,8,2,1024]{3,1,2,0:T(8,128)(2,1)}, bf16[160,8,2,1024]{3,1,2,0:T(8,128)(2,1)S(1)}, u32[]{:S(2)}) %copy-start) | copy-done | bytes 5242904
  104.0 0.0 copy-done.1
  104.0 2.4 %convolution_convert_fusion.1 = bf16[1280,256]{1,0:T(8,128)(2,1)} fusion(bf16[1280,2048]{1,0:T(8,128)(2,1)S(1)} %bitcast.40, bf16[256,2048]{1,0:T(8,128)(2,1)S(1)} %bitcast.45), kind=kOutput, calls=%fused_computation.5 | convolution fusion | flops 1342504960 | bytes 6946816 | tf_op jit(solution)/shard_map/dot_general | solution.py:69
  106.4 0.0 all-to-all-done.2
  106.4 6.8 %all-to-all-start.6 = ((bf16[4,320,256]{2,1,0:T(8,128)(2,1)}), bf16[4,320,256]{2,1,0:T(8,128)(2,1)S(1)}, u32[]{:S(2)}, u32[]{:S(2)}) async-start(bf16[4,320,256]{2,1,0:T(8,128)(2,1)} %bitcast.15), calls=%async_computation.6 | async-start | bytes 1310720 | tf_op jit(solution)/shard_map/all_to_all | solution.py:72
  113.2 2.2 %copy.35 = bf16[64,8,2,1024]{3,1,2,0:T(8,128)(2,1)S(1)} copy(bf16[64,8,2,1024]{3,2,1,0:T(2,128)(2,1)} %bitcast.23) | data formatting | bytes 4194304
  115.4 6.5 %convolution_convert_fusion = bf16[1280,512]{1,0:T(8,128)(2,1)} fusion(bf16[1280,2048]{1,0:T(8,128)(2,1)} %bitcast.41, bf16[512,2048]{1,0:T(8,128)(2,1)S(1)} %bitcast.42), kind=kOutput, calls=%fused_computation.1 | convolution fusion | flops 2685009920 | bytes 8650752 | tf_op jit(solution)/shard_map/dot_general | solution.py:69
  121.9 4.8 %all-to-all-done.6 = bf16[4,320,256]{2,1,0:T(8,128)(2,1)S(1)} async-done(((bf16[4,320,256]{2,1,0:T(8,128)(2,1)}), bf16[4,320,256]{2,1,0:T(8,128)(2,1)S(1)}, u32[]{:S(2)}, u32[]{:S(2)}) %all-to-all-start.6) | async-done | bytes 655392 | tf_op jit(solution)/shard_map/all_to_all | solution.py:72
  126.7 0.0 copy-start.2
  126.7 6.8 %all-to-all-start.3 = ((bf16[4,320,512]{2,1,0:T(8,128)(2,1)}), bf16[4,320,512]{2,1,0:T(8,128)(2,1)S(1)}, u32[]{:S(2)}, u32[]{:S(2)}) async-start(bf16[4,320,512]{2,1,0:T(8,128)(2,1)} %bitcast.11), calls=%async_computation.3 | async-start | bytes 2621440 | tf_op jit(solution)/shard_map/all_to_all | solution.py:72
  133.4 0.8 reduce_sum.25
  134.2 27.5 %all-to-all-done.3 = bf16[4,320,512]{2,1,0:T(8,128)(2,1)S(1)} async-done(((bf16[4,320,512]{2,1,0:T(8,128)(2,1)}), bf16[4,320,512]{2,1,0:T(8,128)(2,1)S(1)}, u32[]{:S(2)}, u32[]{:S(2)}) %all-to-all-start.3) | async-done | bytes 1310752 | tf_op jit(solution)/shard_map/all_to_all | solution.py:72
  161.7 17.2 %all-to-all-start.7 = ((bf16[8,40,256]{2,1,0:T(8,128)(2,1)}), bf16[8,40,256]{2,1,0:T(8,128)(2,1)S(1)}, u32[]{:S(2)}, u32[]{:S(2)}) async-start(bf16[8,40,256]{2,1,0:T(8,128)(2,1)} %bitcast.16), calls=%async_computation.7 | async-start | bytes 327680 | tf_op jit(solution)/shard_map/all_to_all | solution.py:74
  179.0 1.0 reduce_sum.24
  180.0 10.4 %all-to-all-done.7 = bf16[8,40,256]{2,1,0:T(8,128)(2,1)S(1)} async-done(((bf16[8,40,256]{2,1,0:T(8,128)(2,1)}), bf16[8,40,256]{2,1,0:T(8,128)(2,1)S(1)}, u32[]{:S(2)}, u32[]{:S(2)}) %all-to-all-start.7) | async-done | bytes 163872 | tf_op jit(solution)/shard_map/all_to_all | solution.py:74
  190.3 3.7 %all-to-all-start.4 = ((bf16[8,40,512]{2,1,0:T(8,128)(2,1)}), bf16[8,40,512]{2,1,0:T(8,128)(2,1)S(1)}, u32[]{:S(2)}, u32[]{:S(2)}) async-start(bf16[8,40,512]{2,1,0:T(8,128)(2,1)} %bitcast.12), calls=%async_computation.4 | async-start | bytes 655360 | tf_op jit(solution)/shard_map/all_to_all | solution.py:74
  194.1 0.0 copy-done.2
  194.1 0.1 copy.27
  194.2 0.2 reduce_window_sum.11
  194.4 0.1 copy.28
  194.5 0.1 copy.29
  194.6 0.1 copy.31
  194.7 0.1 eq.45
  194.8 18.6 %all-to-all-done.4 = bf16[8,40,512]{2,1,0:T(8,128)(2,1)S(1)} async-done(((bf16[8,40,512]{2,1,0:T(8,128)(2,1)}), bf16[8,40,512]{2,1,0:T(8,128)(2,1)S(1)}, u32[]{:S(2)}, u32[]{:S(2)}) %all-to-all-start.4) | async-done | bytes 327712 | tf_op jit(solution)/shard_map/all_to_all | solution.py:74
  213.4 1.6 shard_map.37
  (7 shorter events, 0.1 us)
Async XLA Ops:
  0.0 40.8 %collective-permute-start = (bf16[8,80,1024]{2,1,0:T(8,128)(2,1)}, bf16[8,80,1024]{2,1,0:T(8,128)(2,1)}, u32[]{:S(2)}, u32[]{:S(2)}) collective-permute-start(bf16[8,80,1024]{2,1,0:T(8,128)(2,1)} %bitcast.43), channel_id=1, source_target_pairs={{0,1},{1,0},{2,3},{3,2},{4,5},{5,4},{6,7},{7,6},{8,9},{9,8},{10,11... | collective-permute-start | bytes 3932168 | tf_op jit(solution)/shard_map/ppermute | solution.py:29
  4.8 29.8 %all-to-all-start = ((bf16[4,32,1024]{2,1,0:T(8,128)(2,1)}), bf16[4,32,1024]{2,1,0:T(8,128)(2,1)S(1)}, u32[]{:S(2)}, u32[]{:S(2)}) async-start(bf16[4,32,1024]{2,1,0:T(8,128)(2,1)} %bitcast.8), calls=%async_computation | async-start | bytes 524288 | tf_op jit(solution)/shard_map/all_to_all | solution.py:21
  36.2 16.3 %all-to-all-start.1 = ((bf16[3,2,32,2,1024]{4,3,2,1,0:T(2,128)(2,1)}), bf16[3,2,32,2,1024]{4,3,2,1,0:T(2,128)(2,1)S(1)}, u32[]{:S(2)}, u32[]{:S(2)}) async-start(bf16[3,2,32,2,1024]{4,3,2,1,0:T(2,128)(2,1)} %broadcast_in_dim.14), calls=%async_computation.1 | async-start | bytes 1572864 | tf_op jit(solution)/shard_map/all_to_all | solution.py:14
  44.4 37.5 %collective-permute-start.1 = (bf16[8,80,2,1024]{3,1,0,2:T(8,128)(2,1)}, bf16[8,80,2,1024]{3,1,0,2:T(8,128)(2,1)}, u32[]{:S(2)}, u32[]{:S(2)}) collective-permute-start(bf16[8,80,2,1024]{3,1,0,2:T(8,128)(2,1)} %pad_maximum_fusion.1), channel_id=1, source_target_pairs={{0,16},{16,0},{1,17},{17,1},{2,18},{18,2},{3,19},{19,3},{4,20},{20... | collective-permute-start | bytes 7864328 | tf_op jit(solution)/shard_map/ppermute | solution.py:29
  54.2 16.5 %all-to-all-start.5 = ((bf16[4,1,2,32,2,1024]{5,4,3,2,1,0:T(2,128)(2,1)}), bf16[4,1,2,32,2,1024]{5,4,3,2,1,0:T(2,128)(2,1)}, u32[]{:S(2)}, u32[]{:S(2)}) async-start(bf16[4,1,2,32,2,1024]{5,4,3,2,1,0:T(2,128)(2,1)} %broadcast_in_dim.17), calls=%async_computation.5 | async-start | bytes 2097152 | tf_op jit(solution)/shard_map/all_to_all | solution.py:14
  74.8 31.6 %all-to-all-start.2 = ((bf16[4,2,2,32,2,1024]{5,4,3,2,1,0:T(2,128)(2,1)}), bf16[4,2,2,32,2,1024]{5,4,3,2,1,0:T(2,128)(2,1)}, u32[]{:S(2)}, u32[]{:S(2)}) async-start(bf16[4,2,2,32,2,1024]{5,4,3,2,1,0:T(2,128)(2,1)} %broadcast_in_dim.15), calls=%async_computation.2 | async-start | bytes 4194304 | tf_op jit(solution)/shard_map/all_to_all | solution.py:14
  97.0 7.0 %copy-start.1 = (bf16[32,8,2,1024]{3,1,2,0:T(8,128)(2,1)S(1)}, bf16[32,8,2,1024]{3,1,2,0:T(8,128)(2,1)}, u32[]{:S(2)}) copy-start(bf16[32,8,2,1024]{3,1,2,0:T(8,128)(2,1)} %copy.36) | copy-start | bytes 3145732
  101.7 2.3 %copy-start = (bf16[160,8,2,1024]{3,1,2,0:T(8,128)(2,1)}, bf16[160,8,2,1024]{3,1,2,0:T(8,128)(2,1)S(1)}, u32[]{:S(2)}) copy-start(bf16[160,8,2,1024]{3,1,2,0:T(8,128)(2,1)S(1)} %copy.34) | copy-start | bytes 15728644
  106.4 20.3 %all-to-all-start.6 = ((bf16[4,320,256]{2,1,0:T(8,128)(2,1)}), bf16[4,320,256]{2,1,0:T(8,128)(2,1)S(1)}, u32[]{:S(2)}, u32[]{:S(2)}) async-start(bf16[4,320,256]{2,1,0:T(8,128)(2,1)} %bitcast.15), calls=%async_computation.6 | async-start | bytes 1310720 | tf_op jit(solution)/shard_map/all_to_all | solution.py:72
  126.7 67.4 %copy-start.2 = (s32[128,2]{0,1:T(2,128)S(1)}, s32[128,2]{0,1:T(2,128)}, u32[]{:S(2)}) copy-start(s32[128,2]{0,1:T(2,128)} %param.3) | copy-start | bytes 3076
  126.7 35.0 %all-to-all-start.3 = ((bf16[4,320,512]{2,1,0:T(8,128)(2,1)}), bf16[4,320,512]{2,1,0:T(8,128)(2,1)S(1)}, u32[]{:S(2)}, u32[]{:S(2)}) async-start(bf16[4,320,512]{2,1,0:T(8,128)(2,1)} %bitcast.11), calls=%async_computation.3 | async-start | bytes 2621440 | tf_op jit(solution)/shard_map/all_to_all | solution.py:72
  161.7 28.6 %all-to-all-start.7 = ((bf16[8,40,256]{2,1,0:T(8,128)(2,1)}), bf16[8,40,256]{2,1,0:T(8,128)(2,1)S(1)}, u32[]{:S(2)}, u32[]{:S(2)}) async-start(bf16[8,40,256]{2,1,0:T(8,128)(2,1)} %bitcast.16), calls=%async_computation.7 | async-start | bytes 327680 | tf_op jit(solution)/shard_map/all_to_all | solution.py:74
  190.3 23.1 %all-to-all-start.4 = ((bf16[8,40,512]{2,1,0:T(8,128)(2,1)}), bf16[8,40,512]{2,1,0:T(8,128)(2,1)S(1)}, u32[]{:S(2)}, u32[]{:S(2)}) async-start(bf16[8,40,512]{2,1,0:T(8,128)(2,1)} %bitcast.12), calls=%async_computation.4 | async-start | bytes 655360 | tf_op jit(solution)/shard_map/all_to_all | solution.py:74

commit v3 on v0

v3 whole, which is shorter than its diff:
```python
import jax
import jax.numpy as jnp
from jax import lax
from jax.experimental import pallas as pl
from jax.experimental.pallas import tpu as pltpu
from jax.sharding import Mesh, PartitionSpec as P

SIZES = {"xh": 2, "xp": 2, "h": 2, "m": 3, "c": 2, "e": 2, "t": 8}
DP = ("xh", "xp", "h", "m", "c")
SWAP = [(0, 1), (1, 0)]
WEIGHT_SWAP = [(i, 3 - i) for i in range(4)]


def turn(shift):
    return [(i, (i + shift) % SIZES["m"]) for i in range(SIZES["m"])]


def gather_column(slab):
    pair = jnp.stack([slab, lax.ppermute(slab, "h", SWAP)])
    return jnp.concatenate([pair, lax.ppermute(pair, "m", turn(1)), lax.ppermute(pair, "m", turn(-1))])


def block_places():
    x_high, h, m = lax.axis_index("xh"), lax.axis_index("h"), lax.axis_index("m")
    count = SIZES["m"]
    zs = []
    for shift in (0, -1, 1):
        at = (m + shift + count) % count
        zs += [h * count + at, (1 - h) * count + at]
    xs = [2 * x_high + xp for xp in range(2)] + [3 - 2 * x_high - xp for xp in range(2)]
    return jnp.stack([x * SIZES["h"] * count + z for x in xs for z in zs]).astype(jnp.int32)


def product(rows, blocks):
    tensor_count, count, hidden = rows.shape
    features = blocks.shape[0] * blocks.shape[1]
    partial = lax.dot_general(
        rows.reshape(tensor_count * count, hidden),
        blocks.reshape(features, hidden),
        (((1,), (1,)), ((), ())),
        preferred_element_type=jnp.float32,
    )
    return partial.astype(jnp.bfloat16).reshape(tensor_count, count, features)


def sum_direct(partial):
    parts = lax.all_to_all(partial, "t", 0, 0)
    return jnp.sum(parts.astype(jnp.float32), axis=0).astype(jnp.bfloat16)


def sum_by_arms(low, high):
    n = low.shape[0]
    mid = n // 2
    me = lax.axis_index("t")
    up = [(i, (i + 1) % n) for i in range(n)]
    down = [(i, (i - 1) % n) for i in range(n)]
    pick = lambda value, k: lax.dynamic_index_in_dim(value, (me + k) % n, 0, keepdims=False)
    both = lambda k: jnp.concatenate([pick(low, k), pick(high, k)])
    wide = lambda value: value.astype(jnp.float32)
    narrow = lambda value: value.astype(jnp.bfloat16)

    first = lax.ppermute(pick(low, mid), "t", up)
    last = lax.ppermute(pick(high, mid), "t", down)
    going_up = jnp.concatenate([narrow(wide(pick(low, mid - 1)) + wide(first)), pick(high, mid - 1)])
    going_down = jnp.concatenate([pick(low, mid + 1), narrow(wide(pick(high, mid + 1)) + wide(last))])
    for step in range(1, mid):
        from_below = lax.ppermute(going_up, "t", up)
        from_above = lax.ppermute(going_down, "t", down)
        if step < mid - 1:
            going_up = narrow(wide(both(mid - 1 - step)) + wide(from_below))
            going_down = narrow(wide(both(mid + 1 + step)) + wide(from_above))
    return narrow(wide(both(0)) + wide(from_below) + wide(from_above))


def give_back(near, far, owners, capacity):
    features = near.shape[-1]
    rows = owners * capacity
    x_first = lax.axis_index("xp") == 0
    c_first = lax.axis_index("c") == 0
    rest = near.shape[0] // 2
    swap = lambda value: jnp.concatenate([value[rest:], value[:rest]])
    near = jnp.where(c_first, near, swap(near))
    far = jnp.where(c_first, far, swap(far))
    both = jnp.concatenate([jnp.where(x_first, near, far), jnp.where(x_first, far, near)])
    got = lax.all_to_all(both.reshape(-1, capacity, features), ("xp", "c", "e"), 0, 0)
    return got.reshape(-1, rows, features)


def place_kernel(places, onehot, *refs, width):
    out = refs[-1]
    cores = SIZES["c"]
    at = 0
    for piece in refs[:-1]:
        for xp in range(SIZES["xp"]):
            for b in range(piece.shape[2] // width):
                block = jnp.concatenate(
                    [piece[xp * cores + c, :, b * width:(b + 1) * width] for c in range(cores)], axis=1
                )
                result = jnp.dot(onehot[...], block, preferred_element_type=jnp.float32)
                start = pl.multiple_of(places[at] * (cores * width), cores * width)
                out[:, pl.ds(start, cores * width)] = result.astype(out.dtype)
                at += 1


def shards(routes, upgrad, weight):
    _, _, tensor_count, owners, capacity, hidden = upgrad.shape
    slab = weight[0]
    width = slab.shape[0]
    rows = owners * capacity

    own = upgrad.reshape(tensor_count, rows, hidden)
    column = gather_column(slab)
    x_rows = lax.ppermute(own, "xp", SWAP)
    near_rows = jnp.concatenate([own, lax.ppermute(own, "c", SWAP)], axis=1)
    far_rows = jnp.concatenate([x_rows, lax.ppermute(x_rows, "c", SWAP)], axis=1)
    other_column = lax.ppermute(column, ("xh", "xp"), WEIGHT_SWAP)

    near = sum_direct(product(near_rows, column))
    far = sum_direct(product(far_rows, column))
    summed = sum_by_arms(product(near_rows, other_column), product(far_rows, other_column))
    half = summed.shape[0] // 2
    pieces = [
        give_back(near, far, owners, capacity),
        give_back(summed[:half], summed[half:], owners, capacity),
    ]

    owner_ids = lax.iota(jnp.int32, owners)
    is_routed = jnp.any(routes[:, :, None] == owner_ids[None, None, :], axis=1)
    slot_index = jnp.cumsum(is_routed.astype(jnp.int32), axis=0) - 1
    onehot = is_routed[:, :, None] & (slot_index[:, :, None] == lax.iota(jnp.int32, capacity)[None, None, :])
    onehot = onehot.reshape(routes.shape[0], rows).astype(jnp.bfloat16)

    def body(*refs):
        place_kernel(*refs, width=width)

    smem = pl.BlockSpec(memory_space=pltpu.SMEM)
    vmem = pl.BlockSpec(memory_space=pltpu.VMEM)
    total = sum(piece.shape[0] * piece.shape[2] for piece in pieces)
    return pl.pallas_call(
        body,
        out_shape=jax.ShapeDtypeStruct((routes.shape[0], total), jnp.bfloat16),
        in_specs=[smem, vmem] + [vmem] * len(pieces),
        out_specs=vmem,
        compiler_params=pltpu.CompilerParams(vmem_limit_bytes=32 * 1024 * 1024),
    )(block_places(), onehot, *pieces)


def solution(mesh):
    fine = Mesh(mesh.devices.reshape(tuple(SIZES.values())), tuple(SIZES))
    return jax.shard_map(
        shards,
        mesh=fine,
        in_specs=(
            P(DP + ("e", "t"), None),
            P(DP, "e", None, None, None, "t"),
            P("e", DP, "t"),
        ),
        out_specs=P(DP + ("e", "t"), None),
        check_vma=False,
    )
```

time: 224 us -> 188 us (0.84)
  the two profiles are of different devices: /device:TPU:64 before, /device:TPU:153 now
where the time goes in v3:
time: 188 us; the launch traced here: 187 us
  starting transfers between devices  85.7 us (46%)
  waiting for transfers between devices  75.4 us (40%)
  matrix products  11.2 us (6%)
  other arithmetic  9.53 us (5%)
  local copies, waits for them, and re-layouts  2.36 us (1%)
    all_to_all x2, waiting for transfers between devices, give_back(): lax.all_to_all(both.reshape(-1, capacity, features), ('xp', 'c', 'e'), 0, 0)  26.8 us
    ppermute x3, waiting for transfers between devices, sum_by_arms(): from_above = lax.ppermute(going_down, 't', down)  26.3 us
    all_to_all x2, starting transfers between devices, give_back(): lax.all_to_all(both.reshape(-1, capacity, features), ('xp', 'c', 'e'), 0, 0)  20.2 us
    ppermute x3, starting transfers between devices, sum_by_arms(): from_below = lax.ppermute(going_up, 't', up)  12.8 us
    all_to_all x2, starting transfers between devices, sum_direct(): parts = lax.all_to_all(partial, 't', 0, 0)  12 us
    dot_general x4, matrix products, product(): lax.dot_general(rows.reshape(tensor_count * count, hidden), blocks.reshap...  11.2 us
    ppermute x1, starting transfers between devices, gather_column(): pair = jnp.stack([slab, lax.ppermute(slab, 'h', SWAP)])  8.83 us
    ppermute x1, waiting for transfers between devices, shards(): other_column = lax.ppermute(column, ('xh', 'xp'), WEIGHT_SWAP)  6.99 us
  transfers between devices with their start and end apart: 19, of which 9 were waited for; matrix products, arithmetic and copies ran while one was open for 12% of the time, Pallas kernels for 0%

profile of v3, /device:TPU:153, one launch (start us, length us, event | category | flops | bytes accessed | tf_op | source)
XLA Modules:
  0.0 186.5 jit_solution(13174289525660459123)
XLA Ops:
  0.0 3.2 %collective-permute-start.4 = (bf16[8,80,1024]{2,1,0:T(8,128)(2,1)}, bf16[8,80,1024]{2,1,0:T(8,128)(2,1)S(1)}, u32[]{:S(2)}, u32[]{:S(2)}) collective-permute-start(bf16[8,80,1024]{2,1,0:T(8,128)(2,1)} %bitcast.89), channel_id=1, source_target_pairs={{0,192},{192,0},{1,193},{193,1},{2,194},{194,2},{3,195},{195,3},{4... | collective-permute-start | bytes 3932168 | tf_op jit(solution)/shard_map/ppermute | solution.py:113
  3.2 2.9 %collective-permute-start = (bf16[8,80,1024]{2,1,0:T(8,128)(2,1)}, bf16[8,80,1024]{2,1,0:T(8,128)(2,1)}, u32[]{:S(2)}, u32[]{:S(2)}) collective-permute-start(bf16[8,80,1024]{2,1,0:T(8,128)(2,1)} %bitcast.90), channel_id=1, source_target_pairs={{0,16},{16,0},{1,17},{17,1},{2,18},{18,2},{3,19},{19,3},{4,20},{20... | collective-permute-start | bytes 3932168 | tf_op jit(solution)/shard_map/ppermute | solution.py:114
  6.1 8.8 %collective-permute-start.1 = (bf16[64,1024]{1,0:T(8,128)(2,1)}, bf16[64,1024]{1,0:T(8,128)(2,1)S(1)}, u32[]{:S(2)}, u32[]{:S(2)}) collective-permute-start(bf16[64,1024]{1,0:T(8,128)(2,1)} %bitcast.98), channel_id=1, source_target_pairs={{0,96},{96,0},{1,97},{97,1},{2,98},{98,2},{3,99},{99,3},{4,100},{1... | collective-permute-start | bytes 393224 | tf_op jit(solution)/shard_map/ppermute | solution.py:19
  15.0 6.2 %collective-permute-done.1 = bf16[64,1024]{1,0:T(8,128)(2,1)S(1)} collective-permute-done((bf16[64,1024]{1,0:T(8,128)(2,1)}, bf16[64,1024]{1,0:T(8,128)(2,1)S(1)}, u32[]{:S(2)}, u32[]{:S(2)}) %collective-permute-start.1) | collective-permute-done | bytes 131104 | tf_op jit(solution)/shard_map/ppermute | solution.py:19
  21.1 0.9 pad_maximum_fusion.3
  22.0 2.0 %collective-permute-start.3 = (bf16[2,64,1024]{2,1,0:T(8,128)(2,1)S(1)}, bf16[2,64,1024]{2,1,0:T(8,128)(2,1)S(1)}, u32[]{:S(2)}, u32[]{:S(2)}) collective-permute-start(bf16[2,64,1024]{2,1,0:T(8,128)(2,1)S(1)} %pad_maximum_fusion.3), channel_id=1, source_target_pairs={{0,64},{32,0},{64,32},{1,65},{33,1},{65,33},{2,66},{34,2},{66,34},... | collective-permute-start | bytes 786440 | tf_op jit(solution)/shard_map/ppermute | solution.py:20
  24.0 4.2 %collective-permute-start.2 = (bf16[2,64,1024]{2,1,0:T(8,128)(2,1)S(1)}, bf16[2,64,1024]{2,1,0:T(8,128)(2,1)S(1)}, u32[]{:S(2)}, u32[]{:S(2)}) collective-permute-start(bf16[2,64,1024]{2,1,0:T(8,128)(2,1)S(1)} %pad_maximum_fusion.3), channel_id=1, source_target_pairs={{0,32},{32,64},{64,0},{1,33},{33,65},{65,1},{2,34},{34,66},{66,2},... | collective-permute-start | bytes 786440 | tf_op jit(solution)/shard_map/ppermute | solution.py:20
  28.2 3.6 %collective-permute-done.4 = bf16[8,80,1024]{2,1,0:T(8,128)(2,1)S(1)} collective-permute-done((bf16[8,80,1024]{2,1,0:T(8,128)(2,1)}, bf16[8,80,1024]{2,1,0:T(8,128)(2,1)S(1)}, u32[]{:S(2)}, u32[]{:S(2)}) %collective-permute-start.4) | collective-permute-done | bytes 1310752 | tf_op jit(solution)/shard_map/ppermute | solution.py:113
  31.9 3.4 %collective-permute-start.5 = (bf16[8,80,1024]{2,1,0:T(8,128)(2,1)S(1)}, bf16[8,80,1024]{2,1,0:T(8,128)(2,1)}, u32[]{:S(2)}, u32[]{:S(2)}) collective-permute-start(bf16[8,80,1024]{2,1,0:T(8,128)(2,1)S(1)} %collective-permute-done.4), channel_id=1, source_target_pairs={{0,16},{16,0},{1,17},{17,1},{2,18},{18,2},{3,19},{19,3},{4,20},{20... | collective-permute-start | bytes 3932168 | tf_op jit(solution)/shard_map/ppermute | solution.py:115
  35.3 3.4 %collective-permute-done.2 = bf16[2,64,1024]{2,1,0:T(8,128)(2,1)S(1)} collective-permute-done((bf16[2,64,1024]{2,1,0:T(8,128)(2,1)S(1)}, bf16[2,64,1024]{2,1,0:T(8,128)(2,1)S(1)}, u32[]{:S(2)}, u32[]{:S(2)}) %collective-permute-start.2) | collective-permute-done | bytes 262176 | tf_op jit(solution)/shard_map/ppermute | solution.py:20
  38.7 1.0 pad_maximum_fusion.2
  39.7 3.7 %collective-permute-start.6 = (bf16[6,64,1024]{2,1,0:T(8,128)(2,1)S(1)}, bf16[6,64,1024]{2,1,0:T(8,128)(2,1)}, u32[]{:S(2)}, u32[]{:S(2)}) collective-permute-start(bf16[6,64,1024]{2,1,0:T(8,128)(2,1)S(1)} %pad_maximum_fusion.2), channel_id=1, source_target_pairs={{0,576},{192,384},{384,192},{576,0},{1,577},{193,385},{385,193},{5... | collective-permute-start | bytes 2359304 | tf_op jit(solution)/shard_map/ppermute | solution.py:116
  43.5 0.0 collective-permute-done
  43.5 1.7 pad_maximum_fusion
  45.3 2.5 %convolution_convert_fusion.3 = bf16[1280,384]{1,0:T(8,128)(2,1)} fusion(bf16[1280,1024]{1,0:T(8,128)(2,1)S(1)} %bitcast.87, bf16[384,1024]{1,0:T(8,128)(2,1)S(1)} %bitcast.96), kind=kOutput, calls=%fused_computation.3 | convolution fusion | flops 1007124480 | bytes 4390912 | tf_op jit(solution)/shard_map/dot_general | solution.py:37
  47.8 6.8 %all-to-all-start = ((bf16[8,160,384]{2,1,0:T(8,128)(2,1)}), bf16[8,160,384]{2,1,0:T(8,128)(2,1)S(1)}, u32[]{:S(2)}, u32[]{:S(2)}) async-start(bf16[8,160,384]{2,1,0:T(8,128)(2,1)} %bitcast.31), calls=%async_computation | async-start | bytes 1966080 | tf_op jit(solution)/shard_map/all_to_all | solution.py:47
  54.5 7.0 %collective-permute-done.6 = bf16[6,64,1024]{2,1,0:T(8,128)(2,1)} collective-permute-done((bf16[6,64,1024]{2,1,0:T(8,128)(2,1)S(1)}, bf16[6,64,1024]{2,1,0:T(8,128)(2,1)}, u32[]{:S(2)}, u32[]{:S(2)}) %collective-permute-start.6) | collective-permute-done | bytes 786464 | tf_op jit(solution)/shard_map/ppermute | solution.py:116
  61.5 3.5 %convolution_convert_fusion.1 = bf16[1280,384]{1,0:T(8,128)(2,1)S(1)} fusion(bf16[1280,1024]{1,0:T(8,128)(2,1)} %bitcast.88, bf16[384,1024]{1,0:T(8,128)(2,1)} %bitcast.36), kind=kOutput, calls=%fused_computation.1 | convolution fusion | flops 1007124480 | bytes 4390912 | tf_op jit(solution)/shard_map/dot_general | solution.py:37
  65.0 0.8 dynamic-slice_bitcast_fusion.13
  65.8 4.4 %collective-permute-start.7 = (bf16[160,384]{1,0:T(8,128)(2,1)S(1)}, bf16[160,384]{1,0:T(8,128)(2,1)S(1)}, u32[]{:S(2)}, u32[]{:S(2)}) collective-permute-start(bf16[160,384]{1,0:T(8,128)(2,1)S(1)} %get-tuple-element.9), channel_id=1, source_target_pairs={{0,1},{1,2},{2,3},{3,4},{4,5},{5,6},{6,7},{7,0},{8,9},{9,10},{10,1... | collective-permute-start | bytes 368648 | tf_op jit(solution)/shard_map/ppermute | solution.py:62
  70.2 1.7 pad_maximum_fusion.1
  71.9 2.7 %convolution_convert_fusion = bf16[1280,384]{1,0:T(8,128)(2,1)S(1)} fusion(bf16[1280,1024]{1,0:T(8,128)(2,1)S(1)} %bitcast.85, bf16[384,1024]{1,0:T(8,128)(2,1)} %bitcast.36), kind=kOutput, calls=%fused_computation | convolution fusion | flops 1007124480 | bytes 4390912 | tf_op jit(solution)/shard_map/dot_general | solution.py:37
  74.6 0.8 dynamic-slice_bitcast_fusion.12
  75.4 1.9 %collective-permute-start.11 = (bf16[160,384]{1,0:T(8,128)(2,1)S(1)}, bf16[160,384]{1,0:T(8,128)(2,1)S(1)}, u32[]{:S(2)}, u32[]{:S(2)}) collective-permute-start(bf16[160,384]{1,0:T(8,128)(2,1)S(1)} %get-tuple-element.13), channel_id=1, source_target_pairs={{0,7},{1,0},{2,1},{3,2},{4,3},{5,4},{6,5},{7,6},{8,15},{9,8},{10,9... | collective-permute-start | bytes 368648 | tf_op jit(solution)/shard_map/ppermute | solution.py:63
  77.3 2.2 %collective-permute-done.7 = bf16[160,384]{1,0:T(8,128)(2,1)S(1)} collective-permute-done((bf16[160,384]{1,0:T(8,128)(2,1)S(1)}, bf16[160,384]{1,0:T(8,128)(2,1)S(1)}, u32[]{:S(2)}, u32[]{:S(2)}) %collective-permute-start.7) | collective-permute-done | bytes 122912 | tf_op jit(solution)/shard_map/ppermute | solution.py:62
  79.6 3.8 %collective-permute-start.8 = (bf16[320,384]{1,0:T(8,128)(2,1)S(1)}, bf16[320,384]{1,0:T(8,128)(2,1)S(1)}, u32[]{:S(2)}, u32[]{:S(2)}) collective-permute-start(bf16[320,384]{1,0:T(8,128)(2,1)S(1)} %pad_maximum_fusion.5), channel_id=1, source_target_pairs={{0,1},{1,2},{2,3},{3,4},{4,5},{5,6},{6,7},{7,0},{8,9},{9,10},{10,1... | collective-permute-start | bytes 737288 | tf_op jit(solution)/shard_map/ppermute | solution.py:67
  83.4 0.7 pad_maximum_fusion.6
  84.2 1.9 %collective-permute-start.12 = (bf16[320,384]{1,0:T(8,128)(2,1)}, bf16[320,384]{1,0:T(8,128)(2,1)}, u32[]{:S(2)}, u32[]{:S(2)}) collective-permute-start(bf16[320,384]{1,0:T(8,128)(2,1)} %pad_maximum_fusion.6), channel_id=1, source_target_pairs={{0,7},{1,0},{2,1},{3,2},{4,3},{5,4},{6,5},{7,6},{8,15},{9,8},{10,9... | collective-permute-start | bytes 737288 | tf_op jit(solution)/shard_map/ppermute | solution.py:68
  86.1 2.5 %convolution_convert_fusion.2 = bf16[1280,384]{1,0:T(8,128)(2,1)} fusion(bf16[1280,1024]{1,0:T(8,128)(2,1)S(1)} %bitcast.86, bf16[384,1024]{1,0:T(8,128)(2,1)S(1)} %bitcast.97), kind=kOutput, calls=%fused_computation.2 | convolution fusion | flops 1007124480 | bytes 4390912 | tf_op jit(solution)/shard_map/dot_general | solution.py:37
  88.6 0.0 collective-permute-done.8
  88.6 0.1 add_convert_fusion.4
  88.7 4.7 %collective-permute-start.9 = (bf16[320,384]{1,0:T(8,128)(2,1)S(1)}, bf16[320,384]{1,0:T(8,128)(2,1)S(1)}, u32[]{:S(2)}, u32[]{:S(2)}) collective-permute-start(bf16[320,384]{1,0:T(8,128)(2,1)S(1)} %add_convert_fusion.4), channel_id=1, source_target_pairs={{0,1},{1,2},{2,3},{3,4},{4,5},{5,6},{6,7},{7,0},{8,9},{9,10},{10,1... | collective-permute-start | bytes 737288 | tf_op jit(solution)/shard_map/ppermute | solution.py:67
  93.4 0.0 all-to-all-done
  93.4 5.3 %all-to-all-start.1 = ((bf16[8,160,384]{2,1,0:T(8,128)(2,1)}), bf16[8,160,384]{2,1,0:T(8,128)(2,1)S(1)}, u32[]{:S(2)}, u32[]{:S(2)}) async-start(bf16[8,160,384]{2,1,0:T(8,128)(2,1)} %bitcast.33), calls=%async_computation.1 | async-start | bytes 1966080 | tf_op jit(solution)/shard_map/all_to_all | solution.py:47
  98.7 0.0 collective-permute-done.12
  98.7 1.0 add_convert_fusion.2
  99.7 2.2 %collective-permute-start.13 = (bf16[320,384]{1,0:T(8,128)(2,1)S(1)}, bf16[320,384]{1,0:T(8,128)(2,1)S(1)}, u32[]{:S(2)}, u32[]{:S(2)}) collective-permute-start(bf16[320,384]{1,0:T(8,128)(2,1)S(1)} %add_convert_fusion.2), channel_id=1, source_target_pairs={{0,7},{1,0},{2,1},{3,2},{4,3},{5,4},{6,5},{7,6},{8,15},{9,8},{10,9... | collective-permute-start | bytes 737288 | tf_op jit(solution)/shard_map/ppermute | solution.py:68
  101.9 0.1 add_convert_fusion.3
  102.0 4.3 %collective-permute-start.10 = (bf16[320,384]{1,0:T(8,128)(2,1)S(1)}, bf16[320,384]{1,0:T(8,128)(2,1)S(1)}, u32[]{:S(2)}, u32[]{:S(2)}) collective-permute-start(bf16[320,384]{1,0:T(8,128)(2,1)S(1)} %add_convert_fusion.3), channel_id=1, source_target_pairs={{0,1},{1,2},{2,3},{3,4},{4,5},{5,6},{6,7},{7,0},{8,9},{9,10},{10,1... | collective-permute-start | bytes 737288 | tf_op jit(solution)/shard_map/ppermute | solution.py:67
  106.3 20.2 %collective-permute-done.13 = bf16[320,384]{1,0:T(8,128)(2,1)S(1)} collective-permute-done((bf16[320,384]{1,0:T(8,128)(2,1)S(1)}, bf16[320,384]{1,0:T(8,128)(2,1)S(1)}, u32[]{:S(2)}, u32[]{:S(2)}) %collective-permute-start.13) | collective-permute-done | bytes 245792 | tf_op jit(solution)/shard_map/ppermute | solution.py:68
  126.5 0.1 add_convert_fusion.1
  126.6 1.9 %collective-permute-start.14 = (bf16[320,384]{1,0:T(8,128)(2,1)S(1)}, bf16[320,384]{1,0:T(8,128)(2,1)S(1)}, u32[]{:S(2)}, u32[]{:S(2)}) collective-permute-start(bf16[320,384]{1,0:T(8,128)(2,1)S(1)} %add_convert_fusion.1), channel_id=1, source_target_pairs={{0,7},{1,0},{2,1},{3,2},{4,3},{5,4},{6,5},{7,6},{8,15},{9,8},{10,9... | collective-permute-start | bytes 737288 | tf_op jit(solution)/shard_map/ppermute | solution.py:68
  128.6 0.1 reduce_sum.24
  128.7 0.0 collective-permute-done.10
  128.7 6.1 %collective-permute-done.14 = bf16[320,384]{1,0:T(8,128)(2,1)S(1)} collective-permute-done((bf16[320,384]{1,0:T(8,128)(2,1)S(1)}, bf16[320,384]{1,0:T(8,128)(2,1)S(1)}, u32[]{:S(2)}, u32[]{:S(2)}) %collective-permute-start.14) | collective-permute-done | bytes 245792 | tf_op jit(solution)/shard_map/ppermute | solution.py:68
  134.8 0.1 add_convert_fusion
  134.9 0.0 copy-start.7
  134.9 0.1 broadcast_select_fusion.1
  135.0 0.7 pad_maximum_fusion.7
  135.7 16.0 %all-to-all-start.3 = ((bf16[8,40,384]{2,1,0:T(8,128)(2,1)}), bf16[8,40,384]{2,1,0:T(8,128)(2,1)S(1)}, u32[]{:S(2)}, u32[]{:S(2)}) async-start(bf16[8,40,384]{2,1,0:T(8,128)(2,1)} %bitcast.55), calls=%async_computation.3 | async-start | bytes 491520 | tf_op jit(solution)/shard_map/all_to_all | solution.py:85
  151.7 0.1 reduce_sum.25
  151.9 0.1 broadcast_select_fusion.3
  152.0 0.7 pad_maximum_fusion.4
  152.7 13.5 %all-to-all-done.3 = bf16[8,40,384]{2,1,0:T(8,128)(2,1)S(1)} async-done(((bf16[8,40,384]{2,1,0:T(8,128)(2,1)}), bf16[8,40,384]{2,1,0:T(8,128)(2,1)S(1)}, u32[]{:S(2)}, u32[]{:S(2)}) %all-to-all-start.3) | async-done | bytes 245792 | tf_op jit(solution)/shard_map/all_to_all | solution.py:85
  166.2 4.3 %all-to-all-start.2 = ((bf16[8,40,384]{2,1,0:T(8,128)(2,1)}), bf16[8,40,384]{2,1,0:T(8,128)(2,1)S(1)}, u32[]{:S(2)}, u32[]{:S(2)}) async-start(bf16[8,40,384]{2,1,0:T(8,128)(2,1)} %bitcast.34), calls=%async_computation.2 | async-start | bytes 491520 | tf_op jit(solution)/shard_map/all_to_all | solution.py:85
  170.6 0.1 eq.67
  170.6 0.1 copy.18
  170.8 0.1 copy.14
  170.9 0.2 reduce_window_sum.11
  171.1 0.1 copy.15
  171.1 0.1 copy.16
  171.3 0.1 stack.105.refs_0_
  171.4 13.2 %all-to-all-done.2 = bf16[8,40,384]{2,1,0:T(8,128)(2,1)S(1)} async-done(((bf16[8,40,384]{2,1,0:T(8,128)(2,1)}), bf16[8,40,384]{2,1,0:T(8,128)(2,1)S(1)}, u32[]{:S(2)}, u32[]{:S(2)}) %all-to-all-start.2) | async-done | bytes 245792 | tf_op jit(solution)/shard_map/all_to_all | solution.py:85
  184.6 1.9 %shard_map.37 = bf16[128,3072]{1,0:T(8,128)(2,1)} custom-call(s32[24]{0:T(128)S(1)} %stack.105.refs_0_, bf16[128,80]{1,0:T(8,128)(2,1)S(1)} %and_convert_fusion.refs_1_, bf16[4,80,384]{2,1,0:T(8,128)(2,1)S(1)} %bitcast.84, bf16[4,80,384]{2,1,0:T(8,128)(2,1)S(1)} %bitcast.83), custom_call_target="tpu_custom_call" | custom-call | tf_op jit(solution)/shard_map/pallas_call | solution.py:139
  (33 shorter events, 0.3 us)
Async XLA Ops:
  0.0 43.5 %copy-start.1 = (bf16[1,1,8,2,40,1024]{5,4,3,2,1,0:T(8,128)(2,1)S(1)}, bf16[1,1,8,2,40,1024]{5,4,3,2,1,0:T(8,128)(2,1)}, u32[]{:S(2)}) copy-start(bf16[1,1,8,2,40,1024]{5,4,3,2,1,0:T(8,128)(2,1)} %param.4) | copy-start | bytes 3932164
  0.0 31.9 %collective-permute-start.4 = (bf16[8,80,1024]{2,1,0:T(8,128)(2,1)}, bf16[8,80,1024]{2,1,0:T(8,128)(2,1)S(1)}, u32[]{:S(2)}, u32[]{:S(2)}) collective-permute-start(bf16[8,80,1024]{2,1,0:T(8,128)(2,1)} %bitcast.89), channel_id=1, source_target_pairs={{0,192},{192,0},{1,193},{193,1},{2,194},{194,2},{3,195},{195,3},{4... | collective-permute-start | bytes 3932168 | tf_op jit(solution)/shard_map/ppermute | solution.py:113
  3.2 40.3 %collective-permute-start = (bf16[8,80,1024]{2,1,0:T(8,128)(2,1)}, bf16[8,80,1024]{2,1,0:T(8,128)(2,1)}, u32[]{:S(2)}, u32[]{:S(2)}) collective-permute-start(bf16[8,80,1024]{2,1,0:T(8,128)(2,1)} %bitcast.90), channel_id=1, source_target_pairs={{0,16},{16,0},{1,17},{17,1},{2,18},{18,2},{3,19},{19,3},{4,20},{20... | collective-permute-start | bytes 3932168 | tf_op jit(solution)/shard_map/ppermute | solution.py:114
  6.1 15.0 %collective-permute-start.1 = (bf16[64,1024]{1,0:T(8,128)(2,1)}, bf16[64,1024]{1,0:T(8,128)(2,1)S(1)}, u32[]{:S(2)}, u32[]{:S(2)}) collective-permute-start(bf16[64,1024]{1,0:T(8,128)(2,1)} %bitcast.98), channel_id=1, source_target_pairs={{0,96},{96,0},{1,97},{97,1},{2,98},{98,2},{3,99},{99,3},{4,100},{1... | collective-permute-start | bytes 393224 | tf_op jit(solution)/shard_map/ppermute | solution.py:19
  22.0 13.3 %collective-permute-start.3 = (bf16[2,64,1024]{2,1,0:T(8,128)(2,1)S(1)}, bf16[2,64,1024]{2,1,0:T(8,128)(2,1)S(1)}, u32[]{:S(2)}, u32[]{:S(2)}) collective-permute-start(bf16[2,64,1024]{2,1,0:T(8,128)(2,1)S(1)} %pad_maximum_fusion.3), channel_id=1, source_target_pairs={{0,64},{32,0},{64,32},{1,65},{33,1},{65,33},{2,66},{34,2},{66,34},... | collective-permute-start | bytes 786440 | tf_op jit(solution)/shard_map/ppermute | solution.py:20
  24.0 14.6 %collective-permute-start.2 = (bf16[2,64,1024]{2,1,0:T(8,128)(2,1)S(1)}, bf16[2,64,1024]{2,1,0:T(8,128)(2,1)S(1)}, u32[]{:S(2)}, u32[]{:S(2)}) collective-permute-start(bf16[2,64,1024]{2,1,0:T(8,128)(2,1)S(1)} %pad_maximum_fusion.3), channel_id=1, source_target_pairs={{0,32},{32,64},{64,0},{1,33},{33,65},{65,1},{2,34},{34,66},{66,2},... | collective-permute-start | bytes 786440 | tf_op jit(solution)/shard_map/ppermute | solution.py:20
  31.9 38.3 %collective-permute-start.5 = (bf16[8,80,1024]{2,1,0:T(8,128)(2,1)S(1)}, bf16[8,80,1024]{2,1,0:T(8,128)(2,1)}, u32[]{:S(2)}, u32[]{:S(2)}) collective-permute-start(bf16[8,80,1024]{2,1,0:T(8,128)(2,1)S(1)} %collective-permute-done.4), channel_id=1, source_target_pairs={{0,16},{16,0},{1,17},{17,1},{2,18},{18,2},{3,19},{19,3},{4,20},{20... | collective-permute-start | bytes 3932168 | tf_op jit(solution)/shard_map/ppermute | solution.py:115
  39.7 21.8 %collective-permute-start.6 = (bf16[6,64,1024]{2,1,0:T(8,128)(2,1)S(1)}, bf16[6,64,1024]{2,1,0:T(8,128)(2,1)}, u32[]{:S(2)}, u32[]{:S(2)}) collective-permute-start(bf16[6,64,1024]{2,1,0:T(8,128)(2,1)S(1)} %pad_maximum_fusion.2), channel_id=1, source_target_pairs={{0,576},{192,384},{384,192},{576,0},{1,577},{193,385},{385,193},{5... | collective-permute-start | bytes 2359304 | tf_op jit(solution)/shard_map/ppermute | solution.py:116
  45.2 2.5 %copy-start = (bf16[8,160,1024]{2,1,0:T(8,128)(2,1)}, bf16[8,160,1024]{2,1,0:T(8,128)(2,1)S(1)}, u32[]{:S(2)}) copy-start(bf16[8,160,1024]{2,1,0:T(8,128)(2,1)S(1)} %pad_maximum_fusion) | copy-start | bytes 7864324
  47.8 45.7 %all-to-all-start = ((bf16[8,160,384]{2,1,0:T(8,128)(2,1)}), bf16[8,160,384]{2,1,0:T(8,128)(2,1)S(1)}, u32[]{:S(2)}, u32[]{:S(2)}) async-start(bf16[8,160,384]{2,1,0:T(8,128)(2,1)} %bitcast.31), calls=%async_computation | async-start | bytes 1966080 | tf_op jit(solution)/shard_map/all_to_all | solution.py:47
  65.8 13.7 %collective-permute-start.7 = (bf16[160,384]{1,0:T(8,128)(2,1)S(1)}, bf16[160,384]{1,0:T(8,128)(2,1)S(1)}, u32[]{:S(2)}, u32[]{:S(2)}) collective-permute-start(bf16[160,384]{1,0:T(8,128)(2,1)S(1)} %get-tuple-element.9), channel_id=1, source_target_pairs={{0,1},{1,2},{2,3},{3,4},{4,5},{5,6},{6,7},{7,0},{8,9},{9,10},{10,1... | collective-permute-start | bytes 368648 | tf_op jit(solution)/shard_map/ppermute | solution.py:62
  75.4 8.0 %collective-permute-start.11 = (bf16[160,384]{1,0:T(8,128)(2,1)S(1)}, bf16[160,384]{1,0:T(8,128)(2,1)S(1)}, u32[]{:S(2)}, u32[]{:S(2)}) collective-permute-start(bf16[160,384]{1,0:T(8,128)(2,1)S(1)} %get-tuple-element.13), channel_id=1, source_target_pairs={{0,7},{1,0},{2,1},{3,2},{4,3},{5,4},{6,5},{7,6},{8,15},{9,8},{10,9... | collective-permute-start | bytes 368648 | tf_op jit(solution)/shard_map/ppermute | solution.py:63
  79.6 9.0 %collective-permute-start.8 = (bf16[320,384]{1,0:T(8,128)(2,1)S(1)}, bf16[320,384]{1,0:T(8,128)(2,1)S(1)}, u32[]{:S(2)}, u32[]{:S(2)}) collective-permute-start(bf16[320,384]{1,0:T(8,128)(2,1)S(1)} %pad_maximum_fusion.5), channel_id=1, source_target_pairs={{0,1},{1,2},{2,3},{3,4},{4,5},{5,6},{6,7},{7,0},{8,9},{9,10},{10,1... | collective-permute-start | bytes 737288 | tf_op jit(solution)/shard_map/ppermute | solution.py:67
  84.2 14.5 %collective-permute-start.12 = (bf16[320,384]{1,0:T(8,128)(2,1)}, bf16[320,384]{1,0:T(8,128)(2,1)}, u32[]{:S(2)}, u32[]{:S(2)}) collective-permute-start(bf16[320,384]{1,0:T(8,128)(2,1)} %pad_maximum_fusion.6), channel_id=1, source_target_pairs={{0,7},{1,0},{2,1},{3,2},{4,3},{5,4},{6,5},{7,6},{8,15},{9,8},{10,9... | collective-permute-start | bytes 737288 | tf_op jit(solution)/shard_map/ppermute | solution.py:68
  88.6 10.1 %copy-start.4 = (bf16[160,384]{1,0:T(8,128)(2,1)S(1)}, bf16[160,384]{1,0:T(8,128)(2,1)}, u32[]{:S(2)}) copy-start(bf16[160,384]{1,0:T(8,128)(2,1)} %get-tuple-element.7) | copy-start | bytes 368644
  88.6 10.1 %copy-start.6 = (bf16[160,384]{1,0:T(8,128)(2,1)S(1)}, bf16[160,384]{1,0:T(8,128)(2,1)}, u32[]{:S(2)}) copy-start(bf16[160,384]{1,0:T(8,128)(2,1)} %get-tuple-element.14) | copy-start | bytes 368644
  88.6 13.3 %copy-start.2 = (bf16[160,384]{1,0:T(8,128)(2,1)S(1)}, bf16[160,384]{1,0:T(8,128)(2,1)}, u32[]{:S(2)}) copy-start(bf16[160,384]{1,0:T(8,128)(2,1)} %get-tuple-element.11) | copy-start | bytes 368644
  88.6 13.3 %copy-start.5 = (bf16[160,384]{1,0:T(8,128)(2,1)S(1)}, bf16[160,384]{1,0:T(8,128)(2,1)}, u32[]{:S(2)}) copy-start(bf16[160,384]{1,0:T(8,128)(2,1)} %get-tuple-element.18) | copy-start | bytes 368644
  88.6 37.9 %copy-start.3 = (bf16[160,384]{1,0:T(8,128)(2,1)S(1)}, bf16[160,384]{1,0:T(8,128)(2,1)}, u32[]{:S(2)}) copy-start(bf16[160,384]{1,0:T(8,128)(2,1)} %get-tuple-element.15) | copy-start | bytes 368644
  88.7 13.2 %collective-permute-start.9 = (bf16[320,384]{1,0:T(8,128)(2,1)S(1)}, bf16[320,384]{1,0:T(8,128)(2,1)S(1)}, u32[]{:S(2)}, u32[]{:S(2)}) collective-permute-start(bf16[320,384]{1,0:T(8,128)(2,1)S(1)} %add_convert_fusion.4), channel_id=1, source_target_pairs={{0,1},{1,2},{2,3},{3,4},{4,5},{5,6},{6,7},{7,0},{8,9},{9,10},{10,1... | collective-permute-start | bytes 737288 | tf_op jit(solution)/shard_map/ppermute | solution.py:67
  93.4 42.3 %all-to-all-start.1 = ((bf16[8,160,384]{2,1,0:T(8,128)(2,1)}), bf16[8,160,384]{2,1,0:T(8,128)(2,1)S(1)}, u32[]{:S(2)}, u32[]{:S(2)}) async-start(bf16[8,160,384]{2,1,0:T(8,128)(2,1)} %bitcast.33), calls=%async_computation.1 | async-start | bytes 1966080 | tf_op jit(solution)/shard_map/all_to_all | solution.py:47
  99.7 26.8 %collective-permute-start.13 = (bf16[320,384]{1,0:T(8,128)(2,1)S(1)}, bf16[320,384]{1,0:T(8,128)(2,1)S(1)}, u32[]{:S(2)}, u32[]{:S(2)}) collective-permute-start(bf16[320,384]{1,0:T(8,128)(2,1)S(1)} %add_convert_fusion.2), channel_id=1, source_target_pairs={{0,7},{1,0},{2,1},{3,2},{4,3},{5,4},{6,5},{7,6},{8,15},{9,8},{10,9... | collective-permute-start | bytes 737288 | tf_op jit(solution)/shard_map/ppermute | solution.py:68
  102.0 26.7 %collective-permute-start.10 = (bf16[320,384]{1,0:T(8,128)(2,1)S(1)}, bf16[320,384]{1,0:T(8,128)(2,1)S(1)}, u32[]{:S(2)}, u32[]{:S(2)}) collective-permute-start(bf16[320,384]{1,0:T(8,128)(2,1)S(1)} %add_convert_fusion.3), channel_id=1, source_target_pairs={{0,1},{1,2},{2,3},{3,4},{4,5},{5,6},{6,7},{7,0},{8,9},{9,10},{10,1... | collective-permute-start | bytes 737288 | tf_op jit(solution)/shard_map/ppermute | solution.py:67
  126.6 8.2 %collective-permute-start.14 = (bf16[320,384]{1,0:T(8,128)(2,1)S(1)}, bf16[320,384]{1,0:T(8,128)(2,1)S(1)}, u32[]{:S(2)}, u32[]{:S(2)}) collective-permute-start(bf16[320,384]{1,0:T(8,128)(2,1)S(1)} %add_convert_fusion.1), channel_id=1, source_target_pairs={{0,7},{1,0},{2,1},{3,2},{4,3},{5,4},{6,5},{7,6},{8,15},{9,8},{10,9... | collective-permute-start | bytes 737288 | tf_op jit(solution)/shard_map/ppermute | solution.py:68
  134.9 35.6 %copy-start.7 = (s32[128,2]{0,1:T(2,128)S(1)}, s32[128,2]{0,1:T(2,128)}, u32[]{:S(2)}) copy-start(s32[128,2]{0,1:T(2,128)} %param.3) | copy-start | bytes 3076
  135.7 30.5 %all-to-all-start.3 = ((bf16[8,40,384]{2,1,0:T(8,128)(2,1)}), bf16[8,40,384]{2,1,0:T(8,128)(2,1)S(1)}, u32[]{:S(2)}, u32[]{:S(2)}) async-start(bf16[8,40,384]{2,1,0:T(8,128)(2,1)} %bitcast.55), calls=%async_computation.3 | async-start | bytes 491520 | tf_op jit(solution)/shard_map/all_to_all | solution.py:85
  166.2 18.4 %all-to-all-start.2 = ((bf16[8,40,384]{2,1,0:T(8,128)(2,1)}), bf16[8,40,384]{2,1,0:T(8,128)(2,1)S(1)}, u32[]{:S(2)}, u32[]{:S(2)}) async-start(bf16[8,40,384]{2,1,0:T(8,128)(2,1)} %bitcast.34), calls=%async_computation.2 | async-start | bytes 491520 | tf_op jit(solution)/shard_map/all_to_all | solution.py:85

commit v4 on v3

--- a/solution.py
+++ b/solution.py
@@ -15,9 +15,11 @@
     return [(i, (i + shift) % SIZES["m"]) for i in range(SIZES["m"])]
 
 
-def gather_column(slab):
+def gather_columns(slab):
+    opposite = lambda value: lax.ppermute(value, ("xh", "xp"), WEIGHT_SWAP)
     pair = jnp.stack([slab, lax.ppermute(slab, "h", SWAP)])
-    return jnp.concatenate([pair, lax.ppermute(pair, "m", turn(1)), lax.ppermute(pair, "m", turn(-1))])
+    rest = jnp.concatenate([lax.ppermute(pair, "m", turn(1)), lax.ppermute(pair, "m", turn(-1))])
+    return jnp.concatenate([pair, rest]), opposite(pair), opposite(rest)
 
 
 def block_places():
@@ -27,7 +29,7 @@
     for shift in (0, -1, 1):
         at = (m + shift + count) % count
         zs += [h * count + at, (1 - h) * count + at]
-    xs = [2 * x_high + xp for xp in range(2)] + [3 - 2 * x_high - xp for xp in range(2)]
+    xs = [x for xp in range(2) for x in (2 * x_high + xp, 3 - 2 * x_high - xp)]
     return jnp.stack([x * SIZES["h"] * count + z for x in xs for z in zs]).astype(jnp.int32)
 
 
@@ -48,7 +50,7 @@
     return jnp.sum(parts.astype(jnp.float32), axis=0).astype(jnp.bfloat16)
 
 
-def sum_by_arms(low, high):
+def sum_by_arms(low, high, before):
     n = low.shape[0]
     mid = n // 2
     me = lax.axis_index("t")
@@ -63,13 +65,14 @@
     last = lax.ppermute(pick(high, mid), "t", down)
     going_up = jnp.concatenate([narrow(wide(pick(low, mid - 1)) + wide(first)), pick(high, mid - 1)])
     going_down = jnp.concatenate([pick(low, mid + 1), narrow(wide(pick(high, mid + 1)) + wide(last))])
+    going_up, going_down, before = lax.optimization_barrier((going_up, going_down, before))
     for step in range(1, mid):
         from_below = lax.ppermute(going_up, "t", up)
         from_above = lax.ppermute(going_down, "t", down)
         if step < mid - 1:
             going_up = narrow(wide(both(mid - 1 - step)) + wide(from_below))
             going_down = narrow(wide(both(mid + 1 + step)) + wide(from_above))
-    return narrow(wide(both(0)) + wide(from_below) + wide(from_above))
+    return narrow(wide(both(0)) + wide(from_below) + wide(from_above)), before
 
 
 def give_back(near, far, owners, capacity):
@@ -86,20 +89,17 @@
     return got.reshape(-1, rows, features)
 
 
-def place_kernel(places, onehot, *refs, width):
-    out = refs[-1]
+def place_kernel(places, onehot, piece, out, *, width):
     cores = SIZES["c"]
-    at = 0
-    for piece in refs[:-1]:
-        for xp in range(SIZES["xp"]):
-            for b in range(piece.shape[2] // width):
-                block = jnp.concatenate(
-                    [piece[xp * cores + c, :, b * width:(b + 1) * width] for c in range(cores)], axis=1
-                )
-                result = jnp.dot(onehot[...], block, preferred_element_type=jnp.float32)
-                start = pl.multiple_of(places[at] * (cores * width), cores * width)
-                out[:, pl.ds(start, cores * width)] = result.astype(out.dtype)
-                at += 1
+    count = piece.shape[2] // width
+    for xp in range(SIZES["xp"]):
+        for b in range(count):
+            block = jnp.concatenate(
+                [piece[xp * cores + c, :, b * width:(b + 1) * width] for c in range(cores)], axis=1
+            )
+            result = jnp.dot(onehot[...], block, preferred_element_type=jnp.float32)
+            start = pl.multiple_of(places[xp * count + b] * (cores * width), cores * width)
+            out[:, pl.ds(start, cores * width)] = result.astype(out.dtype)
 
 
 def shards(routes, upgrad, weight):
@@ -109,20 +109,23 @@
     rows = owners * capacity
 
     own = upgrad.reshape(tensor_count, rows, hidden)
-    column = gather_column(slab)
+    column, other_first, other_rest = gather_columns(slab)
     x_rows = lax.ppermute(own, "xp", SWAP)
     near_rows = jnp.concatenate([own, lax.ppermute(own, "c", SWAP)], axis=1)
+    x_rows, _, other_first = lax.optimization_barrier((x_rows, column, other_first))
     far_rows = jnp.concatenate([x_rows, lax.ppermute(x_rows, "c", SWAP)], axis=1)
-    other_column = lax.ppermute(column, ("xh", "xp"), WEIGHT_SWAP)
 
-    near = sum_direct(product(near_rows, column))
-    far = sum_direct(product(far_rows, column))
-    summed = sum_by_arms(product(near_rows, other_column), product(far_rows, other_column))
+    near = product(near_rows, column)
+    far = product(far_rows, column)
+    _, _, other_first, other_rest = lax.optimization_barrier((near, far, other_first, other_rest))
+    other_column = jnp.concatenate([other_first, other_rest])
+    near = sum_direct(near)
+    summed, near = sum_by_arms(product(near_rows, other_column), product(far_rows, other_column), near)
+    far = sum_direct(far)
     half = summed.shape[0] // 2
-    pieces = [
-        give_back(near, far, owners, capacity),
-        give_back(summed[:half], summed[half:], owners, capacity),
-    ]
+    near = jnp.concatenate([near, summed[:half]], axis=1)
+    far = jnp.concatenate([far, summed[half:]], axis=1)
+    piece = give_back(near, far, owners, capacity)
 
     owner_ids = lax.iota(jnp.int32, owners)
     is_routed = jnp.any(routes[:, :, None] == owner_ids[None, None, :], axis=1)
@@ -135,14 +138,14 @@
 
     smem = pl.BlockSpec(memory_space=pltpu.SMEM)
     vmem = pl.BlockSpec(memory_space=pltpu.VMEM)
-    total = sum(piece.shape[0] * piece.shape[2] for piece in pieces)
+    total = piece.shape[0] * piece.shape[2]
     return pl.pallas_call(
         body,
         out_shape=jax.ShapeDtypeStruct((routes.shape[0], total), jnp.bfloat16),
-        in_specs=[smem, vmem] + [vmem] * len(pieces),
+        in_specs=[smem, vmem, vmem],
         out_specs=vmem,
         compiler_params=pltpu.CompilerParams(vmem_limit_bytes=32 * 1024 * 1024),
-    )(block_places(), onehot, *pieces)
+    )(block_places(), onehot, piece)
 
 
 def solution(mesh):

time: 188 us -> 178 us (0.947)
  the two profiles are of different devices: /device:TPU:153 before, /device:TPU:129 now
where the time goes in v4:
time: 178 us; the launch traced here: 177 us
  starting transfers between devices  80.7 us (45%)
  waiting for transfers between devices  72.4 us (41%)
  other arithmetic  11.5 us (6%)
  matrix products  8.11 us (5%)
  Pallas kernels  1.87 us (1%)
    all_to_all x1, waiting for transfers between devices, give_back(): lax.all_to_all(both.reshape(-1, capacity, features), ('xp', 'c', 'e'), 0, 0)  23.8 us
    ppermute x3, waiting for transfers between devices, sum_by_arms(): from_above = lax.ppermute(going_down, 't', down)  22 us
    all_to_all x1, starting transfers between devices, give_back(): lax.all_to_all(both.reshape(-1, capacity, features), ('xp', 'c', 'e'), 0, 0)  14.5 us
    all_to_all x2, starting transfers between devices, sum_direct(): parts = lax.all_to_all(partial, 't', 0, 0)  12.7 us
    ppermute x3, starting transfers between devices, sum_by_arms(): from_above = lax.ppermute(going_down, 't', down)  11.1 us
    ppermute x1, waiting for transfers between devices, sum_by_arms(): first = lax.ppermute(pick(low, mid), 't', up)  10.7 us
    ppermute x1, starting transfers between devices, gather_columns(): pair = jnp.stack([slab, lax.ppermute(slab, 'h', SWAP)])  8.83 us
    dot_general x4, matrix products, product(): lax.dot_general(rows.reshape(tensor_count * count, hidden), blocks.reshap...  8.11 us
  transfers between devices with their start and end apart: 19, of which 9 were waited for; matrix products, arithmetic and copies ran while one was open for 11% of the time, Pallas kernels for 0%

profile of v4, /device:TPU:129, one launch (start us, length us, event | category | flops | bytes accessed | tf_op | source)
XLA Modules:
  0.0 176.8 jit_solution(14360040873053751049)
XLA Ops:
  0.0 3.2 %collective-permute-start.4 = (bf16[8,80,1024]{2,1,0:T(8,128)(2,1)}, bf16[8,80,1024]{2,1,0:T(8,128)(2,1)S(1)}, u32[]{:S(2)}, u32[]{:S(2)}) collective-permute-start(bf16[8,80,1024]{2,1,0:T(8,128)(2,1)} %bitcast.86), channel_id=1, source_target_pairs={{0,192},{192,0},{1,193},{193,1},{2,194},{194,2},{3,195},{195,3},{4... | collective-permute-start | bytes 3932168 | tf_op jit(solution)/shard_map/ppermute | solution.py:113
  3.2 8.8 %collective-permute-start.1 = (bf16[64,1024]{1,0:T(8,128)(2,1)}, bf16[64,1024]{1,0:T(8,128)(2,1)S(1)}, u32[]{:S(2)}, u32[]{:S(2)}) collective-permute-start(bf16[64,1024]{1,0:T(8,128)(2,1)} %bitcast.97), channel_id=1, source_target_pairs={{0,96},{96,0},{1,97},{97,1},{2,98},{98,2},{3,99},{99,3},{4,100},{1... | collective-permute-start | bytes 393224 | tf_op jit(solution)/shard_map/ppermute | solution.py:20
  12.1 3.1 %collective-permute-start = (bf16[8,80,1024]{2,1,0:T(8,128)(2,1)}, bf16[8,80,1024]{2,1,0:T(8,128)(2,1)}, u32[]{:S(2)}, u32[]{:S(2)}) collective-permute-start(bf16[8,80,1024]{2,1,0:T(8,128)(2,1)} %bitcast.87), channel_id=1, source_target_pairs={{0,16},{16,0},{1,17},{17,1},{2,18},{18,2},{3,19},{19,3},{4,20},{20... | collective-permute-start | bytes 3932168 | tf_op jit(solution)/shard_map/ppermute | solution.py:114
  15.2 3.7 %collective-permute-done.1 = bf16[64,1024]{1,0:T(8,128)(2,1)S(1)} collective-permute-done((bf16[64,1024]{1,0:T(8,128)(2,1)}, bf16[64,1024]{1,0:T(8,128)(2,1)S(1)}, u32[]{:S(2)}, u32[]{:S(2)}) %collective-permute-start.1) | collective-permute-done | bytes 131104 | tf_op jit(solution)/shard_map/ppermute | solution.py:20
  18.9 0.9 pad_maximum_fusion.8
  19.8 1.9 %collective-permute-start.3 = (bf16[2,64,1024]{2,1,0:T(8,128)(2,1)S(1)}, bf16[2,64,1024]{2,1,0:T(8,128)(2,1)S(1)}, u32[]{:S(2)}, u32[]{:S(2)}) collective-permute-start(bf16[2,64,1024]{2,1,0:T(8,128)(2,1)S(1)} %pad_maximum_fusion.8), channel_id=1, source_target_pairs={{0,64},{32,0},{64,32},{1,65},{33,1},{65,33},{2,66},{34,2},{66,34},... | collective-permute-start | bytes 786440 | tf_op jit(solution)/shard_map/ppermute | solution.py:21
  21.8 4.3 %collective-permute-start.2 = (bf16[2,64,1024]{2,1,0:T(8,128)(2,1)S(1)}, bf16[2,64,1024]{2,1,0:T(8,128)(2,1)S(1)}, u32[]{:S(2)}, u32[]{:S(2)}) collective-permute-start(bf16[2,64,1024]{2,1,0:T(8,128)(2,1)S(1)} %pad_maximum_fusion.8), channel_id=1, source_target_pairs={{0,32},{32,64},{64,0},{1,33},{33,65},{65,1},{2,34},{34,66},{66,2},... | collective-permute-start | bytes 786440 | tf_op jit(solution)/shard_map/ppermute | solution.py:21
  26.0 3.0 %collective-permute-start.5 = (bf16[2,64,1024]{2,1,0:T(8,128)(2,1)S(1)}, bf16[2,64,1024]{2,1,0:T(8,128)(2,1)S(1)}, u32[]{:S(2)}, u32[]{:S(2)}) collective-permute-start(bf16[2,64,1024]{2,1,0:T(8,128)(2,1)S(1)} %pad_maximum_fusion.8), channel_id=1, source_target_pairs={{0,576},{192,384},{384,192},{576,0},{1,577},{193,385},{385,193},{5... | collective-permute-start | bytes 786440 | tf_op jit(solution)/shard_map/ppermute | solution.py:19
  29.1 1.0 collective-permute-done.3
  30.1 6.4 %collective-permute-done.2 = bf16[2,64,1024]{2,1,0:T(8,128)(2,1)S(1)} collective-permute-done((bf16[2,64,1024]{2,1,0:T(8,128)(2,1)S(1)}, bf16[2,64,1024]{2,1,0:T(8,128)(2,1)S(1)}, u32[]{:S(2)}, u32[]{:S(2)}) %collective-permute-start.2) | collective-permute-done | bytes 262176 | tf_op jit(solution)/shard_map/ppermute | solution.py:21
  36.5 1.9 %pad_maximum_fusion.2 = bf16[6,64,1024]{2,1,0:T(8,128)(2,1)} fusion(bf16[2,64,1024]{2,1,0:T(8,128)(2,1)S(1)} %collective-permute-done.3, bf16[2,64,1024]{2,1,0:T(8,128)(2,1)S(1)} %collective-permute-done.2, bf16[1,64,1024]{2,1,0:T(8,128)(2,1)S(1)} %bitcast.99, bf16[1,64,1024]{2,1,0:T(8,128)(2,1)} %param.5), kind=kLoop, calls=%fused_computation.6 | loop fusion | flops 1179648 | bytes 1572864 | tf_op jit(solution)/shard_map/concatenate | solution.py:22
  38.3 0.0 collective-permute-done.5
  38.4 0.7 copy-done.4
  39.1 2.4 %collective-permute-start.6 = (bf16[8,80,1024]{2,1,0:T(8,128)(2,1)S(1)}, bf16[8,80,1024]{2,1,0:T(8,128)(2,1)}, u32[]{:S(2)}, u32[]{:S(2)}) collective-permute-start(bf16[8,80,1024]{2,1,0:T(8,128)(2,1)S(1)} %collective-permute-done.4), channel_id=1, source_target_pairs={{0,16},{16,0},{1,17},{17,1},{2,18},{18,2},{3,19},{19,3},{4,20},{20... | collective-permute-start | bytes 3932168 | tf_op jit(solution)/shard_map/ppermute | solution.py:116
  41.6 0.8 pad_maximum_fusion.4
  42.4 3.1 %collective-permute-start.7 = (bf16[4,64,1024]{2,1,0:T(8,128)(2,1)}, bf16[4,64,1024]{2,1,0:T(8,128)(2,1)}, u32[]{:S(2)}, u32[]{:S(2)}) collective-permute-start(bf16[4,64,1024]{2,1,0:T(8,128)(2,1)} %pad_maximum_fusion.4), channel_id=1, source_target_pairs={{0,576},{192,384},{384,192},{576,0},{1,577},{193,385},{385,193},{5... | collective-permute-start | bytes 1572872 | tf_op jit(solution)/shard_map/ppermute | solution.py:19
  45.6 1.7 pad_maximum_fusion
  47.3 2.5 %convolution_convert_fusion.3 = bf16[1280,384]{1,0:T(8,128)(2,1)} fusion(bf16[1280,1024]{1,0:T(8,128)(2,1)S(1)} %bitcast.84, bf16[384,1024]{1,0:T(8,128)(2,1)S(1)} %bitcast.93), kind=kOutput, calls=%fused_computation.3 | convolution fusion | flops 1007124480 | bytes 4390912 | tf_op jit(solution)/shard_map/dot_general | solution.py:39
  49.8 6.8 %all-to-all-start = ((bf16[8,160,384]{2,1,0:T(8,128)(2,1)}), bf16[8,160,384]{2,1,0:T(8,128)(2,1)S(1)}, u32[]{:S(2)}, u32[]{:S(2)}) async-start(bf16[8,160,384]{2,1,0:T(8,128)(2,1)} %bitcast.31), calls=%async_computation | async-start | bytes 1966080 | tf_op jit(solution)/shard_map/all_to_all | solution.py:49
  56.6 1.7 pad_maximum_fusion.1
  58.3 2.5 %convolution_convert_fusion.2 = bf16[1280,384]{1,0:T(8,128)(2,1)} fusion(bf16[1280,1024]{1,0:T(8,128)(2,1)S(1)} %bitcast.82, bf16[384,1024]{1,0:T(8,128)(2,1)S(1)} %bitcast.94), kind=kOutput, calls=%fused_computation.2 | convolution fusion | flops 1007124480 | bytes 4390912 | tf_op jit(solution)/shard_map/dot_general | solution.py:39
  60.8 1.1 pad_maximum_fusion.3
  62.0 1.6 convolution_convert_fusion.1
  63.5 0.1 dynamic-slice_bitcast_fusion.9
  63.6 3.4 %collective-permute-start.8 = (bf16[160,384]{1,0:T(8,128)(2,1)S(1)}, bf16[160,384]{1,0:T(8,128)(2,1)S(1)}, u32[]{:S(2)}, u32[]{:S(2)}) collective-permute-start(bf16[160,384]{1,0:T(8,128)(2,1)S(1)} %get-tuple-element.27), channel_id=1, source_target_pairs={{0,1},{1,2},{2,3},{3,4},{4,5},{5,6},{6,7},{7,0},{8,9},{9,10},{10,1... | collective-permute-start | bytes 368648 | tf_op jit(solution)/shard_map/ppermute | solution.py:64
  67.0 1.6 convolution_convert_fusion
  68.6 0.1 dynamic-slice_bitcast_fusion.8
  68.7 3.1 %collective-permute-start.9 = (bf16[160,384]{1,0:T(8,128)(2,1)S(1)}, bf16[160,384]{1,0:T(8,128)(2,1)S(1)}, u32[]{:S(2)}, u32[]{:S(2)}) collective-permute-start(bf16[160,384]{1,0:T(8,128)(2,1)S(1)} %get-tuple-element.33), channel_id=1, source_target_pairs={{0,7},{1,0},{2,1},{3,2},{4,3},{5,4},{6,5},{7,6},{8,15},{9,8},{10,9... | collective-permute-start | bytes 368648 | tf_op jit(solution)/shard_map/ppermute | solution.py:65
  71.8 10.7 %collective-permute-done.8 = bf16[160,384]{1,0:T(8,128)(2,1)S(1)} collective-permute-done((bf16[160,384]{1,0:T(8,128)(2,1)S(1)}, bf16[160,384]{1,0:T(8,128)(2,1)S(1)}, u32[]{:S(2)}, u32[]{:S(2)}) %collective-permute-start.8) | collective-permute-done | bytes 122912 | tf_op jit(solution)/shard_map/ppermute | solution.py:64
  82.6 0.7 pad_maximum_fusion.9
  83.4 0.7 pad_maximum_fusion.10
  84.1 0.3 all-to-all-done
  84.4 0.1 reduce_sum.24
  84.6 3.4 %collective-permute-start.13 = (bf16[320,384]{1,0:T(8,128)(2,1)}, bf16[320,384]{1,0:T(8,128)(2,1)S(1)}, u32[]{:S(2)}, u32[]{:S(2)}) collective-permute-start(bf16[320,384]{1,0:T(8,128)(2,1)} %pad_maximum_fusion.10), channel_id=1, source_target_pairs={{0,7},{1,0},{2,1},{3,2},{4,3},{5,4},{6,5},{7,6},{8,15},{9,8},{10,9... | collective-permute-start | bytes 737288 | tf_op jit(solution)/shard_map/ppermute | solution.py:71
  88.0 1.9 %collective-permute-start.10 = (bf16[320,384]{1,0:T(8,128)(2,1)}, bf16[320,384]{1,0:T(8,128)(2,1)S(1)}, u32[]{:S(2)}, u32[]{:S(2)}) collective-permute-start(bf16[320,384]{1,0:T(8,128)(2,1)} %pad_maximum_fusion.9), channel_id=1, source_target_pairs={{0,1},{1,2},{2,3},{3,4},{4,5},{5,6},{6,7},{7,0},{8,9},{9,10},{10,1... | collective-permute-start | bytes 737288 | tf_op jit(solution)/shard_map/ppermute | solution.py:70
  89.9 5.9 %all-to-all-start.1 = ((bf16[8,160,384]{2,1,0:T(8,128)(2,1)}), bf16[8,160,384]{2,1,0:T(8,128)(2,1)S(1)}, u32[]{:S(2)}, u32[]{:S(2)}) async-start(bf16[8,160,384]{2,1,0:T(8,128)(2,1)} %bitcast.33), calls=%async_computation.1 | async-start | bytes 1966080 | tf_op jit(solution)/shard_map/all_to_all | solution.py:49
  95.7 0.0 collective-permute-done.13
  95.8 0.1 add_convert_fusion.2
  95.8 4.6 %collective-permute-start.14 = (bf16[320,384]{1,0:T(8,128)(2,1)S(1)}, bf16[320,384]{1,0:T(8,128)(2,1)S(1)}, u32[]{:S(2)}, u32[]{:S(2)}) collective-permute-start(bf16[320,384]{1,0:T(8,128)(2,1)S(1)} %add_convert_fusion.2), channel_id=1, source_target_pairs={{0,7},{1,0},{2,1},{3,2},{4,3},{5,4},{6,5},{7,6},{8,15},{9,8},{10,9... | collective-permute-start | bytes 737288 | tf_op jit(solution)/shard_map/ppermute | solution.py:71
  100.4 0.0 collective-permute-done.10
  100.4 0.1 add_convert_fusion.4
  100.5 1.9 %collective-permute-start.11 = (bf16[320,384]{1,0:T(8,128)(2,1)S(1)}, bf16[320,384]{1,0:T(8,128)(2,1)S(1)}, u32[]{:S(2)}, u32[]{:S(2)}) collective-permute-start(bf16[320,384]{1,0:T(8,128)(2,1)S(1)} %add_convert_fusion.4), channel_id=1, source_target_pairs={{0,1},{1,2},{2,3},{3,4},{4,5},{5,6},{6,7},{7,0},{8,9},{9,10},{10,1... | collective-permute-start | bytes 737288 | tf_op jit(solution)/shard_map/ppermute | solution.py:70
  102.4 20.4 %collective-permute-done.14 = bf16[320,384]{1,0:T(8,128)(2,1)S(1)} collective-permute-done((bf16[320,384]{1,0:T(8,128)(2,1)S(1)}, bf16[320,384]{1,0:T(8,128)(2,1)S(1)}, u32[]{:S(2)}, u32[]{:S(2)}) %collective-permute-start.14) | collective-permute-done | bytes 245792 | tf_op jit(solution)/shard_map/ppermute | solution.py:71
  122.9 0.1 add_convert_fusion.1
  122.9 3.2 %collective-permute-start.15 = (bf16[320,384]{1,0:T(8,128)(2,1)S(1)}, bf16[320,384]{1,0:T(8,128)(2,1)S(1)}, u32[]{:S(2)}, u32[]{:S(2)}) collective-permute-start(bf16[320,384]{1,0:T(8,128)(2,1)S(1)} %add_convert_fusion.1), channel_id=1, source_target_pairs={{0,7},{1,0},{2,1},{3,2},{4,3},{5,4},{6,5},{7,6},{8,15},{9,8},{10,9... | collective-permute-start | bytes 737288 | tf_op jit(solution)/shard_map/ppermute | solution.py:71
  126.1 0.1 add_convert_fusion.3
  126.2 2.1 %collective-permute-start.12 = (bf16[320,384]{1,0:T(8,128)(2,1)S(1)}, bf16[320,384]{1,0:T(8,128)(2,1)S(1)}, u32[]{:S(2)}, u32[]{:S(2)}) collective-permute-start(bf16[320,384]{1,0:T(8,128)(2,1)S(1)} %add_convert_fusion.3), channel_id=1, source_target_pairs={{0,1},{1,2},{2,3},{3,4},{4,5},{5,6},{6,7},{7,0},{8,9},{9,10},{10,1... | collective-permute-start | bytes 737288 | tf_op jit(solution)/shard_map/ppermute | solution.py:70
  128.3 1.6 collective-permute-done.15
  129.9 4.5 %collective-permute-done.12 = bf16[320,384]{1,0:T(8,128)(2,1)S(1)} collective-permute-done((bf16[320,384]{1,0:T(8,128)(2,1)S(1)}, bf16[320,384]{1,0:T(8,128)(2,1)S(1)}, u32[]{:S(2)}, u32[]{:S(2)}) %collective-permute-start.12) | collective-permute-done | bytes 245792 | tf_op jit(solution)/shard_map/ppermute | solution.py:70
  134.3 0.1 add_convert_fusion
  134.5 0.0 copy-start.6
  134.5 0.1 reduce_sum.25
  134.7 0.2 broadcast_select_fusion.1
  134.9 0.8 pad_maximum_fusion.5
  135.7 14.5 %all-to-all-start.2 = ((bf16[8,40,768]{2,1,0:T(8,128)(2,1)}), bf16[8,40,768]{2,1,0:T(8,128)(2,1)S(1)}, u32[]{:S(2)}, u32[]{:S(2)}) async-start(bf16[8,40,768]{2,1,0:T(8,128)(2,1)} %bitcast.53), calls=%async_computation.2 | async-start | bytes 983040 | tf_op jit(solution)/shard_map/all_to_all | solution.py:88
  150.3 0.1 copy.18
  150.4 0.1 copy.14
  150.5 0.2 reduce_window_sum.11
  150.7 0.1 copy.15
  150.7 0.1 copy.16
  150.9 0.1 eq.65
  151.0 0.1 stack.105.refs_0_
  151.1 23.8 %all-to-all-done.2 = bf16[8,40,768]{2,1,0:T(8,128)(2,1)S(1)} async-done(((bf16[8,40,768]{2,1,0:T(8,128)(2,1)}), bf16[8,40,768]{2,1,0:T(8,128)(2,1)S(1)}, u32[]{:S(2)}, u32[]{:S(2)}) %all-to-all-start.2) | async-done | bytes 491552 | tf_op jit(solution)/shard_map/all_to_all | solution.py:88
  174.9 1.9 %shard_map.37 = bf16[128,3072]{1,0:T(8,128)(2,1)} custom-call(s32[24]{0:T(128)S(1)} %stack.105.refs_0_, bf16[128,80]{1,0:T(8,128)(2,1)S(1)} %and_convert_fusion.refs_1_, bf16[4,80,768]{2,1,0:T(8,128)(2,1)S(1)} %bitcast.81), custom_call_target="tpu_custom_call" | custom-call | tf_op jit(solution)/shard_map/pallas_call | solution.py:142
  (31 shorter events, 0.2 us)
Async XLA Ops:
  0.0 45.6 %copy-start.2 = (bf16[1,1,8,2,40,1024]{5,4,3,2,1,0:T(8,128)(2,1)S(1)}, bf16[1,1,8,2,40,1024]{5,4,3,2,1,0:T(8,128)(2,1)}, u32[]{:S(2)}) copy-start(bf16[1,1,8,2,40,1024]{5,4,3,2,1,0:T(8,128)(2,1)} %param.4) | copy-start | bytes 3932164
  0.0 38.3 %collective-permute-start.4 = (bf16[8,80,1024]{2,1,0:T(8,128)(2,1)}, bf16[8,80,1024]{2,1,0:T(8,128)(2,1)S(1)}, u32[]{:S(2)}, u32[]{:S(2)}) collective-permute-start(bf16[8,80,1024]{2,1,0:T(8,128)(2,1)} %bitcast.86), channel_id=1, source_target_pairs={{0,192},{192,0},{1,193},{193,1},{2,194},{194,2},{3,195},{195,3},{4... | collective-permute-start | bytes 3932168 | tf_op jit(solution)/shard_map/ppermute | solution.py:113
  3.2 15.7 %collective-permute-start.1 = (bf16[64,1024]{1,0:T(8,128)(2,1)}, bf16[64,1024]{1,0:T(8,128)(2,1)S(1)}, u32[]{:S(2)}, u32[]{:S(2)}) collective-permute-start(bf16[64,1024]{1,0:T(8,128)(2,1)} %bitcast.97), channel_id=1, source_target_pairs={{0,96},{96,0},{1,97},{97,1},{2,98},{98,2},{3,99},{99,3},{4,100},{1... | collective-permute-start | bytes 393224 | tf_op jit(solution)/shard_map/ppermute | solution.py:20
  12.1 33.5 %collective-permute-start = (bf16[8,80,1024]{2,1,0:T(8,128)(2,1)}, bf16[8,80,1024]{2,1,0:T(8,128)(2,1)}, u32[]{:S(2)}, u32[]{:S(2)}) collective-permute-start(bf16[8,80,1024]{2,1,0:T(8,128)(2,1)} %bitcast.87), channel_id=1, source_target_pairs={{0,16},{16,0},{1,17},{17,1},{2,18},{18,2},{3,19},{19,3},{4,20},{20... | collective-permute-start | bytes 3932168 | tf_op jit(solution)/shard_map/ppermute | solution.py:114
  19.8 10.2 %collective-permute-start.3 = (bf16[2,64,1024]{2,1,0:T(8,128)(2,1)S(1)}, bf16[2,64,1024]{2,1,0:T(8,128)(2,1)S(1)}, u32[]{:S(2)}, u32[]{:S(2)}) collective-permute-start(bf16[2,64,1024]{2,1,0:T(8,128)(2,1)S(1)} %pad_maximum_fusion.8), channel_id=1, source_target_pairs={{0,64},{32,0},{64,32},{1,65},{33,1},{65,33},{2,66},{34,2},{66,34},... | collective-permute-start | bytes 786440 | tf_op jit(solution)/shard_map/ppermute | solution.py:21
  21.8 14.7 %collective-permute-start.2 = (bf16[2,64,1024]{2,1,0:T(8,128)(2,1)S(1)}, bf16[2,64,1024]{2,1,0:T(8,128)(2,1)S(1)}, u32[]{:S(2)}, u32[]{:S(2)}) collective-permute-start(bf16[2,64,1024]{2,1,0:T(8,128)(2,1)S(1)} %pad_maximum_fusion.8), channel_id=1, source_target_pairs={{0,32},{32,64},{64,0},{1,33},{33,65},{65,1},{2,34},{34,66},{66,2},... | collective-permute-start | bytes 786440 | tf_op jit(solution)/shard_map/ppermute | solution.py:21
  26.0 12.3 %collective-permute-start.5 = (bf16[2,64,1024]{2,1,0:T(8,128)(2,1)S(1)}, bf16[2,64,1024]{2,1,0:T(8,128)(2,1)S(1)}, u32[]{:S(2)}, u32[]{:S(2)}) collective-permute-start(bf16[2,64,1024]{2,1,0:T(8,128)(2,1)S(1)} %pad_maximum_fusion.8), channel_id=1, source_target_pairs={{0,576},{192,384},{384,192},{576,0},{1,577},{193,385},{385,193},{5... | collective-permute-start | bytes 786440 | tf_op jit(solution)/shard_map/ppermute | solution.py:19
  38.3 0.7 copy-start.4
  39.1 17.6 %collective-permute-start.6 = (bf16[8,80,1024]{2,1,0:T(8,128)(2,1)S(1)}, bf16[8,80,1024]{2,1,0:T(8,128)(2,1)}, u32[]{:S(2)}, u32[]{:S(2)}) collective-permute-start(bf16[8,80,1024]{2,1,0:T(8,128)(2,1)S(1)} %collective-permute-done.4), channel_id=1, source_target_pairs={{0,16},{16,0},{1,17},{17,1},{2,18},{18,2},{3,19},{19,3},{4,20},{20... | collective-permute-start | bytes 3932168 | tf_op jit(solution)/shard_map/ppermute | solution.py:116
  42.4 4.9 %copy-start.3 = (bf16[6,64,1024]{2,1,0:T(8,128)(2,1)S(1)}, bf16[6,64,1024]{2,1,0:T(8,128)(2,1)}, u32[]{:S(2)}) copy-start(bf16[6,64,1024]{2,1,0:T(8,128)(2,1)} %pad_maximum_fusion.2) | copy-start | bytes 2359300
  42.4 18.4 %collective-permute-start.7 = (bf16[4,64,1024]{2,1,0:T(8,128)(2,1)}, bf16[4,64,1024]{2,1,0:T(8,128)(2,1)}, u32[]{:S(2)}, u32[]{:S(2)}) collective-permute-start(bf16[4,64,1024]{2,1,0:T(8,128)(2,1)} %pad_maximum_fusion.4), channel_id=1, source_target_pairs={{0,576},{192,384},{384,192},{576,0},{1,577},{193,385},{385,193},{5... | collective-permute-start | bytes 1572872 | tf_op jit(solution)/shard_map/ppermute | solution.py:19
  47.3 2.5 %copy-start = (bf16[8,160,1024]{2,1,0:T(8,128)(2,1)}, bf16[8,160,1024]{2,1,0:T(8,128)(2,1)S(1)}, u32[]{:S(2)}) copy-start(bf16[8,160,1024]{2,1,0:T(8,128)(2,1)S(1)} %pad_maximum_fusion) | copy-start | bytes 7864324
  49.8 34.7 %all-to-all-start = ((bf16[8,160,384]{2,1,0:T(8,128)(2,1)}), bf16[8,160,384]{2,1,0:T(8,128)(2,1)S(1)}, u32[]{:S(2)}, u32[]{:S(2)}) async-start(bf16[8,160,384]{2,1,0:T(8,128)(2,1)} %bitcast.31), calls=%async_computation | async-start | bytes 1966080 | tf_op jit(solution)/shard_map/all_to_all | solution.py:49
  58.3 2.5 %copy-start.5 = (bf16[2,64,1024]{2,1,0:T(8,128)(2,1)S(1)}, bf16[2,64,1024]{2,1,0:T(8,128)(2,1)}, u32[]{:S(2)}) copy-start(bf16[2,64,1024]{2,1,0:T(8,128)(2,1)} %copy-done.4) | copy-start | bytes 786436
  58.3 3.6 %copy-start.1 = (bf16[8,160,1024]{2,1,0:T(8,128)(2,1)S(1)}, bf16[8,160,1024]{2,1,0:T(8,128)(2,1)}, u32[]{:S(2)}) copy-start(bf16[8,160,1024]{2,1,0:T(8,128)(2,1)} %copy-done) | copy-start | bytes 7864324
  63.6 18.9 %collective-permute-start.8 = (bf16[160,384]{1,0:T(8,128)(2,1)S(1)}, bf16[160,384]{1,0:T(8,128)(2,1)S(1)}, u32[]{:S(2)}, u32[]{:S(2)}) collective-permute-start(bf16[160,384]{1,0:T(8,128)(2,1)S(1)} %get-tuple-element.27), channel_id=1, source_target_pairs={{0,1},{1,2},{2,3},{3,4},{4,5},{5,6},{6,7},{7,0},{8,9},{9,10},{10,1... | collective-permute-start | bytes 368648 | tf_op jit(solution)/shard_map/ppermute | solution.py:64
  68.7 14.6 %collective-permute-start.9 = (bf16[160,384]{1,0:T(8,128)(2,1)S(1)}, bf16[160,384]{1,0:T(8,128)(2,1)S(1)}, u32[]{:S(2)}, u32[]{:S(2)}) collective-permute-start(bf16[160,384]{1,0:T(8,128)(2,1)S(1)} %get-tuple-element.33), channel_id=1, source_target_pairs={{0,7},{1,0},{2,1},{3,2},{4,3},{5,4},{6,5},{7,6},{8,15},{9,8},{10,9... | collective-permute-start | bytes 368648 | tf_op jit(solution)/shard_map/ppermute | solution.py:65
  84.6 11.2 %collective-permute-start.13 = (bf16[320,384]{1,0:T(8,128)(2,1)}, bf16[320,384]{1,0:T(8,128)(2,1)S(1)}, u32[]{:S(2)}, u32[]{:S(2)}) collective-permute-start(bf16[320,384]{1,0:T(8,128)(2,1)} %pad_maximum_fusion.10), channel_id=1, source_target_pairs={{0,7},{1,0},{2,1},{3,2},{4,3},{5,4},{6,5},{7,6},{8,15},{9,8},{10,9... | collective-permute-start | bytes 737288 | tf_op jit(solution)/shard_map/ppermute | solution.py:71
  88.0 12.4 %collective-permute-start.10 = (bf16[320,384]{1,0:T(8,128)(2,1)}, bf16[320,384]{1,0:T(8,128)(2,1)S(1)}, u32[]{:S(2)}, u32[]{:S(2)}) collective-permute-start(bf16[320,384]{1,0:T(8,128)(2,1)} %pad_maximum_fusion.9), channel_id=1, source_target_pairs={{0,1},{1,2},{2,3},{3,4},{4,5},{5,6},{6,7},{7,0},{8,9},{9,10},{10,1... | collective-permute-start | bytes 737288 | tf_op jit(solution)/shard_map/ppermute | solution.py:70
  89.9 44.6 %all-to-all-start.1 = ((bf16[8,160,384]{2,1,0:T(8,128)(2,1)}), bf16[8,160,384]{2,1,0:T(8,128)(2,1)S(1)}, u32[]{:S(2)}, u32[]{:S(2)}) async-start(bf16[8,160,384]{2,1,0:T(8,128)(2,1)} %bitcast.33), calls=%async_computation.1 | async-start | bytes 1966080 | tf_op jit(solution)/shard_map/all_to_all | solution.py:49
  95.8 27.0 %collective-permute-start.14 = (bf16[320,384]{1,0:T(8,128)(2,1)S(1)}, bf16[320,384]{1,0:T(8,128)(2,1)S(1)}, u32[]{:S(2)}, u32[]{:S(2)}) collective-permute-start(bf16[320,384]{1,0:T(8,128)(2,1)S(1)} %add_convert_fusion.2), channel_id=1, source_target_pairs={{0,7},{1,0},{2,1},{3,2},{4,3},{5,4},{6,5},{7,6},{8,15},{9,8},{10,9... | collective-permute-start | bytes 737288 | tf_op jit(solution)/shard_map/ppermute | solution.py:71
  100.5 25.6 %collective-permute-start.11 = (bf16[320,384]{1,0:T(8,128)(2,1)S(1)}, bf16[320,384]{1,0:T(8,128)(2,1)S(1)}, u32[]{:S(2)}, u32[]{:S(2)}) collective-permute-start(bf16[320,384]{1,0:T(8,128)(2,1)S(1)} %add_convert_fusion.4), channel_id=1, source_target_pairs={{0,1},{1,2},{2,3},{3,4},{4,5},{5,6},{6,7},{7,0},{8,9},{9,10},{10,1... | collective-permute-start | bytes 737288 | tf_op jit(solution)/shard_map/ppermute | solution.py:70
  122.9 6.9 %collective-permute-start.15 = (bf16[320,384]{1,0:T(8,128)(2,1)S(1)}, bf16[320,384]{1,0:T(8,128)(2,1)S(1)}, u32[]{:S(2)}, u32[]{:S(2)}) collective-permute-start(bf16[320,384]{1,0:T(8,128)(2,1)S(1)} %add_convert_fusion.1), channel_id=1, source_target_pairs={{0,7},{1,0},{2,1},{3,2},{4,3},{5,4},{6,5},{7,6},{8,15},{9,8},{10,9... | collective-permute-start | bytes 737288 | tf_op jit(solution)/shard_map/ppermute | solution.py:71
  126.2 8.2 %collective-permute-start.12 = (bf16[320,384]{1,0:T(8,128)(2,1)S(1)}, bf16[320,384]{1,0:T(8,128)(2,1)S(1)}, u32[]{:S(2)}, u32[]{:S(2)}) collective-permute-start(bf16[320,384]{1,0:T(8,128)(2,1)S(1)} %add_convert_fusion.3), channel_id=1, source_target_pairs={{0,1},{1,2},{2,3},{3,4},{4,5},{5,6},{6,7},{7,0},{8,9},{9,10},{10,1... | collective-permute-start | bytes 737288 | tf_op jit(solution)/shard_map/ppermute | solution.py:70
  134.5 15.7 %copy-start.6 = (s32[128,2]{0,1:T(2,128)S(1)}, s32[128,2]{0,1:T(2,128)}, u32[]{:S(2)}) copy-start(s32[128,2]{0,1:T(2,128)} %param.3) | copy-start | bytes 3076
  135.7 39.2 %all-to-all-start.2 = ((bf16[8,40,768]{2,1,0:T(8,128)(2,1)}), bf16[8,40,768]{2,1,0:T(8,128)(2,1)S(1)}, u32[]{:S(2)}, u32[]{:S(2)}) async-start(bf16[8,40,768]{2,1,0:T(8,128)(2,1)} %bitcast.53), calls=%async_computation.2 | async-start | bytes 983040 | tf_op jit(solution)/shard_map/all_to_all | solution.py:88

commit v5 on v4

v5 whole, which is shorter than its diff:
```python
import jax
import jax.numpy as jnp
from jax import lax
from jax.experimental import pallas as pl
from jax.experimental.pallas import tpu as pltpu
from jax.sharding import Mesh, PartitionSpec as P

SIZES = {"xh": 2, "xp": 2, "h": 2, "m": 3, "c": 2, "e": 2, "t": 8}
DP = ("xh", "xp", "h", "m", "c")
SWAP = [(0, 1), (1, 0)]
WEIGHT_SWAP = [(i, 3 - i) for i in range(4)]


def turn(shift):
    return [(i, (i + shift) % SIZES["m"]) for i in range(SIZES["m"])]


def gather_columns(slab):
    opposite = lambda value: lax.ppermute(value, ("xh", "xp"), WEIGHT_SWAP)
    pair = jnp.stack([slab, lax.ppermute(slab, "h", SWAP)])
    rest = jnp.concatenate([lax.ppermute(pair, "m", turn(1)), lax.ppermute(pair, "m", turn(-1))])
    return (pair, rest), (opposite(pair), opposite(rest))


def block_places():
    x_high, h, m = lax.axis_index("xh"), lax.axis_index("h"), lax.axis_index("m")
    count = SIZES["m"]
    zs = []
    for shift in (0, -1, 1):
        at = (m + shift + count) % count
        zs += [h * count + at, (1 - h) * count + at]
    xs = [x for xp in range(2) for x in (2 * x_high + xp, 3 - 2 * x_high - xp)]
    return jnp.stack([x * SIZES["h"] * count + z for x in xs for z in zs]).astype(jnp.int32)


def product_kernel(place, *refs):
    (*pieces, first, rest), out = refs[:-1], refs[-1]
    step, rows, hidden = pieces[0].shape
    flat = jnp.concatenate([piece[...] for piece in pieces], axis=1).reshape(-1, hidden)
    dims = (((1,), (1,)), ((), ()))
    results = [
        lax.dot_general(flat, block[...].reshape(-1, hidden), dims, preferred_element_type=jnp.float32)
        for block in (first, rest)
    ]
    result = jnp.concatenate(results, axis=1).astype(out.dtype).reshape(out.shape)
    for k in range(len(pieces)):
        at = pl.multiple_of((place[0] ^ k) * rows, rows)
        out[:, pl.ds(at, rows), :] = result[:, k * rows:(k + 1) * rows]


def product(pieces, blocks):
    tensor_count, rows, hidden = pieces[0].shape
    rows_out = rows * len(pieces)
    features = sum(block.shape[0] * block.shape[1] for block in blocks)
    step = 2
    flops = 2 * tensor_count * rows_out * hidden * features
    moved = 2 * (tensor_count * rows_out * (hidden + features) + features * hidden)
    place = (lax.axis_index("xp") * SIZES["c"] + lax.axis_index("c")).astype(jnp.int32).reshape(1)
    return pl.pallas_call(
        product_kernel,
        grid=(tensor_count // step,),
        out_shape=jax.ShapeDtypeStruct((tensor_count, rows_out, features), jnp.bfloat16),
        in_specs=[pl.BlockSpec(memory_space=pltpu.SMEM)]
        + [pl.BlockSpec((step, rows, hidden), lambda i: (i, 0, 0))] * len(pieces)
        + [pl.BlockSpec(block.shape, lambda i: (0, 0, 0)) for block in blocks],
        out_specs=pl.BlockSpec((step, rows_out, features), lambda i: (i, 0, 0)),
        cost_estimate=pl.CostEstimate(flops=flops, bytes_accessed=moved, transcendentals=0),
        compiler_params=pltpu.CompilerParams(vmem_limit_bytes=14 * 1024 * 1024),
    )(place, *pieces, *blocks)


def sum_by_arms(partial):
    n = partial.shape[0]
    mid = n // 2
    half = partial.shape[1] // 2
    me = lax.axis_index("t")
    up = [(i, (i + 1) % n) for i in range(n)]
    down = [(i, (i - 1) % n) for i in range(n)]
    pick = lambda k: lax.dynamic_index_in_dim(partial, (me + k) % n, 0, keepdims=False)
    wide = lambda value: value.astype(jnp.float32)
    narrow = lambda value: value.astype(jnp.bfloat16)

    first = lax.ppermute(pick(mid)[:half], "t", up)
    last = lax.ppermute(pick(mid)[half:], "t", down)
    above, below = pick(mid - 1), pick(mid + 1)
    going_up = jnp.concatenate([narrow(wide(above[:half]) + wide(first)), above[half:]])
    going_down = jnp.concatenate([below[:half], narrow(wide(below[half:]) + wide(last))])
    for step in range(1, mid):
        from_below = lax.ppermute(going_up, "t", up)
        from_above = lax.ppermute(going_down, "t", down)
        if step < mid - 1:
            going_up = narrow(wide(pick(mid - 1 - step)) + wide(from_below))
            going_down = narrow(wide(pick(mid + 1 + step)) + wide(from_above))
    return narrow(wide(pick(0)) + wide(from_below) + wide(from_above))


def give_back(summed, owners, capacity):
    features = summed.shape[-1]
    got = lax.all_to_all(summed.reshape(-1, capacity, features), ("xp", "c", "e"), 0, 0)
    return got.reshape(-1, owners * capacity, features)


def place_kernel(places, onehot, piece, out, *, width):
    cores = SIZES["c"]
    count = piece.shape[2] // width
    for xp in range(SIZES["xp"]):
        for b in range(count):
            block = jnp.concatenate(
                [piece[xp * cores + c, :, b * width:(b + 1) * width] for c in range(cores)], axis=1
            )
            result = jnp.dot(onehot[...], block, preferred_element_type=jnp.float32)
            start = pl.multiple_of(places[xp * count + b] * (cores * width), cores * width)
            out[:, pl.ds(start, cores * width)] = result.astype(out.dtype)


def shards(routes, upgrad, weight):
    _, _, tensor_count, owners, capacity, hidden = upgrad.shape
    slab = weight[0]
    width = slab.shape[0]
    rows = owners * capacity

    own = upgrad.reshape(tensor_count, rows, hidden)
    column, other = gather_columns(slab)
    x_rows = lax.ppermute(own, "xp", SWAP)
    c_rows = lax.ppermute(own, "c", SWAP)
    x_rows, _, _, first = lax.optimization_barrier((x_rows, *column, other[0]))
    pieces = (own, c_rows, x_rows, lax.ppermute(x_rows, "c", SWAP))

    partial = product(pieces, column)
    partial, *other = lax.optimization_barrier((partial, first, other[1]))
    near = lax.psum_scatter(partial, "t", scatter_dimension=0, tiled=False)
    far = sum_by_arms(product(pieces, other))
    piece = give_back(jnp.concatenate([near, far], axis=1), owners, capacity)

    owner_ids = lax.iota(jnp.int32, owners)
    is_routed = jnp.any(routes[:, :, None] == owner_ids[None, None, :], axis=1)
    slot_index = jnp.cumsum(is_routed.astype(jnp.int32), axis=0) - 1
    onehot = is_routed[:, :, None] & (slot_index[:, :, None] == lax.iota(jnp.int32, capacity)[None, None, :])
    onehot = onehot.reshape(routes.shape[0], rows).astype(jnp.bfloat16)

    def body(*refs):
        place_kernel(*refs, width=width)

    smem = pl.BlockSpec(memory_space=pltpu.SMEM)
    vmem = pl.BlockSpec(memory_space=pltpu.VMEM)
    total = piece.shape[0] * piece.shape[2]
    return pl.pallas_call(
        body,
        out_shape=jax.ShapeDtypeStruct((routes.shape[0], total), jnp.bfloat16),
        in_specs=[smem, vmem, vmem],
        out_specs=vmem,
        compiler_params=pltpu.CompilerParams(vmem_limit_bytes=8 * 1024 * 1024),
    )(block_places(), onehot, piece)


def solution(mesh):
    fine = Mesh(mesh.devices.reshape(tuple(SIZES.values())), tuple(SIZES))
    return jax.shard_map(
        shards,
        mesh=fine,
        in_specs=(
            P(DP + ("e", "t"), None),
            P(DP, "e", None, None, None, "t"),
            P("e", DP, "t"),
        ),
        out_specs=P(DP + ("e", "t"), None),
        check_vma=False,
    )
```

time: 178 us -> 181 us (1.017)
  the two profiles are of different devices: /device:TPU:129 before, /device:TPU:64 now
where the time goes in v5:
time: 181 us
  waiting for transfers between devices  78 us (43%)
  starting transfers between devices  69.8 us (39%)
  between operations  13.8 us (8%)
  Pallas kernels  12.8 us (7%)
  other arithmetic  3.41 us (2%)
  local copies, waits for them, and re-layouts  2.74 us (2%)
    all_to_all x1, waiting for transfers between devices, give_back(): lax.all_to_all(summed.reshape(-1, capacity, features), ('xp', 'c', 'e'),...  24.9 us
    ppermute x3, waiting for transfers between devices, sum_by_arms(): from_below = lax.ppermute(going_up, 't', up)  20 us
    all_to_all x1, starting transfers between devices, give_back(): lax.all_to_all(summed.reshape(-1, capacity, features), ('xp', 'c', 'e'),...  15.4 us
    pallas_call x2, Pallas kernels, product(): pl.pallas_call(product_kernel, grid=(tensor_count // step,), out_shape=ja...  10.9 us
    ppermute x3, starting transfers between devices, sum_by_arms(): from_above = lax.ppermute(going_down, 't', down)  10.5 us
    ppermute x2, waiting for transfers between devices, gather_columns(): opposite = lambda value: lax.ppermute(value, ('xh', 'xp'), WEIGHT_SWAP)  9.2 us
    ppermute x1, starting transfers between devices, gather_columns(): pair = jnp.stack([slab, lax.ppermute(slab, 'h', SWAP)])  9.11 us
    ppermute x3, starting transfers between devices, sum_by_arms(): from_below = lax.ppermute(going_up, 't', up)  7.76 us
  transfers between devices with their start and end apart: 18, of which 13 were waited for; matrix products, arithmetic and copies ran while one was open for 1% of the time, Pallas kernels for 6%

profile of v5, /device:TPU:64, one launch (start us, length us, event | category | flops | bytes accessed | tf_op | source)
XLA Modules:
  0.0 180.6 jit_solution(7650371503786736001)
XLA Ops:
  6.5 0.0 copy-start
  6.5 0.0 reduce-scatter.2.cloned.1.call-start
  6.5 3.5 %collective-permute-start.1 = (bf16[8,80,1024]{2,1,0:T(8,128)(2,1)}, bf16[8,80,1024]{2,1,0:T(8,128)(2,1)S(1)}, u32[]{:S(2)}, u32[]{:S(2)}) collective-permute-start(bf16[8,80,1024]{2,1,0:T(8,128)(2,1)} %bitcast.66), channel_id=1, source_target_pairs={{0,192},{192,0},{1,193},{193,1},{2,194},{194,2},{3,195},{195,3},{4... | collective-permute-start | bytes 3932168 | tf_op jit(solution)/shard_map/ppermute | solution.py:124
  10.1 9.1 %collective-permute-start.2 = (bf16[64,1024]{1,0:T(8,128)(2,1)}, bf16[64,1024]{1,0:T(8,128)(2,1)S(1)}, u32[]{:S(2)}, u32[]{:S(2)}) collective-permute-start(bf16[64,1024]{1,0:T(8,128)(2,1)} %bitcast.74), channel_id=1, source_target_pairs={{0,96},{96,0},{1,97},{97,1},{2,98},{98,2},{3,99},{99,3},{4,100},{1... | collective-permute-start | bytes 393224 | tf_op jit(solution)/shard_map/ppermute | solution.py:20
  19.2 6.3 %collective-permute-done.2 = bf16[64,1024]{1,0:T(8,128)(2,1)S(1)} collective-permute-done((bf16[64,1024]{1,0:T(8,128)(2,1)}, bf16[64,1024]{1,0:T(8,128)(2,1)S(1)}, u32[]{:S(2)}, u32[]{:S(2)}) %collective-permute-start.2) | collective-permute-done | bytes 131104 | tf_op jit(solution)/shard_map/ppermute | solution.py:20
  25.5 0.9 pad_maximum_fusion.1.refs_4_
  26.4 4.0 %collective-permute-start.3 = (bf16[2,64,1024]{2,1,0:T(8,128)(2,1)S(1)}, bf16[2,64,1024]{2,1,0:T(8,128)(2,1)S(1)}, u32[]{:S(2)}, u32[]{:S(2)}) collective-permute-start(bf16[2,64,1024]{2,1,0:T(8,128)(2,1)S(1)} %pad_maximum_fusion.1.refs_4_), channel_id=1, source_target_pairs={{0,32},{32,64},{64,0},{1,33},{33,65},{65,1},{2,34},{34,66},{66,2},... | collective-permute-start | bytes 786440 | tf_op jit(solution)/shard_map/ppermute | solution.py:21
  30.5 2.6 %collective-permute-start.4 = (bf16[2,64,1024]{2,1,0:T(8,128)(2,1)S(1)}, bf16[2,64,1024]{2,1,0:T(8,128)(2,1)S(1)}, u32[]{:S(2)}, u32[]{:S(2)}) collective-permute-start(bf16[2,64,1024]{2,1,0:T(8,128)(2,1)S(1)} %pad_maximum_fusion.1.refs_4_), channel_id=1, source_target_pairs={{0,64},{32,0},{64,32},{1,65},{33,1},{65,33},{2,66},{34,2},{66,34},... | collective-permute-start | bytes 786440 | tf_op jit(solution)/shard_map/ppermute | solution.py:21
  33.0 3.2 %collective-permute-start.5 = (bf16[2,64,1024]{2,1,0:T(8,128)(2,1)S(1)}, bf16[2,64,1024]{2,1,0:T(8,128)(2,1)S(1)}, u32[]{:S(2)}, u32[]{:S(2)}) collective-permute-start(bf16[2,64,1024]{2,1,0:T(8,128)(2,1)S(1)} %pad_maximum_fusion.1.refs_4_), channel_id=1, source_target_pairs={{0,576},{192,384},{384,192},{576,0},{1,577},{193,385},{385,193},{5... | collective-permute-start | bytes 786440 | tf_op jit(solution)/shard_map/ppermute | solution.py:19
  36.2 1.9 %collective-permute-start = (bf16[8,80,1024]{2,1,0:T(8,128)(2,1)}, bf16[8,80,1024]{2,1,0:T(8,128)(2,1)}, u32[]{:S(2)}, u32[]{:S(2)}) collective-permute-start(bf16[8,80,1024]{2,1,0:T(8,128)(2,1)} %bitcast.67), channel_id=1, source_target_pairs={{0,16},{16,0},{1,17},{17,1},{2,18},{18,2},{3,19},{19,3},{4,20},{20... | collective-permute-start | bytes 3932168 | tf_op jit(solution)/shard_map/ppermute | solution.py:125
  38.1 3.7 %collective-permute-done.3 = bf16[2,64,1024]{2,1,0:T(8,128)(2,1)S(1)} collective-permute-done((bf16[2,64,1024]{2,1,0:T(8,128)(2,1)S(1)}, bf16[2,64,1024]{2,1,0:T(8,128)(2,1)S(1)}, u32[]{:S(2)}, u32[]{:S(2)}) %collective-permute-start.3) | collective-permute-done | bytes 262176 | tf_op jit(solution)/shard_map/ppermute | solution.py:21
  41.8 0.7 collective-permute-done.4
  42.6 0.9 collective-permute-done.5.refs_4_
  43.5 0.7 copy-done.3
  44.2 0.0 collective-permute-done.1.refs_2_
  44.2 1.9 %collective-permute-start.6 = (bf16[8,80,1024]{2,1,0:T(8,128)(2,1)S(1)}, bf16[8,80,1024]{2,1,0:T(8,128)(2,1)}, u32[]{:S(2)}, u32[]{:S(2)}) collective-permute-start(bf16[8,80,1024]{2,1,0:T(8,128)(2,1)S(1)} %collective-permute-done.1.refs_2_), channel_id=1, source_target_pairs={{0,16},{16,0},{1,17},{17,1},{2,18},{18,2},{3,19},{19,3},{4,20},{20... | collective-permute-start | bytes 3932168 | tf_op jit(solution)/shard_map/ppermute | solution.py:127
  46.1 3.3 %collective-permute-start.7 = (bf16[4,64,1024]{2,1,0:T(8,128)(2,1)S(1)}, bf16[4,64,1024]{2,1,0:T(8,128)(2,1)}, u32[]{:S(2)}, u32[]{:S(2)}) collective-permute-start(bf16[4,64,1024]{2,1,0:T(8,128)(2,1)S(1)} %constant_dynamic-update-slice_fusion.refs_5_), channel_id=1, source_target_pairs={{0,576},{192,384},{384,192},{576,0},{1,577},{193,385},{385,193},{5... | collective-permute-start | bytes 1572872 | tf_op jit(solution)/shard_map/ppermute | solution.py:19
  49.4 0.0 collective-permute-done.refs_1_
  49.4 0.0 collective-permute-done.6.refs_3_
  49.4 0.0 copy-done
  49.4 5.9 %shard_map.37 = bf16[8,320,384]{2,1,0:T(8,128)(2,1)} custom-call(s32[1]{0:T(128)} %bitcast.26.place, bf16[8,80,1024]{2,1,0:T(8,128)(2,1)S(1)} %bitcast.68, bf16[8,80,1024]{2,1,0:T(8,128)(2,1)} %collective-permute-done.refs_1_, bf16[8,80,1024]{2,1,0:T(8,128)(2,1)S(1)} %collective-permute-done.1.refs_2_, bf16[8,80,1024]{2,1,0:T(8,128)(2,1)} %collective-permute-done.6.refs_3_, ...), custom_call_target="tpu_custom_call" | custom-call | flops 2013265920 | bytes 7995392 | tf_op jit(solution)/shard_map/pallas_call | solution.py:59
  55.3 0.0 copy-done.1
  55.3 8.3 %collective-permute-done.7.refs_5_ = bf16[4,64,1024]{2,1,0:T(8,128)(2,1)} collective-permute-done((bf16[4,64,1024]{2,1,0:T(8,128)(2,1)S(1)}, bf16[4,64,1024]{2,1,0:T(8,128)(2,1)}, u32[]{:S(2)}, u32[]{:S(2)}) %collective-permute-start.7) | collective-permute-done | bytes 524320 | tf_op jit(solution)/shard_map/ppermute | solution.py:19
  63.6 0.0 reduce-scatter.2.cloned.1.call-update
  63.7 0.0 copy-done.4
  63.7 0.0 copy-start.2
  63.7 1.3 copy-done.2
  65.0 5.1 %shard_map.38 = bf16[8,320,384]{2,1,0:T(8,128)(2,1)S(1)} custom-call(s32[1]{0:T(128)} %bitcast.26.place, bf16[8,80,1024]{2,1,0:T(8,128)(2,1)S(1)} %bitcast.69, bf16[8,80,1024]{2,1,0:T(8,128)(2,1)} %collective-permute-done.refs_1_, bf16[8,80,1024]{2,1,0:T(8,128)(2,1)S(1)} %copy-done.2, bf16[8,80,1024]{2,1,0:T(8,128)(2,1)} %collective-permute-done.6.refs_3_, ...), custom_call_target="tpu_custom_call" | custom-call | flops 2013265920 | bytes 7995392 | tf_op jit(solution)/shard_map/pallas_call | solution.py:59
  70.1 0.1 dynamic-slice_bitcast_fusion.4
  70.2 4.7 %collective-permute-start.12 = (bf16[160,384]{1,0:T(8,128)(2,1)S(1)}, bf16[160,384]{1,0:T(8,128)(2,1)S(1)}, u32[]{:S(2)}, u32[]{:S(2)}) collective-permute-start(bf16[160,384]{1,0:T(8,128)(2,1)S(1)} %get-tuple-element.21), channel_id=1, source_target_pairs={{0,7},{1,0},{2,1},{3,2},{4,3},{5,4},{6,5},{7,6},{8,15},{9,8},{10,9... | collective-permute-start | bytes 368648 | tf_op jit(solution)/shard_map/ppermute | solution.py:84
  74.8 1.9 %collective-permute-start.8 = (bf16[160,384]{1,0:T(8,128)(2,1)S(1)}, bf16[160,384]{1,0:T(8,128)(2,1)S(1)}, u32[]{:S(2)}, u32[]{:S(2)}) collective-permute-start(bf16[160,384]{1,0:T(8,128)(2,1)S(1)} %get-tuple-element.19), channel_id=1, source_target_pairs={{0,1},{1,2},{2,3},{3,4},{4,5},{5,6},{6,7},{7,0},{8,9},{9,10},{10,1... | collective-permute-start | bytes 368648 | tf_op jit(solution)/shard_map/ppermute | solution.py:83
  76.8 0.5 collective-permute-done.12
  77.3 5.5 %collective-permute-done.8 = bf16[160,384]{1,0:T(8,128)(2,1)S(1)} collective-permute-done((bf16[160,384]{1,0:T(8,128)(2,1)S(1)}, bf16[160,384]{1,0:T(8,128)(2,1)S(1)}, u32[]{:S(2)}, u32[]{:S(2)}) %collective-permute-start.8) | collective-permute-done | bytes 122912 | tf_op jit(solution)/shard_map/ppermute | solution.py:83
  82.8 0.1 fusion.7
  82.9 1.9 %collective-permute-start.9 = (bf16[320,384]{1,0:T(8,128)(2,1)S(1)}, bf16[320,384]{1,0:T(8,128)(2,1)S(1)}, u32[]{:S(2)}, u32[]{:S(2)}) collective-permute-start(bf16[320,384]{1,0:T(8,128)(2,1)S(1)} %pad_maximum_fusion.2), channel_id=1, source_target_pairs={{0,1},{1,2},{2,3},{3,4},{4,5},{5,6},{6,7},{7,0},{8,9},{9,10},{10,1... | collective-permute-start | bytes 737288 | tf_op jit(solution)/shard_map/ppermute | solution.py:89
  84.9 5.1 %collective-permute-start.13 = (bf16[320,384]{1,0:T(8,128)(2,1)S(1)}, bf16[320,384]{1,0:T(8,128)(2,1)S(1)}, u32[]{:S(2)}, u32[]{:S(2)}) collective-permute-start(bf16[320,384]{1,0:T(8,128)(2,1)S(1)} %pad_maximum_fusion.3), channel_id=1, source_target_pairs={{0,7},{1,0},{2,1},{3,2},{4,3},{5,4},{6,5},{7,6},{8,15},{9,8},{10,9... | collective-permute-start | bytes 737288 | tf_op jit(solution)/shard_map/ppermute | solution.py:90
  90.1 7.4 %collective-permute-done.9 = bf16[320,384]{1,0:T(8,128)(2,1)S(1)} collective-permute-done((bf16[320,384]{1,0:T(8,128)(2,1)S(1)}, bf16[320,384]{1,0:T(8,128)(2,1)S(1)}, u32[]{:S(2)}, u32[]{:S(2)}) %collective-permute-start.9) | collective-permute-done | bytes 245792 | tf_op jit(solution)/shard_map/ppermute | solution.py:89
  97.5 0.1 fusion.2
  97.5 1.9 %collective-permute-start.10 = (bf16[320,384]{1,0:T(8,128)(2,1)S(1)}, bf16[320,384]{1,0:T(8,128)(2,1)S(1)}, u32[]{:S(2)}, u32[]{:S(2)}) collective-permute-start(bf16[320,384]{1,0:T(8,128)(2,1)S(1)} %fusion.2), channel_id=1, source_target_pairs={{0,1},{1,2},{2,3},{3,4},{4,5},{5,6},{6,7},{7,0},{8,9},{9,10},{10,1... | collective-permute-start | bytes 737288 | tf_op jit(solution)/shard_map/ppermute | solution.py:89
  99.5 0.3 collective-permute-done.13
  99.8 12.6 %collective-permute-done.10 = bf16[320,384]{1,0:T(8,128)(2,1)S(1)} collective-permute-done((bf16[320,384]{1,0:T(8,128)(2,1)S(1)}, bf16[320,384]{1,0:T(8,128)(2,1)S(1)}, u32[]{:S(2)}, u32[]{:S(2)}) %collective-permute-start.10) | collective-permute-done | bytes 245792 | tf_op jit(solution)/shard_map/ppermute | solution.py:89
  112.4 0.1 fusion.3
  112.5 0.0 copy-start.5
  112.5 1.9 %collective-permute-start.14 = (bf16[320,384]{1,0:T(8,128)(2,1)S(1)}, bf16[320,384]{1,0:T(8,128)(2,1)S(1)}, u32[]{:S(2)}, u32[]{:S(2)}) collective-permute-start(bf16[320,384]{1,0:T(8,128)(2,1)S(1)} %get-tuple-element.16), channel_id=1, source_target_pairs={{0,7},{1,0},{2,1},{3,2},{4,3},{5,4},{6,5},{7,6},{8,15},{9,8},{10,9... | collective-permute-start | bytes 737288 | tf_op jit(solution)/shard_map/ppermute | solution.py:90
  114.4 3.9 %collective-permute-start.11 = (bf16[320,384]{1,0:T(8,128)(2,1)S(1)}, bf16[320,384]{1,0:T(8,128)(2,1)S(1)}, u32[]{:S(2)}, u32[]{:S(2)}) collective-permute-start(bf16[320,384]{1,0:T(8,128)(2,1)S(1)} %get-tuple-element.15), channel_id=1, source_target_pairs={{0,1},{1,2},{2,3},{3,4},{4,5},{5,6},{6,7},{7,0},{8,9},{9,10},{10,1... | collective-permute-start | bytes 737288 | tf_op jit(solution)/shard_map/ppermute | solution.py:89
  118.4 2.2 %collective-permute-done.14 = bf16[320,384]{1,0:T(8,128)(2,1)S(1)} collective-permute-done((bf16[320,384]{1,0:T(8,128)(2,1)S(1)}, bf16[320,384]{1,0:T(8,128)(2,1)S(1)}, u32[]{:S(2)}, u32[]{:S(2)}) %collective-permute-start.14) | collective-permute-done | bytes 245792 | tf_op jit(solution)/shard_map/ppermute | solution.py:90
  120.6 0.1 fusion.1
  120.7 3.5 %collective-permute-start.15 = (bf16[320,384]{1,0:T(8,128)(2,1)S(1)}, bf16[320,384]{1,0:T(8,128)(2,1)S(1)}, u32[]{:S(2)}, u32[]{:S(2)}) collective-permute-start(bf16[320,384]{1,0:T(8,128)(2,1)S(1)} %fusion.1), channel_id=1, source_target_pairs={{0,7},{1,0},{2,1},{3,2},{4,3},{5,4},{6,5},{7,6},{8,15},{9,8},{10,9... | collective-permute-start | bytes 737288 | tf_op jit(solution)/shard_map/ppermute | solution.py:90
  124.1 0.0 collective-permute-done.11
  124.2 4.6 %collective-permute-done.15 = bf16[320,384]{1,0:T(8,128)(2,1)S(1)} collective-permute-done((bf16[320,384]{1,0:T(8,128)(2,1)S(1)}, bf16[320,384]{1,0:T(8,128)(2,1)S(1)}, u32[]{:S(2)}, u32[]{:S(2)}) %collective-permute-start.15) | collective-permute-done | bytes 245792 | tf_op jit(solution)/shard_map/ppermute | solution.py:90
  128.8 0.1 fusion.5
  128.9 0.0 reduce-scatter.2.cloned.1.call-done
  128.9 1.8 pad_maximum_fusion
  130.6 15.4 %all-to-all-start = ((bf16[8,40,768]{2,1,0:T(8,128)(2,1)}), bf16[8,40,768]{2,1,0:T(8,128)(2,1)S(1)}, u32[]{:S(2)}, u32[]{:S(2)}) async-start(bf16[8,40,768]{2,1,0:T(8,128)(2,1)} %pad_maximum_fusion), calls=%async_computation.1 | async-start | bytes 983040 | tf_op jit(solution)/shard_map/all_to_all | solution.py:99
  146.1 0.0 copy-done.5
  146.1 0.1 copy.14
  146.2 0.2 reduce_window_sum.11
  146.4 0.1 copy.15
  146.5 0.1 copy.16
  146.6 0.1 copy.18
  146.7 0.1 eq.52
  146.8 0.1 stack.105.refs_0_
  146.9 24.9 %all-to-all-done = bf16[8,40,768]{2,1,0:T(8,128)(2,1)S(1)} async-done(((bf16[8,40,768]{2,1,0:T(8,128)(2,1)}), bf16[8,40,768]{2,1,0:T(8,128)(2,1)S(1)}, u32[]{:S(2)}, u32[]{:S(2)}) %all-to-all-start) | async-done | bytes 491552 | tf_op jit(solution)/shard_map/all_to_all | solution.py:99
  171.8 1.9 %shard_map.39 = bf16[128,3072]{1,0:T(8,128)(2,1)} custom-call(s32[24]{0:T(128)S(1)} %stack.105.refs_0_, bf16[128,80]{1,0:T(8,128)(2,1)S(1)} %and_convert_fusion.refs_1_, bf16[4,80,768]{2,1,0:T(8,128)(2,1)S(1)} %bitcast.70), custom_call_target="tpu_custom_call" | custom-call | tf_op jit(solution)/shard_map/pallas_call | solution.py:147
  (14 shorter events, 0.2 us)
Async XLA Ops:
  6.5 42.9 %copy-start = (bf16[1,1,8,2,40,1024]{5,4,3,2,1,0:T(8,128)(2,1)S(1)}, bf16[1,1,8,2,40,1024]{5,4,3,2,1,0:T(8,128)(2,1)}, u32[]{:S(2)}) copy-start(bf16[1,1,8,2,40,1024]{5,4,3,2,1,0:T(8,128)(2,1)} %param.4) | copy-start | bytes 3932164
  6.5 122.3 %reduce-scatter.2.cloned.1.call-start = ((), (), s32[]{:S(2)}) async-start(), calls=%async_computation.2 | async-start | bytes 2211840 | tf_op jit(solution)/shard_map/reduce_scatter | solution.py:131
  6.5 37.6 %collective-permute-start.1 = (bf16[8,80,1024]{2,1,0:T(8,128)(2,1)}, bf16[8,80,1024]{2,1,0:T(8,128)(2,1)S(1)}, u32[]{:S(2)}, u32[]{:S(2)}) collective-permute-start(bf16[8,80,1024]{2,1,0:T(8,128)(2,1)} %bitcast.66), channel_id=1, source_target_pairs={{0,192},{192,0},{1,193},{193,1},{2,194},{194,2},{3,195},{195,3},{4... | collective-permute-start | bytes 3932168 | tf_op jit(solution)/shard_map/ppermute | solution.py:124
  10.1 15.4 %collective-permute-start.2 = (bf16[64,1024]{1,0:T(8,128)(2,1)}, bf16[64,1024]{1,0:T(8,128)(2,1)S(1)}, u32[]{:S(2)}, u32[]{:S(2)}) collective-permute-start(bf16[64,1024]{1,0:T(8,128)(2,1)} %bitcast.74), channel_id=1, source_target_pairs={{0,96},{96,0},{1,97},{97,1},{2,98},{98,2},{3,99},{99,3},{4,100},{1... | collective-permute-start | bytes 393224 | tf_op jit(solution)/shard_map/ppermute | solution.py:20
  26.4 15.4 %collective-permute-start.3 = (bf16[2,64,1024]{2,1,0:T(8,128)(2,1)S(1)}, bf16[2,64,1024]{2,1,0:T(8,128)(2,1)S(1)}, u32[]{:S(2)}, u32[]{:S(2)}) collective-permute-start(bf16[2,64,1024]{2,1,0:T(8,128)(2,1)S(1)} %pad_maximum_fusion.1.refs_4_), channel_id=1, source_target_pairs={{0,32},{32,64},{64,0},{1,33},{33,65},{65,1},{2,34},{34,66},{66,2},... | collective-permute-start | bytes 786440 | tf_op jit(solution)/shard_map/ppermute | solution.py:21
  30.5 12.1 %collective-permute-start.4 = (bf16[2,64,1024]{2,1,0:T(8,128)(2,1)S(1)}, bf16[2,64,1024]{2,1,0:T(8,128)(2,1)S(1)}, u32[]{:S(2)}, u32[]{:S(2)}) collective-permute-start(bf16[2,64,1024]{2,1,0:T(8,128)(2,1)S(1)} %pad_maximum_fusion.1.refs_4_), channel_id=1, source_target_pairs={{0,64},{32,0},{64,32},{1,65},{33,1},{65,33},{2,66},{34,2},{66,34},... | collective-permute-start | bytes 786440 | tf_op jit(solution)/shard_map/ppermute | solution.py:21
  33.0 10.4 %collective-permute-start.5 = (bf16[2,64,1024]{2,1,0:T(8,128)(2,1)S(1)}, bf16[2,64,1024]{2,1,0:T(8,128)(2,1)S(1)}, u32[]{:S(2)}, u32[]{:S(2)}) collective-permute-start(bf16[2,64,1024]{2,1,0:T(8,128)(2,1)S(1)} %pad_maximum_fusion.1.refs_4_), channel_id=1, source_target_pairs={{0,576},{192,384},{384,192},{576,0},{1,577},{193,385},{385,193},{5... | collective-permute-start | bytes 786440 | tf_op jit(solution)/shard_map/ppermute | solution.py:19
  36.2 13.2 %collective-permute-start = (bf16[8,80,1024]{2,1,0:T(8,128)(2,1)}, bf16[8,80,1024]{2,1,0:T(8,128)(2,1)}, u32[]{:S(2)}, u32[]{:S(2)}) collective-permute-start(bf16[8,80,1024]{2,1,0:T(8,128)(2,1)} %bitcast.67), channel_id=1, source_target_pairs={{0,16},{16,0},{1,17},{17,1},{2,18},{18,2},{3,19},{19,3},{4,20},{20... | collective-permute-start | bytes 3932168 | tf_op jit(solution)/shard_map/ppermute | solution.py:125
  43.5 0.7 copy-start.3
  44.2 11.1 %copy-start.1 = (bf16[8,80,1024]{2,1,0:T(8,128)(2,1)}, bf16[8,80,1024]{2,1,0:T(8,128)(2,1)S(1)}, u32[]{:S(2)}) copy-start(bf16[8,80,1024]{2,1,0:T(8,128)(2,1)S(1)} %collective-permute-done.1.refs_2_) | copy-start | bytes 3932164
  44.2 5.2 %collective-permute-start.6 = (bf16[8,80,1024]{2,1,0:T(8,128)(2,1)S(1)}, bf16[8,80,1024]{2,1,0:T(8,128)(2,1)}, u32[]{:S(2)}, u32[]{:S(2)}) collective-permute-start(bf16[8,80,1024]{2,1,0:T(8,128)(2,1)S(1)} %collective-permute-done.1.refs_2_), channel_id=1, source_target_pairs={{0,16},{16,0},{1,17},{17,1},{2,18},{18,2},{3,19},{19,3},{4,20},{20... | collective-permute-start | bytes 3932168 | tf_op jit(solution)/shard_map/ppermute | solution.py:127
  46.1 17.5 %collective-permute-start.7 = (bf16[4,64,1024]{2,1,0:T(8,128)(2,1)S(1)}, bf16[4,64,1024]{2,1,0:T(8,128)(2,1)}, u32[]{:S(2)}, u32[]{:S(2)}) collective-permute-start(bf16[4,64,1024]{2,1,0:T(8,128)(2,1)S(1)} %constant_dynamic-update-slice_fusion.refs_5_), channel_id=1, source_target_pairs={{0,576},{192,384},{384,192},{576,0},{1,577},{193,385},{385,193},{5... | collective-permute-start | bytes 1572872 | tf_op jit(solution)/shard_map/ppermute | solution.py:19
  55.3 8.4 %copy-start.4 = (bf16[2,64,1024]{2,1,0:T(8,128)(2,1)S(1)}, bf16[2,64,1024]{2,1,0:T(8,128)(2,1)}, u32[]{:S(2)}) copy-start(bf16[2,64,1024]{2,1,0:T(8,128)(2,1)} %copy-done.3) | copy-start | bytes 786436
  63.7 1.3 copy-start.2
  70.2 7.1 %collective-permute-start.12 = (bf16[160,384]{1,0:T(8,128)(2,1)S(1)}, bf16[160,384]{1,0:T(8,128)(2,1)S(1)}, u32[]{:S(2)}, u32[]{:S(2)}) collective-permute-start(bf16[160,384]{1,0:T(8,128)(2,1)S(1)} %get-tuple-element.21), channel_id=1, source_target_pairs={{0,7},{1,0},{2,1},{3,2},{4,3},{5,4},{6,5},{7,6},{8,15},{9,8},{10,9... | collective-permute-start | bytes 368648 | tf_op jit(solution)/shard_map/ppermute | solution.py:84
  74.8 8.0 %collective-permute-start.8 = (bf16[160,384]{1,0:T(8,128)(2,1)S(1)}, bf16[160,384]{1,0:T(8,128)(2,1)S(1)}, u32[]{:S(2)}, u32[]{:S(2)}) collective-permute-start(bf16[160,384]{1,0:T(8,128)(2,1)S(1)} %get-tuple-element.19), channel_id=1, source_target_pairs={{0,1},{1,2},{2,3},{3,4},{4,5},{5,6},{6,7},{7,0},{8,9},{9,10},{10,1... | collective-permute-start | bytes 368648 | tf_op jit(solution)/shard_map/ppermute | solution.py:83
  82.9 14.5 %collective-permute-start.9 = (bf16[320,384]{1,0:T(8,128)(2,1)S(1)}, bf16[320,384]{1,0:T(8,128)(2,1)S(1)}, u32[]{:S(2)}, u32[]{:S(2)}) collective-permute-start(bf16[320,384]{1,0:T(8,128)(2,1)S(1)} %pad_maximum_fusion.2), channel_id=1, source_target_pairs={{0,1},{1,2},{2,3},{3,4},{4,5},{5,6},{6,7},{7,0},{8,9},{9,10},{10,1... | collective-permute-start | bytes 737288 | tf_op jit(solution)/shard_map/ppermute | solution.py:89
  84.9 14.9 %collective-permute-start.13 = (bf16[320,384]{1,0:T(8,128)(2,1)S(1)}, bf16[320,384]{1,0:T(8,128)(2,1)S(1)}, u32[]{:S(2)}, u32[]{:S(2)}) collective-permute-start(bf16[320,384]{1,0:T(8,128)(2,1)S(1)} %pad_maximum_fusion.3), channel_id=1, source_target_pairs={{0,7},{1,0},{2,1},{3,2},{4,3},{5,4},{6,5},{7,6},{8,15},{9,8},{10,9... | collective-permute-start | bytes 737288 | tf_op jit(solution)/shard_map/ppermute | solution.py:90
  97.5 14.8 %collective-permute-start.10 = (bf16[320,384]{1,0:T(8,128)(2,1)S(1)}, bf16[320,384]{1,0:T(8,128)(2,1)S(1)}, u32[]{:S(2)}, u32[]{:S(2)}) collective-permute-start(bf16[320,384]{1,0:T(8,128)(2,1)S(1)} %fusion.2), channel_id=1, source_target_pairs={{0,1},{1,2},{2,3},{3,4},{4,5},{5,6},{6,7},{7,0},{8,9},{9,10},{10,1... | collective-permute-start | bytes 737288 | tf_op jit(solution)/shard_map/ppermute | solution.py:89
  112.5 33.6 %copy-start.5 = (s32[128,2]{0,1:T(2,128)S(1)}, s32[128,2]{0,1:T(2,128)}, u32[]{:S(2)}) copy-start(s32[128,2]{0,1:T(2,128)} %param.3) | copy-start | bytes 3076
  112.5 8.1 %collective-permute-start.14 = (bf16[320,384]{1,0:T(8,128)(2,1)S(1)}, bf16[320,384]{1,0:T(8,128)(2,1)S(1)}, u32[]{:S(2)}, u32[]{:S(2)}) collective-permute-start(bf16[320,384]{1,0:T(8,128)(2,1)S(1)} %get-tuple-element.16), channel_id=1, source_target_pairs={{0,7},{1,0},{2,1},{3,2},{4,3},{5,4},{6,5},{7,6},{8,15},{9,8},{10,9... | collective-permute-start | bytes 737288 | tf_op jit(solution)/shard_map/ppermute | solution.py:90
  114.4 9.7 %collective-permute-start.11 = (bf16[320,384]{1,0:T(8,128)(2,1)S(1)}, bf16[320,384]{1,0:T(8,128)(2,1)S(1)}, u32[]{:S(2)}, u32[]{:S(2)}) collective-permute-start(bf16[320,384]{1,0:T(8,128)(2,1)S(1)} %get-tuple-element.15), channel_id=1, source_target_pairs={{0,1},{1,2},{2,3},{3,4},{4,5},{5,6},{6,7},{7,0},{8,9},{9,10},{10,1... | collective-permute-start | bytes 737288 | tf_op jit(solution)/shard_map/ppermute | solution.py:89
  120.7 8.1 %collective-permute-start.15 = (bf16[320,384]{1,0:T(8,128)(2,1)S(1)}, bf16[320,384]{1,0:T(8,128)(2,1)S(1)}, u32[]{:S(2)}, u32[]{:S(2)}) collective-permute-start(bf16[320,384]{1,0:T(8,128)(2,1)S(1)} %fusion.1), channel_id=1, source_target_pairs={{0,7},{1,0},{2,1},{3,2},{4,3},{5,4},{6,5},{7,6},{8,15},{9,8},{10,9... | collective-permute-start | bytes 737288 | tf_op jit(solution)/shard_map/ppermute | solution.py:90
  130.6 41.2 %all-to-all-start = ((bf16[8,40,768]{2,1,0:T(8,128)(2,1)}), bf16[8,40,768]{2,1,0:T(8,128)(2,1)S(1)}, u32[]{:S(2)}, u32[]{:S(2)}) async-start(bf16[8,40,768]{2,1,0:T(8,128)(2,1)} %pad_maximum_fusion), calls=%async_computation.1 | async-start | bytes 983040 | tf_op jit(solution)/shard_map/all_to_all | solution.py:99
Sparse Core Ops, SparseCore 0:
  63.8 55.6 reduce-scatter.1

commit v6 on v5

--- a/solution.py
+++ b/solution.py
@@ -1,3 +1,5 @@
+import functools
+
 import jax
 import jax.numpy as jnp
 from jax import lax
@@ -33,65 +35,71 @@
     return jnp.stack([x * SIZES["h"] * count + z for x in xs for z in zs]).astype(jnp.int32)
 
 
-def product_kernel(place, *refs):
-    (*pieces, first, rest), out = refs[:-1], refs[-1]
-    step, rows, hidden = pieces[0].shape
-    flat = jnp.concatenate([piece[...] for piece in pieces], axis=1).reshape(-1, hidden)
+def product_kernel(where, *refs, pieces):
+    rows, hidden = refs[0].shape[1:]
+    out = refs[-1]
+    flat = jnp.concatenate([piece[0] for piece in refs[:pieces]])
     dims = (((1,), (1,)), ((), ()))
-    results = [
-        lax.dot_general(flat, block[...].reshape(-1, hidden), dims, preferred_element_type=jnp.float32)
-        for block in (first, rest)
-    ]
-    result = jnp.concatenate(results, axis=1).astype(out.dtype).reshape(out.shape)
-    for k in range(len(pieces)):
-        at = pl.multiple_of((place[0] ^ k) * rows, rows)
-        out[:, pl.ds(at, rows), :] = result[:, k * rows:(k + 1) * rows]
+    at = 0
+    for block in refs[pieces:-1]:
+        features = block.shape[0] * block.shape[1]
+        result = lax.dot_general(
+            flat, block[...].reshape(features, hidden), dims, preferred_element_type=jnp.float32
+        ).astype(out.dtype)
+        for k in range(pieces):
+            start = pl.multiple_of((where[1] ^ k) * rows, rows)
+            out[0, pl.ds(start, rows), at:at + features] = result[k * rows:(k + 1) * rows]
+        at += features
 
 
-def product(pieces, blocks):
+def product(where, pieces, blocks, first, stride, count):
     tensor_count, rows, hidden = pieces[0].shape
     rows_out = rows * len(pieces)
     features = sum(block.shape[0] * block.shape[1] for block in blocks)
-    step = 2
-    flops = 2 * tensor_count * rows_out * hidden * features
-    moved = 2 * (tensor_count * rows_out * (hidden + features) + features * hidden)
-    place = (lax.axis_index("xp") * SIZES["c"] + lax.axis_index("c")).astype(jnp.int32).reshape(1)
+    flops = 2 * count * rows_out * hidden * features
+    moved = 2 * (count * rows_out * (hidden + features) + features * hidden)
+
+    def source(i, where):
+        return ((where[0] + first + i * stride) % tensor_count, 0, 0)
+
     return pl.pallas_call(
-        product_kernel,
-        grid=(tensor_count // step,),
-        out_shape=jax.ShapeDtypeStruct((tensor_count, rows_out, features), jnp.bfloat16),
-        in_specs=[pl.BlockSpec(memory_space=pltpu.SMEM)]
-        + [pl.BlockSpec((step, rows, hidden), lambda i: (i, 0, 0))] * len(pieces)
-        + [pl.BlockSpec(block.shape, lambda i: (0, 0, 0)) for block in blocks],
-        out_specs=pl.BlockSpec((step, rows_out, features), lambda i: (i, 0, 0)),
+        functools.partial(product_kernel, pieces=len(pieces)),
+        grid_spec=pltpu.PrefetchScalarGridSpec(
+            num_scalar_prefetch=1,
+            grid=(count,),
+            in_specs=[pl.BlockSpec((1, rows, hidden), source)] * len(pieces)
+            + [pl.BlockSpec(block.shape, lambda i, where: (0, 0, 0)) for block in blocks],
+            out_specs=pl.BlockSpec((1, rows_out, features), lambda i, where: (i, 0, 0)),
+        ),
+        out_shape=jax.ShapeDtypeStruct((count, rows_out, features), jnp.bfloat16),
         cost_estimate=pl.CostEstimate(flops=flops, bytes_accessed=moved, transcendentals=0),
         compiler_params=pltpu.CompilerParams(vmem_limit_bytes=14 * 1024 * 1024),
-    )(place, *pieces, *blocks)
+    )(where, *pieces, *blocks)
 
 
-def sum_by_arms(partial):
-    n = partial.shape[0]
+def sum_by_arms(partial, n):
     mid = n // 2
-    half = partial.shape[1] // 2
-    me = lax.axis_index("t")
     up = [(i, (i + 1) % n) for i in range(n)]
     down = [(i, (i - 1) % n) for i in range(n)]
-    pick = lambda k: lax.dynamic_index_in_dim(partial, (me + k) % n, 0, keepdims=False)
     wide = lambda value: value.astype(jnp.float32)
     narrow = lambda value: value.astype(jnp.bfloat16)
 
-    first = lax.ppermute(pick(mid)[:half], "t", up)
-    last = lax.ppermute(pick(mid)[half:], "t", down)
-    above, below = pick(mid - 1), pick(mid + 1)
+    opposite = partial(mid, 1, 1)[0]
+    half = opposite.shape[0] // 2
+    first = lax.ppermute(opposite[:half], "t", up)
+    last = lax.ppermute(opposite[half:], "t", down)
+    sides = partial(mid - 1, 2, 2)
+    others = partial(mid + 2, 1, n - 3)
+    above, below = sides[0], sides[1]
     going_up = jnp.concatenate([narrow(wide(above[:half]) + wide(first)), above[half:]])
     going_down = jnp.concatenate([below[:half], narrow(wide(below[half:]) + wide(last))])
     for step in range(1, mid):
         from_below = lax.ppermute(going_up, "t", up)
         from_above = lax.ppermute(going_down, "t", down)
         if step < mid - 1:
-            going_up = narrow(wide(pick(mid - 1 - step)) + wide(from_below))
-            going_down = narrow(wide(pick(mid + 1 + step)) + wide(from_above))
-    return narrow(wide(pick(0)) + wide(from_below) + wide(from_above))
+            going_up = narrow(wide(others[n - 3 - step]) + wide(from_below))
+            going_down = narrow(wide(others[step - 1]) + wide(from_above))
+    return narrow(wide(others[mid - 2]) + wide(from_below) + wide(from_above))
 
 
 def give_back(summed, owners, capacity):
@@ -126,11 +134,13 @@
     x_rows, _, _, first = lax.optimization_barrier((x_rows, *column, other[0]))
     pieces = (own, c_rows, x_rows, lax.ppermute(x_rows, "c", SWAP))
 
-    partial = product(pieces, column)
-    partial, *other = lax.optimization_barrier((partial, first, other[1]))
-    near = lax.psum_scatter(partial, "t", scatter_dimension=0, tiled=False)
-    far = sum_by_arms(product(pieces, other))
-    piece = give_back(jnp.concatenate([near, far], axis=1), owners, capacity)
+    places = [lax.axis_index("t"), lax.axis_index("xp") * SIZES["c"] + lax.axis_index("c")]
+    where = jnp.stack(places).astype(jnp.int32)
+    blocks = (*column, first, other[1])
+    summed = sum_by_arms(
+        lambda k, stride, count: product(where, pieces, blocks, k, stride, count), tensor_count
+    )
+    piece = give_back(summed, owners, capacity)
 
     owner_ids = lax.iota(jnp.int32, owners)
     is_routed = jnp.any(routes[:, :, None] == owner_ids[None, None, :], axis=1)

time: 181 us -> 170 us (0.939)
  the two profiles are of different devices: /device:TPU:64 before, /device:TPU:1 now
where the time goes in v6:
time: 170 us; the launch traced here: 167 us
  starting transfers between devices  80.9 us (48%)
  waiting for transfers between devices  65.6 us (39%)
  Pallas kernels  14.5 us (9%)
  other arithmetic  2.91 us (2%)
  local copies, waits for them, and re-layouts  2.37 us (1%)
    all_to_all x1, starting transfers between devices, give_back(): lax.all_to_all(summed.reshape(-1, capacity, features), ('xp', 'c', 'e'),...  20 us
    all_to_all x1, waiting for transfers between devices, give_back(): lax.all_to_all(summed.reshape(-1, capacity, features), ('xp', 'c', 'e'),...  18 us
    ppermute x3, waiting for transfers between devices, sum_by_arms(): from_above = lax.ppermute(going_down, 't', down)  16.9 us
    ppermute x2, waiting for transfers between devices, gather_columns(): opposite = lambda value: lax.ppermute(value, ('xh', 'xp'), WEIGHT_SWAP)  14.2 us
    pallas_call x3, Pallas kernels, product(): pl.pallas_call(functools.partial(product_kernel, pieces=len(pieces)), gri...  12.6 us
    ppermute x3, starting transfers between devices, sum_by_arms(): from_above = lax.ppermute(going_down, 't', down)  9.9 us
    ppermute x1, starting transfers between devices, gather_columns(): pair = jnp.stack([slab, lax.ppermute(slab, 'h', SWAP)])  7.62 us
    ppermute x3, starting transfers between devices, sum_by_arms(): from_below = lax.ppermute(going_up, 't', up)  7.2 us
  transfers between devices with their start and end apart: 17, of which 10 were waited for; matrix products, arithmetic and copies ran while one was open for 1% of the time, Pallas kernels for 6%

profile of v6, /device:TPU:1, one launch (start us, length us, event | category | flops | bytes accessed | tf_op | source)
XLA Modules:
  0.0 166.6 jit_solution(4629726959746391143)
XLA Ops:
  0.0 0.0 copy-start
  0.0 4.1 %collective-permute-start.1 = (bf16[8,80,1024]{2,1,0:T(8,128)(2,1)}, bf16[8,80,1024]{2,1,0:T(8,128)(2,1)S(1)}, u32[]{:S(2)}, u32[]{:S(2)}) collective-permute-start(bf16[8,80,1024]{2,1,0:T(8,128)(2,1)} %bitcast.76), channel_id=1, source_target_pairs={{0,192},{192,0},{1,193},{193,1},{2,194},{194,2},{3,195},{195,3},{4... | collective-permute-start | bytes 3932168 | tf_op jit(solution)/shard_map/ppermute | solution.py:132
  4.1 7.6 %collective-permute-start.2 = (bf16[64,1024]{1,0:T(8,128)(2,1)}, bf16[64,1024]{1,0:T(8,128)(2,1)S(1)}, u32[]{:S(2)}, u32[]{:S(2)}) collective-permute-start(bf16[64,1024]{1,0:T(8,128)(2,1)} %bitcast.83), channel_id=1, source_target_pairs={{0,96},{96,0},{1,97},{97,1},{2,98},{98,2},{3,99},{99,3},{4,100},{1... | collective-permute-start | bytes 393224 | tf_op jit(solution)/shard_map/ppermute | solution.py:22
  11.7 2.6 %collective-permute-done.2 = bf16[64,1024]{1,0:T(8,128)(2,1)S(1)} collective-permute-done((bf16[64,1024]{1,0:T(8,128)(2,1)}, bf16[64,1024]{1,0:T(8,128)(2,1)S(1)}, u32[]{:S(2)}, u32[]{:S(2)}) %collective-permute-start.2) | collective-permute-done | bytes 131104 | tf_op jit(solution)/shard_map/ppermute | solution.py:22
  14.3 0.9 pad_maximum_fusion.2.refs_4_
  15.2 6.7 %collective-permute-start.3 = (bf16[2,64,1024]{2,1,0:T(8,128)(2,1)S(1)}, bf16[2,64,1024]{2,1,0:T(8,128)(2,1)S(1)}, u32[]{:S(2)}, u32[]{:S(2)}) collective-permute-start(bf16[2,64,1024]{2,1,0:T(8,128)(2,1)S(1)} %pad_maximum_fusion.2.refs_4_), channel_id=1, source_target_pairs={{0,32},{32,64},{64,0},{1,33},{33,65},{65,1},{2,34},{34,66},{66,2},... | collective-permute-start | bytes 786440 | tf_op jit(solution)/shard_map/ppermute | solution.py:23
  21.9 6.5 %collective-permute-start.4 = (bf16[2,64,1024]{2,1,0:T(8,128)(2,1)S(1)}, bf16[2,64,1024]{2,1,0:T(8,128)(2,1)S(1)}, u32[]{:S(2)}, u32[]{:S(2)}) collective-permute-start(bf16[2,64,1024]{2,1,0:T(8,128)(2,1)S(1)} %pad_maximum_fusion.2.refs_4_), channel_id=1, source_target_pairs={{0,64},{32,0},{64,32},{1,65},{33,1},{65,33},{2,66},{34,2},{66,34},... | collective-permute-start | bytes 786440 | tf_op jit(solution)/shard_map/ppermute | solution.py:23
  28.4 3.0 %collective-permute-start.5 = (bf16[2,64,1024]{2,1,0:T(8,128)(2,1)S(1)}, bf16[2,64,1024]{2,1,0:T(8,128)(2,1)S(1)}, u32[]{:S(2)}, u32[]{:S(2)}) collective-permute-start(bf16[2,64,1024]{2,1,0:T(8,128)(2,1)S(1)} %pad_maximum_fusion.2.refs_4_), channel_id=1, source_target_pairs={{0,576},{192,384},{384,192},{576,0},{1,577},{193,385},{385,193},{5... | collective-permute-start | bytes 786440 | tf_op jit(solution)/shard_map/ppermute | solution.py:21
  31.4 3.7 %collective-permute-start = (bf16[8,80,1024]{2,1,0:T(8,128)(2,1)}, bf16[8,80,1024]{2,1,0:T(8,128)(2,1)}, u32[]{:S(2)}, u32[]{:S(2)}) collective-permute-start(bf16[8,80,1024]{2,1,0:T(8,128)(2,1)} %bitcast.77), channel_id=1, source_target_pairs={{0,16},{16,0},{1,17},{17,1},{2,18},{18,2},{3,19},{19,3},{4,20},{20... | collective-permute-start | bytes 3932168 | tf_op jit(solution)/shard_map/ppermute | solution.py:133
  35.1 0.0 collective-permute-done.3
  35.2 3.5 %collective-permute-done.4 = bf16[2,64,1024]{2,1,0:T(8,128)(2,1)S(1)} collective-permute-done((bf16[2,64,1024]{2,1,0:T(8,128)(2,1)S(1)}, bf16[2,64,1024]{2,1,0:T(8,128)(2,1)S(1)}, u32[]{:S(2)}, u32[]{:S(2)}) %collective-permute-start.4) | collective-permute-done | bytes 262176 | tf_op jit(solution)/shard_map/ppermute | solution.py:23
  38.7 0.0 collective-permute-done.5.refs_6_
  38.7 0.0 copy-start.1
  38.8 0.7 copy-done.1
  39.4 0.0 collective-permute-done.1.refs_2_
  39.4 3.9 %collective-permute-start.6 = (bf16[8,80,1024]{2,1,0:T(8,128)(2,1)S(1)}, bf16[8,80,1024]{2,1,0:T(8,128)(2,1)}, u32[]{:S(2)}, u32[]{:S(2)}) collective-permute-start(bf16[8,80,1024]{2,1,0:T(8,128)(2,1)S(1)} %collective-permute-done.1.refs_2_), channel_id=1, source_target_pairs={{0,16},{16,0},{1,17},{17,1},{2,18},{18,2},{3,19},{19,3},{4,20},{20... | collective-permute-start | bytes 3932168 | tf_op jit(solution)/shard_map/ppermute | solution.py:135
  43.4 2.5 %collective-permute-start.7 = (bf16[4,64,1024]{2,1,0:T(8,128)(2,1)S(1)}, bf16[4,64,1024]{2,1,0:T(8,128)(2,1)}, u32[]{:S(2)}, u32[]{:S(2)}) collective-permute-start(bf16[4,64,1024]{2,1,0:T(8,128)(2,1)S(1)} %constant_dynamic-update-slice_fusion.refs_5_), channel_id=1, source_target_pairs={{0,576},{192,384},{384,192},{576,0},{1,577},{193,385},{385,193},{5... | collective-permute-start | bytes 1572872 | tf_op jit(solution)/shard_map/ppermute | solution.py:21
  45.9 0.1 pad_add_fusion.where
  46.0 14.2 %collective-permute-done.7.refs_7_ = bf16[4,64,1024]{2,1,0:T(8,128)(2,1)} collective-permute-done((bf16[4,64,1024]{2,1,0:T(8,128)(2,1)S(1)}, bf16[4,64,1024]{2,1,0:T(8,128)(2,1)}, u32[]{:S(2)}, u32[]{:S(2)}) %collective-permute-start.7) | collective-permute-done | bytes 524320 | tf_op jit(solution)/shard_map/ppermute | solution.py:21
  60.1 0.0 collective-permute-done.refs_1_
  60.1 0.0 collective-permute-done.6.refs_3_
  60.1 0.0 copy-done
  60.1 0.0 copy-start.2
  60.1 0.9 copy-done.2
  61.1 2.6 %shard_map.39 = bf16[1,320,768]{2,1,0:T(8,128)(2,1)S(1)} custom-call(s32[2]{0:T(128)S(1)} %pad_add_fusion.where, bf16[8,80,1024]{2,1,0:T(8,128)(2,1)S(1)} %bitcast.78, bf16[8,80,1024]{2,1,0:T(8,128)(2,1)} %collective-permute-done.refs_1_, bf16[8,80,1024]{2,1,0:T(8,128)(2,1)S(1)} %collective-permute-done.1.refs_2_, ...), custom_call_target="tpu_custom_call" | custom-call | flops 503316480 | bytes 2719744 | tf_op jit(solution)/shard_map/pallas_call | solution.py:65
  63.7 3.9 %collective-permute-start.12 = (bf16[160,768]{1,0:T(8,128)(2,1)S(1)}, bf16[160,768]{1,0:T(8,128)(2,1)S(1)}, u32[]{:S(2)}, u32[]{:S(2)}) collective-permute-start(bf16[160,768]{1,0:T(8,128)(2,1)S(1)} %get-tuple-element.16), channel_id=1, source_target_pairs={{0,7},{1,0},{2,1},{3,2},{4,3},{5,4},{6,5},{7,6},{8,15},{9,8},{10,9... | collective-permute-start | bytes 737288 | tf_op jit(solution)/shard_map/ppermute | solution.py:90
  67.6 1.9 %collective-permute-start.8 = (bf16[160,768]{1,0:T(8,128)(2,1)S(1)}, bf16[160,768]{1,0:T(8,128)(2,1)S(1)}, u32[]{:S(2)}, u32[]{:S(2)}) collective-permute-start(bf16[160,768]{1,0:T(8,128)(2,1)S(1)} %get-tuple-element.15), channel_id=1, source_target_pairs={{0,1},{1,2},{2,3},{3,4},{4,5},{5,6},{6,7},{7,0},{8,9},{9,10},{10,1... | collective-permute-start | bytes 737288 | tf_op jit(solution)/shard_map/ppermute | solution.py:89
  69.6 3.6 %shard_map.38 = bf16[2,320,768]{2,1,0:T(8,128)(2,1)S(1)} custom-call(s32[2]{0:T(128)S(1)} %pad_add_fusion.where, bf16[8,80,1024]{2,1,0:T(8,128)(2,1)S(1)} %bitcast.79, bf16[8,80,1024]{2,1,0:T(8,128)(2,1)} %collective-permute-done.refs_1_, bf16[8,80,1024]{2,1,0:T(8,128)(2,1)S(1)} %collective-permute-done.1.refs_2_, ...), custom_call_target="tpu_custom_call" | custom-call | flops 1006632960 | bytes 3866624 | tf_op jit(solution)/shard_map/pallas_call | solution.py:65
  73.2 0.0 collective-permute-done.12
  73.2 3.9 %collective-permute-done.8 = bf16[160,768]{1,0:T(8,128)(2,1)S(1)} collective-permute-done((bf16[160,768]{1,0:T(8,128)(2,1)S(1)}, bf16[160,768]{1,0:T(8,128)(2,1)S(1)}, u32[]{:S(2)}, u32[]{:S(2)}) %collective-permute-start.8) | collective-permute-done | bytes 245792 | tf_op jit(solution)/shard_map/ppermute | solution.py:89
  77.1 0.1 fusion.7
  77.3 1.9 %collective-permute-start.9 = (bf16[320,768]{1,0:T(8,128)(2,1)S(1)}, bf16[320,768]{1,0:T(8,128)(2,1)S(1)}, u32[]{:S(2)}, u32[]{:S(2)}) collective-permute-start(bf16[320,768]{1,0:T(8,128)(2,1)S(1)} %pad_maximum_fusion), channel_id=1, source_target_pairs={{0,1},{1,2},{2,3},{3,4},{4,5},{5,6},{6,7},{7,0},{8,9},{9,10},{10,1... | collective-permute-start | bytes 1474568 | tf_op jit(solution)/shard_map/ppermute | solution.py:97
  79.2 6.4 %shard_map.37 = bf16[5,320,768]{2,1,0:T(8,128)(2,1)S(1)} custom-call(s32[2]{0:T(128)S(1)} %pad_add_fusion.where, bf16[8,80,1024]{2,1,0:T(8,128)(2,1)S(1)} %bitcast.80, bf16[8,80,1024]{2,1,0:T(8,128)(2,1)} %collective-permute-done.refs_1_, bf16[8,80,1024]{2,1,0:T(8,128)(2,1)S(1)} %collective-permute-done.1.refs_2_, ...), custom_call_target="tpu_custom_call" | custom-call | flops 2516582400 | bytes 7307264 | tf_op jit(solution)/shard_map/pallas_call | solution.py:65
  85.7 4.6 %collective-permute-start.13 = (bf16[320,768]{1,0:T(8,128)(2,1)S(1)}, bf16[320,768]{1,0:T(8,128)(2,1)S(1)}, u32[]{:S(2)}, u32[]{:S(2)}) collective-permute-start(bf16[320,768]{1,0:T(8,128)(2,1)S(1)} %pad_maximum_fusion.1), channel_id=1, source_target_pairs={{0,7},{1,0},{2,1},{3,2},{4,3},{5,4},{6,5},{7,6},{8,15},{9,8},{10,9... | collective-permute-start | bytes 1474568 | tf_op jit(solution)/shard_map/ppermute | solution.py:98
  90.3 0.8 collective-permute-done.9
  91.1 0.1 fusion.2
  91.2 1.9 %collective-permute-start.10 = (bf16[320,768]{1,0:T(8,128)(2,1)S(1)}, bf16[320,768]{1,0:T(8,128)(2,1)S(1)}, u32[]{:S(2)}, u32[]{:S(2)}) collective-permute-start(bf16[320,768]{1,0:T(8,128)(2,1)S(1)} %fusion.2), channel_id=1, source_target_pairs={{0,1},{1,2},{2,3},{3,4},{4,5},{5,6},{6,7},{7,0},{8,9},{9,10},{10,1... | collective-permute-start | bytes 1474568 | tf_op jit(solution)/shard_map/ppermute | solution.py:97
  93.2 5.3 %collective-permute-done.13 = bf16[320,768]{1,0:T(8,128)(2,1)S(1)} collective-permute-done((bf16[320,768]{1,0:T(8,128)(2,1)S(1)}, bf16[320,768]{1,0:T(8,128)(2,1)S(1)}, u32[]{:S(2)}, u32[]{:S(2)}) %collective-permute-start.13) | collective-permute-done | bytes 491552 | tf_op jit(solution)/shard_map/ppermute | solution.py:98
  98.5 5.7 %collective-permute-done.10 = bf16[320,768]{1,0:T(8,128)(2,1)S(1)} collective-permute-done((bf16[320,768]{1,0:T(8,128)(2,1)S(1)}, bf16[320,768]{1,0:T(8,128)(2,1)S(1)}, u32[]{:S(2)}, u32[]{:S(2)}) %collective-permute-start.10) | collective-permute-done | bytes 491552 | tf_op jit(solution)/shard_map/ppermute | solution.py:97
  104.1 0.3 fusion.3
  104.4 0.0 copy-start.3
  104.4 1.9 %collective-permute-start.14 = (bf16[320,768]{1,0:T(8,128)(2,1)S(1)}, bf16[320,768]{1,0:T(8,128)(2,1)S(1)}, u32[]{:S(2)}, u32[]{:S(2)}) collective-permute-start(bf16[320,768]{1,0:T(8,128)(2,1)S(1)} %get-tuple-element.10), channel_id=1, source_target_pairs={{0,7},{1,0},{2,1},{3,2},{4,3},{5,4},{6,5},{7,6},{8,15},{9,8},{10,9... | collective-permute-start | bytes 1474568 | tf_op jit(solution)/shard_map/ppermute | solution.py:98
  106.3 3.4 %collective-permute-start.11 = (bf16[320,768]{1,0:T(8,128)(2,1)S(1)}, bf16[320,768]{1,0:T(8,128)(2,1)S(1)}, u32[]{:S(2)}, u32[]{:S(2)}) collective-permute-start(bf16[320,768]{1,0:T(8,128)(2,1)S(1)} %get-tuple-element.9), channel_id=1, source_target_pairs={{0,1},{1,2},{2,3},{3,4},{4,5},{5,6},{6,7},{7,0},{8,9},{9,10},{10,1... | collective-permute-start | bytes 1474568 | tf_op jit(solution)/shard_map/ppermute | solution.py:97
  109.7 5.5 %collective-permute-done.14 = bf16[320,768]{1,0:T(8,128)(2,1)S(1)} collective-permute-done((bf16[320,768]{1,0:T(8,128)(2,1)S(1)}, bf16[320,768]{1,0:T(8,128)(2,1)S(1)}, u32[]{:S(2)}, u32[]{:S(2)}) %collective-permute-start.14) | collective-permute-done | bytes 491552 | tf_op jit(solution)/shard_map/ppermute | solution.py:98
  115.2 0.1 fusion.1
  115.3 3.4 %collective-permute-start.15 = (bf16[320,768]{1,0:T(8,128)(2,1)S(1)}, bf16[320,768]{1,0:T(8,128)(2,1)S(1)}, u32[]{:S(2)}, u32[]{:S(2)}) collective-permute-start(bf16[320,768]{1,0:T(8,128)(2,1)S(1)} %fusion.1), channel_id=1, source_target_pairs={{0,7},{1,0},{2,1},{3,2},{4,3},{5,4},{6,5},{7,6},{8,15},{9,8},{10,9... | collective-permute-start | bytes 1474568 | tf_op jit(solution)/shard_map/ppermute | solution.py:98
  118.7 0.0 collective-permute-done.11
  118.7 6.1 %collective-permute-done.15 = bf16[320,768]{1,0:T(8,128)(2,1)S(1)} collective-permute-done((bf16[320,768]{1,0:T(8,128)(2,1)S(1)}, bf16[320,768]{1,0:T(8,128)(2,1)S(1)}, u32[]{:S(2)}, u32[]{:S(2)}) %collective-permute-start.15) | collective-permute-done | bytes 491552 | tf_op jit(solution)/shard_map/ppermute | solution.py:98
  124.9 1.0 fusion.5
  125.9 20.0 %all-to-all-start = ((bf16[8,40,768]{2,1,0:T(8,128)(2,1)}), bf16[8,40,768]{2,1,0:T(8,128)(2,1)S(1)}, u32[]{:S(2)}, u32[]{:S(2)}) async-start(bf16[8,40,768]{2,1,0:T(8,128)(2,1)} %bitcast.42), calls=%async_computation | async-start | bytes 983040 | tf_op jit(solution)/shard_map/all_to_all | solution.py:107
  145.9 0.0 copy-done.3
  145.9 0.1 copy.14
  146.0 0.2 reduce_window_sum.11
  146.2 0.1 copy.15
  146.3 0.1 copy.16
  146.4 0.1 copy.18
  146.5 0.1 eq.43
  146.6 0.1 stack.114.refs_0_
  146.8 18.0 %all-to-all-done = bf16[8,40,768]{2,1,0:T(8,128)(2,1)S(1)} async-done(((bf16[8,40,768]{2,1,0:T(8,128)(2,1)}), bf16[8,40,768]{2,1,0:T(8,128)(2,1)S(1)}, u32[]{:S(2)}, u32[]{:S(2)}) %all-to-all-start) | async-done | bytes 491552 | tf_op jit(solution)/shard_map/all_to_all | solution.py:107
  164.8 1.9 %shard_map.40 = bf16[128,3072]{1,0:T(8,128)(2,1)} custom-call(s32[24]{0:T(128)S(1)} %stack.114.refs_0_, bf16[128,80]{1,0:T(8,128)(2,1)S(1)} %and_convert_fusion.refs_1_, bf16[4,80,768]{2,1,0:T(8,128)(2,1)S(1)} %bitcast.81), custom_call_target="tpu_custom_call" | custom-call | tf_op jit(solution)/shard_map/pallas_call | solution.py:157
  (13 shorter events, 0.2 us)
Async XLA Ops:
  0.0 60.1 %copy-start = (bf16[1,1,8,2,40,1024]{5,4,3,2,1,0:T(8,128)(2,1)S(1)}, bf16[1,1,8,2,40,1024]{5,4,3,2,1,0:T(8,128)(2,1)}, u32[]{:S(2)}) copy-start(bf16[1,1,8,2,40,1024]{5,4,3,2,1,0:T(8,128)(2,1)} %param.4) | copy-start | bytes 3932164
  0.0 39.4 %collective-permute-start.1 = (bf16[8,80,1024]{2,1,0:T(8,128)(2,1)}, bf16[8,80,1024]{2,1,0:T(8,128)(2,1)S(1)}, u32[]{:S(2)}, u32[]{:S(2)}) collective-permute-start(bf16[8,80,1024]{2,1,0:T(8,128)(2,1)} %bitcast.76), channel_id=1, source_target_pairs={{0,192},{192,0},{1,193},{193,1},{2,194},{194,2},{3,195},{195,3},{4... | collective-permute-start | bytes 3932168 | tf_op jit(solution)/shard_map/ppermute | solution.py:132
  4.1 10.2 %collective-permute-start.2 = (bf16[64,1024]{1,0:T(8,128)(2,1)}, bf16[64,1024]{1,0:T(8,128)(2,1)S(1)}, u32[]{:S(2)}, u32[]{:S(2)}) collective-permute-start(bf16[64,1024]{1,0:T(8,128)(2,1)} %bitcast.83), channel_id=1, source_target_pairs={{0,96},{96,0},{1,97},{97,1},{2,98},{98,2},{3,99},{99,3},{4,100},{1... | collective-permute-start | bytes 393224 | tf_op jit(solution)/shard_map/ppermute | solution.py:22
  15.2 19.9 %collective-permute-start.3 = (bf16[2,64,1024]{2,1,0:T(8,128)(2,1)S(1)}, bf16[2,64,1024]{2,1,0:T(8,128)(2,1)S(1)}, u32[]{:S(2)}, u32[]{:S(2)}) collective-permute-start(bf16[2,64,1024]{2,1,0:T(8,128)(2,1)S(1)} %pad_maximum_fusion.2.refs_4_), channel_id=1, source_target_pairs={{0,32},{32,64},{64,0},{1,33},{33,65},{65,1},{2,34},{34,66},{66,2},... | collective-permute-start | bytes 786440 | tf_op jit(solution)/shard_map/ppermute | solution.py:23
  21.9 16.8 %collective-permute-start.4 = (bf16[2,64,1024]{2,1,0:T(8,128)(2,1)S(1)}, bf16[2,64,1024]{2,1,0:T(8,128)(2,1)S(1)}, u32[]{:S(2)}, u32[]{:S(2)}) collective-permute-start(bf16[2,64,1024]{2,1,0:T(8,128)(2,1)S(1)} %pad_maximum_fusion.2.refs_4_), channel_id=1, source_target_pairs={{0,64},{32,0},{64,32},{1,65},{33,1},{65,33},{2,66},{34,2},{66,34},... | collective-permute-start | bytes 786440 | tf_op jit(solution)/shard_map/ppermute | solution.py:23
  28.4 10.3 %collective-permute-start.5 = (bf16[2,64,1024]{2,1,0:T(8,128)(2,1)S(1)}, bf16[2,64,1024]{2,1,0:T(8,128)(2,1)S(1)}, u32[]{:S(2)}, u32[]{:S(2)}) collective-permute-start(bf16[2,64,1024]{2,1,0:T(8,128)(2,1)S(1)} %pad_maximum_fusion.2.refs_4_), channel_id=1, source_target_pairs={{0,576},{192,384},{384,192},{576,0},{1,577},{193,385},{385,193},{5... | collective-permute-start | bytes 786440 | tf_op jit(solution)/shard_map/ppermute | solution.py:21
  31.4 28.7 %collective-permute-start = (bf16[8,80,1024]{2,1,0:T(8,128)(2,1)}, bf16[8,80,1024]{2,1,0:T(8,128)(2,1)}, u32[]{:S(2)}, u32[]{:S(2)}) collective-permute-start(bf16[8,80,1024]{2,1,0:T(8,128)(2,1)} %bitcast.77), channel_id=1, source_target_pairs={{0,16},{16,0},{1,17},{17,1},{2,18},{18,2},{3,19},{19,3},{4,20},{20... | collective-permute-start | bytes 3932168 | tf_op jit(solution)/shard_map/ppermute | solution.py:133
  38.7 0.7 copy-start.1
  39.4 20.7 %collective-permute-start.6 = (bf16[8,80,1024]{2,1,0:T(8,128)(2,1)S(1)}, bf16[8,80,1024]{2,1,0:T(8,128)(2,1)}, u32[]{:S(2)}, u32[]{:S(2)}) collective-permute-start(bf16[8,80,1024]{2,1,0:T(8,128)(2,1)S(1)} %collective-permute-done.1.refs_2_), channel_id=1, source_target_pairs={{0,16},{16,0},{1,17},{17,1},{2,18},{18,2},{3,19},{19,3},{4,20},{20... | collective-permute-start | bytes 3932168 | tf_op jit(solution)/shard_map/ppermute | solution.py:135
  43.4 16.8 %collective-permute-start.7 = (bf16[4,64,1024]{2,1,0:T(8,128)(2,1)S(1)}, bf16[4,64,1024]{2,1,0:T(8,128)(2,1)}, u32[]{:S(2)}, u32[]{:S(2)}) collective-permute-start(bf16[4,64,1024]{2,1,0:T(8,128)(2,1)S(1)} %constant_dynamic-update-slice_fusion.refs_5_), channel_id=1, source_target_pairs={{0,576},{192,384},{384,192},{576,0},{1,577},{193,385},{385,193},{5... | collective-permute-start | bytes 1572872 | tf_op jit(solution)/shard_map/ppermute | solution.py:21
  60.1 1.0 copy-start.2
  63.7 9.4 %collective-permute-start.12 = (bf16[160,768]{1,0:T(8,128)(2,1)S(1)}, bf16[160,768]{1,0:T(8,128)(2,1)S(1)}, u32[]{:S(2)}, u32[]{:S(2)}) collective-permute-start(bf16[160,768]{1,0:T(8,128)(2,1)S(1)} %get-tuple-element.16), channel_id=1, source_target_pairs={{0,7},{1,0},{2,1},{3,2},{4,3},{5,4},{6,5},{7,6},{8,15},{9,8},{10,9... | collective-permute-start | bytes 737288 | tf_op jit(solution)/shard_map/ppermute | solution.py:90
  67.6 9.5 %collective-permute-start.8 = (bf16[160,768]{1,0:T(8,128)(2,1)S(1)}, bf16[160,768]{1,0:T(8,128)(2,1)S(1)}, u32[]{:S(2)}, u32[]{:S(2)}) collective-permute-start(bf16[160,768]{1,0:T(8,128)(2,1)S(1)} %get-tuple-element.15), channel_id=1, source_target_pairs={{0,1},{1,2},{2,3},{3,4},{4,5},{5,6},{6,7},{7,0},{8,9},{9,10},{10,1... | collective-permute-start | bytes 737288 | tf_op jit(solution)/shard_map/ppermute | solution.py:89
  77.3 13.8 %collective-permute-start.9 = (bf16[320,768]{1,0:T(8,128)(2,1)S(1)}, bf16[320,768]{1,0:T(8,128)(2,1)S(1)}, u32[]{:S(2)}, u32[]{:S(2)}) collective-permute-start(bf16[320,768]{1,0:T(8,128)(2,1)S(1)} %pad_maximum_fusion), channel_id=1, source_target_pairs={{0,1},{1,2},{2,3},{3,4},{4,5},{5,6},{6,7},{7,0},{8,9},{9,10},{10,1... | collective-permute-start | bytes 1474568 | tf_op jit(solution)/shard_map/ppermute | solution.py:97
  85.7 12.8 %collective-permute-start.13 = (bf16[320,768]{1,0:T(8,128)(2,1)S(1)}, bf16[320,768]{1,0:T(8,128)(2,1)S(1)}, u32[]{:S(2)}, u32[]{:S(2)}) collective-permute-start(bf16[320,768]{1,0:T(8,128)(2,1)S(1)} %pad_maximum_fusion.1), channel_id=1, source_target_pairs={{0,7},{1,0},{2,1},{3,2},{4,3},{5,4},{6,5},{7,6},{8,15},{9,8},{10,9... | collective-permute-start | bytes 1474568 | tf_op jit(solution)/shard_map/ppermute | solution.py:98
  91.2 12.9 %collective-permute-start.10 = (bf16[320,768]{1,0:T(8,128)(2,1)S(1)}, bf16[320,768]{1,0:T(8,128)(2,1)S(1)}, u32[]{:S(2)}, u32[]{:S(2)}) collective-permute-start(bf16[320,768]{1,0:T(8,128)(2,1)S(1)} %fusion.2), channel_id=1, source_target_pairs={{0,1},{1,2},{2,3},{3,4},{4,5},{5,6},{6,7},{7,0},{8,9},{9,10},{10,1... | collective-permute-start | bytes 1474568 | tf_op jit(solution)/shard_map/ppermute | solution.py:97
  104.4 41.5 %copy-start.3 = (s32[128,2]{0,1:T(2,128)S(1)}, s32[128,2]{0,1:T(2,128)}, u32[]{:S(2)}) copy-start(s32[128,2]{0,1:T(2,128)} %param.3) | copy-start | bytes 3076
  104.4 10.8 %collective-permute-start.14 = (bf16[320,768]{1,0:T(8,128)(2,1)S(1)}, bf16[320,768]{1,0:T(8,128)(2,1)S(1)}, u32[]{:S(2)}, u32[]{:S(2)}) collective-permute-start(bf16[320,768]{1,0:T(8,128)(2,1)S(1)} %get-tuple-element.10), channel_id=1, source_target_pairs={{0,7},{1,0},{2,1},{3,2},{4,3},{5,4},{6,5},{7,6},{8,15},{9,8},{10,9... | collective-permute-start | bytes 1474568 | tf_op jit(solution)/shard_map/ppermute | solution.py:98
  106.3 12.4 %collective-permute-start.11 = (bf16[320,768]{1,0:T(8,128)(2,1)S(1)}, bf16[320,768]{1,0:T(8,128)(2,1)S(1)}, u32[]{:S(2)}, u32[]{:S(2)}) collective-permute-start(bf16[320,768]{1,0:T(8,128)(2,1)S(1)} %get-tuple-element.9), channel_id=1, source_target_pairs={{0,1},{1,2},{2,3},{3,4},{4,5},{5,6},{6,7},{7,0},{8,9},{9,10},{10,1... | collective-permute-start | bytes 1474568 | tf_op jit(solution)/shard_map/ppermute | solution.py:97
  115.3 9.6 %collective-permute-start.15 = (bf16[320,768]{1,0:T(8,128)(2,1)S(1)}, bf16[320,768]{1,0:T(8,128)(2,1)S(1)}, u32[]{:S(2)}, u32[]{:S(2)}) collective-permute-start(bf16[320,768]{1,0:T(8,128)(2,1)S(1)} %fusion.1), channel_id=1, source_target_pairs={{0,7},{1,0},{2,1},{3,2},{4,3},{5,4},{6,5},{7,6},{8,15},{9,8},{10,9... | collective-permute-start | bytes 1474568 | tf_op jit(solution)/shard_map/ppermute | solution.py:98
  125.9 38.9 %all-to-all-start = ((bf16[8,40,768]{2,1,0:T(8,128)(2,1)}), bf16[8,40,768]{2,1,0:T(8,128)(2,1)S(1)}, u32[]{:S(2)}, u32[]{:S(2)}) async-start(bf16[8,40,768]{2,1,0:T(8,128)(2,1)} %bitcast.42), calls=%async_computation | async-start | bytes 983040 | tf_op jit(solution)/shard_map/all_to_all | solution.py:107

commit v7 on v6

--- a/solution.py
+++ b/solution.py
@@ -88,35 +88,38 @@
     half = opposite.shape[0] // 2
     first = lax.ppermute(opposite[:half], "t", up)
     last = lax.ppermute(opposite[half:], "t", down)
-    sides = partial(mid - 1, 2, 2)
-    others = partial(mid + 2, 1, n - 3)
-    above, below = sides[0], sides[1]
+    above, below = partial(mid - 1, 1, 1)[0], partial(mid + 1, 1, 1)[0]
     going_up = jnp.concatenate([narrow(wide(above[:half]) + wide(first)), above[half:]])
     going_down = jnp.concatenate([below[:half], narrow(wide(below[half:]) + wide(last))])
+    uppers, lowers = partial(mid - 2, -1, mid - 2), partial(mid + 2, 1, mid - 1)
     for step in range(1, mid):
         from_below = lax.ppermute(going_up, "t", up)
         from_above = lax.ppermute(going_down, "t", down)
         if step < mid - 1:
-            going_up = narrow(wide(others[n - 3 - step]) + wide(from_below))
-            going_down = narrow(wide(others[step - 1]) + wide(from_above))
-    return narrow(wide(others[mid - 2]) + wide(from_below) + wide(from_above))
+            going_up = narrow(wide(uppers[step - 1]) + wide(from_below))
+            going_down = narrow(wide(lowers[step - 1]) + wide(from_above))
+    return narrow(wide(lowers[mid - 2]) + wide(from_below) + wide(from_above))
 
 
-def give_back(summed, owners, capacity):
+def give_back(summed, capacity):
     features = summed.shape[-1]
-    got = lax.all_to_all(summed.reshape(-1, capacity, features), ("xp", "c", "e"), 0, 0)
-    return got.reshape(-1, owners * capacity, features)
+    near = lax.all_to_all(summed.reshape(SIZES["xp"] * SIZES["c"], -1, features), ("xp", "c"), 0, 0)
+    other = 1 - lax.axis_index("e")
+    far = lax.ppermute(lax.dynamic_slice_in_dim(near, other * capacity, capacity, 1), "e", SWAP)
+    return near, far
 
 
-def place_kernel(places, onehot, piece, out, *, width):
+def place_kernel(places, near_hot, far_hot, near, far, out, *, width):
     cores = SIZES["c"]
-    count = piece.shape[2] // width
+    count = near.shape[2] // width
     for xp in range(SIZES["xp"]):
         for b in range(count):
-            block = jnp.concatenate(
-                [piece[xp * cores + c, :, b * width:(b + 1) * width] for c in range(cores)], axis=1
-            )
-            result = jnp.dot(onehot[...], block, preferred_element_type=jnp.float32)
+            result = 0.0
+            for hot, piece in ((near_hot, near), (far_hot, far)):
+                block = jnp.concatenate(
+                    [piece[xp * cores + c, :, b * width:(b + 1) * width] for c in range(cores)], axis=1
+                )
+                result += jnp.dot(hot[...], block, preferred_element_type=jnp.float32)
             start = pl.multiple_of(places[xp * count + b] * (cores * width), cores * width)
             out[:, pl.ds(start, cores * width)] = result.astype(out.dtype)
 
@@ -140,27 +143,30 @@
     summed = sum_by_arms(
         lambda k, stride, count: product(where, pieces, blocks, k, stride, count), tensor_count
     )
-    piece = give_back(summed, owners, capacity)
+    near, far = give_back(summed, capacity)
 
-    owner_ids = lax.iota(jnp.int32, owners)
+    me = lax.axis_index("e")
+    owner_ids = jnp.stack([me, 1 - me])
     is_routed = jnp.any(routes[:, :, None] == owner_ids[None, None, :], axis=1)
     slot_index = jnp.cumsum(is_routed.astype(jnp.int32), axis=0) - 1
-    onehot = is_routed[:, :, None] & (slot_index[:, :, None] == lax.iota(jnp.int32, capacity)[None, None, :])
-    onehot = onehot.reshape(routes.shape[0], rows).astype(jnp.bfloat16)
+    near_at = jnp.where(is_routed[:, :1], slot_index[:, :1] + me * capacity, -1)
+    far_at = jnp.where(is_routed[:, 1:], slot_index[:, 1:], -1)
+    near_hot = (near_at == lax.iota(jnp.int32, rows)[None, :]).astype(jnp.bfloat16)
+    far_hot = (far_at == lax.iota(jnp.int32, capacity)[None, :]).astype(jnp.bfloat16)
 
     def body(*refs):
         place_kernel(*refs, width=width)
 
     smem = pl.BlockSpec(memory_space=pltpu.SMEM)
     vmem = pl.BlockSpec(memory_space=pltpu.VMEM)
-    total = piece.shape[0] * piece.shape[2]
+    total = near.shape[0] * near.shape[2]
     return pl.pallas_call(
         body,
         out_shape=jax.ShapeDtypeStruct((routes.shape[0], total), jnp.bfloat16),
-        in_specs=[smem, vmem, vmem],
+        in_specs=[smem] + [vmem] * 4,
         out_specs=vmem,
         compiler_params=pltpu.CompilerParams(vmem_limit_bytes=8 * 1024 * 1024),
-    )(block_places(), onehot, piece)
+    )(block_places(), near_hot, far_hot, near, far)
 
 
 def solution(mesh):

time: 170 us -> 168 us (0.988)
  the two profiles are of different devices: /device:TPU:1 before, /device:TPU:88 now
where the time goes in v7:
time: 168 us; the launch traced here: 167 us
  starting transfers between devices  75.3 us (45%)
  waiting for transfers between devices  66.6 us (40%)
  Pallas kernels  18 us (11%)
  other arithmetic  4.36 us (3%)
  local copies, waits for them, and re-layouts  2.29 us (1%)
    ppermute x1, waiting for transfers between devices, give_back(): lax.ppermute(lax.dynamic_slice_in_dim(near, other * capacity, capacity, 1...  16.1 us
    pallas_call x5, Pallas kernels, product(): pl.pallas_call(functools.partial(product_kernel, pieces=len(pieces)), gri...  16 us
    ppermute x3, starting transfers between devices, sum_by_arms(): from_below = lax.ppermute(going_up, 't', up)  15.9 us
    ppermute x2, waiting for transfers between devices, gather_columns(): opposite = lambda value: lax.ppermute(value, ('xh', 'xp'), WEIGHT_SWAP)  14.3 us
    ppermute x1, starting transfers between devices, give_back(): lax.ppermute(lax.dynamic_slice_in_dim(near, other * capacity, capacity, 1...  13.3 us
    ppermute x3, waiting for transfers between devices, sum_by_arms(): from_below = lax.ppermute(going_up, 't', up)  12.5 us
    ppermute x1, starting transfers between devices, gather_columns(): pair = jnp.stack([slab, lax.ppermute(slab, 'h', SWAP)])  9.11 us
    ppermute x2, starting transfers between devices, gather_columns(): opposite = lambda value: lax.ppermute(value, ('xh', 'xp'), WEIGHT_SWAP)  8.01 us
  transfers between devices with their start and end apart: 18, of which 11 were waited for; matrix products, arithmetic and copies ran while one was open for 2% of the time, Pallas kernels for 8%

profile of v7, /device:TPU:88, one launch (start us, length us, event | category | flops | bytes accessed | tf_op | source)
XLA Modules:
  0.0 167.1 jit_solution(2031060107787956724)
XLA Ops:
  0.0 3.5 %collective-permute-start.1 = (bf16[8,80,1024]{2,1,0:T(8,128)(2,1)}, bf16[8,80,1024]{2,1,0:T(8,128)(2,1)S(1)}, u32[]{:S(2)}, u32[]{:S(2)}) collective-permute-start(bf16[8,80,1024]{2,1,0:T(8,128)(2,1)} %bitcast.75), channel_id=1, source_target_pairs={{0,192},{192,0},{1,193},{193,1},{2,194},{194,2},{3,195},{195,3},{4... | collective-permute-start | bytes 3932168 | tf_op jit(solution)/shard_map/ppermute | solution.py:135
  3.5 9.1 %collective-permute-start.2 = (bf16[64,1024]{1,0:T(8,128)(2,1)}, bf16[64,1024]{1,0:T(8,128)(2,1)S(1)}, u32[]{:S(2)}, u32[]{:S(2)}) collective-permute-start(bf16[64,1024]{1,0:T(8,128)(2,1)} %bitcast.82), channel_id=1, source_target_pairs={{0,96},{96,0},{1,97},{97,1},{2,98},{98,2},{3,99},{99,3},{4,100},{1... | collective-permute-start | bytes 393224 | tf_op jit(solution)/shard_map/ppermute | solution.py:22
  12.6 6.2 %collective-permute-done.2 = bf16[64,1024]{1,0:T(8,128)(2,1)S(1)} collective-permute-done((bf16[64,1024]{1,0:T(8,128)(2,1)}, bf16[64,1024]{1,0:T(8,128)(2,1)S(1)}, u32[]{:S(2)}, u32[]{:S(2)}) %collective-permute-start.2) | collective-permute-done | bytes 131104 | tf_op jit(solution)/shard_map/ppermute | solution.py:22
  18.9 0.9 pad_maximum_fusion.2.refs_4_
  19.8 3.4 %collective-permute-start.3 = (bf16[2,64,1024]{2,1,0:T(8,128)(2,1)S(1)}, bf16[2,64,1024]{2,1,0:T(8,128)(2,1)S(1)}, u32[]{:S(2)}, u32[]{:S(2)}) collective-permute-start(bf16[2,64,1024]{2,1,0:T(8,128)(2,1)S(1)} %pad_maximum_fusion.2.refs_4_), channel_id=1, source_target_pairs={{0,32},{32,64},{64,0},{1,33},{33,65},{65,1},{2,34},{34,66},{66,2},... | collective-permute-start | bytes 786440 | tf_op jit(solution)/shard_map/ppermute | solution.py:23
  23.2 2.4 %collective-permute-start.4 = (bf16[2,64,1024]{2,1,0:T(8,128)(2,1)S(1)}, bf16[2,64,1024]{2,1,0:T(8,128)(2,1)S(1)}, u32[]{:S(2)}, u32[]{:S(2)}) collective-permute-start(bf16[2,64,1024]{2,1,0:T(8,128)(2,1)S(1)} %pad_maximum_fusion.2.refs_4_), channel_id=1, source_target_pairs={{0,64},{32,0},{64,32},{1,65},{33,1},{65,33},{2,66},{34,2},{66,34},... | collective-permute-start | bytes 786440 | tf_op jit(solution)/shard_map/ppermute | solution.py:23
  25.7 4.0 %collective-permute-start.5 = (bf16[2,64,1024]{2,1,0:T(8,128)(2,1)S(1)}, bf16[2,64,1024]{2,1,0:T(8,128)(2,1)S(1)}, u32[]{:S(2)}, u32[]{:S(2)}) collective-permute-start(bf16[2,64,1024]{2,1,0:T(8,128)(2,1)S(1)} %pad_maximum_fusion.2.refs_4_), channel_id=1, source_target_pairs={{0,576},{192,384},{384,192},{576,0},{1,577},{193,385},{385,193},{5... | collective-permute-start | bytes 786440 | tf_op jit(solution)/shard_map/ppermute | solution.py:21
  29.7 1.9 %collective-permute-start = (bf16[8,80,1024]{2,1,0:T(8,128)(2,1)}, bf16[8,80,1024]{2,1,0:T(8,128)(2,1)}, u32[]{:S(2)}, u32[]{:S(2)}) collective-permute-start(bf16[8,80,1024]{2,1,0:T(8,128)(2,1)} %bitcast.76), channel_id=1, source_target_pairs={{0,16},{16,0},{1,17},{17,1},{2,18},{18,2},{3,19},{19,3},{4,20},{20... | collective-permute-start | bytes 3932168 | tf_op jit(solution)/shard_map/ppermute | solution.py:136
  31.6 3.0 %collective-permute-done.3 = bf16[2,64,1024]{2,1,0:T(8,128)(2,1)S(1)} collective-permute-done((bf16[2,64,1024]{2,1,0:T(8,128)(2,1)S(1)}, bf16[2,64,1024]{2,1,0:T(8,128)(2,1)S(1)}, u32[]{:S(2)}, u32[]{:S(2)}) %collective-permute-start.3) | collective-permute-done | bytes 262176 | tf_op jit(solution)/shard_map/ppermute | solution.py:23
  34.6 0.8 collective-permute-done.4
  35.4 0.8 collective-permute-done.5.refs_6_
  36.2 0.7 copy-done.1
  36.9 0.0 collective-permute-done.1.refs_2_
  36.9 1.9 %collective-permute-start.6 = (bf16[8,80,1024]{2,1,0:T(8,128)(2,1)S(1)}, bf16[8,80,1024]{2,1,0:T(8,128)(2,1)}, u32[]{:S(2)}, u32[]{:S(2)}) collective-permute-start(bf16[8,80,1024]{2,1,0:T(8,128)(2,1)S(1)} %collective-permute-done.1.refs_2_), channel_id=1, source_target_pairs={{0,16},{16,0},{1,17},{17,1},{2,18},{18,2},{3,19},{19,3},{4,20},{20... | collective-permute-start | bytes 3932168 | tf_op jit(solution)/shard_map/ppermute | solution.py:138
  38.8 4.0 %collective-permute-start.7 = (bf16[4,64,1024]{2,1,0:T(8,128)(2,1)S(1)}, bf16[4,64,1024]{2,1,0:T(8,128)(2,1)}, u32[]{:S(2)}, u32[]{:S(2)}) collective-permute-start(bf16[4,64,1024]{2,1,0:T(8,128)(2,1)S(1)} %constant_dynamic-update-slice_fusion.refs_5_), channel_id=1, source_target_pairs={{0,576},{192,384},{384,192},{576,0},{1,577},{193,385},{385,193},{5... | collective-permute-start | bytes 1572872 | tf_op jit(solution)/shard_map/ppermute | solution.py:21
  42.9 0.1 pad_add_fusion.1.where
  42.9 13.4 %collective-permute-done.7.refs_7_ = bf16[4,64,1024]{2,1,0:T(8,128)(2,1)} collective-permute-done((bf16[4,64,1024]{2,1,0:T(8,128)(2,1)S(1)}, bf16[4,64,1024]{2,1,0:T(8,128)(2,1)}, u32[]{:S(2)}, u32[]{:S(2)}) %collective-permute-start.7) | collective-permute-done | bytes 524320 | tf_op jit(solution)/shard_map/ppermute | solution.py:21
  56.4 0.0 collective-permute-done.refs_1_
  56.4 0.0 collective-permute-done.6.refs_3_
  56.4 0.0 copy-start.2
  56.4 0.9 copy-done.2
  57.3 2.6 %shard_map.40 = bf16[1,320,768]{2,1,0:T(8,128)(2,1)S(1)} custom-call(s32[2]{0:T(128)S(1)} %pad_add_fusion.1.where, bf16[8,80,1024]{2,1,0:T(8,128)(2,1)S(1)} %bitcast.77, bf16[8,80,1024]{2,1,0:T(8,128)(2,1)} %collective-permute-done.refs_1_, bf16[8,80,1024]{2,1,0:T(8,128)(2,1)S(1)} %collective-permute-done.1.refs_2_, ...), custom_call_target="tpu_custom_call" | custom-call | flops 503316480 | bytes 2719744 | tf_op jit(solution)/shard_map/pallas_call | solution.py:65
  60.0 4.7 %collective-permute-start.8 = (bf16[160,768]{1,0:T(8,128)(2,1)S(1)}, bf16[160,768]{1,0:T(8,128)(2,1)S(1)}, u32[]{:S(2)}, u32[]{:S(2)}) collective-permute-start(bf16[160,768]{1,0:T(8,128)(2,1)S(1)} %get-tuple-element.11), channel_id=1, source_target_pairs={{0,1},{1,2},{2,3},{3,4},{4,5},{5,6},{6,7},{7,0},{8,9},{9,10},{10,1... | collective-permute-start | bytes 737288 | tf_op jit(solution)/shard_map/ppermute | solution.py:89
  64.7 2.6 %shard_map.39 = bf16[1,320,768]{2,1,0:T(8,128)(2,1)S(1)} custom-call(s32[2]{0:T(128)S(1)} %pad_add_fusion.1.where, bf16[8,80,1024]{2,1,0:T(8,128)(2,1)S(1)} %bitcast.78, bf16[8,80,1024]{2,1,0:T(8,128)(2,1)} %collective-permute-done.refs_1_, bf16[8,80,1024]{2,1,0:T(8,128)(2,1)S(1)} %collective-permute-done.1.refs_2_, ...), custom_call_target="tpu_custom_call" | custom-call | flops 503316480 | bytes 2719744 | tf_op jit(solution)/shard_map/pallas_call | solution.py:65
  67.4 1.9 %collective-permute-start.12 = (bf16[160,768]{1,0:T(8,128)(2,1)S(1)}, bf16[160,768]{1,0:T(8,128)(2,1)S(1)}, u32[]{:S(2)}, u32[]{:S(2)}) collective-permute-start(bf16[160,768]{1,0:T(8,128)(2,1)S(1)} %get-tuple-element.12), channel_id=1, source_target_pairs={{0,7},{1,0},{2,1},{3,2},{4,3},{5,4},{6,5},{7,6},{8,15},{9,8},{10,9... | collective-permute-start | bytes 737288 | tf_op jit(solution)/shard_map/ppermute | solution.py:90
  69.3 2.6 %shard_map.41 = bf16[1,320,768]{2,1,0:T(8,128)(2,1)S(1)} custom-call(s32[2]{0:T(128)S(1)} %pad_add_fusion.1.where, bf16[8,80,1024]{2,1,0:T(8,128)(2,1)S(1)} %bitcast.79, bf16[8,80,1024]{2,1,0:T(8,128)(2,1)} %collective-permute-done.refs_1_, bf16[8,80,1024]{2,1,0:T(8,128)(2,1)S(1)} %collective-permute-done.1.refs_2_, ...), custom_call_target="tpu_custom_call" | custom-call | flops 503316480 | bytes 2719744 | tf_op jit(solution)/shard_map/pallas_call | solution.py:65
  71.9 0.0 collective-permute-done.8
  71.9 0.1 fusion.7
  72.1 5.1 %collective-permute-start.9 = (bf16[320,768]{1,0:T(8,128)(2,1)S(1)}, bf16[320,768]{1,0:T(8,128)(2,1)S(1)}, u32[]{:S(2)}, u32[]{:S(2)}) collective-permute-start(bf16[320,768]{1,0:T(8,128)(2,1)S(1)} %pad_maximum_fusion), channel_id=1, source_target_pairs={{0,1},{1,2},{2,3},{3,4},{4,5},{5,6},{6,7},{7,0},{8,9},{9,10},{10,1... | collective-permute-start | bytes 1474568 | tf_op jit(solution)/shard_map/ppermute | solution.py:96
  77.2 0.6 collective-permute-done.12
  77.8 0.1 fusion.6
  77.9 1.9 %collective-permute-start.13 = (bf16[320,768]{1,0:T(8,128)(2,1)S(1)}, bf16[320,768]{1,0:T(8,128)(2,1)S(1)}, u32[]{:S(2)}, u32[]{:S(2)}) collective-permute-start(bf16[320,768]{1,0:T(8,128)(2,1)S(1)} %pad_maximum_fusion.1), channel_id=1, source_target_pairs={{0,7},{1,0},{2,1},{3,2},{4,3},{5,4},{6,5},{7,6},{8,15},{9,8},{10,9... | collective-permute-start | bytes 1474568 | tf_op jit(solution)/shard_map/ppermute | solution.py:97
  79.8 3.6 %shard_map.38 = bf16[2,320,768]{2,1,0:T(8,128)(2,1)S(1)} custom-call(s32[2]{0:T(128)S(1)} %pad_add_fusion.1.where, bf16[8,80,1024]{2,1,0:T(8,128)(2,1)S(1)} %bitcast.80, bf16[8,80,1024]{2,1,0:T(8,128)(2,1)} %collective-permute-done.refs_1_, bf16[8,80,1024]{2,1,0:T(8,128)(2,1)S(1)} %collective-permute-done.1.refs_2_, ...), custom_call_target="tpu_custom_call" | custom-call | flops 1006632960 | bytes 3866624 | tf_op jit(solution)/shard_map/pallas_call | solution.py:65
  83.4 4.5 %shard_map.37 = bf16[3,320,768]{2,1,0:T(8,128)(2,1)S(1)} custom-call(s32[2]{0:T(128)S(1)} %pad_add_fusion.1.where, bf16[8,80,1024]{2,1,0:T(8,128)(2,1)S(1)} %bitcast.81, bf16[8,80,1024]{2,1,0:T(8,128)(2,1)} %collective-permute-done.refs_1_, bf16[8,80,1024]{2,1,0:T(8,128)(2,1)S(1)} %collective-permute-done.1.refs_2_, ...), custom_call_target="tpu_custom_call" | custom-call | flops 1509949440 | bytes 5013504 | tf_op jit(solution)/shard_map/pallas_call | solution.py:65
  87.9 0.1 fusion.2
  88.1 5.1 %collective-permute-start.10 = (bf16[320,768]{1,0:T(8,128)(2,1)S(1)}, bf16[320,768]{1,0:T(8,128)(2,1)S(1)}, u32[]{:S(2)}, u32[]{:S(2)}) collective-permute-start(bf16[320,768]{1,0:T(8,128)(2,1)S(1)} %fusion.2), channel_id=1, source_target_pairs={{0,1},{1,2},{2,3},{3,4},{4,5},{5,6},{6,7},{7,0},{8,9},{9,10},{10,1... | collective-permute-start | bytes 1474568 | tf_op jit(solution)/shard_map/ppermute | solution.py:96
  93.2 0.0 collective-permute-done.13
  93.2 0.1 fusion
  93.3 0.0 copy-start.4
  93.4 1.9 %collective-permute-start.14 = (bf16[320,768]{1,0:T(8,128)(2,1)S(1)}, bf16[320,768]{1,0:T(8,128)(2,1)S(1)}, u32[]{:S(2)}, u32[]{:S(2)}) collective-permute-start(bf16[320,768]{1,0:T(8,128)(2,1)S(1)} %fusion), channel_id=1, source_target_pairs={{0,7},{1,0},{2,1},{3,2},{4,3},{5,4},{6,5},{7,6},{8,15},{9,8},{10,9... | collective-permute-start | bytes 1474568 | tf_op jit(solution)/shard_map/ppermute | solution.py:97
  95.3 6.8 %collective-permute-done.10 = bf16[320,768]{1,0:T(8,128)(2,1)S(1)} collective-permute-done((bf16[320,768]{1,0:T(8,128)(2,1)S(1)}, bf16[320,768]{1,0:T(8,128)(2,1)S(1)}, u32[]{:S(2)}, u32[]{:S(2)}) %collective-permute-start.10) | collective-permute-done | bytes 491552 | tf_op jit(solution)/shard_map/ppermute | solution.py:96
  102.1 0.1 fusion.3
  102.2 5.6 %collective-permute-start.11 = (bf16[320,768]{1,0:T(8,128)(2,1)S(1)}, bf16[320,768]{1,0:T(8,128)(2,1)S(1)}, u32[]{:S(2)}, u32[]{:S(2)}) collective-permute-start(bf16[320,768]{1,0:T(8,128)(2,1)S(1)} %fusion.3), channel_id=1, source_target_pairs={{0,1},{1,2},{2,3},{3,4},{4,5},{5,6},{6,7},{7,0},{8,9},{9,10},{10,1... | collective-permute-start | bytes 1474568 | tf_op jit(solution)/shard_map/ppermute | solution.py:96
  107.8 0.0 collective-permute-done.14
  107.8 0.1 fusion.1
  108.0 1.9 %collective-permute-start.15 = (bf16[320,768]{1,0:T(8,128)(2,1)S(1)}, bf16[320,768]{1,0:T(8,128)(2,1)S(1)}, u32[]{:S(2)}, u32[]{:S(2)}) collective-permute-start(bf16[320,768]{1,0:T(8,128)(2,1)S(1)} %fusion.1), channel_id=1, source_target_pairs={{0,7},{1,0},{2,1},{3,2},{4,3},{5,4},{6,5},{7,6},{8,15},{9,8},{10,9... | collective-permute-start | bytes 1474568 | tf_op jit(solution)/shard_map/ppermute | solution.py:97
  109.9 0.1 pad_add_fusion
  110.0 0.1 compare_reduce_fusion
  110.0 5.7 %collective-permute-done.11 = bf16[320,768]{1,0:T(8,128)(2,1)S(1)} collective-permute-done((bf16[320,768]{1,0:T(8,128)(2,1)S(1)}, bf16[320,768]{1,0:T(8,128)(2,1)S(1)}, u32[]{:S(2)}, u32[]{:S(2)}) %collective-permute-start.11) | collective-permute-done | bytes 491552 | tf_op jit(solution)/shard_map/ppermute | solution.py:96
  115.7 5.5 %collective-permute-done.15 = bf16[320,768]{1,0:T(8,128)(2,1)S(1)} collective-permute-done((bf16[320,768]{1,0:T(8,128)(2,1)S(1)}, bf16[320,768]{1,0:T(8,128)(2,1)S(1)}, u32[]{:S(2)}, u32[]{:S(2)}) %collective-permute-start.15) | collective-permute-done | bytes 491552 | tf_op jit(solution)/shard_map/ppermute | solution.py:97
  121.2 2.0 %fusion.5 = bf16[320,768]{1,0:T(8,128)(2,1)} fusion(bf16[320,768]{1,0:T(8,128)(2,1)S(1)} %collective-permute-done.15, bf16[320,768]{1,0:T(8,128)(2,1)S(1)} %collective-permute-done.11, bf16[3,320,768]{2,1,0:T(8,128)(2,1)} %copy-done.3), kind=kLoop, calls=%fused_computation.10 | loop fusion | flops 1474560 | bytes 1966080 | tf_op jit(solution)/shard_map/convert_element_type | solution.py:85
  123.2 3.5 %all-to-all-start = ((bf16[4,80,768]{2,1,0:T(8,128)(2,1)}), bf16[4,80,768]{2,1,0:T(8,128)(2,1)S(1)}, u32[]{:S(2)}, u32[]{:S(2)}) async-start(bf16[4,80,768]{2,1,0:T(8,128)(2,1)} %bitcast.42), calls=%async_computation | async-start | bytes 983040 | tf_op jit(solution)/shard_map/all_to_all | solution.py:106
  126.7 0.1 copy.7
  126.8 0.1 copy.8
  127.0 0.1 copy.6
  127.1 0.2 reduce_window_sum.11
  127.3 0.2 fusion.8
  127.5 7.7 %all-to-all-done.refs_3_ = bf16[4,80,768]{2,1,0:T(8,128)(2,1)S(1)} async-done(((bf16[4,80,768]{2,1,0:T(8,128)(2,1)}), bf16[4,80,768]{2,1,0:T(8,128)(2,1)S(1)}, u32[]{:S(2)}, u32[]{:S(2)}) %all-to-all-start) | async-done | bytes 491552 | tf_op jit(solution)/shard_map/all_to_all | solution.py:106
  135.2 13.3 %collective-permute-start.16 = (bf16[4,40,768]{2,1,0:T(8,128)(2,1)S(1)}, bf16[4,40,768]{2,1,0:T(8,128)(2,1)S(1)}, u32[]{:S(2)}, u32[]{:S(2)}) collective-permute-start(bf16[4,40,768]{2,1,0:T(8,128)(2,1)S(1)} %constant_dynamic-slice_fusion), channel_id=1, source_target_pairs={{0,8},{8,0},{1,9},{9,1},{2,10},{10,2},{3,11},{11,3},{4,12},{12,4},... | collective-permute-start | bytes 737288 | tf_op jit(solution)/shard_map/ppermute | solution.py:108
  148.5 0.1 fusion.11.refs_1_
  148.7 0.1 stack.123.refs_0_
  148.8 0.1 fusion.12.refs_2_
  148.9 16.1 %collective-permute-done.16.refs_4_ = bf16[4,40,768]{2,1,0:T(8,128)(2,1)S(1)} collective-permute-done((bf16[4,40,768]{2,1,0:T(8,128)(2,1)S(1)}, bf16[4,40,768]{2,1,0:T(8,128)(2,1)S(1)}, u32[]{:S(2)}, u32[]{:S(2)}) %collective-permute-start.16) | collective-permute-done | bytes 245792 | tf_op jit(solution)/shard_map/ppermute | solution.py:108
  165.0 2.1 %shard_map.42 = bf16[128,3072]{1,0:T(8,128)(2,1)} custom-call(s32[24]{0:T(128)S(1)} %stack.123.refs_0_, bf16[128,80]{1,0:T(8,128)(2,1)S(1)} %fusion.11.refs_1_, bf16[128,40]{1,0:T(8,128)(2,1)S(1)} %fusion.12.refs_2_, bf16[4,80,768]{2,1,0:T(8,128)(2,1)S(1)} %all-to-all-done.refs_3_, bf16[4,40,768]{2,1,0:T(8,128)(2,1)S(1)} %collective-permute-done.16.refs_4_), custom_call_target="tpu_custom_call" | custom-call | tf_op jit(solution)/shard_map/pallas_call | solution.py:163
  (18 shorter events, 0.2 us)
Async XLA Ops:
  0.0 56.4 %copy-start = (bf16[1,1,8,2,40,1024]{5,4,3,2,1,0:T(8,128)(2,1)S(1)}, bf16[1,1,8,2,40,1024]{5,4,3,2,1,0:T(8,128)(2,1)}, u32[]{:S(2)}) copy-start(bf16[1,1,8,2,40,1024]{5,4,3,2,1,0:T(8,128)(2,1)} %param.4) | copy-start | bytes 3932164
  0.0 36.9 %collective-permute-start.1 = (bf16[8,80,1024]{2,1,0:T(8,128)(2,1)}, bf16[8,80,1024]{2,1,0:T(8,128)(2,1)S(1)}, u32[]{:S(2)}, u32[]{:S(2)}) collective-permute-start(bf16[8,80,1024]{2,1,0:T(8,128)(2,1)} %bitcast.75), channel_id=1, source_target_pairs={{0,192},{192,0},{1,193},{193,1},{2,194},{194,2},{3,195},{195,3},{4... | collective-permute-start | bytes 3932168 | tf_op jit(solution)/shard_map/ppermute | solution.py:135
  3.5 15.3 %collective-permute-start.2 = (bf16[64,1024]{1,0:T(8,128)(2,1)}, bf16[64,1024]{1,0:T(8,128)(2,1)S(1)}, u32[]{:S(2)}, u32[]{:S(2)}) collective-permute-start(bf16[64,1024]{1,0:T(8,128)(2,1)} %bitcast.82), channel_id=1, source_target_pairs={{0,96},{96,0},{1,97},{97,1},{2,98},{98,2},{3,99},{99,3},{4,100},{1... | collective-permute-start | bytes 393224 | tf_op jit(solution)/shard_map/ppermute | solution.py:22
  19.8 14.8 %collective-permute-start.3 = (bf16[2,64,1024]{2,1,0:T(8,128)(2,1)S(1)}, bf16[2,64,1024]{2,1,0:T(8,128)(2,1)S(1)}, u32[]{:S(2)}, u32[]{:S(2)}) collective-permute-start(bf16[2,64,1024]{2,1,0:T(8,128)(2,1)S(1)} %pad_maximum_fusion.2.refs_4_), channel_id=1, source_target_pairs={{0,32},{32,64},{64,0},{1,33},{33,65},{65,1},{2,34},{34,66},{66,2},... | collective-permute-start | bytes 786440 | tf_op jit(solution)/shard_map/ppermute | solution.py:23
  23.2 12.1 %collective-permute-start.4 = (bf16[2,64,1024]{2,1,0:T(8,128)(2,1)S(1)}, bf16[2,64,1024]{2,1,0:T(8,128)(2,1)S(1)}, u32[]{:S(2)}, u32[]{:S(2)}) collective-permute-start(bf16[2,64,1024]{2,1,0:T(8,128)(2,1)S(1)} %pad_maximum_fusion.2.refs_4_), channel_id=1, source_target_pairs={{0,64},{32,0},{64,32},{1,65},{33,1},{65,33},{2,66},{34,2},{66,34},... | collective-permute-start | bytes 786440 | tf_op jit(solution)/shard_map/ppermute | solution.py:23
  25.7 10.6 %collective-permute-start.5 = (bf16[2,64,1024]{2,1,0:T(8,128)(2,1)S(1)}, bf16[2,64,1024]{2,1,0:T(8,128)(2,1)S(1)}, u32[]{:S(2)}, u32[]{:S(2)}) collective-permute-start(bf16[2,64,1024]{2,1,0:T(8,128)(2,1)S(1)} %pad_maximum_fusion.2.refs_4_), channel_id=1, source_target_pairs={{0,576},{192,384},{384,192},{576,0},{1,577},{193,385},{385,193},{5... | collective-permute-start | bytes 786440 | tf_op jit(solution)/shard_map/ppermute | solution.py:21
  29.7 26.7 %collective-permute-start = (bf16[8,80,1024]{2,1,0:T(8,128)(2,1)}, bf16[8,80,1024]{2,1,0:T(8,128)(2,1)}, u32[]{:S(2)}, u32[]{:S(2)}) collective-permute-start(bf16[8,80,1024]{2,1,0:T(8,128)(2,1)} %bitcast.76), channel_id=1, source_target_pairs={{0,16},{16,0},{1,17},{17,1},{2,18},{18,2},{3,19},{19,3},{4,20},{20... | collective-permute-start | bytes 3932168 | tf_op jit(solution)/shard_map/ppermute | solution.py:136
  36.2 0.7 copy-start.1
  36.9 19.5 %collective-permute-start.6 = (bf16[8,80,1024]{2,1,0:T(8,128)(2,1)S(1)}, bf16[8,80,1024]{2,1,0:T(8,128)(2,1)}, u32[]{:S(2)}, u32[]{:S(2)}) collective-permute-start(bf16[8,80,1024]{2,1,0:T(8,128)(2,1)S(1)} %collective-permute-done.1.refs_2_), channel_id=1, source_target_pairs={{0,16},{16,0},{1,17},{17,1},{2,18},{18,2},{3,19},{19,3},{4,20},{20... | collective-permute-start | bytes 3932168 | tf_op jit(solution)/shard_map/ppermute | solution.py:138
  38.8 17.5 %collective-permute-start.7 = (bf16[4,64,1024]{2,1,0:T(8,128)(2,1)S(1)}, bf16[4,64,1024]{2,1,0:T(8,128)(2,1)}, u32[]{:S(2)}, u32[]{:S(2)}) collective-permute-start(bf16[4,64,1024]{2,1,0:T(8,128)(2,1)S(1)} %constant_dynamic-update-slice_fusion.refs_5_), channel_id=1, source_target_pairs={{0,576},{192,384},{384,192},{576,0},{1,577},{193,385},{385,193},{5... | collective-permute-start | bytes 1572872 | tf_op jit(solution)/shard_map/ppermute | solution.py:21
  56.4 1.0 copy-start.2
  60.0 11.9 %collective-permute-start.8 = (bf16[160,768]{1,0:T(8,128)(2,1)S(1)}, bf16[160,768]{1,0:T(8,128)(2,1)S(1)}, u32[]{:S(2)}, u32[]{:S(2)}) collective-permute-start(bf16[160,768]{1,0:T(8,128)(2,1)S(1)} %get-tuple-element.11), channel_id=1, source_target_pairs={{0,1},{1,2},{2,3},{3,4},{4,5},{5,6},{6,7},{7,0},{8,9},{9,10},{10,1... | collective-permute-start | bytes 737288 | tf_op jit(solution)/shard_map/ppermute | solution.py:89
  67.4 10.4 %collective-permute-start.12 = (bf16[160,768]{1,0:T(8,128)(2,1)S(1)}, bf16[160,768]{1,0:T(8,128)(2,1)S(1)}, u32[]{:S(2)}, u32[]{:S(2)}) collective-permute-start(bf16[160,768]{1,0:T(8,128)(2,1)S(1)} %get-tuple-element.12), channel_id=1, source_target_pairs={{0,7},{1,0},{2,1},{3,2},{4,3},{5,4},{6,5},{7,6},{8,15},{9,8},{10,9... | collective-permute-start | bytes 737288 | tf_op jit(solution)/shard_map/ppermute | solution.py:90
  72.1 15.9 %collective-permute-start.9 = (bf16[320,768]{1,0:T(8,128)(2,1)S(1)}, bf16[320,768]{1,0:T(8,128)(2,1)S(1)}, u32[]{:S(2)}, u32[]{:S(2)}) collective-permute-start(bf16[320,768]{1,0:T(8,128)(2,1)S(1)} %pad_maximum_fusion), channel_id=1, source_target_pairs={{0,1},{1,2},{2,3},{3,4},{4,5},{5,6},{6,7},{7,0},{8,9},{9,10},{10,1... | collective-permute-start | bytes 1474568 | tf_op jit(solution)/shard_map/ppermute | solution.py:96
  77.9 15.3 %collective-permute-start.13 = (bf16[320,768]{1,0:T(8,128)(2,1)S(1)}, bf16[320,768]{1,0:T(8,128)(2,1)S(1)}, u32[]{:S(2)}, u32[]{:S(2)}) collective-permute-start(bf16[320,768]{1,0:T(8,128)(2,1)S(1)} %pad_maximum_fusion.1), channel_id=1, source_target_pairs={{0,7},{1,0},{2,1},{3,2},{4,3},{5,4},{6,5},{7,6},{8,15},{9,8},{10,9... | collective-permute-start | bytes 1474568 | tf_op jit(solution)/shard_map/ppermute | solution.py:97
  87.9 19.9 %copy-start.3 = (bf16[3,320,768]{2,1,0:T(8,128)(2,1)}, bf16[3,320,768]{2,1,0:T(8,128)(2,1)S(1)}, u32[]{:S(2)}) copy-start(bf16[3,320,768]{2,1,0:T(8,128)(2,1)S(1)} %shard_map.37) | copy-start | bytes 4423684
  88.1 14.0 %collective-permute-start.10 = (bf16[320,768]{1,0:T(8,128)(2,1)S(1)}, bf16[320,768]{1,0:T(8,128)(2,1)S(1)}, u32[]{:S(2)}, u32[]{:S(2)}) collective-permute-start(bf16[320,768]{1,0:T(8,128)(2,1)S(1)} %fusion.2), channel_id=1, source_target_pairs={{0,1},{1,2},{2,3},{3,4},{4,5},{5,6},{6,7},{7,0},{8,9},{9,10},{10,1... | collective-permute-start | bytes 1474568 | tf_op jit(solution)/shard_map/ppermute | solution.py:96
  93.3 16.6 %copy-start.4 = (s32[128,2]{0,1:T(2,128)S(1)}, s32[128,2]{0,1:T(2,128)}, u32[]{:S(2)}) copy-start(s32[128,2]{0,1:T(2,128)} %param.3) | copy-start | bytes 3076
  93.4 14.5 %collective-permute-start.14 = (bf16[320,768]{1,0:T(8,128)(2,1)S(1)}, bf16[320,768]{1,0:T(8,128)(2,1)S(1)}, u32[]{:S(2)}, u32[]{:S(2)}) collective-permute-start(bf16[320,768]{1,0:T(8,128)(2,1)S(1)} %fusion), channel_id=1, source_target_pairs={{0,7},{1,0},{2,1},{3,2},{4,3},{5,4},{6,5},{7,6},{8,15},{9,8},{10,9... | collective-permute-start | bytes 1474568 | tf_op jit(solution)/shard_map/ppermute | solution.py:97
  102.2 13.5 %collective-permute-start.11 = (bf16[320,768]{1,0:T(8,128)(2,1)S(1)}, bf16[320,768]{1,0:T(8,128)(2,1)S(1)}, u32[]{:S(2)}, u32[]{:S(2)}) collective-permute-start(bf16[320,768]{1,0:T(8,128)(2,1)S(1)} %fusion.3), channel_id=1, source_target_pairs={{0,1},{1,2},{2,3},{3,4},{4,5},{5,6},{6,7},{7,0},{8,9},{9,10},{10,1... | collective-permute-start | bytes 1474568 | tf_op jit(solution)/shard_map/ppermute | solution.py:96
  108.0 13.3 %collective-permute-start.15 = (bf16[320,768]{1,0:T(8,128)(2,1)S(1)}, bf16[320,768]{1,0:T(8,128)(2,1)S(1)}, u32[]{:S(2)}, u32[]{:S(2)}) collective-permute-start(bf16[320,768]{1,0:T(8,128)(2,1)S(1)} %fusion.1), channel_id=1, source_target_pairs={{0,7},{1,0},{2,1},{3,2},{4,3},{5,4},{6,5},{7,6},{8,15},{9,8},{10,9... | collective-permute-start | bytes 1474568 | tf_op jit(solution)/shard_map/ppermute | solution.py:97
  123.2 11.9 %all-to-all-start = ((bf16[4,80,768]{2,1,0:T(8,128)(2,1)}), bf16[4,80,768]{2,1,0:T(8,128)(2,1)S(1)}, u32[]{:S(2)}, u32[]{:S(2)}) async-start(bf16[4,80,768]{2,1,0:T(8,128)(2,1)} %bitcast.42), calls=%async_computation | async-start | bytes 983040 | tf_op jit(solution)/shard_map/all_to_all | solution.py:106
  135.2 29.8 %collective-permute-start.16 = (bf16[4,40,768]{2,1,0:T(8,128)(2,1)S(1)}, bf16[4,40,768]{2,1,0:T(8,128)(2,1)S(1)}, u32[]{:S(2)}, u32[]{:S(2)}) collective-permute-start(bf16[4,40,768]{2,1,0:T(8,128)(2,1)S(1)} %constant_dynamic-slice_fusion), channel_id=1, source_target_pairs={{0,8},{8,0},{1,9},{9,1},{2,10},{10,2},{3,11},{11,3},{4,12},{12,4},... | collective-permute-start | bytes 737288 | tf_op jit(solution)/shard_map/ppermute | solution.py:108

commit v8 on v6

--- a/solution.py
+++ b/solution.py
@@ -20,8 +20,8 @@
 def gather_columns(slab):
     opposite = lambda value: lax.ppermute(value, ("xh", "xp"), WEIGHT_SWAP)
     pair = jnp.stack([slab, lax.ppermute(slab, "h", SWAP)])
-    rest = jnp.concatenate([lax.ppermute(pair, "m", turn(1)), lax.ppermute(pair, "m", turn(-1))])
-    return (pair, rest), (opposite(pair), opposite(rest))
+    blocks = (pair, lax.ppermute(pair, "m", turn(1)), lax.ppermute(pair, "m", turn(-1)))
+    return blocks, [opposite(block) for block in blocks]
 
 
 def block_places():
@@ -35,21 +35,20 @@
     return jnp.stack([x * SIZES["h"] * count + z for x in xs for z in zs]).astype(jnp.int32)
 
 
-def product_kernel(where, *refs, pieces):
+def product_kernel(where, *refs, pieces, outs):
     rows, hidden = refs[0].shape[1:]
-    out = refs[-1]
     flat = jnp.concatenate([piece[0] for piece in refs[:pieces]])
-    dims = (((1,), (1,)), ((), ()))
-    at = 0
-    for block in refs[pieces:-1]:
-        features = block.shape[0] * block.shape[1]
-        result = lax.dot_general(
-            flat, block[...].reshape(features, hidden), dims, preferred_element_type=jnp.float32
-        ).astype(out.dtype)
-        for k in range(pieces):
-            start = pl.multiple_of((where[1] ^ k) * rows, rows)
-            out[0, pl.ds(start, rows), at:at + features] = result[k * rows:(k + 1) * rows]
-        at += features
+    weights = jnp.concatenate([block[...].reshape(-1, hidden) for block in refs[pieces:-outs]])
+    result = lax.dot_general(
+        flat, weights, (((1,), (1,)), ((), ())), preferred_element_type=jnp.float32
+    ).astype(jnp.bfloat16)
+    for i, out in enumerate(refs[-outs:]):
+
+        @pl.when(pl.program_id(0) == i)
+        def _():
+            for k in range(pieces):
+                start = pl.multiple_of((where[1] ^ k) * rows, rows)
+                out[pl.ds(start, rows), :] = result[k * rows:(k + 1) * rows]
 
 
 def product(where, pieces, blocks, first, stride, count):
@@ -63,17 +62,17 @@
         return ((where[0] + first + i * stride) % tensor_count, 0, 0)
 
     return pl.pallas_call(
-        functools.partial(product_kernel, pieces=len(pieces)),
+        functools.partial(product_kernel, pieces=len(pieces), outs=count),
         grid_spec=pltpu.PrefetchScalarGridSpec(
             num_scalar_prefetch=1,
             grid=(count,),
             in_specs=[pl.BlockSpec((1, rows, hidden), source)] * len(pieces)
             + [pl.BlockSpec(block.shape, lambda i, where: (0, 0, 0)) for block in blocks],
-            out_specs=pl.BlockSpec((1, rows_out, features), lambda i, where: (i, 0, 0)),
+            out_specs=[pl.BlockSpec((rows_out, features), lambda i, where: (0, 0))] * count,
         ),
-        out_shape=jax.ShapeDtypeStruct((count, rows_out, features), jnp.bfloat16),
+        out_shape=[jax.ShapeDtypeStruct((rows_out, features), jnp.bfloat16)] * count,
         cost_estimate=pl.CostEstimate(flops=flops, bytes_accessed=moved, transcendentals=0),
-        compiler_params=pltpu.CompilerParams(vmem_limit_bytes=14 * 1024 * 1024),
+        compiler_params=pltpu.CompilerParams(vmem_limit_bytes=20 * 1024 * 1024),
     )(where, *pieces, *blocks)
 
 
@@ -84,22 +83,22 @@
     wide = lambda value: value.astype(jnp.float32)
     narrow = lambda value: value.astype(jnp.bfloat16)
 
-    opposite = partial(mid, 1, 1)[0]
+    (opposite,) = partial(mid, 1, 1)
     half = opposite.shape[0] // 2
     first = lax.ppermute(opposite[:half], "t", up)
     last = lax.ppermute(opposite[half:], "t", down)
-    sides = partial(mid - 1, 2, 2)
-    others = partial(mid + 2, 1, n - 3)
-    above, below = sides[0], sides[1]
+    above, below = partial(mid - 1, 2, 2)
     going_up = jnp.concatenate([narrow(wide(above[:half]) + wide(first)), above[half:]])
     going_down = jnp.concatenate([below[:half], narrow(wide(below[half:]) + wide(last))])
+    others = partial(mid + 2, 1, n - 3)
+    lowers, uppers = others[:mid - 1], others[:mid - 2:-1]
     for step in range(1, mid):
         from_below = lax.ppermute(going_up, "t", up)
         from_above = lax.ppermute(going_down, "t", down)
         if step < mid - 1:
-            going_up = narrow(wide(others[n - 3 - step]) + wide(from_below))
-            going_down = narrow(wide(others[step - 1]) + wide(from_above))
-    return narrow(wide(others[mid - 2]) + wide(from_below) + wide(from_above))
+            going_up = narrow(wide(uppers[step - 1]) + wide(from_below))
+            going_down = narrow(wide(lowers[step - 1]) + wide(from_above))
+    return narrow(wide(lowers[mid - 2]) + wide(from_below) + wide(from_above))
 
 
 def give_back(summed, owners, capacity):
@@ -131,12 +130,12 @@
     column, other = gather_columns(slab)
     x_rows = lax.ppermute(own, "xp", SWAP)
     c_rows = lax.ppermute(own, "c", SWAP)
-    x_rows, _, _, first = lax.optimization_barrier((x_rows, *column, other[0]))
+    x_rows, *_ = lax.optimization_barrier((x_rows, *column, *other[:2]))
     pieces = (own, c_rows, x_rows, lax.ppermute(x_rows, "c", SWAP))
 
     places = [lax.axis_index("t"), lax.axis_index("xp") * SIZES["c"] + lax.axis_index("c")]
     where = jnp.stack(places).astype(jnp.int32)
-    blocks = (*column, first, other[1])
+    blocks = (*column, *other)
     summed = sum_by_arms(
         lambda k, stride, count: product(where, pieces, blocks, k, stride, count), tensor_count
     )

time: 170 us -> 162 us (0.953)
  the two profiles are of different devices: /device:TPU:1 before, /device:TPU:153 now
where the time goes in v8:
time: 162 us; the launch traced here: 161 us
  starting transfers between devices  74.9 us (46%)
  waiting for transfers between devices  64.4 us (40%)
  Pallas kernels  13.1 us (8%)
  local copies, waits for them, and re-layouts  5.29 us (3%)
  other arithmetic  2.84 us (2%)
    all_to_all x1, waiting for transfers between devices, give_back(): lax.all_to_all(summed.reshape(-1, capacity, features), ('xp', 'c', 'e'),...  23.8 us
    ppermute x3, starting transfers between devices, sum_by_arms(): from_below = lax.ppermute(going_up, 't', up)  14.5 us
    all_to_all x1, starting transfers between devices, give_back(): lax.all_to_all(summed.reshape(-1, capacity, features), ('xp', 'c', 'e'),...  12.3 us
    pallas_call x3, Pallas kernels, product(): pl.pallas_call(functools.partial(product_kernel, pieces=len(pieces), outs...  11.3 us
    ppermute x3, starting transfers between devices, gather_columns(): opposite = lambda value: lax.ppermute(value, ('xh', 'xp'), WEIGHT_SWAP)  11.2 us
    ppermute x3, waiting for transfers between devices, sum_by_arms(): from_below = lax.ppermute(going_up, 't', up)  9.38 us
    ppermute x3, waiting for transfers between devices, gather_columns(): opposite = lambda value: lax.ppermute(value, ('xh', 'xp'), WEIGHT_SWAP)  8.89 us
    ppermute x1, starting transfers between devices, gather_columns(): pair = jnp.stack([slab, lax.ppermute(slab, 'h', SWAP)])  8.83 us
  transfers between devices with their start and end apart: 18, of which 11 were waited for; matrix products, arithmetic and copies ran while one was open for 2% of the time, Pallas kernels for 6%

profile of v8, /device:TPU:153, one launch (start us, length us, event | category | flops | bytes accessed | tf_op | source)
XLA Modules:
  0.0 160.9 jit_solution(6134395849960011932)
XLA Ops:
  0.0 3.1 %collective-permute-start.1 = (bf16[8,80,1024]{2,1,0:T(8,128)(2,1)}, bf16[8,80,1024]{2,1,0:T(8,128)(2,1)S(1)}, u32[]{:S(2)}, u32[]{:S(2)}) collective-permute-start(bf16[8,80,1024]{2,1,0:T(8,128)(2,1)} %bitcast.33), channel_id=1, source_target_pairs={{0,192},{192,0},{1,193},{193,1},{2,194},{194,2},{3,195},{195,3},{4... | collective-permute-start | bytes 3932168 | tf_op jit(solution)/shard_map/ppermute | solution.py:131
  3.1 8.8 %collective-permute-start.2 = (bf16[64,1024]{1,0:T(8,128)(2,1)}, bf16[64,1024]{1,0:T(8,128)(2,1)S(1)}, u32[]{:S(2)}, u32[]{:S(2)}) collective-permute-start(bf16[64,1024]{1,0:T(8,128)(2,1)} %bitcast.40), channel_id=1, source_target_pairs={{0,96},{96,0},{1,97},{97,1},{2,98},{98,2},{3,99},{99,3},{4,100},{1... | collective-permute-start | bytes 393224 | tf_op jit(solution)/shard_map/ppermute | solution.py:22
  12.0 6.1 %collective-permute-done.2 = bf16[64,1024]{1,0:T(8,128)(2,1)S(1)} collective-permute-done((bf16[64,1024]{1,0:T(8,128)(2,1)}, bf16[64,1024]{1,0:T(8,128)(2,1)S(1)}, u32[]{:S(2)}, u32[]{:S(2)}) %collective-permute-start.2) | collective-permute-done | bytes 131104 | tf_op jit(solution)/shard_map/ppermute | solution.py:22
  18.1 0.9 pad_maximum_fusion.2.refs_4_
  19.0 1.9 %collective-permute-start.3 = (bf16[2,64,1024]{2,1,0:T(8,128)(2,1)S(1)}, bf16[2,64,1024]{2,1,0:T(8,128)(2,1)S(1)}, u32[]{:S(2)}, u32[]{:S(2)}) collective-permute-start(bf16[2,64,1024]{2,1,0:T(8,128)(2,1)S(1)} %pad_maximum_fusion.2.refs_4_), channel_id=1, source_target_pairs={{0,32},{32,64},{64,0},{1,33},{33,65},{65,1},{2,34},{34,66},{66,2},... | collective-permute-start | bytes 786440 | tf_op jit(solution)/shard_map/ppermute | solution.py:23
  20.9 3.4 %collective-permute-start.4 = (bf16[2,64,1024]{2,1,0:T(8,128)(2,1)S(1)}, bf16[2,64,1024]{2,1,0:T(8,128)(2,1)S(1)}, u32[]{:S(2)}, u32[]{:S(2)}) collective-permute-start(bf16[2,64,1024]{2,1,0:T(8,128)(2,1)S(1)} %pad_maximum_fusion.2.refs_4_), channel_id=1, source_target_pairs={{0,64},{32,0},{64,32},{1,65},{33,1},{65,33},{2,66},{34,2},{66,34},... | collective-permute-start | bytes 786440 | tf_op jit(solution)/shard_map/ppermute | solution.py:23
  24.3 3.7 %collective-permute-start.5 = (bf16[2,64,1024]{2,1,0:T(8,128)(2,1)S(1)}, bf16[2,64,1024]{2,1,0:T(8,128)(2,1)S(1)}, u32[]{:S(2)}, u32[]{:S(2)}) collective-permute-start(bf16[2,64,1024]{2,1,0:T(8,128)(2,1)S(1)} %pad_maximum_fusion.2.refs_4_), channel_id=1, source_target_pairs={{0,576},{192,384},{384,192},{576,0},{1,577},{193,385},{385,193},{5... | collective-permute-start | bytes 786440 | tf_op jit(solution)/shard_map/ppermute | solution.py:21
  28.0 5.9 %collective-permute-done.3.refs_5_ = bf16[2,64,1024]{2,1,0:T(8,128)(2,1)S(1)} collective-permute-done((bf16[2,64,1024]{2,1,0:T(8,128)(2,1)S(1)}, bf16[2,64,1024]{2,1,0:T(8,128)(2,1)S(1)}, u32[]{:S(2)}, u32[]{:S(2)}) %collective-permute-start.3) | collective-permute-done | bytes 262176 | tf_op jit(solution)/shard_map/ppermute | solution.py:23
  33.9 3.7 %collective-permute-start.6 = (bf16[2,64,1024]{2,1,0:T(8,128)(2,1)S(1)}, bf16[2,64,1024]{2,1,0:T(8,128)(2,1)S(1)}, u32[]{:S(2)}, u32[]{:S(2)}) collective-permute-start(bf16[2,64,1024]{2,1,0:T(8,128)(2,1)S(1)} %collective-permute-done.3.refs_5_), channel_id=1, source_target_pairs={{0,576},{192,384},{384,192},{576,0},{1,577},{193,385},{385,193},{5... | collective-permute-start | bytes 786440 | tf_op jit(solution)/shard_map/ppermute | solution.py:21
  37.6 3.5 %collective-permute-start = (bf16[8,80,1024]{2,1,0:T(8,128)(2,1)}, bf16[8,80,1024]{2,1,0:T(8,128)(2,1)S(1)}, u32[]{:S(2)}, u32[]{:S(2)}) collective-permute-start(bf16[8,80,1024]{2,1,0:T(8,128)(2,1)} %bitcast.34), channel_id=1, source_target_pairs={{0,16},{16,0},{1,17},{17,1},{2,18},{18,2},{3,19},{19,3},{4,20},{20... | collective-permute-start | bytes 3932168 | tf_op jit(solution)/shard_map/ppermute | solution.py:132
  41.1 0.0 collective-permute-done.4.refs_6_
  41.2 0.0 collective-permute-done.5.refs_7_
  41.2 0.0 copy-start.1
  41.2 0.7 copy-done.1
  41.9 1.6 collective-permute-done.6.refs_8_
  43.4 0.0 copy-start.3
  43.4 0.7 copy-done.3
  44.1 0.0 collective-permute-done.1.refs_2_
  44.1 4.2 %collective-permute-start.7 = (bf16[8,80,1024]{2,1,0:T(8,128)(2,1)S(1)}, bf16[8,80,1024]{2,1,0:T(8,128)(2,1)}, u32[]{:S(2)}, u32[]{:S(2)}) collective-permute-start(bf16[8,80,1024]{2,1,0:T(8,128)(2,1)S(1)} %collective-permute-done.1.refs_2_), channel_id=1, source_target_pairs={{0,16},{16,0},{1,17},{17,1},{2,18},{18,2},{3,19},{19,3},{4,20},{20... | collective-permute-start | bytes 3932168 | tf_op jit(solution)/shard_map/ppermute | solution.py:134
  48.3 3.7 %collective-permute-start.8 = (bf16[2,64,1024]{2,1,0:T(8,128)(2,1)S(1)}, bf16[2,64,1024]{2,1,0:T(8,128)(2,1)}, u32[]{:S(2)}, u32[]{:S(2)}) collective-permute-start(bf16[2,64,1024]{2,1,0:T(8,128)(2,1)S(1)} %collective-permute-done.4.refs_6_), channel_id=1, source_target_pairs={{0,576},{192,384},{384,192},{576,0},{1,577},{193,385},{385,193},{5... | collective-permute-start | bytes 786440 | tf_op jit(solution)/shard_map/ppermute | solution.py:21
  52.0 0.1 pad_add_fusion.where
  52.1 7.3 %collective-permute-done.8.refs_9_ = bf16[2,64,1024]{2,1,0:T(8,128)(2,1)} collective-permute-done((bf16[2,64,1024]{2,1,0:T(8,128)(2,1)S(1)}, bf16[2,64,1024]{2,1,0:T(8,128)(2,1)}, u32[]{:S(2)}, u32[]{:S(2)}) %collective-permute-start.8) | collective-permute-done | bytes 262176 | tf_op jit(solution)/shard_map/ppermute | solution.py:21
  59.4 0.0 collective-permute-done.refs_1_
  59.4 0.0 collective-permute-done.7.refs_3_
  59.5 1.3 copy-done
  60.8 0.9 copy-done.2
  61.7 0.9 copy-done.4
  62.7 2.2 %shard_map.39 = bf16[320,768]{1,0:T(8,128)(2,1)S(1)} custom-call(s32[2]{0:T(128)S(1)} %pad_add_fusion.where, bf16[8,80,1024]{2,1,0:T(8,128)(2,1)S(1)} %bitcast.35, bf16[8,80,1024]{2,1,0:T(8,128)(2,1)S(1)} %collective-permute-done.refs_1_, bf16[8,80,1024]{2,1,0:T(8,128)(2,1)S(1)} %collective-permute-done.1.refs_2_, ...), custom_call_target="tpu_custom_call" | custom-call | flops 503316480 | bytes 2719744 | tf_op jit(solution)/shard_map/pallas_call | solution.py:64
  65.0 4.4 %collective-permute-start.9 = (bf16[160,768]{1,0:T(8,128)(2,1)S(1)}, bf16[160,768]{1,0:T(8,128)(2,1)S(1)}, u32[]{:S(2)}, u32[]{:S(2)}) collective-permute-start(bf16[160,768]{1,0:T(8,128)(2,1)S(1)} %get-tuple-element.21), channel_id=1, source_target_pairs={{0,1},{1,2},{2,3},{3,4},{4,5},{5,6},{6,7},{7,0},{8,9},{9,10},{10,1... | collective-permute-start | bytes 737288 | tf_op jit(solution)/shard_map/ppermute | solution.py:88
  69.4 3.2 %shard_map.38 = (bf16[320,768]{1,0:T(8,128)(2,1)S(1)}, bf16[320,768]{1,0:T(8,128)(2,1)S(1)}) custom-call(s32[2]{0:T(128)S(1)} %pad_add_fusion.where, bf16[8,80,1024]{2,1,0:T(8,128)(2,1)S(1)} %bitcast.36, bf16[8,80,1024]{2,1,0:T(8,128)(2,1)S(1)} %collective-permute-done.refs_1_, bf16[8,80,1024]{2,1,0:T(8,128)(2,1)S(1)} %collective-permute-done.1.refs_2_, ...), custom_call_target="tpu_custom_call" | custom-call | flops 1006632960 | bytes 3866624 | tf_op jit(solution)/shard_map/pallas_call | solution.py:64
  72.6 1.9 %collective-permute-start.13 = (bf16[160,768]{1,0:T(8,128)(2,1)S(1)}, bf16[160,768]{1,0:T(8,128)(2,1)S(1)}, u32[]{:S(2)}, u32[]{:S(2)}) collective-permute-start(bf16[160,768]{1,0:T(8,128)(2,1)S(1)} %get-tuple-element.22), channel_id=1, source_target_pairs={{0,7},{1,0},{2,1},{3,2},{4,3},{5,4},{6,5},{7,6},{8,15},{9,8},{10,9... | collective-permute-start | bytes 737288 | tf_op jit(solution)/shard_map/ppermute | solution.py:89
  74.6 0.0 collective-permute-done.9
  74.6 0.1 add_convert_fusion.6
  74.7 4.6 %collective-permute-start.10 = (bf16[320,768]{1,0:T(8,128)(2,1)S(1)}, bf16[320,768]{1,0:T(8,128)(2,1)S(1)}, u32[]{:S(2)}, u32[]{:S(2)}) collective-permute-start(bf16[320,768]{1,0:T(8,128)(2,1)S(1)} %pad_maximum_fusion), channel_id=1, source_target_pairs={{0,1},{1,2},{2,3},{3,4},{4,5},{5,6},{6,7},{7,0},{8,9},{9,10},{10,1... | collective-permute-start | bytes 1474568 | tf_op jit(solution)/shard_map/ppermute | solution.py:96
  79.3 2.8 %collective-permute-done.13 = bf16[160,768]{1,0:T(8,128)(2,1)S(1)} collective-permute-done((bf16[160,768]{1,0:T(8,128)(2,1)S(1)}, bf16[160,768]{1,0:T(8,128)(2,1)S(1)}, u32[]{:S(2)}, u32[]{:S(2)}) %collective-permute-start.13) | collective-permute-done | bytes 245792 | tf_op jit(solution)/shard_map/ppermute | solution.py:89
  82.1 0.1 add_convert_fusion.5
  82.2 1.9 %collective-permute-start.14 = (bf16[320,768]{1,0:T(8,128)(2,1)S(1)}, bf16[320,768]{1,0:T(8,128)(2,1)S(1)}, u32[]{:S(2)}, u32[]{:S(2)}) collective-permute-start(bf16[320,768]{1,0:T(8,128)(2,1)S(1)} %pad_maximum_fusion.1), channel_id=1, source_target_pairs={{0,7},{1,0},{2,1},{3,2},{4,3},{5,4},{6,5},{7,6},{8,15},{9,8},{10,9... | collective-permute-start | bytes 1474568 | tf_op jit(solution)/shard_map/ppermute | solution.py:97
  84.1 5.8 %shard_map.37 = (bf16[320,768]{1,0:T(8,128)(2,1)S(1)}, bf16[320,768]{1,0:T(8,128)(2,1)S(1)}, bf16[320,768]{1,0:T(8,128)(2,1)S(1)}, bf16[320,768]{1,0:T(8,128)(2,1)S(1)}, bf16[320,768]{1,0:T(8,128)(2,1)S(1)}) custom-call(s32[2]{0:T(128)S(1)} %pad_add_fusion.where, bf16[8,80,1024]{2,1,0:T(8,128)(2,1)S(1)} %bitcast.37, ...), custom_call_target="tpu_custom_call" | custom-call | flops 2516582400 | bytes 7307264 | tf_op jit(solution)/shard_map/pallas_call | solution.py:64
  90.0 0.0 collective-permute-done.10
  90.0 0.1 add_convert_fusion.4
  90.1 4.6 %collective-permute-start.11 = (bf16[320,768]{1,0:T(8,128)(2,1)S(1)}, bf16[320,768]{1,0:T(8,128)(2,1)S(1)}, u32[]{:S(2)}, u32[]{:S(2)}) collective-permute-start(bf16[320,768]{1,0:T(8,128)(2,1)S(1)} %add_convert_fusion.4), channel_id=1, source_target_pairs={{0,1},{1,2},{2,3},{3,4},{4,5},{5,6},{6,7},{7,0},{8,9},{9,10},{10,1... | collective-permute-start | bytes 1474568 | tf_op jit(solution)/shard_map/ppermute | solution.py:96
  94.7 1.3 collective-permute-done.14
  96.0 0.1 add_convert_fusion.2
  96.1 1.9 %collective-permute-start.15 = (bf16[320,768]{1,0:T(8,128)(2,1)S(1)}, bf16[320,768]{1,0:T(8,128)(2,1)S(1)}, u32[]{:S(2)}, u32[]{:S(2)}) collective-permute-start(bf16[320,768]{1,0:T(8,128)(2,1)S(1)} %add_convert_fusion.2), channel_id=1, source_target_pairs={{0,7},{1,0},{2,1},{3,2},{4,3},{5,4},{6,5},{7,6},{8,15},{9,8},{10,9... | collective-permute-start | bytes 1474568 | tf_op jit(solution)/shard_map/ppermute | solution.py:97
  98.0 4.8 %collective-permute-done.11 = bf16[320,768]{1,0:T(8,128)(2,1)S(1)} collective-permute-done((bf16[320,768]{1,0:T(8,128)(2,1)S(1)}, bf16[320,768]{1,0:T(8,128)(2,1)S(1)}, u32[]{:S(2)}, u32[]{:S(2)}) %collective-permute-start.11) | collective-permute-done | bytes 491552 | tf_op jit(solution)/shard_map/ppermute | solution.py:96
  102.9 0.1 add_convert_fusion.3
  103.0 5.3 %collective-permute-start.12 = (bf16[320,768]{1,0:T(8,128)(2,1)S(1)}, bf16[320,768]{1,0:T(8,128)(2,1)S(1)}, u32[]{:S(2)}, u32[]{:S(2)}) collective-permute-start(bf16[320,768]{1,0:T(8,128)(2,1)S(1)} %add_convert_fusion.3), channel_id=1, source_target_pairs={{0,1},{1,2},{2,3},{3,4},{4,5},{5,6},{6,7},{7,0},{8,9},{9,10},{10,1... | collective-permute-start | bytes 1474568 | tf_op jit(solution)/shard_map/ppermute | solution.py:96
  108.3 0.7 collective-permute-done.15
  109.0 0.1 add_convert_fusion.1
  109.1 1.9 %collective-permute-start.16 = (bf16[320,768]{1,0:T(8,128)(2,1)S(1)}, bf16[320,768]{1,0:T(8,128)(2,1)S(1)}, u32[]{:S(2)}, u32[]{:S(2)}) collective-permute-start(bf16[320,768]{1,0:T(8,128)(2,1)S(1)} %add_convert_fusion.1), channel_id=1, source_target_pairs={{0,7},{1,0},{2,1},{3,2},{4,3},{5,4},{6,5},{7,6},{8,15},{9,8},{10,9... | collective-permute-start | bytes 1474568 | tf_op jit(solution)/shard_map/ppermute | solution.py:97
  111.1 4.5 %collective-permute-done.12 = bf16[320,768]{1,0:T(8,128)(2,1)S(1)} collective-permute-done((bf16[320,768]{1,0:T(8,128)(2,1)S(1)}, bf16[320,768]{1,0:T(8,128)(2,1)S(1)}, u32[]{:S(2)}, u32[]{:S(2)}) %collective-permute-start.12) | collective-permute-done | bytes 491552 | tf_op jit(solution)/shard_map/ppermute | solution.py:96
  115.6 5.5 %collective-permute-done.16 = bf16[320,768]{1,0:T(8,128)(2,1)S(1)} collective-permute-done((bf16[320,768]{1,0:T(8,128)(2,1)S(1)}, bf16[320,768]{1,0:T(8,128)(2,1)S(1)}, u32[]{:S(2)}, u32[]{:S(2)}) %collective-permute-start.16) | collective-permute-done | bytes 491552 | tf_op jit(solution)/shard_map/ppermute | solution.py:97
  121.1 1.0 add_convert_fusion
  122.1 12.3 %all-to-all-start = ((bf16[8,40,768]{2,1,0:T(8,128)(2,1)}), bf16[8,40,768]{2,1,0:T(8,128)(2,1)S(1)}, u32[]{:S(2)}, u32[]{:S(2)}) async-start(bf16[8,40,768]{2,1,0:T(8,128)(2,1)} %bitcast.31), calls=%async_computation | async-start | bytes 983040 | tf_op jit(solution)/shard_map/all_to_all | solution.py:106
  134.3 0.0 copy-done.5
  134.4 0.1 copy.14
  134.5 0.2 reduce_window_sum.11
  134.7 0.1 copy.15
  134.7 0.1 copy.16
  134.9 0.1 copy.18
  135.0 0.1 eq.43
  135.1 0.1 stack.114.refs_0_
  135.2 23.8 %all-to-all-done = bf16[8,40,768]{2,1,0:T(8,128)(2,1)S(1)} async-done(((bf16[8,40,768]{2,1,0:T(8,128)(2,1)}), bf16[8,40,768]{2,1,0:T(8,128)(2,1)S(1)}, u32[]{:S(2)}, u32[]{:S(2)}) %all-to-all-start) | async-done | bytes 491552 | tf_op jit(solution)/shard_map/all_to_all | solution.py:106
  159.0 1.9 %shard_map.40 = bf16[128,3072]{1,0:T(8,128)(2,1)} custom-call(s32[24]{0:T(128)S(1)} %stack.114.refs_0_, bf16[128,80]{1,0:T(8,128)(2,1)S(1)} %and_convert_fusion.refs_1_, bf16[4,80,768]{2,1,0:T(8,128)(2,1)S(1)} %bitcast.38), custom_call_target="tpu_custom_call" | custom-call | tf_op jit(solution)/shard_map/pallas_call | solution.py:156
  (16 shorter events, 0.2 us)
Async XLA Ops:
  0.0 44.1 %collective-permute-start.1 = (bf16[8,80,1024]{2,1,0:T(8,128)(2,1)}, bf16[8,80,1024]{2,1,0:T(8,128)(2,1)S(1)}, u32[]{:S(2)}, u32[]{:S(2)}) collective-permute-start(bf16[8,80,1024]{2,1,0:T(8,128)(2,1)} %bitcast.33), channel_id=1, source_target_pairs={{0,192},{192,0},{1,193},{193,1},{2,194},{194,2},{3,195},{195,3},{4... | collective-permute-start | bytes 3932168 | tf_op jit(solution)/shard_map/ppermute | solution.py:131
  3.1 14.9 %collective-permute-start.2 = (bf16[64,1024]{1,0:T(8,128)(2,1)}, bf16[64,1024]{1,0:T(8,128)(2,1)S(1)}, u32[]{:S(2)}, u32[]{:S(2)}) collective-permute-start(bf16[64,1024]{1,0:T(8,128)(2,1)} %bitcast.40), channel_id=1, source_target_pairs={{0,96},{96,0},{1,97},{97,1},{2,98},{98,2},{3,99},{99,3},{4,100},{1... | collective-permute-start | bytes 393224 | tf_op jit(solution)/shard_map/ppermute | solution.py:22
  19.0 14.9 %collective-permute-start.3 = (bf16[2,64,1024]{2,1,0:T(8,128)(2,1)S(1)}, bf16[2,64,1024]{2,1,0:T(8,128)(2,1)S(1)}, u32[]{:S(2)}, u32[]{:S(2)}) collective-permute-start(bf16[2,64,1024]{2,1,0:T(8,128)(2,1)S(1)} %pad_maximum_fusion.2.refs_4_), channel_id=1, source_target_pairs={{0,32},{32,64},{64,0},{1,33},{33,65},{65,1},{2,34},{34,66},{66,2},... | collective-permute-start | bytes 786440 | tf_op jit(solution)/shard_map/ppermute | solution.py:23
  20.9 20.2 %collective-permute-start.4 = (bf16[2,64,1024]{2,1,0:T(8,128)(2,1)S(1)}, bf16[2,64,1024]{2,1,0:T(8,128)(2,1)S(1)}, u32[]{:S(2)}, u32[]{:S(2)}) collective-permute-start(bf16[2,64,1024]{2,1,0:T(8,128)(2,1)S(1)} %pad_maximum_fusion.2.refs_4_), channel_id=1, source_target_pairs={{0,64},{32,0},{64,32},{1,65},{33,1},{65,33},{2,66},{34,2},{66,34},... | collective-permute-start | bytes 786440 | tf_op jit(solution)/shard_map/ppermute | solution.py:23
  24.3 16.9 %collective-permute-start.5 = (bf16[2,64,1024]{2,1,0:T(8,128)(2,1)S(1)}, bf16[2,64,1024]{2,1,0:T(8,128)(2,1)S(1)}, u32[]{:S(2)}, u32[]{:S(2)}) collective-permute-start(bf16[2,64,1024]{2,1,0:T(8,128)(2,1)S(1)} %pad_maximum_fusion.2.refs_4_), channel_id=1, source_target_pairs={{0,576},{192,384},{384,192},{576,0},{1,577},{193,385},{385,193},{5... | collective-permute-start | bytes 786440 | tf_op jit(solution)/shard_map/ppermute | solution.py:21
  33.9 9.6 %collective-permute-start.6 = (bf16[2,64,1024]{2,1,0:T(8,128)(2,1)S(1)}, bf16[2,64,1024]{2,1,0:T(8,128)(2,1)S(1)}, u32[]{:S(2)}, u32[]{:S(2)}) collective-permute-start(bf16[2,64,1024]{2,1,0:T(8,128)(2,1)S(1)} %collective-permute-done.3.refs_5_), channel_id=1, source_target_pairs={{0,576},{192,384},{384,192},{576,0},{1,577},{193,385},{385,193},{5... | collective-permute-start | bytes 786440 | tf_op jit(solution)/shard_map/ppermute | solution.py:21
  37.6 21.8 %collective-permute-start = (bf16[8,80,1024]{2,1,0:T(8,128)(2,1)}, bf16[8,80,1024]{2,1,0:T(8,128)(2,1)S(1)}, u32[]{:S(2)}, u32[]{:S(2)}) collective-permute-start(bf16[8,80,1024]{2,1,0:T(8,128)(2,1)} %bitcast.34), channel_id=1, source_target_pairs={{0,16},{16,0},{1,17},{17,1},{2,18},{18,2},{3,19},{19,3},{4,20},{20... | collective-permute-start | bytes 3932168 | tf_op jit(solution)/shard_map/ppermute | solution.py:132
  41.2 0.7 copy-start.1
  43.4 0.7 copy-start.3
  44.1 15.3 %collective-permute-start.7 = (bf16[8,80,1024]{2,1,0:T(8,128)(2,1)S(1)}, bf16[8,80,1024]{2,1,0:T(8,128)(2,1)}, u32[]{:S(2)}, u32[]{:S(2)}) collective-permute-start(bf16[8,80,1024]{2,1,0:T(8,128)(2,1)S(1)} %collective-permute-done.1.refs_2_), channel_id=1, source_target_pairs={{0,16},{16,0},{1,17},{17,1},{2,18},{18,2},{3,19},{19,3},{4,20},{20... | collective-permute-start | bytes 3932168 | tf_op jit(solution)/shard_map/ppermute | solution.py:134
  48.3 11.1 %collective-permute-start.8 = (bf16[2,64,1024]{2,1,0:T(8,128)(2,1)S(1)}, bf16[2,64,1024]{2,1,0:T(8,128)(2,1)}, u32[]{:S(2)}, u32[]{:S(2)}) collective-permute-start(bf16[2,64,1024]{2,1,0:T(8,128)(2,1)S(1)} %collective-permute-done.4.refs_6_), channel_id=1, source_target_pairs={{0,576},{192,384},{384,192},{576,0},{1,577},{193,385},{385,193},{5... | collective-permute-start | bytes 786440 | tf_op jit(solution)/shard_map/ppermute | solution.py:21
  59.5 1.3 copy-start
  60.8 0.9 copy-start.2
  61.7 0.9 copy-start.4
  65.0 9.6 %collective-permute-start.9 = (bf16[160,768]{1,0:T(8,128)(2,1)S(1)}, bf16[160,768]{1,0:T(8,128)(2,1)S(1)}, u32[]{:S(2)}, u32[]{:S(2)}) collective-permute-start(bf16[160,768]{1,0:T(8,128)(2,1)S(1)} %get-tuple-element.21), channel_id=1, source_target_pairs={{0,1},{1,2},{2,3},{3,4},{4,5},{5,6},{6,7},{7,0},{8,9},{9,10},{10,1... | collective-permute-start | bytes 737288 | tf_op jit(solution)/shard_map/ppermute | solution.py:88
  72.6 9.5 %collective-permute-start.13 = (bf16[160,768]{1,0:T(8,128)(2,1)S(1)}, bf16[160,768]{1,0:T(8,128)(2,1)S(1)}, u32[]{:S(2)}, u32[]{:S(2)}) collective-permute-start(bf16[160,768]{1,0:T(8,128)(2,1)S(1)} %get-tuple-element.22), channel_id=1, source_target_pairs={{0,7},{1,0},{2,1},{3,2},{4,3},{5,4},{6,5},{7,6},{8,15},{9,8},{10,9... | collective-permute-start | bytes 737288 | tf_op jit(solution)/shard_map/ppermute | solution.py:89
  74.7 15.3 %collective-permute-start.10 = (bf16[320,768]{1,0:T(8,128)(2,1)S(1)}, bf16[320,768]{1,0:T(8,128)(2,1)S(1)}, u32[]{:S(2)}, u32[]{:S(2)}) collective-permute-start(bf16[320,768]{1,0:T(8,128)(2,1)S(1)} %pad_maximum_fusion), channel_id=1, source_target_pairs={{0,1},{1,2},{2,3},{3,4},{4,5},{5,6},{6,7},{7,0},{8,9},{9,10},{10,1... | collective-permute-start | bytes 1474568 | tf_op jit(solution)/shard_map/ppermute | solution.py:96
  82.2 13.8 %collective-permute-start.14 = (bf16[320,768]{1,0:T(8,128)(2,1)S(1)}, bf16[320,768]{1,0:T(8,128)(2,1)S(1)}, u32[]{:S(2)}, u32[]{:S(2)}) collective-permute-start(bf16[320,768]{1,0:T(8,128)(2,1)S(1)} %pad_maximum_fusion.1), channel_id=1, source_target_pairs={{0,7},{1,0},{2,1},{3,2},{4,3},{5,4},{6,5},{7,6},{8,15},{9,8},{10,9... | collective-permute-start | bytes 1474568 | tf_op jit(solution)/shard_map/ppermute | solution.py:97
  90.1 12.8 %collective-permute-start.11 = (bf16[320,768]{1,0:T(8,128)(2,1)S(1)}, bf16[320,768]{1,0:T(8,128)(2,1)S(1)}, u32[]{:S(2)}, u32[]{:S(2)}) collective-permute-start(bf16[320,768]{1,0:T(8,128)(2,1)S(1)} %add_convert_fusion.4), channel_id=1, source_target_pairs={{0,1},{1,2},{2,3},{3,4},{4,5},{5,6},{6,7},{7,0},{8,9},{9,10},{10,1... | collective-permute-start | bytes 1474568 | tf_op jit(solution)/shard_map/ppermute | solution.py:96
  96.1 12.9 %collective-permute-start.15 = (bf16[320,768]{1,0:T(8,128)(2,1)S(1)}, bf16[320,768]{1,0:T(8,128)(2,1)S(1)}, u32[]{:S(2)}, u32[]{:S(2)}) collective-permute-start(bf16[320,768]{1,0:T(8,128)(2,1)S(1)} %add_convert_fusion.2), channel_id=1, source_target_pairs={{0,7},{1,0},{2,1},{3,2},{4,3},{5,4},{6,5},{7,6},{8,15},{9,8},{10,9... | collective-permute-start | bytes 1474568 | tf_op jit(solution)/shard_map/ppermute | solution.py:97
  103.0 12.6 %collective-permute-start.12 = (bf16[320,768]{1,0:T(8,128)(2,1)S(1)}, bf16[320,768]{1,0:T(8,128)(2,1)S(1)}, u32[]{:S(2)}, u32[]{:S(2)}) collective-permute-start(bf16[320,768]{1,0:T(8,128)(2,1)S(1)} %add_convert_fusion.3), channel_id=1, source_target_pairs={{0,1},{1,2},{2,3},{3,4},{4,5},{5,6},{6,7},{7,0},{8,9},{9,10},{10,1... | collective-permute-start | bytes 1474568 | tf_op jit(solution)/shard_map/ppermute | solution.py:96
  109.1 12.0 %collective-permute-start.16 = (bf16[320,768]{1,0:T(8,128)(2,1)S(1)}, bf16[320,768]{1,0:T(8,128)(2,1)S(1)}, u32[]{:S(2)}, u32[]{:S(2)}) collective-permute-start(bf16[320,768]{1,0:T(8,128)(2,1)S(1)} %add_convert_fusion.1), channel_id=1, source_target_pairs={{0,7},{1,0},{2,1},{3,2},{4,3},{5,4},{6,5},{7,6},{8,15},{9,8},{10,9... | collective-permute-start | bytes 1474568 | tf_op jit(solution)/shard_map/ppermute | solution.py:97
  121.1 13.2 %copy-start.5 = (s32[128,2]{0,1:T(2,128)S(1)}, s32[128,2]{0,1:T(2,128)}, u32[]{:S(2)}) copy-start(s32[128,2]{0,1:T(2,128)} %param.3) | copy-start | bytes 3076
  122.1 37.0 %all-to-all-start = ((bf16[8,40,768]{2,1,0:T(8,128)(2,1)}), bf16[8,40,768]{2,1,0:T(8,128)(2,1)S(1)}, u32[]{:S(2)}, u32[]{:S(2)}) async-start(bf16[8,40,768]{2,1,0:T(8,128)(2,1)} %bitcast.31), calls=%async_computation | async-start | bytes 983040 | tf_op jit(solution)/shard_map/all_to_all | solution.py:106

commit v9 on v8

--- a/solution.py
+++ b/solution.py
@@ -17,11 +17,11 @@
     return [(i, (i + shift) % SIZES["m"]) for i in range(SIZES["m"])]
 
 
-def gather_columns(slab):
+def gather_columns(slab, before):
     opposite = lambda value: lax.ppermute(value, ("xh", "xp"), WEIGHT_SWAP)
-    pair = jnp.stack([slab, lax.ppermute(slab, "h", SWAP)])
+    pair, before = lax.optimization_barrier((jnp.stack([slab, lax.ppermute(slab, "h", SWAP)]), before))
     blocks = (pair, lax.ppermute(pair, "m", turn(1)), lax.ppermute(pair, "m", turn(-1)))
-    return blocks, [opposite(block) for block in blocks]
+    return blocks, [opposite(block) for block in blocks], before
 
 
 def block_places():
@@ -72,7 +72,7 @@
         ),
         out_shape=[jax.ShapeDtypeStruct((rows_out, features), jnp.bfloat16)] * count,
         cost_estimate=pl.CostEstimate(flops=flops, bytes_accessed=moved, transcendentals=0),
-        compiler_params=pltpu.CompilerParams(vmem_limit_bytes=20 * 1024 * 1024),
+        compiler_params=pltpu.CompilerParams(vmem_limit_bytes=56 * 1024 * 1024),
     )(where, *pieces, *blocks)
 
 
@@ -127,10 +127,9 @@
     rows = owners * capacity
 
     own = upgrad.reshape(tensor_count, rows, hidden)
-    column, other = gather_columns(slab)
     x_rows = lax.ppermute(own, "xp", SWAP)
-    c_rows = lax.ppermute(own, "c", SWAP)
-    x_rows, *_ = lax.optimization_barrier((x_rows, *column, *other[:2]))
+    column, other, c_rows = gather_columns(slab, lax.ppermute(own, "c", SWAP))
+    x_rows, *_ = lax.optimization_barrier((x_rows, *column, *other))
     pieces = (own, c_rows, x_rows, lax.ppermute(x_rows, "c", SWAP))
 
     places = [lax.axis_index("t"), lax.axis_index("xp") * SIZES["c"] + lax.axis_index("c")]

time: 162 us -> 168 us (1.037)
  waiting for transfers between devices: 64.4 us -> 57.4 us
  starting transfers between devices: 74.9 us -> 81 us
  Pallas kernels: 13.1 us -> 19.1 us
  other arithmetic: 2.84 us -> 5.45 us
    pallas_call x3, Pallas kernels: 11.3 us -> 17.2 us  [product(): pl.pallas_call(functools.partial(product_kernel, pieces=len(pieces), outs...]
    ppermute x1, waiting for transfers between devices: 5.86 us -> 1.01 us  [gather_columns(): lax.ppermute(pair, 'm', turn(1))]
    unnamed x12 -> x28, local copies, waits for them, and re-layouts: 4.61 us -> 0.05 us
    ppermute x1, starting transfers between devices: 4.16 us -> 8.54 us  [shards(): pieces = (own, c_rows, x_rows, lax.ppermute(x_rows, 'c', SWAP))]
    ppermute x3, waiting for transfers between devices: 8.89 us -> 5.11 us  [gather_columns(): opposite = lambda value: lax.ppermute(value, ('xh', 'xp'), WEIGHT_SWAP)]
    ppermute x3, waiting for transfers between devices: 9.38 us -> 12.1 us  [sum_by_arms(): from_below = lax.ppermute(going_up, 't', up)]
    all_to_all x1, starting transfers between devices: 12.3 us -> 14.6 us  [give_back(): lax.all_to_all(summed.reshape(-1, capacity, features), ('xp', 'c', 'e'),...]
    ppermute x3, waiting for transfers between devices: 7.52 us -> 5.2 us  [sum_by_arms(): from_above = lax.ppermute(going_down, 't', down)]
  transfers between devices with their start and end apart: 18 -> 18, of which waited for: 11 -> 11; matrix products, arithmetic and copies ran while one was open for 2% -> 4% of each run, Pallas kernels for 6% -> 8%
where the time goes in v9:
time: 168 us; the launch traced here: 167 us
  starting transfers between devices  81 us (48%)
  waiting for transfers between devices  57.4 us (34%)
  Pallas kernels  19.1 us (11%)
  other arithmetic  5.45 us (3%)
  local copies, waits for them, and re-layouts  3.74 us (2%)
    all_to_all x1, waiting for transfers between devices, give_back(): lax.all_to_all(summed.reshape(-1, capacity, features), ('xp', 'c', 'e'),...  23.8 us
    pallas_call x3, Pallas kernels, product(): pl.pallas_call(functools.partial(product_kernel, pieces=len(pieces), outs...  17.2 us
    all_to_all x1, starting transfers between devices, give_back(): lax.all_to_all(summed.reshape(-1, capacity, features), ('xp', 'c', 'e'),...  14.6 us
    ppermute x3, starting transfers between devices, sum_by_arms(): from_below = lax.ppermute(going_up, 't', up)  14.6 us
    ppermute x3, waiting for transfers between devices, sum_by_arms(): from_below = lax.ppermute(going_up, 't', up)  12.1 us
    ppermute x3, starting transfers between devices, gather_columns(): opposite = lambda value: lax.ppermute(value, ('xh', 'xp'), WEIGHT_SWAP)  11.1 us
    ppermute x1, starting transfers between devices, gather_columns(): lax.ppermute(slab, 'h', SWAP)  8.83 us
    ppermute x1, starting transfers between devices, shards(): pieces = (own, c_rows, x_rows, lax.ppermute(x_rows, 'c', SWAP))  8.54 us
  transfers between devices with their start and end apart: 18, of which 11 were waited for; matrix products, arithmetic and copies ran while one was open for 4% of the time, Pallas kernels for 8%

profile of v9, /device:TPU:153, one launch (start us, length us, event | category | flops | bytes accessed | tf_op | source)
XLA Modules:
  0.0 167.0 jit_solution(14759739603796437598)
XLA Ops:
  0.0 2.6 %collective-permute-start.1 = (bf16[8,80,1024]{2,1,0:T(8,128)(2,1)}, bf16[8,80,1024]{2,1,0:T(8,128)(2,1)S(1)}, u32[]{:S(2)}, u32[]{:S(2)}) collective-permute-start(bf16[8,80,1024]{2,1,0:T(8,128)(2,1)} %bitcast.34), channel_id=1, source_target_pairs={{0,16},{16,0},{1,17},{17,1},{2,18},{18,2},{3,19},{19,3},{4,20},{20... | collective-permute-start | bytes 3932168 | tf_op jit(solution)/shard_map/ppermute | solution.py:131
  2.6 3.1 %collective-permute-start.2 = (bf16[8,80,1024]{2,1,0:T(8,128)(2,1)}, bf16[8,80,1024]{2,1,0:T(8,128)(2,1)S(1)}, u32[]{:S(2)}, u32[]{:S(2)}) collective-permute-start(bf16[8,80,1024]{2,1,0:T(8,128)(2,1)} %bitcast.35), channel_id=1, source_target_pairs={{0,192},{192,0},{1,193},{193,1},{2,194},{194,2},{3,195},{195,3},{4... | collective-permute-start | bytes 3932168 | tf_op jit(solution)/shard_map/ppermute | solution.py:130
  5.7 8.8 %collective-permute-start = (bf16[64,1024]{1,0:T(8,128)(2,1)}, bf16[64,1024]{1,0:T(8,128)(2,1)S(1)}, u32[]{:S(2)}, u32[]{:S(2)}) collective-permute-start(bf16[64,1024]{1,0:T(8,128)(2,1)} %bitcast.40), channel_id=1, source_target_pairs={{0,96},{96,0},{1,97},{97,1},{2,98},{98,2},{3,99},{99,3},{4,100},{1... | collective-permute-start | bytes 393224 | tf_op jit(solution)/shard_map/ppermute | solution.py:22
  14.5 6.1 %collective-permute-done = bf16[64,1024]{1,0:T(8,128)(2,1)S(1)} collective-permute-done((bf16[64,1024]{1,0:T(8,128)(2,1)}, bf16[64,1024]{1,0:T(8,128)(2,1)S(1)}, u32[]{:S(2)}, u32[]{:S(2)}) %collective-permute-start) | collective-permute-done | bytes 131104 | tf_op jit(solution)/shard_map/ppermute | solution.py:22
  20.7 0.9 pad_maximum_fusion.2.refs_4_
  21.6 0.0 copy-start.2
  21.6 0.0 collective-permute-done.1.refs_1_
  21.6 0.0 copy-start
  21.6 1.9 %collective-permute-start.3 = (bf16[2,64,1024]{2,1,0:T(8,128)(2,1)S(1)}, bf16[2,64,1024]{2,1,0:T(8,128)(2,1)S(1)}, u32[]{:S(2)}, u32[]{:S(2)}) collective-permute-start(bf16[2,64,1024]{2,1,0:T(8,128)(2,1)S(1)} %pad_maximum_fusion.2.refs_4_), channel_id=1, source_target_pairs={{0,32},{32,64},{64,0},{1,33},{33,65},{65,1},{2,34},{34,66},{66,2},... | collective-permute-start | bytes 786440 | tf_op jit(solution)/shard_map/ppermute | solution.py:23
  23.6 3.4 %collective-permute-start.4 = (bf16[2,64,1024]{2,1,0:T(8,128)(2,1)S(1)}, bf16[2,64,1024]{2,1,0:T(8,128)(2,1)S(1)}, u32[]{:S(2)}, u32[]{:S(2)}) collective-permute-start(bf16[2,64,1024]{2,1,0:T(8,128)(2,1)S(1)} %pad_maximum_fusion.2.refs_4_), channel_id=1, source_target_pairs={{0,64},{32,0},{64,32},{1,65},{33,1},{65,33},{2,66},{34,2},{66,34},... | collective-permute-start | bytes 786440 | tf_op jit(solution)/shard_map/ppermute | solution.py:23
  26.9 3.7 %collective-permute-start.5 = (bf16[2,64,1024]{2,1,0:T(8,128)(2,1)S(1)}, bf16[2,64,1024]{2,1,0:T(8,128)(2,1)S(1)}, u32[]{:S(2)}, u32[]{:S(2)}) collective-permute-start(bf16[2,64,1024]{2,1,0:T(8,128)(2,1)S(1)} %pad_maximum_fusion.2.refs_4_), channel_id=1, source_target_pairs={{0,576},{192,384},{384,192},{576,0},{1,577},{193,385},{385,193},{5... | collective-permute-start | bytes 786440 | tf_op jit(solution)/shard_map/ppermute | solution.py:21
  30.7 1.0 collective-permute-done.3.refs_5_
  31.7 3.7 %collective-permute-start.6 = (bf16[2,64,1024]{2,1,0:T(8,128)(2,1)S(1)}, bf16[2,64,1024]{2,1,0:T(8,128)(2,1)S(1)}, u32[]{:S(2)}, u32[]{:S(2)}) collective-permute-start(bf16[2,64,1024]{2,1,0:T(8,128)(2,1)S(1)} %collective-permute-done.3.refs_5_), channel_id=1, source_target_pairs={{0,576},{192,384},{384,192},{576,0},{1,577},{193,385},{385,193},{5... | collective-permute-start | bytes 786440 | tf_op jit(solution)/shard_map/ppermute | solution.py:21
  35.4 0.5 collective-permute-done.4.refs_6_
  35.9 3.7 %collective-permute-start.7 = (bf16[2,64,1024]{2,1,0:T(8,128)(2,1)S(1)}, bf16[2,64,1024]{2,1,0:T(8,128)(2,1)S(1)}, u32[]{:S(2)}, u32[]{:S(2)}) collective-permute-start(bf16[2,64,1024]{2,1,0:T(8,128)(2,1)S(1)} %collective-permute-done.4.refs_6_), channel_id=1, source_target_pairs={{0,576},{192,384},{384,192},{576,0},{1,577},{193,385},{385,193},{5... | collective-permute-start | bytes 786440 | tf_op jit(solution)/shard_map/ppermute | solution.py:21
  39.6 0.0 collective-permute-done.2.refs_2_
  39.6 0.0 collective-permute-done.5.refs_7_
  39.6 1.3 collective-permute-done.6.refs_8_
  40.9 3.8 %collective-permute-done.7.refs_9_ = bf16[2,64,1024]{2,1,0:T(8,128)(2,1)S(1)} collective-permute-done((bf16[2,64,1024]{2,1,0:T(8,128)(2,1)S(1)}, bf16[2,64,1024]{2,1,0:T(8,128)(2,1)S(1)}, u32[]{:S(2)}, u32[]{:S(2)}) %collective-permute-start.7) | collective-permute-done | bytes 262176 | tf_op jit(solution)/shard_map/ppermute | solution.py:21
  44.7 8.5 %collective-permute-start.8 = (bf16[8,80,1024]{2,1,0:T(8,128)(2,1)S(1)}, bf16[8,80,1024]{2,1,0:T(8,128)(2,1)}, u32[]{:S(2)}, u32[]{:S(2)}) collective-permute-start(bf16[8,80,1024]{2,1,0:T(8,128)(2,1)S(1)} %collective-permute-done.2.refs_2_), channel_id=1, source_target_pairs={{0,16},{16,0},{1,17},{17,1},{2,18},{18,2},{3,19},{19,3},{4,20},{20... | collective-permute-start | bytes 3932168 | tf_op jit(solution)/shard_map/ppermute | solution.py:133
  53.3 0.6 pad_add_fusion.where
  54.0 2.1 %collective-permute-done.8.refs_3_ = bf16[8,80,1024]{2,1,0:T(8,128)(2,1)} collective-permute-done((bf16[8,80,1024]{2,1,0:T(8,128)(2,1)S(1)}, bf16[8,80,1024]{2,1,0:T(8,128)(2,1)}, u32[]{:S(2)}, u32[]{:S(2)}) %collective-permute-start.8) | collective-permute-done | bytes 1310752 | tf_op jit(solution)/shard_map/ppermute | solution.py:133
  56.1 0.0 copy-done.3
  56.1 3.7 %shard_map.39 = bf16[320,768]{1,0:T(8,128)(2,1)} custom-call(s32[2]{0:T(128)} %pad_add_fusion.where, bf16[8,80,1024]{2,1,0:T(8,128)(2,1)} %bitcast.36, bf16[8,80,1024]{2,1,0:T(8,128)(2,1)} %copy-done, bf16[8,80,1024]{2,1,0:T(8,128)(2,1)} %copy-done.1, bf16[8,80,1024]{2,1,0:T(8,128)(2,1)} %collective-permute-done.8.refs_3_, bf16[2,64,1024]{2,1,0:T(8,128)(2,1)} %copy-done.2, ...), custom_call_target="tpu_custom_call" | custom-call | flops 503316480 | bytes 2719744 | tf_op jit(solution)/shard_map/pallas_call | solution.py:64
  59.8 1.1 fusion
  60.9 4.4 %collective-permute-start.9 = (bf16[160,768]{1,0:T(8,128)(2,1)S(1)}, bf16[160,768]{1,0:T(8,128)(2,1)S(1)}, u32[]{:S(2)}, u32[]{:S(2)}) collective-permute-start(bf16[160,768]{1,0:T(8,128)(2,1)S(1)} %get-tuple-element.25), channel_id=1, source_target_pairs={{0,1},{1,2},{2,3},{3,4},{4,5},{5,6},{6,7},{7,0},{8,9},{9,10},{10,1... | collective-permute-start | bytes 737288 | tf_op jit(solution)/shard_map/ppermute | solution.py:88
  65.3 5.0 %shard_map.38 = (bf16[320,768]{1,0:T(8,128)(2,1)}, bf16[320,768]{1,0:T(8,128)(2,1)}) custom-call(s32[2]{0:T(128)} %pad_add_fusion.where, bf16[8,80,1024]{2,1,0:T(8,128)(2,1)} %bitcast.37, bf16[8,80,1024]{2,1,0:T(8,128)(2,1)} %copy-done, bf16[8,80,1024]{2,1,0:T(8,128)(2,1)} %copy-done.1, bf16[8,80,1024]{2,1,0:T(8,128)(2,1)} %collective-permute-done.8.refs_3_, ...), custom_call_target="tpu_custom_call" | custom-call | flops 1006632960 | bytes 3866624 | tf_op jit(solution)/shard_map/pallas_call | solution.py:64
  70.3 1.0 slice.20
  71.3 1.9 %collective-permute-start.13 = (bf16[160,768]{1,0:T(8,128)(2,1)S(1)}, bf16[160,768]{1,0:T(8,128)(2,1)S(1)}, u32[]{:S(2)}, u32[]{:S(2)}) collective-permute-start(bf16[160,768]{1,0:T(8,128)(2,1)S(1)} %get-tuple-element.26), channel_id=1, source_target_pairs={{0,7},{1,0},{2,1},{3,2},{4,3},{5,4},{6,5},{7,6},{8,15},{9,8},{10,9... | collective-permute-start | bytes 737288 | tf_op jit(solution)/shard_map/ppermute | solution.py:89
  73.2 1.0 slice.21
  74.2 0.0 collective-permute-done.9
  74.2 1.0 add_convert_fusion.6
  75.2 4.6 %collective-permute-start.10 = (bf16[320,768]{1,0:T(8,128)(2,1)S(1)}, bf16[320,768]{1,0:T(8,128)(2,1)S(1)}, u32[]{:S(2)}, u32[]{:S(2)}) collective-permute-start(bf16[320,768]{1,0:T(8,128)(2,1)S(1)} %pad_maximum_fusion), channel_id=1, source_target_pairs={{0,1},{1,2},{2,3},{3,4},{4,5},{5,6},{6,7},{7,0},{8,9},{9,10},{10,1... | collective-permute-start | bytes 1474568 | tf_op jit(solution)/shard_map/ppermute | solution.py:96
  79.8 1.4 collective-permute-done.13
  81.2 0.1 add_convert_fusion.5
  81.3 1.9 %collective-permute-start.14 = (bf16[320,768]{1,0:T(8,128)(2,1)S(1)}, bf16[320,768]{1,0:T(8,128)(2,1)S(1)}, u32[]{:S(2)}, u32[]{:S(2)}) collective-permute-start(bf16[320,768]{1,0:T(8,128)(2,1)S(1)} %pad_maximum_fusion.1), channel_id=1, source_target_pairs={{0,7},{1,0},{2,1},{3,2},{4,3},{5,4},{6,5},{7,6},{8,15},{9,8},{10,9... | collective-permute-start | bytes 1474568 | tf_op jit(solution)/shard_map/ppermute | solution.py:97
  83.3 8.6 %shard_map.37 = (bf16[320,768]{1,0:T(8,128)(2,1)}, bf16[320,768]{1,0:T(8,128)(2,1)}, bf16[320,768]{1,0:T(8,128)(2,1)}, bf16[320,768]{1,0:T(8,128)(2,1)}, bf16[320,768]{1,0:T(8,128)(2,1)}) custom-call(s32[2]{0:T(128)} %pad_add_fusion.where, bf16[8,80,1024]{2,1,0:T(8,128)(2,1)} %bitcast.38, bf16[8,80,1024]{2,1,0:T(8,128)(2,1)} %copy-done, ...), custom_call_target="tpu_custom_call" | custom-call | flops 2516582400 | bytes 7307264 | tf_op jit(solution)/shard_map/pallas_call | solution.py:64
  91.8 0.0 collective-permute-done.10
  91.9 1.2 add_convert_fusion.4
  93.1 4.6 %collective-permute-start.11 = (bf16[320,768]{1,0:T(8,128)(2,1)S(1)}, bf16[320,768]{1,0:T(8,128)(2,1)S(1)}, u32[]{:S(2)}, u32[]{:S(2)}) collective-permute-start(bf16[320,768]{1,0:T(8,128)(2,1)S(1)} %add_convert_fusion.4), channel_id=1, source_target_pairs={{0,1},{1,2},{2,3},{3,4},{4,5},{5,6},{6,7},{7,0},{8,9},{9,10},{10,1... | collective-permute-start | bytes 1474568 | tf_op jit(solution)/shard_map/ppermute | solution.py:96
  97.7 0.0 collective-permute-done.14
  97.7 0.1 add_convert_fusion.2
  97.8 2.1 %collective-permute-start.15 = (bf16[320,768]{1,0:T(8,128)(2,1)S(1)}, bf16[320,768]{1,0:T(8,128)(2,1)S(1)}, u32[]{:S(2)}, u32[]{:S(2)}) collective-permute-start(bf16[320,768]{1,0:T(8,128)(2,1)S(1)} %add_convert_fusion.2), channel_id=1, source_target_pairs={{0,7},{1,0},{2,1},{3,2},{4,3},{5,4},{6,5},{7,6},{8,15},{9,8},{10,9... | collective-permute-start | bytes 1474568 | tf_op jit(solution)/shard_map/ppermute | solution.py:97
  99.9 6.5 %collective-permute-done.11 = bf16[320,768]{1,0:T(8,128)(2,1)S(1)} collective-permute-done((bf16[320,768]{1,0:T(8,128)(2,1)S(1)}, bf16[320,768]{1,0:T(8,128)(2,1)S(1)}, u32[]{:S(2)}, u32[]{:S(2)}) %collective-permute-start.11) | collective-permute-done | bytes 491552 | tf_op jit(solution)/shard_map/ppermute | solution.py:96
  106.3 0.0 copy-done.9
  106.3 0.1 add_convert_fusion.3
  106.5 5.5 %collective-permute-start.12 = (bf16[320,768]{1,0:T(8,128)(2,1)S(1)}, bf16[320,768]{1,0:T(8,128)(2,1)S(1)}, u32[]{:S(2)}, u32[]{:S(2)}) collective-permute-start(bf16[320,768]{1,0:T(8,128)(2,1)S(1)} %add_convert_fusion.3), channel_id=1, source_target_pairs={{0,1},{1,2},{2,3},{3,4},{4,5},{5,6},{6,7},{7,0},{8,9},{9,10},{10,1... | collective-permute-start | bytes 1474568 | tf_op jit(solution)/shard_map/ppermute | solution.py:96
  111.9 0.0 collective-permute-done.15
  111.9 0.1 add_convert_fusion.1
  112.1 1.9 %collective-permute-start.16 = (bf16[320,768]{1,0:T(8,128)(2,1)S(1)}, bf16[320,768]{1,0:T(8,128)(2,1)S(1)}, u32[]{:S(2)}, u32[]{:S(2)}) collective-permute-start(bf16[320,768]{1,0:T(8,128)(2,1)S(1)} %add_convert_fusion.1), channel_id=1, source_target_pairs={{0,7},{1,0},{2,1},{3,2},{4,3},{5,4},{6,5},{7,6},{8,15},{9,8},{10,9... | collective-permute-start | bytes 1474568 | tf_op jit(solution)/shard_map/ppermute | solution.py:97
  114.0 5.7 %collective-permute-done.12 = bf16[320,768]{1,0:T(8,128)(2,1)S(1)} collective-permute-done((bf16[320,768]{1,0:T(8,128)(2,1)S(1)}, bf16[320,768]{1,0:T(8,128)(2,1)S(1)}, u32[]{:S(2)}, u32[]{:S(2)}) %collective-permute-start.12) | collective-permute-done | bytes 491552 | tf_op jit(solution)/shard_map/ppermute | solution.py:96
  119.7 5.2 %collective-permute-done.16 = bf16[320,768]{1,0:T(8,128)(2,1)S(1)} collective-permute-done((bf16[320,768]{1,0:T(8,128)(2,1)S(1)}, bf16[320,768]{1,0:T(8,128)(2,1)S(1)}, u32[]{:S(2)}, u32[]{:S(2)}) %collective-permute-start.16) | collective-permute-done | bytes 491552 | tf_op jit(solution)/shard_map/ppermute | solution.py:97
  124.9 1.0 add_convert_fusion
  125.8 14.6 %all-to-all-start = ((bf16[8,40,768]{2,1,0:T(8,128)(2,1)}), bf16[8,40,768]{2,1,0:T(8,128)(2,1)S(1)}, u32[]{:S(2)}, u32[]{:S(2)}) async-start(bf16[8,40,768]{2,1,0:T(8,128)(2,1)} %bitcast.31), calls=%async_computation | async-start | bytes 983040 | tf_op jit(solution)/shard_map/all_to_all | solution.py:106
  140.5 0.0 copy-done.13
  140.5 0.1 copy.14
  140.6 0.2 reduce_window_sum.11
  140.8 0.1 copy.15
  140.9 0.1 copy.16
  141.0 0.1 copy.18
  141.1 0.1 eq.43
  141.2 0.1 stack.114.refs_0_
  141.3 23.8 %all-to-all-done = bf16[8,40,768]{2,1,0:T(8,128)(2,1)S(1)} async-done(((bf16[8,40,768]{2,1,0:T(8,128)(2,1)}), bf16[8,40,768]{2,1,0:T(8,128)(2,1)S(1)}, u32[]{:S(2)}, u32[]{:S(2)}) %all-to-all-start) | async-done | bytes 491552 | tf_op jit(solution)/shard_map/all_to_all | solution.py:106
  165.2 1.9 %shard_map.40 = bf16[128,3072]{1,0:T(8,128)(2,1)} custom-call(s32[24]{0:T(128)S(1)} %stack.114.refs_0_, bf16[128,80]{1,0:T(8,128)(2,1)S(1)} %and_convert_fusion.refs_1_, bf16[4,80,768]{2,1,0:T(8,128)(2,1)S(1)} %bitcast.33), custom_call_target="tpu_custom_call" | custom-call | tf_op jit(solution)/shard_map/pallas_call | solution.py:155
  (32 shorter events, 0.2 us)
Async XLA Ops:
  0.0 21.6 %collective-permute-start.1 = (bf16[8,80,1024]{2,1,0:T(8,128)(2,1)}, bf16[8,80,1024]{2,1,0:T(8,128)(2,1)S(1)}, u32[]{:S(2)}, u32[]{:S(2)}) collective-permute-start(bf16[8,80,1024]{2,1,0:T(8,128)(2,1)} %bitcast.34), channel_id=1, source_target_pairs={{0,16},{16,0},{1,17},{17,1},{2,18},{18,2},{3,19},{19,3},{4,20},{20... | collective-permute-start | bytes 3932168 | tf_op jit(solution)/shard_map/ppermute | solution.py:131
  2.6 37.0 %collective-permute-start.2 = (bf16[8,80,1024]{2,1,0:T(8,128)(2,1)}, bf16[8,80,1024]{2,1,0:T(8,128)(2,1)S(1)}, u32[]{:S(2)}, u32[]{:S(2)}) collective-permute-start(bf16[8,80,1024]{2,1,0:T(8,128)(2,1)} %bitcast.35), channel_id=1, source_target_pairs={{0,192},{192,0},{1,193},{193,1},{2,194},{194,2},{3,195},{195,3},{4... | collective-permute-start | bytes 3932168 | tf_op jit(solution)/shard_map/ppermute | solution.py:130
  5.7 15.0 %collective-permute-start = (bf16[64,1024]{1,0:T(8,128)(2,1)}, bf16[64,1024]{1,0:T(8,128)(2,1)S(1)}, u32[]{:S(2)}, u32[]{:S(2)}) collective-permute-start(bf16[64,1024]{1,0:T(8,128)(2,1)} %bitcast.40), channel_id=1, source_target_pairs={{0,96},{96,0},{1,97},{97,1},{2,98},{98,2},{3,99},{99,3},{4,100},{1... | collective-permute-start | bytes 393224 | tf_op jit(solution)/shard_map/ppermute | solution.py:22
  21.6 34.4 %copy-start.2 = (bf16[2,64,1024]{2,1,0:T(8,128)(2,1)}, bf16[2,64,1024]{2,1,0:T(8,128)(2,1)S(1)}, u32[]{:S(2)}) copy-start(bf16[2,64,1024]{2,1,0:T(8,128)(2,1)S(1)} %pad_maximum_fusion.2.refs_4_) | copy-start | bytes 786436
  21.6 34.4 %copy-start = (bf16[8,80,1024]{2,1,0:T(8,128)(2,1)}, bf16[8,80,1024]{2,1,0:T(8,128)(2,1)S(1)}, u32[]{:S(2)}) copy-start(bf16[8,80,1024]{2,1,0:T(8,128)(2,1)S(1)} %collective-permute-done.1.refs_1_) | copy-start | bytes 3932164
  21.6 10.0 %collective-permute-start.3 = (bf16[2,64,1024]{2,1,0:T(8,128)(2,1)S(1)}, bf16[2,64,1024]{2,1,0:T(8,128)(2,1)S(1)}, u32[]{:S(2)}, u32[]{:S(2)}) collective-permute-start(bf16[2,64,1024]{2,1,0:T(8,128)(2,1)S(1)} %pad_maximum_fusion.2.refs_4_), channel_id=1, source_target_pairs={{0,32},{32,64},{64,0},{1,33},{33,65},{65,1},{2,34},{34,66},{66,2},... | collective-permute-start | bytes 786440 | tf_op jit(solution)/shard_map/ppermute | solution.py:23
  23.6 12.3 %collective-permute-start.4 = (bf16[2,64,1024]{2,1,0:T(8,128)(2,1)S(1)}, bf16[2,64,1024]{2,1,0:T(8,128)(2,1)S(1)}, u32[]{:S(2)}, u32[]{:S(2)}) collective-permute-start(bf16[2,64,1024]{2,1,0:T(8,128)(2,1)S(1)} %pad_maximum_fusion.2.refs_4_), channel_id=1, source_target_pairs={{0,64},{32,0},{64,32},{1,65},{33,1},{65,33},{2,66},{34,2},{66,34},... | collective-permute-start | bytes 786440 | tf_op jit(solution)/shard_map/ppermute | solution.py:23
  26.9 12.7 %collective-permute-start.5 = (bf16[2,64,1024]{2,1,0:T(8,128)(2,1)S(1)}, bf16[2,64,1024]{2,1,0:T(8,128)(2,1)S(1)}, u32[]{:S(2)}, u32[]{:S(2)}) collective-permute-start(bf16[2,64,1024]{2,1,0:T(8,128)(2,1)S(1)} %pad_maximum_fusion.2.refs_4_), channel_id=1, source_target_pairs={{0,576},{192,384},{384,192},{576,0},{1,577},{193,385},{385,193},{5... | collective-permute-start | bytes 786440 | tf_op jit(solution)/shard_map/ppermute | solution.py:21
  31.7 24.4 %copy-start.3 = (bf16[2,64,1024]{2,1,0:T(8,128)(2,1)}, bf16[2,64,1024]{2,1,0:T(8,128)(2,1)S(1)}, u32[]{:S(2)}) copy-start(bf16[2,64,1024]{2,1,0:T(8,128)(2,1)S(1)} %collective-permute-done.3.refs_5_) | copy-start | bytes 786436
  31.7 9.2 %collective-permute-start.6 = (bf16[2,64,1024]{2,1,0:T(8,128)(2,1)S(1)}, bf16[2,64,1024]{2,1,0:T(8,128)(2,1)S(1)}, u32[]{:S(2)}, u32[]{:S(2)}) collective-permute-start(bf16[2,64,1024]{2,1,0:T(8,128)(2,1)S(1)} %collective-permute-done.3.refs_5_), channel_id=1, source_target_pairs={{0,576},{192,384},{384,192},{576,0},{1,577},{193,385},{385,193},{5... | collective-permute-start | bytes 786440 | tf_op jit(solution)/shard_map/ppermute | solution.py:21
  35.9 5.0 %copy-start.4 = (bf16[2,64,1024]{2,1,0:T(8,128)(2,1)}, bf16[2,64,1024]{2,1,0:T(8,128)(2,1)S(1)}, u32[]{:S(2)}) copy-start(bf16[2,64,1024]{2,1,0:T(8,128)(2,1)S(1)} %collective-permute-done.4.refs_6_) | copy-start | bytes 786436
  35.9 8.9 %collective-permute-start.7 = (bf16[2,64,1024]{2,1,0:T(8,128)(2,1)S(1)}, bf16[2,64,1024]{2,1,0:T(8,128)(2,1)S(1)}, u32[]{:S(2)}, u32[]{:S(2)}) collective-permute-start(bf16[2,64,1024]{2,1,0:T(8,128)(2,1)S(1)} %collective-permute-done.4.refs_6_), channel_id=1, source_target_pairs={{0,576},{192,384},{384,192},{576,0},{1,577},{193,385},{385,193},{5... | collective-permute-start | bytes 786440 | tf_op jit(solution)/shard_map/ppermute | solution.py:21
  39.6 16.5 %copy-start.1 = (bf16[8,80,1024]{2,1,0:T(8,128)(2,1)}, bf16[8,80,1024]{2,1,0:T(8,128)(2,1)S(1)}, u32[]{:S(2)}) copy-start(bf16[8,80,1024]{2,1,0:T(8,128)(2,1)S(1)} %collective-permute-done.2.refs_2_) | copy-start | bytes 3932164
  39.6 5.1 %copy-start.5 = (bf16[2,64,1024]{2,1,0:T(8,128)(2,1)}, bf16[2,64,1024]{2,1,0:T(8,128)(2,1)S(1)}, u32[]{:S(2)}) copy-start(bf16[2,64,1024]{2,1,0:T(8,128)(2,1)S(1)} %collective-permute-done.5.refs_7_) | copy-start | bytes 786436
  40.9 12.4 %copy-start.6 = (bf16[2,64,1024]{2,1,0:T(8,128)(2,1)}, bf16[2,64,1024]{2,1,0:T(8,128)(2,1)S(1)}, u32[]{:S(2)}) copy-start(bf16[2,64,1024]{2,1,0:T(8,128)(2,1)S(1)} %collective-permute-done.6.refs_8_) | copy-start | bytes 786436
  44.7 8.6 %copy-start.7 = (bf16[2,64,1024]{2,1,0:T(8,128)(2,1)}, bf16[2,64,1024]{2,1,0:T(8,128)(2,1)S(1)}, u32[]{:S(2)}) copy-start(bf16[2,64,1024]{2,1,0:T(8,128)(2,1)S(1)} %collective-permute-done.7.refs_9_) | copy-start | bytes 786436
  44.7 11.3 %collective-permute-start.8 = (bf16[8,80,1024]{2,1,0:T(8,128)(2,1)S(1)}, bf16[8,80,1024]{2,1,0:T(8,128)(2,1)}, u32[]{:S(2)}, u32[]{:S(2)}) collective-permute-start(bf16[8,80,1024]{2,1,0:T(8,128)(2,1)S(1)} %collective-permute-done.2.refs_2_), channel_id=1, source_target_pairs={{0,16},{16,0},{1,17},{17,1},{2,18},{18,2},{3,19},{19,3},{4,20},{20... | collective-permute-start | bytes 3932168 | tf_op jit(solution)/shard_map/ppermute | solution.py:133
  60.9 13.3 %collective-permute-start.9 = (bf16[160,768]{1,0:T(8,128)(2,1)S(1)}, bf16[160,768]{1,0:T(8,128)(2,1)S(1)}, u32[]{:S(2)}, u32[]{:S(2)}) collective-permute-start(bf16[160,768]{1,0:T(8,128)(2,1)S(1)} %get-tuple-element.25), channel_id=1, source_target_pairs={{0,1},{1,2},{2,3},{3,4},{4,5},{5,6},{6,7},{7,0},{8,9},{9,10},{10,1... | collective-permute-start | bytes 737288 | tf_op jit(solution)/shard_map/ppermute | solution.py:88
  70.3 11.0 %copy-start.11 = (bf16[320,768]{1,0:T(8,128)(2,1)S(1)}, bf16[320,768]{1,0:T(8,128)(2,1)}, u32[]{:S(2)}) copy-start(bf16[320,768]{1,0:T(8,128)(2,1)} %get-tuple-element.24) | copy-start | bytes 1474564
  71.3 9.9 %collective-permute-start.13 = (bf16[160,768]{1,0:T(8,128)(2,1)S(1)}, bf16[160,768]{1,0:T(8,128)(2,1)S(1)}, u32[]{:S(2)}, u32[]{:S(2)}) collective-permute-start(bf16[160,768]{1,0:T(8,128)(2,1)S(1)} %get-tuple-element.26), channel_id=1, source_target_pairs={{0,7},{1,0},{2,1},{3,2},{4,3},{5,4},{6,5},{7,6},{8,15},{9,8},{10,9... | collective-permute-start | bytes 737288 | tf_op jit(solution)/shard_map/ppermute | solution.py:89
  75.2 16.6 %collective-permute-start.10 = (bf16[320,768]{1,0:T(8,128)(2,1)S(1)}, bf16[320,768]{1,0:T(8,128)(2,1)S(1)}, u32[]{:S(2)}, u32[]{:S(2)}) collective-permute-start(bf16[320,768]{1,0:T(8,128)(2,1)S(1)} %pad_maximum_fusion), channel_id=1, source_target_pairs={{0,1},{1,2},{2,3},{3,4},{4,5},{5,6},{6,7},{7,0},{8,9},{9,10},{10,1... | collective-permute-start | bytes 1474568 | tf_op jit(solution)/shard_map/ppermute | solution.py:96
  81.3 16.3 %collective-permute-start.14 = (bf16[320,768]{1,0:T(8,128)(2,1)S(1)}, bf16[320,768]{1,0:T(8,128)(2,1)S(1)}, u32[]{:S(2)}, u32[]{:S(2)}) collective-permute-start(bf16[320,768]{1,0:T(8,128)(2,1)S(1)} %pad_maximum_fusion.1), channel_id=1, source_target_pairs={{0,7},{1,0},{2,1},{3,2},{4,3},{5,4},{6,5},{7,6},{8,15},{9,8},{10,9... | collective-permute-start | bytes 1474568 | tf_op jit(solution)/shard_map/ppermute | solution.py:97
  91.8 5.8 %copy-start.10 = (bf16[320,768]{1,0:T(8,128)(2,1)S(1)}, bf16[320,768]{1,0:T(8,128)(2,1)}, u32[]{:S(2)}) copy-start(bf16[320,768]{1,0:T(8,128)(2,1)} %get-tuple-element.23) | copy-start | bytes 1474564
  91.8 14.5 %copy-start.9 = (bf16[320,768]{1,0:T(8,128)(2,1)S(1)}, bf16[320,768]{1,0:T(8,128)(2,1)}, u32[]{:S(2)}) copy-start(bf16[320,768]{1,0:T(8,128)(2,1)} %get-tuple-element.19) | copy-start | bytes 1474564
  93.1 13.3 %collective-permute-start.11 = (bf16[320,768]{1,0:T(8,128)(2,1)S(1)}, bf16[320,768]{1,0:T(8,128)(2,1)S(1)}, u32[]{:S(2)}, u32[]{:S(2)}) collective-permute-start(bf16[320,768]{1,0:T(8,128)(2,1)S(1)} %add_convert_fusion.4), channel_id=1, source_target_pairs={{0,1},{1,2},{2,3},{3,4},{4,5},{5,6},{6,7},{7,0},{8,9},{9,10},{10,1... | collective-permute-start | bytes 1474568 | tf_op jit(solution)/shard_map/ppermute | solution.py:96
  97.7 14.2 %copy-start.8 = (bf16[320,768]{1,0:T(8,128)(2,1)S(1)}, bf16[320,768]{1,0:T(8,128)(2,1)}, u32[]{:S(2)}) copy-start(bf16[320,768]{1,0:T(8,128)(2,1)} %get-tuple-element.22) | copy-start | bytes 1474564
  97.8 14.1 %collective-permute-start.15 = (bf16[320,768]{1,0:T(8,128)(2,1)S(1)}, bf16[320,768]{1,0:T(8,128)(2,1)S(1)}, u32[]{:S(2)}, u32[]{:S(2)}) collective-permute-start(bf16[320,768]{1,0:T(8,128)(2,1)S(1)} %add_convert_fusion.2), channel_id=1, source_target_pairs={{0,7},{1,0},{2,1},{3,2},{4,3},{5,4},{6,5},{7,6},{8,15},{9,8},{10,9... | collective-permute-start | bytes 1474568 | tf_op jit(solution)/shard_map/ppermute | solution.py:97
  106.3 18.5 %copy-start.12 = (bf16[320,768]{1,0:T(8,128)(2,1)S(1)}, bf16[320,768]{1,0:T(8,128)(2,1)}, u32[]{:S(2)}) copy-start(bf16[320,768]{1,0:T(8,128)(2,1)} %get-tuple-element.18) | copy-start | bytes 1474564
  106.5 13.2 %collective-permute-start.12 = (bf16[320,768]{1,0:T(8,128)(2,1)S(1)}, bf16[320,768]{1,0:T(8,128)(2,1)S(1)}, u32[]{:S(2)}, u32[]{:S(2)}) collective-permute-start(bf16[320,768]{1,0:T(8,128)(2,1)S(1)} %add_convert_fusion.3), channel_id=1, source_target_pairs={{0,1},{1,2},{2,3},{3,4},{4,5},{5,6},{6,7},{7,0},{8,9},{9,10},{10,1... | collective-permute-start | bytes 1474568 | tf_op jit(solution)/shard_map/ppermute | solution.py:96
  112.1 12.8 %collective-permute-start.16 = (bf16[320,768]{1,0:T(8,128)(2,1)S(1)}, bf16[320,768]{1,0:T(8,128)(2,1)S(1)}, u32[]{:S(2)}, u32[]{:S(2)}) collective-permute-start(bf16[320,768]{1,0:T(8,128)(2,1)S(1)} %add_convert_fusion.1), channel_id=1, source_target_pairs={{0,7},{1,0},{2,1},{3,2},{4,3},{5,4},{6,5},{7,6},{8,15},{9,8},{10,9... | collective-permute-start | bytes 1474568 | tf_op jit(solution)/shard_map/ppermute | solution.py:97
  124.9 15.6 %copy-start.13 = (s32[128,2]{0,1:T(2,128)S(1)}, s32[128,2]{0,1:T(2,128)}, u32[]{:S(2)}) copy-start(s32[128,2]{0,1:T(2,128)} %param.3) | copy-start | bytes 3076
  125.8 39.3 %all-to-all-start = ((bf16[8,40,768]{2,1,0:T(8,128)(2,1)}), bf16[8,40,768]{2,1,0:T(8,128)(2,1)S(1)}, u32[]{:S(2)}, u32[]{:S(2)}) async-start(bf16[8,40,768]{2,1,0:T(8,128)(2,1)} %bitcast.31), calls=%async_computation | async-start | bytes 983040 | tf_op jit(solution)/shard_map/all_to_all | solution.py:106

commit v10 on v8

--- a/solution.py
+++ b/solution.py
@@ -35,7 +35,7 @@
     return jnp.stack([x * SIZES["h"] * count + z for x in xs for z in zs]).astype(jnp.int32)
 
 
-def product_kernel(where, *refs, pieces, outs):
+def product_kernel(here, place, *refs, pieces, outs):
     rows, hidden = refs[0].shape[1:]
     flat = jnp.concatenate([piece[0] for piece in refs[:pieces]])
     weights = jnp.concatenate([block[...].reshape(-1, hidden) for block in refs[pieces:-outs]])
@@ -47,7 +47,7 @@
         @pl.when(pl.program_id(0) == i)
         def _():
             for k in range(pieces):
-                start = pl.multiple_of((where[1] ^ k) * rows, rows)
+                start = pl.multiple_of((place[0] ^ k) * rows, rows)
                 out[pl.ds(start, rows), :] = result[k * rows:(k + 1) * rows]
 
 
@@ -58,22 +58,22 @@
     flops = 2 * count * rows_out * hidden * features
     moved = 2 * (count * rows_out * (hidden + features) + features * hidden)
 
-    def source(i, where):
-        return ((where[0] + first + i * stride) % tensor_count, 0, 0)
+    def source(i, here, place):
+        return ((here[0] + first + i * stride) % tensor_count, 0, 0)
 
     return pl.pallas_call(
         functools.partial(product_kernel, pieces=len(pieces), outs=count),
         grid_spec=pltpu.PrefetchScalarGridSpec(
-            num_scalar_prefetch=1,
+            num_scalar_prefetch=2,
             grid=(count,),
             in_specs=[pl.BlockSpec((1, rows, hidden), source)] * len(pieces)
-            + [pl.BlockSpec(block.shape, lambda i, where: (0, 0, 0)) for block in blocks],
-            out_specs=[pl.BlockSpec((rows_out, features), lambda i, where: (0, 0))] * count,
+            + [pl.BlockSpec(block.shape, lambda i, here, place: (0, 0, 0)) for block in blocks],
+            out_specs=[pl.BlockSpec((rows_out, features), lambda i, here, place: (0, 0))] * count,
         ),
         out_shape=[jax.ShapeDtypeStruct((rows_out, features), jnp.bfloat16)] * count,
         cost_estimate=pl.CostEstimate(flops=flops, bytes_accessed=moved, transcendentals=0),
-        compiler_params=pltpu.CompilerParams(vmem_limit_bytes=20 * 1024 * 1024),
-    )(where, *pieces, *blocks)
+        compiler_params=pltpu.CompilerParams(vmem_limit_bytes=14 * 1024 * 1024),
+    )(*where, *pieces, *blocks)
 
 
 def sum_by_arms(partial, n):
@@ -90,8 +90,7 @@
     above, below = partial(mid - 1, 2, 2)
     going_up = jnp.concatenate([narrow(wide(above[:half]) + wide(first)), above[half:]])
     going_down = jnp.concatenate([below[:half], narrow(wide(below[half:]) + wide(last))])
-    others = partial(mid + 2, 1, n - 3)
-    lowers, uppers = others[:mid - 1], others[:mid - 2:-1]
+    uppers, lowers = partial(mid - 2, -1, mid - 2), partial(mid + 2, 1, mid - 1)
     for step in range(1, mid):
         from_below = lax.ppermute(going_up, "t", up)
         from_above = lax.ppermute(going_down, "t", down)
@@ -127,14 +126,14 @@
     rows = owners * capacity
 
     own = upgrad.reshape(tensor_count, rows, hidden)
-    column, other = gather_columns(slab)
     x_rows = lax.ppermute(own, "xp", SWAP)
     c_rows = lax.ppermute(own, "c", SWAP)
-    x_rows, *_ = lax.optimization_barrier((x_rows, *column, *other[:2]))
+    column, other = gather_columns(slab)
+    x_rows, *_ = lax.optimization_barrier((x_rows, *column, *other))
     pieces = (own, c_rows, x_rows, lax.ppermute(x_rows, "c", SWAP))
 
     places = [lax.axis_index("t"), lax.axis_index("xp") * SIZES["c"] + lax.axis_index("c")]
-    where = jnp.stack(places).astype(jnp.int32)
+    where = [place.astype(jnp.int32).reshape(1) for place in places]
     blocks = (*column, *other)
     summed = sum_by_arms(
         lambda k, stride, count: product(where, pieces, blocks, k, stride, count), tensor_count

time: 162 us -> 159 us (0.981)
  the two profiles are of different devices: /device:TPU:153 before, /device:TPU:1 now
where the time goes in v10:
time: 159 us; the launch traced here: 157 us
  starting transfers between devices  89 us (56%)
  waiting for transfers between devices  46 us (29%)
  Pallas kernels  11.9 us (7%)
  local copies, waits for them, and re-layouts  6.94 us (4%)
  other arithmetic  2.77 us (2%)
    all_to_all x1, starting transfers between devices, give_back(): lax.all_to_all(summed.reshape(-1, capacity, features), ('xp', 'c', 'e'),...  18.9 us
    all_to_all x1, waiting for transfers between devices, give_back(): lax.all_to_all(summed.reshape(-1, capacity, features), ('xp', 'c', 'e'),...  17.4 us
    ppermute x3, starting transfers between devices, sum_by_arms(): from_above = lax.ppermute(going_down, 't', down)  16 us
    ppermute x3, starting transfers between devices, gather_columns(): opposite = lambda value: lax.ppermute(value, ('xh', 'xp'), WEIGHT_SWAP)  10.5 us
    ppermute x3, waiting for transfers between devices, sum_by_arms(): from_below = lax.ppermute(going_up, 't', up)  10.2 us
    pallas_call x4, Pallas kernels, product(): pl.pallas_call(functools.partial(product_kernel, pieces=len(pieces), outs...  10 us
    ppermute x1, starting transfers between devices, gather_columns(): pair = jnp.stack([slab, lax.ppermute(slab, 'h', SWAP)])  7.62 us
    ppermute x1, starting transfers between devices, gather_columns(): lax.ppermute(pair, 'm', turn(1))  6.71 us
  transfers between devices with their start and end apart: 18, of which 12 were waited for; matrix products, arithmetic and copies ran while one was open for 2% of the time, Pallas kernels for 5%

profile of v10, /device:TPU:1, one launch (start us, length us, event | category | flops | bytes accessed | tf_op | source)
XLA Modules:
  0.0 156.9 jit_solution(16320988398771631665)
XLA Ops:
  0.0 3.9 %collective-permute-start.1 = (bf16[8,80,1024]{2,1,0:T(8,128)(2,1)}, bf16[8,80,1024]{2,1,0:T(8,128)(2,1)S(1)}, u32[]{:S(2)}, u32[]{:S(2)}) collective-permute-start(bf16[8,80,1024]{2,1,0:T(8,128)(2,1)} %bitcast.33), channel_id=1, source_target_pairs={{0,192},{192,0},{1,193},{193,1},{2,194},{194,2},{3,195},{195,3},{4... | collective-permute-start | bytes 3932168 | tf_op jit(solution)/shard_map/ppermute | solution.py:129
  3.9 7.6 %collective-permute-start.2 = (bf16[64,1024]{1,0:T(8,128)(2,1)}, bf16[64,1024]{1,0:T(8,128)(2,1)S(1)}, u32[]{:S(2)}, u32[]{:S(2)}) collective-permute-start(bf16[64,1024]{1,0:T(8,128)(2,1)} %bitcast.41), channel_id=1, source_target_pairs={{0,96},{96,0},{1,97},{97,1},{2,98},{98,2},{3,99},{99,3},{4,100},{1... | collective-permute-start | bytes 393224 | tf_op jit(solution)/shard_map/ppermute | solution.py:22
  11.6 2.6 %collective-permute-done.2 = bf16[64,1024]{1,0:T(8,128)(2,1)S(1)} collective-permute-done((bf16[64,1024]{1,0:T(8,128)(2,1)}, bf16[64,1024]{1,0:T(8,128)(2,1)S(1)}, u32[]{:S(2)}, u32[]{:S(2)}) %collective-permute-start.2) | collective-permute-done | bytes 131104 | tf_op jit(solution)/shard_map/ppermute | solution.py:22
  14.1 0.9 pad_maximum_fusion.2.refs_4_
  15.1 6.7 %collective-permute-start.3 = (bf16[2,64,1024]{2,1,0:T(8,128)(2,1)S(1)}, bf16[2,64,1024]{2,1,0:T(8,128)(2,1)S(1)}, u32[]{:S(2)}, u32[]{:S(2)}) collective-permute-start(bf16[2,64,1024]{2,1,0:T(8,128)(2,1)S(1)} %pad_maximum_fusion.2.refs_4_), channel_id=1, source_target_pairs={{0,32},{32,64},{64,0},{1,33},{33,65},{65,1},{2,34},{34,66},{66,2},... | collective-permute-start | bytes 786440 | tf_op jit(solution)/shard_map/ppermute | solution.py:23
  21.8 6.5 %collective-permute-start.4 = (bf16[2,64,1024]{2,1,0:T(8,128)(2,1)S(1)}, bf16[2,64,1024]{2,1,0:T(8,128)(2,1)S(1)}, u32[]{:S(2)}, u32[]{:S(2)}) collective-permute-start(bf16[2,64,1024]{2,1,0:T(8,128)(2,1)S(1)} %pad_maximum_fusion.2.refs_4_), channel_id=1, source_target_pairs={{0,64},{32,0},{64,32},{1,65},{33,1},{65,33},{2,66},{34,2},{66,34},... | collective-permute-start | bytes 786440 | tf_op jit(solution)/shard_map/ppermute | solution.py:23
  28.3 3.0 %collective-permute-start.5 = (bf16[2,64,1024]{2,1,0:T(8,128)(2,1)S(1)}, bf16[2,64,1024]{2,1,0:T(8,128)(2,1)S(1)}, u32[]{:S(2)}, u32[]{:S(2)}) collective-permute-start(bf16[2,64,1024]{2,1,0:T(8,128)(2,1)S(1)} %pad_maximum_fusion.2.refs_4_), channel_id=1, source_target_pairs={{0,576},{192,384},{384,192},{576,0},{1,577},{193,385},{385,193},{5... | collective-permute-start | bytes 786440 | tf_op jit(solution)/shard_map/ppermute | solution.py:21
  31.3 0.0 collective-permute-done.3.refs_5_
  31.3 4.3 %collective-permute-start.6 = (bf16[2,64,1024]{2,1,0:T(8,128)(2,1)S(1)}, bf16[2,64,1024]{2,1,0:T(8,128)(2,1)S(1)}, u32[]{:S(2)}, u32[]{:S(2)}) collective-permute-start(bf16[2,64,1024]{2,1,0:T(8,128)(2,1)S(1)} %collective-permute-done.3.refs_5_), channel_id=1, source_target_pairs={{0,576},{192,384},{384,192},{576,0},{1,577},{193,385},{385,193},{5... | collective-permute-start | bytes 786440 | tf_op jit(solution)/shard_map/ppermute | solution.py:21
  35.6 2.9 %collective-permute-done.4.refs_6_ = bf16[2,64,1024]{2,1,0:T(8,128)(2,1)S(1)} collective-permute-done((bf16[2,64,1024]{2,1,0:T(8,128)(2,1)S(1)}, bf16[2,64,1024]{2,1,0:T(8,128)(2,1)S(1)}, u32[]{:S(2)}, u32[]{:S(2)}) %collective-permute-start.4) | collective-permute-done | bytes 262176 | tf_op jit(solution)/shard_map/ppermute | solution.py:23
  38.6 3.2 %collective-permute-start.7 = (bf16[2,64,1024]{2,1,0:T(8,128)(2,1)S(1)}, bf16[2,64,1024]{2,1,0:T(8,128)(2,1)S(1)}, u32[]{:S(2)}, u32[]{:S(2)}) collective-permute-start(bf16[2,64,1024]{2,1,0:T(8,128)(2,1)S(1)} %collective-permute-done.4.refs_6_), channel_id=1, source_target_pairs={{0,576},{192,384},{384,192},{576,0},{1,577},{193,385},{385,193},{5... | collective-permute-start | bytes 786440 | tf_op jit(solution)/shard_map/ppermute | solution.py:21
  41.7 3.1 %collective-permute-start = (bf16[8,80,1024]{2,1,0:T(8,128)(2,1)}, bf16[8,80,1024]{2,1,0:T(8,128)(2,1)S(1)}, u32[]{:S(2)}, u32[]{:S(2)}) collective-permute-start(bf16[8,80,1024]{2,1,0:T(8,128)(2,1)} %bitcast.34), channel_id=1, source_target_pairs={{0,16},{16,0},{1,17},{17,1},{2,18},{18,2},{3,19},{19,3},{4,20},{20... | collective-permute-start | bytes 3932168 | tf_op jit(solution)/shard_map/ppermute | solution.py:130
  44.9 0.0 collective-permute-done.5.refs_7_
  44.9 0.0 copy-start.1
  44.9 0.7 copy-done.1
  45.6 0.0 collective-permute-done.6.refs_8_
  45.6 0.7 copy-done.3
  46.3 3.8 %collective-permute-done.7.refs_9_ = bf16[2,64,1024]{2,1,0:T(8,128)(2,1)S(1)} collective-permute-done((bf16[2,64,1024]{2,1,0:T(8,128)(2,1)S(1)}, bf16[2,64,1024]{2,1,0:T(8,128)(2,1)S(1)}, u32[]{:S(2)}, u32[]{:S(2)}) %collective-permute-start.7) | collective-permute-done | bytes 262176 | tf_op jit(solution)/shard_map/ppermute | solution.py:21
  50.1 0.7 copy-done.5
  50.8 0.0 collective-permute-done.1.refs_2_
  50.8 3.4 %collective-permute-start.8 = (bf16[8,80,1024]{2,1,0:T(8,128)(2,1)S(1)}, bf16[8,80,1024]{2,1,0:T(8,128)(2,1)}, u32[]{:S(2)}, u32[]{:S(2)}) collective-permute-start(bf16[8,80,1024]{2,1,0:T(8,128)(2,1)S(1)} %collective-permute-done.1.refs_2_), channel_id=1, source_target_pairs={{0,16},{16,0},{1,17},{17,1},{2,18},{18,2},{3,19},{19,3},{4,20},{20... | collective-permute-start | bytes 3932168 | tf_op jit(solution)/shard_map/ppermute | solution.py:133
  54.2 0.0 collective-permute-done.refs_1_
  54.2 2.8 %collective-permute-done.8.refs_3_ = bf16[8,80,1024]{2,1,0:T(8,128)(2,1)} collective-permute-done((bf16[8,80,1024]{2,1,0:T(8,128)(2,1)S(1)}, bf16[8,80,1024]{2,1,0:T(8,128)(2,1)}, u32[]{:S(2)}, u32[]{:S(2)}) %collective-permute-start.8) | collective-permute-done | bytes 1310752 | tf_op jit(solution)/shard_map/ppermute | solution.py:133
  57.0 1.3 copy-done
  58.3 0.9 copy-done.2
  59.2 0.9 copy-done.4
  60.2 0.9 copy-done.6
  61.1 1.6 %shard_map.40 = bf16[320,768]{1,0:T(8,128)(2,1)S(1)} custom-call(s32[1]{0:T(128)} %bitcast.26.here, s32[1]{0:T(128)} %bitcast.27.place, bf16[8,80,1024]{2,1,0:T(8,128)(2,1)S(1)} %bitcast.35, bf16[8,80,1024]{2,1,0:T(8,128)(2,1)S(1)} %collective-permute-done.refs_1_, bf16[8,80,1024]{2,1,0:T(8,128)(2,1)S(1)} %collective-permute-done.1.refs_2_, ...), custom_call_target="tpu_custom_call" | custom-call | flops 503316480 | bytes 2719744 | tf_op jit(solution)/shard_map/pallas_call | solution.py:64
  62.8 2.3 %collective-permute-start.9 = (bf16[160,768]{1,0:T(8,128)(2,1)S(1)}, bf16[160,768]{1,0:T(8,128)(2,1)S(1)}, u32[]{:S(2)}, u32[]{:S(2)}) collective-permute-start(bf16[160,768]{1,0:T(8,128)(2,1)S(1)} %get-tuple-element.21), channel_id=1, source_target_pairs={{0,1},{1,2},{2,3},{3,4},{4,5},{5,6},{6,7},{7,0},{8,9},{9,10},{10,1... | collective-permute-start | bytes 737288 | tf_op jit(solution)/shard_map/ppermute | solution.py:88
  65.1 2.5 %shard_map.39 = (bf16[320,768]{1,0:T(8,128)(2,1)S(1)}, bf16[320,768]{1,0:T(8,128)(2,1)S(1)}) custom-call(s32[1]{0:T(128)} %bitcast.26.here, s32[1]{0:T(128)} %bitcast.27.place, bf16[8,80,1024]{2,1,0:T(8,128)(2,1)S(1)} %bitcast.36, bf16[8,80,1024]{2,1,0:T(8,128)(2,1)S(1)} %collective-permute-done.refs_1_, ...), custom_call_target="tpu_custom_call" | custom-call | flops 1006632960 | bytes 3866624 | tf_op jit(solution)/shard_map/pallas_call | solution.py:64
  67.6 4.2 %collective-permute-start.13 = (bf16[160,768]{1,0:T(8,128)(2,1)S(1)}, bf16[160,768]{1,0:T(8,128)(2,1)S(1)}, u32[]{:S(2)}, u32[]{:S(2)}) collective-permute-start(bf16[160,768]{1,0:T(8,128)(2,1)S(1)} %get-tuple-element.22), channel_id=1, source_target_pairs={{0,7},{1,0},{2,1},{3,2},{4,3},{5,4},{6,5},{7,6},{8,15},{9,8},{10,9... | collective-permute-start | bytes 737288 | tf_op jit(solution)/shard_map/ppermute | solution.py:89
  71.9 1.2 collective-permute-done.9
  73.1 0.1 add_convert_fusion.6
  73.2 1.9 %collective-permute-start.10 = (bf16[320,768]{1,0:T(8,128)(2,1)S(1)}, bf16[320,768]{1,0:T(8,128)(2,1)S(1)}, u32[]{:S(2)}, u32[]{:S(2)}) collective-permute-start(bf16[320,768]{1,0:T(8,128)(2,1)S(1)} %pad_maximum_fusion), channel_id=1, source_target_pairs={{0,1},{1,2},{2,3},{3,4},{4,5},{5,6},{6,7},{7,0},{8,9},{9,10},{10,1... | collective-permute-start | bytes 1474568 | tf_op jit(solution)/shard_map/ppermute | solution.py:95
  75.1 1.4 collective-permute-done.13
  76.5 0.1 add_convert_fusion.5
  76.6 5.3 %collective-permute-start.14 = (bf16[320,768]{1,0:T(8,128)(2,1)S(1)}, bf16[320,768]{1,0:T(8,128)(2,1)S(1)}, u32[]{:S(2)}, u32[]{:S(2)}) collective-permute-start(bf16[320,768]{1,0:T(8,128)(2,1)S(1)} %pad_maximum_fusion.1), channel_id=1, source_target_pairs={{0,7},{1,0},{2,1},{3,2},{4,3},{5,4},{6,5},{7,6},{8,15},{9,8},{10,9... | collective-permute-start | bytes 1474568 | tf_op jit(solution)/shard_map/ppermute | solution.py:96
  81.9 2.5 %shard_map.38 = (bf16[320,768]{1,0:T(8,128)(2,1)S(1)}, bf16[320,768]{1,0:T(8,128)(2,1)S(1)}) custom-call(s32[1]{0:T(128)} %bitcast.26.here, s32[1]{0:T(128)} %bitcast.27.place, bf16[8,80,1024]{2,1,0:T(8,128)(2,1)S(1)} %bitcast.37, bf16[8,80,1024]{2,1,0:T(8,128)(2,1)S(1)} %collective-permute-done.refs_1_, ...), custom_call_target="tpu_custom_call" | custom-call | flops 1006632960 | bytes 3866624 | tf_op jit(solution)/shard_map/pallas_call | solution.py:64
  84.4 3.4 %shard_map.37 = (bf16[320,768]{1,0:T(8,128)(2,1)S(1)}, bf16[320,768]{1,0:T(8,128)(2,1)S(1)}, bf16[320,768]{1,0:T(8,128)(2,1)S(1)}) custom-call(s32[1]{0:T(128)} %bitcast.26.here, s32[1]{0:T(128)} %bitcast.27.place, bf16[8,80,1024]{2,1,0:T(8,128)(2,1)S(1)} %bitcast.38, bf16[8,80,1024]{2,1,0:T(8,128)(2,1)S(1)} %collective-permute-done.refs_1_, ...), custom_call_target="tpu_custom_call" | custom-call | flops 1509949440 | bytes 5013504 | tf_op jit(solution)/shard_map/pallas_call | solution.py:64
  87.8 0.0 collective-permute-done.10
  87.8 0.1 add_convert_fusion.4
  87.9 1.9 %collective-permute-start.11 = (bf16[320,768]{1,0:T(8,128)(2,1)S(1)}, bf16[320,768]{1,0:T(8,128)(2,1)S(1)}, u32[]{:S(2)}, u32[]{:S(2)}) collective-permute-start(bf16[320,768]{1,0:T(8,128)(2,1)S(1)} %add_convert_fusion.4), channel_id=1, source_target_pairs={{0,1},{1,2},{2,3},{3,4},{4,5},{5,6},{6,7},{7,0},{8,9},{9,10},{10,1... | collective-permute-start | bytes 1474568 | tf_op jit(solution)/shard_map/ppermute | solution.py:95
  89.9 1.0 collective-permute-done.14
  90.8 0.1 add_convert_fusion.2
  91.0 5.3 %collective-permute-start.15 = (bf16[320,768]{1,0:T(8,128)(2,1)S(1)}, bf16[320,768]{1,0:T(8,128)(2,1)S(1)}, u32[]{:S(2)}, u32[]{:S(2)}) collective-permute-start(bf16[320,768]{1,0:T(8,128)(2,1)S(1)} %add_convert_fusion.2), channel_id=1, source_target_pairs={{0,7},{1,0},{2,1},{3,2},{4,3},{5,4},{6,5},{7,6},{8,15},{9,8},{10,9... | collective-permute-start | bytes 1474568 | tf_op jit(solution)/shard_map/ppermute | solution.py:96
  96.3 5.4 %collective-permute-done.11 = bf16[320,768]{1,0:T(8,128)(2,1)S(1)} collective-permute-done((bf16[320,768]{1,0:T(8,128)(2,1)S(1)}, bf16[320,768]{1,0:T(8,128)(2,1)S(1)}, u32[]{:S(2)}, u32[]{:S(2)}) %collective-permute-start.11) | collective-permute-done | bytes 491552 | tf_op jit(solution)/shard_map/ppermute | solution.py:95
  101.7 0.1 add_convert_fusion.3
  101.8 1.9 %collective-permute-start.12 = (bf16[320,768]{1,0:T(8,128)(2,1)S(1)}, bf16[320,768]{1,0:T(8,128)(2,1)S(1)}, u32[]{:S(2)}, u32[]{:S(2)}) collective-permute-start(bf16[320,768]{1,0:T(8,128)(2,1)S(1)} %add_convert_fusion.3), channel_id=1, source_target_pairs={{0,1},{1,2},{2,3},{3,4},{4,5},{5,6},{6,7},{7,0},{8,9},{9,10},{10,1... | collective-permute-start | bytes 1474568 | tf_op jit(solution)/shard_map/ppermute | solution.py:95
  103.7 0.6 collective-permute-done.15
  104.3 0.1 add_convert_fusion.1
  104.5 5.3 %collective-permute-start.16 = (bf16[320,768]{1,0:T(8,128)(2,1)S(1)}, bf16[320,768]{1,0:T(8,128)(2,1)S(1)}, u32[]{:S(2)}, u32[]{:S(2)}) collective-permute-start(bf16[320,768]{1,0:T(8,128)(2,1)S(1)} %add_convert_fusion.1), channel_id=1, source_target_pairs={{0,7},{1,0},{2,1},{3,2},{4,3},{5,4},{6,5},{7,6},{8,15},{9,8},{10,9... | collective-permute-start | bytes 1474568 | tf_op jit(solution)/shard_map/ppermute | solution.py:96
  109.8 4.8 %collective-permute-done.12 = bf16[320,768]{1,0:T(8,128)(2,1)S(1)} collective-permute-done((bf16[320,768]{1,0:T(8,128)(2,1)S(1)}, bf16[320,768]{1,0:T(8,128)(2,1)S(1)}, u32[]{:S(2)}, u32[]{:S(2)}) %collective-permute-start.12) | collective-permute-done | bytes 491552 | tf_op jit(solution)/shard_map/ppermute | solution.py:95
  114.6 2.3 %collective-permute-done.16 = bf16[320,768]{1,0:T(8,128)(2,1)S(1)} collective-permute-done((bf16[320,768]{1,0:T(8,128)(2,1)S(1)}, bf16[320,768]{1,0:T(8,128)(2,1)S(1)}, u32[]{:S(2)}, u32[]{:S(2)}) %collective-permute-start.16) | collective-permute-done | bytes 491552 | tf_op jit(solution)/shard_map/ppermute | solution.py:96
  116.9 1.0 add_convert_fusion
  117.9 18.9 %all-to-all-start = ((bf16[8,40,768]{2,1,0:T(8,128)(2,1)}), bf16[8,40,768]{2,1,0:T(8,128)(2,1)S(1)}, u32[]{:S(2)}, u32[]{:S(2)}) async-start(bf16[8,40,768]{2,1,0:T(8,128)(2,1)} %bitcast.31), calls=%async_computation | async-start | bytes 983040 | tf_op jit(solution)/shard_map/all_to_all | solution.py:105
  136.9 0.1 copy.14
  137.0 0.2 reduce_window_sum.11
  137.1 0.1 copy.15
  137.2 0.1 copy.16
  137.3 0.1 copy.18
  137.5 0.1 eq.43
  137.6 0.1 stack.105.refs_0_
  137.7 17.4 %all-to-all-done = bf16[8,40,768]{2,1,0:T(8,128)(2,1)S(1)} async-done(((bf16[8,40,768]{2,1,0:T(8,128)(2,1)}), bf16[8,40,768]{2,1,0:T(8,128)(2,1)S(1)}, u32[]{:S(2)}, u32[]{:S(2)}) %all-to-all-start) | async-done | bytes 491552 | tf_op jit(solution)/shard_map/all_to_all | solution.py:105
  155.1 1.9 %shard_map.41 = bf16[128,3072]{1,0:T(8,128)(2,1)} custom-call(s32[24]{0:T(128)S(1)} %stack.105.refs_0_, bf16[128,80]{1,0:T(8,128)(2,1)S(1)} %and_convert_fusion.refs_1_, bf16[4,80,768]{2,1,0:T(8,128)(2,1)S(1)} %bitcast.39), custom_call_target="tpu_custom_call" | custom-call | tf_op jit(solution)/shard_map/pallas_call | solution.py:155
  (20 shorter events, 0.2 us)
Async XLA Ops:
  0.0 50.8 %collective-permute-start.1 = (bf16[8,80,1024]{2,1,0:T(8,128)(2,1)}, bf16[8,80,1024]{2,1,0:T(8,128)(2,1)S(1)}, u32[]{:S(2)}, u32[]{:S(2)}) collective-permute-start(bf16[8,80,1024]{2,1,0:T(8,128)(2,1)} %bitcast.33), channel_id=1, source_target_pairs={{0,192},{192,0},{1,193},{193,1},{2,194},{194,2},{3,195},{195,3},{4... | collective-permute-start | bytes 3932168 | tf_op jit(solution)/shard_map/ppermute | solution.py:129
  3.9 10.2 %collective-permute-start.2 = (bf16[64,1024]{1,0:T(8,128)(2,1)}, bf16[64,1024]{1,0:T(8,128)(2,1)S(1)}, u32[]{:S(2)}, u32[]{:S(2)}) collective-permute-start(bf16[64,1024]{1,0:T(8,128)(2,1)} %bitcast.41), channel_id=1, source_target_pairs={{0,96},{96,0},{1,97},{97,1},{2,98},{98,2},{3,99},{99,3},{4,100},{1... | collective-permute-start | bytes 393224 | tf_op jit(solution)/shard_map/ppermute | solution.py:22
  15.1 16.2 %collective-permute-start.3 = (bf16[2,64,1024]{2,1,0:T(8,128)(2,1)S(1)}, bf16[2,64,1024]{2,1,0:T(8,128)(2,1)S(1)}, u32[]{:S(2)}, u32[]{:S(2)}) collective-permute-start(bf16[2,64,1024]{2,1,0:T(8,128)(2,1)S(1)} %pad_maximum_fusion.2.refs_4_), channel_id=1, source_target_pairs={{0,32},{32,64},{64,0},{1,33},{33,65},{65,1},{2,34},{34,66},{66,2},... | collective-permute-start | bytes 786440 | tf_op jit(solution)/shard_map/ppermute | solution.py:23
  21.8 16.8 %collective-permute-start.4 = (bf16[2,64,1024]{2,1,0:T(8,128)(2,1)S(1)}, bf16[2,64,1024]{2,1,0:T(8,128)(2,1)S(1)}, u32[]{:S(2)}, u32[]{:S(2)}) collective-permute-start(bf16[2,64,1024]{2,1,0:T(8,128)(2,1)S(1)} %pad_maximum_fusion.2.refs_4_), channel_id=1, source_target_pairs={{0,64},{32,0},{64,32},{1,65},{33,1},{65,33},{2,66},{34,2},{66,34},... | collective-permute-start | bytes 786440 | tf_op jit(solution)/shard_map/ppermute | solution.py:23
  28.3 16.6 %collective-permute-start.5 = (bf16[2,64,1024]{2,1,0:T(8,128)(2,1)S(1)}, bf16[2,64,1024]{2,1,0:T(8,128)(2,1)S(1)}, u32[]{:S(2)}, u32[]{:S(2)}) collective-permute-start(bf16[2,64,1024]{2,1,0:T(8,128)(2,1)S(1)} %pad_maximum_fusion.2.refs_4_), channel_id=1, source_target_pairs={{0,576},{192,384},{384,192},{576,0},{1,577},{193,385},{385,193},{5... | collective-permute-start | bytes 786440 | tf_op jit(solution)/shard_map/ppermute | solution.py:21
  31.3 14.3 %collective-permute-start.6 = (bf16[2,64,1024]{2,1,0:T(8,128)(2,1)S(1)}, bf16[2,64,1024]{2,1,0:T(8,128)(2,1)S(1)}, u32[]{:S(2)}, u32[]{:S(2)}) collective-permute-start(bf16[2,64,1024]{2,1,0:T(8,128)(2,1)S(1)} %collective-permute-done.3.refs_5_), channel_id=1, source_target_pairs={{0,576},{192,384},{384,192},{576,0},{1,577},{193,385},{385,193},{5... | collective-permute-start | bytes 786440 | tf_op jit(solution)/shard_map/ppermute | solution.py:21
  38.6 11.5 %collective-permute-start.7 = (bf16[2,64,1024]{2,1,0:T(8,128)(2,1)S(1)}, bf16[2,64,1024]{2,1,0:T(8,128)(2,1)S(1)}, u32[]{:S(2)}, u32[]{:S(2)}) collective-permute-start(bf16[2,64,1024]{2,1,0:T(8,128)(2,1)S(1)} %collective-permute-done.4.refs_6_), channel_id=1, source_target_pairs={{0,576},{192,384},{384,192},{576,0},{1,577},{193,385},{385,193},{5... | collective-permute-start | bytes 786440 | tf_op jit(solution)/shard_map/ppermute | solution.py:21
  41.7 12.5 %collective-permute-start = (bf16[8,80,1024]{2,1,0:T(8,128)(2,1)}, bf16[8,80,1024]{2,1,0:T(8,128)(2,1)S(1)}, u32[]{:S(2)}, u32[]{:S(2)}) collective-permute-start(bf16[8,80,1024]{2,1,0:T(8,128)(2,1)} %bitcast.34), channel_id=1, source_target_pairs={{0,16},{16,0},{1,17},{17,1},{2,18},{18,2},{3,19},{19,3},{4,20},{20... | collective-permute-start | bytes 3932168 | tf_op jit(solution)/shard_map/ppermute | solution.py:130
  44.9 0.7 copy-start.1
  45.6 0.7 copy-start.3
  50.1 0.7 copy-start.5
  50.8 6.2 %collective-permute-start.8 = (bf16[8,80,1024]{2,1,0:T(8,128)(2,1)S(1)}, bf16[8,80,1024]{2,1,0:T(8,128)(2,1)}, u32[]{:S(2)}, u32[]{:S(2)}) collective-permute-start(bf16[8,80,1024]{2,1,0:T(8,128)(2,1)S(1)} %collective-permute-done.1.refs_2_), channel_id=1, source_target_pairs={{0,16},{16,0},{1,17},{17,1},{2,18},{18,2},{3,19},{19,3},{4,20},{20... | collective-permute-start | bytes 3932168 | tf_op jit(solution)/shard_map/ppermute | solution.py:133
  57.0 1.3 copy-start
  58.3 0.9 copy-start.2
  59.2 0.9 copy-start.4
  60.2 0.9 copy-start.6
  62.8 10.3 %collective-permute-start.9 = (bf16[160,768]{1,0:T(8,128)(2,1)S(1)}, bf16[160,768]{1,0:T(8,128)(2,1)S(1)}, u32[]{:S(2)}, u32[]{:S(2)}) collective-permute-start(bf16[160,768]{1,0:T(8,128)(2,1)S(1)} %get-tuple-element.21), channel_id=1, source_target_pairs={{0,1},{1,2},{2,3},{3,4},{4,5},{5,6},{6,7},{7,0},{8,9},{9,10},{10,1... | collective-permute-start | bytes 737288 | tf_op jit(solution)/shard_map/ppermute | solution.py:88
  67.6 8.8 %collective-permute-start.13 = (bf16[160,768]{1,0:T(8,128)(2,1)S(1)}, bf16[160,768]{1,0:T(8,128)(2,1)S(1)}, u32[]{:S(2)}, u32[]{:S(2)}) collective-permute-start(bf16[160,768]{1,0:T(8,128)(2,1)S(1)} %get-tuple-element.22), channel_id=1, source_target_pairs={{0,7},{1,0},{2,1},{3,2},{4,3},{5,4},{6,5},{7,6},{8,15},{9,8},{10,9... | collective-permute-start | bytes 737288 | tf_op jit(solution)/shard_map/ppermute | solution.py:89
  73.2 14.6 %collective-permute-start.10 = (bf16[320,768]{1,0:T(8,128)(2,1)S(1)}, bf16[320,768]{1,0:T(8,128)(2,1)S(1)}, u32[]{:S(2)}, u32[]{:S(2)}) collective-permute-start(bf16[320,768]{1,0:T(8,128)(2,1)S(1)} %pad_maximum_fusion), channel_id=1, source_target_pairs={{0,1},{1,2},{2,3},{3,4},{4,5},{5,6},{6,7},{7,0},{8,9},{9,10},{10,1... | collective-permute-start | bytes 1474568 | tf_op jit(solution)/shard_map/ppermute | solution.py:95
  76.6 14.3 %collective-permute-start.14 = (bf16[320,768]{1,0:T(8,128)(2,1)S(1)}, bf16[320,768]{1,0:T(8,128)(2,1)S(1)}, u32[]{:S(2)}, u32[]{:S(2)}) collective-permute-start(bf16[320,768]{1,0:T(8,128)(2,1)S(1)} %pad_maximum_fusion.1), channel_id=1, source_target_pairs={{0,7},{1,0},{2,1},{3,2},{4,3},{5,4},{6,5},{7,6},{8,15},{9,8},{10,9... | collective-permute-start | bytes 1474568 | tf_op jit(solution)/shard_map/ppermute | solution.py:96
  87.9 13.7 %collective-permute-start.11 = (bf16[320,768]{1,0:T(8,128)(2,1)S(1)}, bf16[320,768]{1,0:T(8,128)(2,1)S(1)}, u32[]{:S(2)}, u32[]{:S(2)}) collective-permute-start(bf16[320,768]{1,0:T(8,128)(2,1)S(1)} %add_convert_fusion.4), channel_id=1, source_target_pairs={{0,1},{1,2},{2,3},{3,4},{4,5},{5,6},{6,7},{7,0},{8,9},{9,10},{10,1... | collective-permute-start | bytes 1474568 | tf_op jit(solution)/shard_map/ppermute | solution.py:95
  91.0 13.4 %collective-permute-start.15 = (bf16[320,768]{1,0:T(8,128)(2,1)S(1)}, bf16[320,768]{1,0:T(8,128)(2,1)S(1)}, u32[]{:S(2)}, u32[]{:S(2)}) collective-permute-start(bf16[320,768]{1,0:T(8,128)(2,1)S(1)} %add_convert_fusion.2), channel_id=1, source_target_pairs={{0,7},{1,0},{2,1},{3,2},{4,3},{5,4},{6,5},{7,6},{8,15},{9,8},{10,9... | collective-permute-start | bytes 1474568 | tf_op jit(solution)/shard_map/ppermute | solution.py:96
  101.8 12.8 %collective-permute-start.12 = (bf16[320,768]{1,0:T(8,128)(2,1)S(1)}, bf16[320,768]{1,0:T(8,128)(2,1)S(1)}, u32[]{:S(2)}, u32[]{:S(2)}) collective-permute-start(bf16[320,768]{1,0:T(8,128)(2,1)S(1)} %add_convert_fusion.3), channel_id=1, source_target_pairs={{0,1},{1,2},{2,3},{3,4},{4,5},{5,6},{6,7},{7,0},{8,9},{9,10},{10,1... | collective-permute-start | bytes 1474568 | tf_op jit(solution)/shard_map/ppermute | solution.py:95
  104.5 12.4 %collective-permute-start.16 = (bf16[320,768]{1,0:T(8,128)(2,1)S(1)}, bf16[320,768]{1,0:T(8,128)(2,1)S(1)}, u32[]{:S(2)}, u32[]{:S(2)}) collective-permute-start(bf16[320,768]{1,0:T(8,128)(2,1)S(1)} %add_convert_fusion.1), channel_id=1, source_target_pairs={{0,7},{1,0},{2,1},{3,2},{4,3},{5,4},{6,5},{7,6},{8,15},{9,8},{10,9... | collective-permute-start | bytes 1474568 | tf_op jit(solution)/shard_map/ppermute | solution.py:96
  116.9 19.9 %copy-start.7 = (s32[128,2]{0,1:T(2,128)S(1)}, s32[128,2]{0,1:T(2,128)}, u32[]{:S(2)}) copy-start(s32[128,2]{0,1:T(2,128)} %param.3) | copy-start | bytes 3076
  117.9 37.2 %all-to-all-start = ((bf16[8,40,768]{2,1,0:T(8,128)(2,1)}), bf16[8,40,768]{2,1,0:T(8,128)(2,1)S(1)}, u32[]{:S(2)}, u32[]{:S(2)}) async-start(bf16[8,40,768]{2,1,0:T(8,128)(2,1)} %bitcast.31), calls=%async_computation | async-start | bytes 983040 | tf_op jit(solution)/shard_map/all_to_all | solution.py:105

commit v11 on v10

--- a/solution.py
+++ b/solution.py
@@ -38,22 +38,31 @@
 def product_kernel(here, place, *refs, pieces, outs):
     rows, hidden = refs[0].shape[1:]
     flat = jnp.concatenate([piece[0] for piece in refs[:pieces]])
-    weights = jnp.concatenate([block[...].reshape(-1, hidden) for block in refs[pieces:-outs]])
+    blocks = refs[pieces:-outs[0] * outs[1]]
+    weights = jnp.concatenate([block[...].reshape(-1, hidden) for block in blocks])
     result = lax.dot_general(
         flat, weights, (((1,), (1,)), ((), ())), preferred_element_type=jnp.float32
     ).astype(jnp.bfloat16)
-    for i, out in enumerate(refs[-outs:]):
-
-        @pl.when(pl.program_id(0) == i)
+    rest = [result[k * rows:(k + 1) * rows] for k in range(pieces)]
+    step = 1
+    while step < pieces:
+        flip = (place[0] // step) % 2 == 1
+        rest = [jnp.where(flip, rest[k ^ step], rest[k]) for k in range(pieces)]
+        step *= 2
+    share = pieces if outs[0] > 1 else pieces // outs[1]
+    for i, out in enumerate(refs[-outs[0] * outs[1]:]):
+        part = i % outs[1]
+
+        @pl.when(pl.program_id(0) == i // outs[1])
         def _():
-            for k in range(pieces):
-                start = pl.multiple_of((place[0] ^ k) * rows, rows)
-                out[pl.ds(start, rows), :] = result[k * rows:(k + 1) * rows]
-
-
-def product(where, pieces, blocks, first, stride, count):
+            for k in range(share):
+                out[k * rows:(k + 1) * rows, :] = rest[part * share + k]
+
+
+def product(where, pieces, blocks, first, stride, count, parts=1):
     tensor_count, rows, hidden = pieces[0].shape
     rows_out = rows * len(pieces)
+    outs = count * parts
     features = sum(block.shape[0] * block.shape[1] for block in blocks)
     flops = 2 * count * rows_out * hidden * features
     moved = 2 * (count * rows_out * (hidden + features) + features * hidden)
@@ -62,42 +71,65 @@
         return ((here[0] + first + i * stride) % tensor_count, 0, 0)
 
     return pl.pallas_call(
-        functools.partial(product_kernel, pieces=len(pieces), outs=count),
+        functools.partial(product_kernel, pieces=len(pieces), outs=(count, parts)),
         grid_spec=pltpu.PrefetchScalarGridSpec(
             num_scalar_prefetch=2,
             grid=(count,),
             in_specs=[pl.BlockSpec((1, rows, hidden), source)] * len(pieces)
             + [pl.BlockSpec(block.shape, lambda i, here, place: (0, 0, 0)) for block in blocks],
-            out_specs=[pl.BlockSpec((rows_out, features), lambda i, here, place: (0, 0))] * count,
+            out_specs=[pl.BlockSpec((rows_out // parts, features), lambda i, here, place: (0, 0))] * outs,
         ),
-        out_shape=[jax.ShapeDtypeStruct((rows_out, features), jnp.bfloat16)] * count,
+        out_shape=[jax.ShapeDtypeStruct((rows_out // parts, features), jnp.bfloat16)] * outs,
         cost_estimate=pl.CostEstimate(flops=flops, bytes_accessed=moved, transcendentals=0),
         compiler_params=pltpu.CompilerParams(vmem_limit_bytes=14 * 1024 * 1024),
     )(*where, *pieces, *blocks)
+
+
+def add_kernel(*refs, at):
+    *terms, out = refs
+    base, came = terms[0], terms[1:]
+    rows = came[0].shape[0]
+    total = base[at:at + rows, :].astype(jnp.float32)
+    for term in came:
+        total += term[...].astype(jnp.float32)
+    out[at:at + rows, :] = total.astype(out.dtype)
+    for low, high in ((0, at), (at + rows, base.shape[0])):
+        if low < high:
+            out[low:high, :] = base[low:high, :]
+
+
+def add(base, *came, at=0):
+    vmem = pl.BlockSpec(memory_space=pltpu.VMEM)
+    size = base.size
+    return pl.pallas_call(
+        functools.partial(add_kernel, at=at),
+        out_shape=jax.ShapeDtypeStruct(base.shape, base.dtype),
+        in_specs=[vmem] * (1 + len(came)),
+        out_specs=vmem,
+        cost_estimate=pl.CostEstimate(flops=size, bytes_accessed=6 * size, transcendentals=0),
+        compiler_params=pltpu.CompilerParams(vmem_limit_bytes=8 * 1024 * 1024),
+    )(base, *came)
 
 
 def sum_by_arms(partial, n):
     mid = n // 2
     up = [(i, (i + 1) % n) for i in range(n)]
     down = [(i, (i - 1) % n) for i in range(n)]
-    wide = lambda value: value.astype(jnp.float32)
-    narrow = lambda value: value.astype(jnp.bfloat16)
-
-    (opposite,) = partial(mid, 1, 1)
-    half = opposite.shape[0] // 2
-    first = lax.ppermute(opposite[:half], "t", up)
-    last = lax.ppermute(opposite[half:], "t", down)
-    above, below = partial(mid - 1, 2, 2)
-    going_up = jnp.concatenate([narrow(wide(above[:half]) + wide(first)), above[half:]])
-    going_down = jnp.concatenate([below[:half], narrow(wide(below[half:]) + wide(last))])
-    uppers, lowers = partial(mid - 2, -1, mid - 2), partial(mid + 2, 1, mid - 1)
+
+    low, high = partial(mid, 1, 1, 2)
+    first = lax.ppermute(low, "t", up)
+    last = lax.ppermute(high, "t", down)
+    above, below = partial(mid - 1, 2, 2, 1)
+    going_up = add(above, first)
+    going_down = add(below, last, at=low.shape[0])
+    uppers, lowers = partial(mid - 2, -1, mid - 2, 1), partial(mid + 2, 1, mid - 1, 1)
     for step in range(1, mid):
         from_below = lax.ppermute(going_up, "t", up)
         from_above = lax.ppermute(going_down, "t", down)
         if step < mid - 1:
-            going_up = narrow(wide(uppers[step - 1]) + wide(from_below))
-            going_down = narrow(wide(lowers[step - 1]) + wide(from_above))
-    return narrow(wide(lowers[mid - 2]) + wide(from_below) + wide(from_above))
+            going_up = add(uppers[step - 1], from_below)
+            going_down = add(lowers[step - 1], from_above)
+    return add(lowers[mid - 2], from_below, from_above)
 
 
 def give_back(summed, owners, capacity):
@@ -136,7 +168,7 @@
     where = [place.astype(jnp.int32).reshape(1) for place in places]
     blocks = (*column, *other)
     summed = sum_by_arms(
-        lambda k, stride, count: product(where, pieces, blocks, k, stride, count), tensor_count
+        lambda *at: product(where, pieces, blocks, *at), tensor_count
     )
     piece = give_back(summed, owners, capacity)
 

time: 159 us -> 159 us (level)
  waiting for transfers between devices: 46 us -> 48.2 us
  other arithmetic: 2.77 us -> 1.15 us
    ppermute x3, waiting for transfers between devices: 3.89 us -> 13.1 us  [sum_by_arms(): from_above = lax.ppermute(going_down, 't', down)]
    ppermute x3, waiting for transfers between devices: 10.2 us -> 5.19 us  [sum_by_arms(): from_below = lax.ppermute(going_up, 't', up)]
    ppermute x2, waiting for transfers between devices: 2.56 us -> 0.52 us  [the longest x1 0.52 us: sum_by_arms(): last = lax.ppermute(high, 't', down)]
  transfers between devices with their start and end apart: 18 -> 18, of which waited for: 12 -> 10; matrix products, arithmetic and copies ran while one was open for 2% -> 1% of each run, Pallas kernels for 5% -> 6%
where the time goes in v11:
time: 159 us; the launch traced here: 158 us
  starting transfers between devices  88 us (55%)
  waiting for transfers between devices  48.2 us (30%)
  Pallas kernels  13.4 us (8%)
  local copies, waits for them, and re-layouts  6.87 us (4%)
    all_to_all x1, starting transfers between devices, give_back(): lax.all_to_all(summed.reshape(-1, capacity, features), ('xp', 'c', 'e'),...  18.4 us
    all_to_all x1, waiting for transfers between devices, give_back(): lax.all_to_all(summed.reshape(-1, capacity, features), ('xp', 'c', 'e'),...  17.4 us
    ppermute x3, starting transfers between devices, sum_by_arms(): from_above = lax.ppermute(going_down, 't', down)  16 us
    ppermute x3, waiting for transfers between devices, sum_by_arms(): from_above = lax.ppermute(going_down, 't', down)  13.1 us
    ppermute x3, starting transfers between devices, gather_columns(): opposite = lambda value: lax.ppermute(value, ('xh', 'xp'), WEIGHT_SWAP)  10.5 us
    pallas_call x4, Pallas kernels, product(): pl.pallas_call(functools.partial(product_kernel, pieces=len(pieces), outs...  10 us
    ppermute x1, starting transfers between devices, gather_columns(): pair = jnp.stack([slab, lax.ppermute(slab, 'h', SWAP)])  7.62 us
    ppermute x1, starting transfers between devices, gather_columns(): lax.ppermute(pair, 'm', turn(1))  6.71 us
  transfers between devices with their start and end apart: 18, of which 10 were waited for; matrix products, arithmetic and copies ran while one was open for 1% of the time, Pallas kernels for 6%

profile of v11, /device:TPU:1, one launch (start us, length us, event | category | flops | bytes accessed | tf_op | source)
XLA Modules:
  0.0 157.9 jit_solution(8437676033115528879)
XLA Ops:
  0.0 3.9 %collective-permute-start.1 = (bf16[8,80,1024]{2,1,0:T(8,128)(2,1)}, bf16[8,80,1024]{2,1,0:T(8,128)(2,1)S(1)}, u32[]{:S(2)}, u32[]{:S(2)}) collective-permute-start(bf16[8,80,1024]{2,1,0:T(8,128)(2,1)} %bitcast.33), channel_id=1, source_target_pairs={{0,192},{192,0},{1,193},{193,1},{2,194},{194,2},{3,195},{195,3},{4... | collective-permute-start | bytes 3932168 | tf_op jit(solution)/shard_map/ppermute | solution.py:161
  3.9 7.6 %collective-permute-start.2 = (bf16[64,1024]{1,0:T(8,128)(2,1)}, bf16[64,1024]{1,0:T(8,128)(2,1)S(1)}, u32[]{:S(2)}, u32[]{:S(2)}) collective-permute-start(bf16[64,1024]{1,0:T(8,128)(2,1)} %bitcast.41), channel_id=1, source_target_pairs={{0,96},{96,0},{1,97},{97,1},{2,98},{98,2},{3,99},{99,3},{4,100},{1... | collective-permute-start | bytes 393224 | tf_op jit(solution)/shard_map/ppermute | solution.py:22
  11.6 2.6 %collective-permute-done.2 = bf16[64,1024]{1,0:T(8,128)(2,1)S(1)} collective-permute-done((bf16[64,1024]{1,0:T(8,128)(2,1)}, bf16[64,1024]{1,0:T(8,128)(2,1)S(1)}, u32[]{:S(2)}, u32[]{:S(2)}) %collective-permute-start.2) | collective-permute-done | bytes 131104 | tf_op jit(solution)/shard_map/ppermute | solution.py:22
  14.1 0.9 pad_maximum_fusion.refs_4_
  15.1 6.7 %collective-permute-start.3 = (bf16[2,64,1024]{2,1,0:T(8,128)(2,1)S(1)}, bf16[2,64,1024]{2,1,0:T(8,128)(2,1)S(1)}, u32[]{:S(2)}, u32[]{:S(2)}) collective-permute-start(bf16[2,64,1024]{2,1,0:T(8,128)(2,1)S(1)} %pad_maximum_fusion.refs_4_), channel_id=1, source_target_pairs={{0,32},{32,64},{64,0},{1,33},{33,65},{65,1},{2,34},{34,66},{66,2},... | collective-permute-start | bytes 786440 | tf_op jit(solution)/shard_map/ppermute | solution.py:23
  21.8 6.5 %collective-permute-start.4 = (bf16[2,64,1024]{2,1,0:T(8,128)(2,1)S(1)}, bf16[2,64,1024]{2,1,0:T(8,128)(2,1)S(1)}, u32[]{:S(2)}, u32[]{:S(2)}) collective-permute-start(bf16[2,64,1024]{2,1,0:T(8,128)(2,1)S(1)} %pad_maximum_fusion.refs_4_), channel_id=1, source_target_pairs={{0,64},{32,0},{64,32},{1,65},{33,1},{65,33},{2,66},{34,2},{66,34},... | collective-permute-start | bytes 786440 | tf_op jit(solution)/shard_map/ppermute | solution.py:23
  28.3 3.0 %collective-permute-start.5 = (bf16[2,64,1024]{2,1,0:T(8,128)(2,1)S(1)}, bf16[2,64,1024]{2,1,0:T(8,128)(2,1)S(1)}, u32[]{:S(2)}, u32[]{:S(2)}) collective-permute-start(bf16[2,64,1024]{2,1,0:T(8,128)(2,1)S(1)} %pad_maximum_fusion.refs_4_), channel_id=1, source_target_pairs={{0,576},{192,384},{384,192},{576,0},{1,577},{193,385},{385,193},{5... | collective-permute-start | bytes 786440 | tf_op jit(solution)/shard_map/ppermute | solution.py:21
  31.3 0.0 collective-permute-done.3.refs_5_
  31.3 4.3 %collective-permute-start.6 = (bf16[2,64,1024]{2,1,0:T(8,128)(2,1)S(1)}, bf16[2,64,1024]{2,1,0:T(8,128)(2,1)S(1)}, u32[]{:S(2)}, u32[]{:S(2)}) collective-permute-start(bf16[2,64,1024]{2,1,0:T(8,128)(2,1)S(1)} %collective-permute-done.3.refs_5_), channel_id=1, source_target_pairs={{0,576},{192,384},{384,192},{576,0},{1,577},{193,385},{385,193},{5... | collective-permute-start | bytes 786440 | tf_op jit(solution)/shard_map/ppermute | solution.py:21
  35.6 2.9 %collective-permute-done.4.refs_6_ = bf16[2,64,1024]{2,1,0:T(8,128)(2,1)S(1)} collective-permute-done((bf16[2,64,1024]{2,1,0:T(8,128)(2,1)S(1)}, bf16[2,64,1024]{2,1,0:T(8,128)(2,1)S(1)}, u32[]{:S(2)}, u32[]{:S(2)}) %collective-permute-start.4) | collective-permute-done | bytes 262176 | tf_op jit(solution)/shard_map/ppermute | solution.py:23
  38.6 3.2 %collective-permute-start.7 = (bf16[2,64,1024]{2,1,0:T(8,128)(2,1)S(1)}, bf16[2,64,1024]{2,1,0:T(8,128)(2,1)S(1)}, u32[]{:S(2)}, u32[]{:S(2)}) collective-permute-start(bf16[2,64,1024]{2,1,0:T(8,128)(2,1)S(1)} %collective-permute-done.4.refs_6_), channel_id=1, source_target_pairs={{0,576},{192,384},{384,192},{576,0},{1,577},{193,385},{385,193},{5... | collective-permute-start | bytes 786440 | tf_op jit(solution)/shard_map/ppermute | solution.py:21
  41.7 3.1 %collective-permute-start = (bf16[8,80,1024]{2,1,0:T(8,128)(2,1)}, bf16[8,80,1024]{2,1,0:T(8,128)(2,1)S(1)}, u32[]{:S(2)}, u32[]{:S(2)}) collective-permute-start(bf16[8,80,1024]{2,1,0:T(8,128)(2,1)} %bitcast.34), channel_id=1, source_target_pairs={{0,16},{16,0},{1,17},{17,1},{2,18},{18,2},{3,19},{19,3},{4,20},{20... | collective-permute-start | bytes 3932168 | tf_op jit(solution)/shard_map/ppermute | solution.py:162
  44.9 0.0 collective-permute-done.5.refs_7_
  44.9 0.0 copy-start.1
  44.9 0.7 copy-done.1
  45.6 0.0 collective-permute-done.6.refs_8_
  45.6 0.7 copy-done.3
  46.3 3.8 %collective-permute-done.7.refs_9_ = bf16[2,64,1024]{2,1,0:T(8,128)(2,1)S(1)} collective-permute-done((bf16[2,64,1024]{2,1,0:T(8,128)(2,1)S(1)}, bf16[2,64,1024]{2,1,0:T(8,128)(2,1)S(1)}, u32[]{:S(2)}, u32[]{:S(2)}) %collective-permute-start.7) | collective-permute-done | bytes 262176 | tf_op jit(solution)/shard_map/ppermute | solution.py:21
  50.1 0.7 copy-done.5
  50.8 0.0 collective-permute-done.1.refs_2_
  50.8 3.4 %collective-permute-start.8 = (bf16[8,80,1024]{2,1,0:T(8,128)(2,1)S(1)}, bf16[8,80,1024]{2,1,0:T(8,128)(2,1)}, u32[]{:S(2)}, u32[]{:S(2)}) collective-permute-start(bf16[8,80,1024]{2,1,0:T(8,128)(2,1)S(1)} %collective-permute-done.1.refs_2_), channel_id=1, source_target_pairs={{0,16},{16,0},{1,17},{17,1},{2,18},{18,2},{3,19},{19,3},{4,20},{20... | collective-permute-start | bytes 3932168 | tf_op jit(solution)/shard_map/ppermute | solution.py:165
  54.2 0.0 collective-permute-done.refs_1_
  54.2 2.8 %collective-permute-done.8.refs_3_ = bf16[8,80,1024]{2,1,0:T(8,128)(2,1)} collective-permute-done((bf16[8,80,1024]{2,1,0:T(8,128)(2,1)S(1)}, bf16[8,80,1024]{2,1,0:T(8,128)(2,1)}, u32[]{:S(2)}, u32[]{:S(2)}) %collective-permute-start.8) | collective-permute-done | bytes 1310752 | tf_op jit(solution)/shard_map/ppermute | solution.py:165
  57.0 1.3 copy-done
  58.3 0.9 copy-done.2
  59.2 0.9 copy-done.4
  60.2 0.9 copy-done.6
  61.1 1.6 %shard_map.40 = (bf16[160,768]{1,0:T(8,128)(2,1)S(1)}, bf16[160,768]{1,0:T(8,128)(2,1)S(1)}) custom-call(s32[1]{0:T(128)} %bitcast.26.here, s32[1]{0:T(128)} %bitcast.27.place, bf16[8,80,1024]{2,1,0:T(8,128)(2,1)S(1)} %bitcast.35, bf16[8,80,1024]{2,1,0:T(8,128)(2,1)S(1)} %collective-permute-done.refs_1_, ...), custom_call_target="tpu_custom_call" | custom-call | flops 503316480 | bytes 2719744 | tf_op jit(solution)/shard_map/pallas_call | solution.py:73
  62.8 4.2 %collective-permute-start.13 = (bf16[160,768]{1,0:T(8,128)(2,1)S(1)}, bf16[160,768]{1,0:T(8,128)(2,1)S(1)}, u32[]{:S(2)}, u32[]{:S(2)}) collective-permute-start(bf16[160,768]{1,0:T(8,128)(2,1)S(1)} %get-tuple-element.24), channel_id=1, source_target_pairs={{0,7},{1,0},{2,1},{3,2},{4,3},{5,4},{6,5},{7,6},{8,15},{9,8},{10,9... | collective-permute-start | bytes 737288 | tf_op jit(solution)/shard_map/ppermute | solution.py:121
  66.9 1.9 %collective-permute-start.9 = (bf16[160,768]{1,0:T(8,128)(2,1)S(1)}, bf16[160,768]{1,0:T(8,128)(2,1)S(1)}, u32[]{:S(2)}, u32[]{:S(2)}) collective-permute-start(bf16[160,768]{1,0:T(8,128)(2,1)S(1)} %get-tuple-element.20), channel_id=1, source_target_pairs={{0,1},{1,2},{2,3},{3,4},{4,5},{5,6},{6,7},{7,0},{8,9},{9,10},{10,1... | collective-permute-start | bytes 737288 | tf_op jit(solution)/shard_map/ppermute | solution.py:120
  68.9 2.5 %shard_map.39 = (bf16[320,768]{1,0:T(8,128)(2,1)S(1)}, bf16[320,768]{1,0:T(8,128)(2,1)S(1)}) custom-call(s32[1]{0:T(128)} %bitcast.26.here, s32[1]{0:T(128)} %bitcast.27.place, bf16[8,80,1024]{2,1,0:T(8,128)(2,1)S(1)} %bitcast.36, bf16[8,80,1024]{2,1,0:T(8,128)(2,1)S(1)} %collective-permute-done.refs_1_, ...), custom_call_target="tpu_custom_call" | custom-call | flops 1006632960 | bytes 3866624 | tf_op jit(solution)/shard_map/pallas_call | solution.py:73
  71.4 0.5 collective-permute-done.13.refs_1_
  71.9 0.1 shard_map.44
  72.0 5.3 %collective-permute-start.14 = (bf16[320,768]{1,0:T(8,128)(2,1)S(1)}, bf16[320,768]{1,0:T(8,128)(2,1)S(1)}, u32[]{:S(2)}, u32[]{:S(2)}) collective-permute-start(bf16[320,768]{1,0:T(8,128)(2,1)S(1)} %shard_map.44), channel_id=1, source_target_pairs={{0,7},{1,0},{2,1},{3,2},{4,3},{5,4},{6,5},{7,6},{8,15},{9,8},{10,9... | collective-permute-start | bytes 1474568 | tf_op jit(solution)/shard_map/ppermute | solution.py:128
  77.3 0.0 collective-permute-done.9.refs_1_
  77.3 0.1 shard_map.41
  77.4 1.9 %collective-permute-start.10 = (bf16[320,768]{1,0:T(8,128)(2,1)S(1)}, bf16[320,768]{1,0:T(8,128)(2,1)S(1)}, u32[]{:S(2)}, u32[]{:S(2)}) collective-permute-start(bf16[320,768]{1,0:T(8,128)(2,1)S(1)} %shard_map.41), channel_id=1, source_target_pairs={{0,1},{1,2},{2,3},{3,4},{4,5},{5,6},{6,7},{7,0},{8,9},{9,10},{10,1... | collective-permute-start | bytes 1474568 | tf_op jit(solution)/shard_map/ppermute | solution.py:127
  79.3 2.5 %shard_map.38 = (bf16[320,768]{1,0:T(8,128)(2,1)S(1)}, bf16[320,768]{1,0:T(8,128)(2,1)S(1)}) custom-call(s32[1]{0:T(128)} %bitcast.26.here, s32[1]{0:T(128)} %bitcast.27.place, bf16[8,80,1024]{2,1,0:T(8,128)(2,1)S(1)} %bitcast.37, bf16[8,80,1024]{2,1,0:T(8,128)(2,1)S(1)} %collective-permute-done.refs_1_, ...), custom_call_target="tpu_custom_call" | custom-call | flops 1006632960 | bytes 3866624 | tf_op jit(solution)/shard_map/pallas_call | solution.py:73
  81.8 3.4 %shard_map.37 = (bf16[320,768]{1,0:T(8,128)(2,1)S(1)}, bf16[320,768]{1,0:T(8,128)(2,1)S(1)}, bf16[320,768]{1,0:T(8,128)(2,1)S(1)}) custom-call(s32[1]{0:T(128)} %bitcast.26.here, s32[1]{0:T(128)} %bitcast.27.place, bf16[8,80,1024]{2,1,0:T(8,128)(2,1)S(1)} %bitcast.38, bf16[8,80,1024]{2,1,0:T(8,128)(2,1)S(1)} %collective-permute-done.refs_1_, ...), custom_call_target="tpu_custom_call" | custom-call | flops 1509949440 | bytes 5013504 | tf_op jit(solution)/shard_map/pallas_call | solution.py:73
  85.2 1.4 collective-permute-done.14.refs_1_
  86.6 0.1 shard_map.45
  86.7 5.3 %collective-permute-start.15 = (bf16[320,768]{1,0:T(8,128)(2,1)S(1)}, bf16[320,768]{1,0:T(8,128)(2,1)S(1)}, u32[]{:S(2)}, u32[]{:S(2)}) collective-permute-start(bf16[320,768]{1,0:T(8,128)(2,1)S(1)} %shard_map.45), channel_id=1, source_target_pairs={{0,7},{1,0},{2,1},{3,2},{4,3},{5,4},{6,5},{7,6},{8,15},{9,8},{10,9... | collective-permute-start | bytes 1474568 | tf_op jit(solution)/shard_map/ppermute | solution.py:128
  92.0 0.0 collective-permute-done.10.refs_1_
  92.0 0.1 shard_map.42
  92.1 1.9 %collective-permute-start.11 = (bf16[320,768]{1,0:T(8,128)(2,1)S(1)}, bf16[320,768]{1,0:T(8,128)(2,1)S(1)}, u32[]{:S(2)}, u32[]{:S(2)}) collective-permute-start(bf16[320,768]{1,0:T(8,128)(2,1)S(1)} %shard_map.42), channel_id=1, source_target_pairs={{0,1},{1,2},{2,3},{3,4},{4,5},{5,6},{6,7},{7,0},{8,9},{9,10},{10,1... | collective-permute-start | bytes 1474568 | tf_op jit(solution)/shard_map/ppermute | solution.py:127
  94.1 6.3 %collective-permute-done.15.refs_1_ = bf16[320,768]{1,0:T(8,128)(2,1)S(1)} collective-permute-done((bf16[320,768]{1,0:T(8,128)(2,1)S(1)}, bf16[320,768]{1,0:T(8,128)(2,1)S(1)}, u32[]{:S(2)}, u32[]{:S(2)}) %collective-permute-start.15) | collective-permute-done | bytes 491552 | tf_op jit(solution)/shard_map/ppermute | solution.py:128
  100.4 0.1 shard_map.46
  100.5 5.3 %collective-permute-start.16 = (bf16[320,768]{1,0:T(8,128)(2,1)S(1)}, bf16[320,768]{1,0:T(8,128)(2,1)S(1)}, u32[]{:S(2)}, u32[]{:S(2)}) collective-permute-start(bf16[320,768]{1,0:T(8,128)(2,1)S(1)} %shard_map.46), channel_id=1, source_target_pairs={{0,7},{1,0},{2,1},{3,2},{4,3},{5,4},{6,5},{7,6},{8,15},{9,8},{10,9... | collective-permute-start | bytes 1474568 | tf_op jit(solution)/shard_map/ppermute | solution.py:128
  105.8 0.0 collective-permute-done.11.refs_1_
  105.8 0.1 shard_map.43
  106.0 1.9 %collective-permute-start.12 = (bf16[320,768]{1,0:T(8,128)(2,1)S(1)}, bf16[320,768]{1,0:T(8,128)(2,1)S(1)}, u32[]{:S(2)}, u32[]{:S(2)}) collective-permute-start(bf16[320,768]{1,0:T(8,128)(2,1)S(1)} %shard_map.43), channel_id=1, source_target_pairs={{0,1},{1,2},{2,3},{3,4},{4,5},{5,6},{6,7},{7,0},{8,9},{9,10},{10,1... | collective-permute-start | bytes 1474568 | tf_op jit(solution)/shard_map/ppermute | solution.py:127
  107.9 5.4 %collective-permute-done.16.refs_2_ = bf16[320,768]{1,0:T(8,128)(2,1)S(1)} collective-permute-done((bf16[320,768]{1,0:T(8,128)(2,1)S(1)}, bf16[320,768]{1,0:T(8,128)(2,1)S(1)}, u32[]{:S(2)}, u32[]{:S(2)}) %collective-permute-start.16) | collective-permute-done | bytes 491552 | tf_op jit(solution)/shard_map/ppermute | solution.py:128
  113.3 5.2 %collective-permute-done.12.refs_1_ = bf16[320,768]{1,0:T(8,128)(2,1)S(1)} collective-permute-done((bf16[320,768]{1,0:T(8,128)(2,1)S(1)}, bf16[320,768]{1,0:T(8,128)(2,1)S(1)}, u32[]{:S(2)}, u32[]{:S(2)}) %collective-permute-start.12) | collective-permute-done | bytes 491552 | tf_op jit(solution)/shard_map/ppermute | solution.py:127
  118.4 1.0 shard_map.47
  119.4 18.4 %all-to-all-start = ((bf16[8,40,768]{2,1,0:T(8,128)(2,1)}), bf16[8,40,768]{2,1,0:T(8,128)(2,1)S(1)}, u32[]{:S(2)}, u32[]{:S(2)}) async-start(bf16[8,40,768]{2,1,0:T(8,128)(2,1)} %bitcast.31), calls=%async_computation | async-start | bytes 983040 | tf_op jit(solution)/shard_map/all_to_all | solution.py:137
  137.8 0.1 copy.14
  137.9 0.2 reduce_window_sum.11
  138.1 0.1 copy.15
  138.2 0.1 copy.16
  138.3 0.1 copy.18
  138.4 0.1 eq.43
  138.5 0.1 stack.105.refs_0_
  138.6 17.4 %all-to-all-done = bf16[8,40,768]{2,1,0:T(8,128)(2,1)S(1)} async-done(((bf16[8,40,768]{2,1,0:T(8,128)(2,1)}), bf16[8,40,768]{2,1,0:T(8,128)(2,1)S(1)}, u32[]{:S(2)}, u32[]{:S(2)}) %all-to-all-start) | async-done | bytes 491552 | tf_op jit(solution)/shard_map/all_to_all | solution.py:137
  156.0 1.9 %shard_map.48 = bf16[128,3072]{1,0:T(8,128)(2,1)} custom-call(s32[24]{0:T(128)S(1)} %stack.105.refs_0_, bf16[128,80]{1,0:T(8,128)(2,1)S(1)} %and_convert_fusion.refs_1_, bf16[4,80,768]{2,1,0:T(8,128)(2,1)S(1)} %bitcast.39), custom_call_target="tpu_custom_call" | custom-call | tf_op jit(solution)/shard_map/pallas_call | solution.py:187
  (15 shorter events, 0.1 us)
Async XLA Ops:
  0.0 50.8 %collective-permute-start.1 = (bf16[8,80,1024]{2,1,0:T(8,128)(2,1)}, bf16[8,80,1024]{2,1,0:T(8,128)(2,1)S(1)}, u32[]{:S(2)}, u32[]{:S(2)}) collective-permute-start(bf16[8,80,1024]{2,1,0:T(8,128)(2,1)} %bitcast.33), channel_id=1, source_target_pairs={{0,192},{192,0},{1,193},{193,1},{2,194},{194,2},{3,195},{195,3},{4... | collective-permute-start | bytes 3932168 | tf_op jit(solution)/shard_map/ppermute | solution.py:161
  3.9 10.2 %collective-permute-start.2 = (bf16[64,1024]{1,0:T(8,128)(2,1)}, bf16[64,1024]{1,0:T(8,128)(2,1)S(1)}, u32[]{:S(2)}, u32[]{:S(2)}) collective-permute-start(bf16[64,1024]{1,0:T(8,128)(2,1)} %bitcast.41), channel_id=1, source_target_pairs={{0,96},{96,0},{1,97},{97,1},{2,98},{98,2},{3,99},{99,3},{4,100},{1... | collective-permute-start | bytes 393224 | tf_op jit(solution)/shard_map/ppermute | solution.py:22
  15.1 16.2 %collective-permute-start.3 = (bf16[2,64,1024]{2,1,0:T(8,128)(2,1)S(1)}, bf16[2,64,1024]{2,1,0:T(8,128)(2,1)S(1)}, u32[]{:S(2)}, u32[]{:S(2)}) collective-permute-start(bf16[2,64,1024]{2,1,0:T(8,128)(2,1)S(1)} %pad_maximum_fusion.refs_4_), channel_id=1, source_target_pairs={{0,32},{32,64},{64,0},{1,33},{33,65},{65,1},{2,34},{34,66},{66,2},... | collective-permute-start | bytes 786440 | tf_op jit(solution)/shard_map/ppermute | solution.py:23
  21.8 16.8 %collective-permute-start.4 = (bf16[2,64,1024]{2,1,0:T(8,128)(2,1)S(1)}, bf16[2,64,1024]{2,1,0:T(8,128)(2,1)S(1)}, u32[]{:S(2)}, u32[]{:S(2)}) collective-permute-start(bf16[2,64,1024]{2,1,0:T(8,128)(2,1)S(1)} %pad_maximum_fusion.refs_4_), channel_id=1, source_target_pairs={{0,64},{32,0},{64,32},{1,65},{33,1},{65,33},{2,66},{34,2},{66,34},... | collective-permute-start | bytes 786440 | tf_op jit(solution)/shard_map/ppermute | solution.py:23
  28.3 16.6 %collective-permute-start.5 = (bf16[2,64,1024]{2,1,0:T(8,128)(2,1)S(1)}, bf16[2,64,1024]{2,1,0:T(8,128)(2,1)S(1)}, u32[]{:S(2)}, u32[]{:S(2)}) collective-permute-start(bf16[2,64,1024]{2,1,0:T(8,128)(2,1)S(1)} %pad_maximum_fusion.refs_4_), channel_id=1, source_target_pairs={{0,576},{192,384},{384,192},{576,0},{1,577},{193,385},{385,193},{5... | collective-permute-start | bytes 786440 | tf_op jit(solution)/shard_map/ppermute | solution.py:21
  31.3 14.3 %collective-permute-start.6 = (bf16[2,64,1024]{2,1,0:T(8,128)(2,1)S(1)}, bf16[2,64,1024]{2,1,0:T(8,128)(2,1)S(1)}, u32[]{:S(2)}, u32[]{:S(2)}) collective-permute-start(bf16[2,64,1024]{2,1,0:T(8,128)(2,1)S(1)} %collective-permute-done.3.refs_5_), channel_id=1, source_target_pairs={{0,576},{192,384},{384,192},{576,0},{1,577},{193,385},{385,193},{5... | collective-permute-start | bytes 786440 | tf_op jit(solution)/shard_map/ppermute | solution.py:21
  38.6 11.5 %collective-permute-start.7 = (bf16[2,64,1024]{2,1,0:T(8,128)(2,1)S(1)}, bf16[2,64,1024]{2,1,0:T(8,128)(2,1)S(1)}, u32[]{:S(2)}, u32[]{:S(2)}) collective-permute-start(bf16[2,64,1024]{2,1,0:T(8,128)(2,1)S(1)} %collective-permute-done.4.refs_6_), channel_id=1, source_target_pairs={{0,576},{192,384},{384,192},{576,0},{1,577},{193,385},{385,193},{5... | collective-permute-start | bytes 786440 | tf_op jit(solution)/shard_map/ppermute | solution.py:21
  41.7 12.5 %collective-permute-start = (bf16[8,80,1024]{2,1,0:T(8,128)(2,1)}, bf16[8,80,1024]{2,1,0:T(8,128)(2,1)S(1)}, u32[]{:S(2)}, u32[]{:S(2)}) collective-permute-start(bf16[8,80,1024]{2,1,0:T(8,128)(2,1)} %bitcast.34), channel_id=1, source_target_pairs={{0,16},{16,0},{1,17},{17,1},{2,18},{18,2},{3,19},{19,3},{4,20},{20... | collective-permute-start | bytes 3932168 | tf_op jit(solution)/shard_map/ppermute | solution.py:162
  44.9 0.7 copy-start.1
  45.6 0.7 copy-start.3
  50.1 0.7 copy-start.5
  50.8 6.2 %collective-permute-start.8 = (bf16[8,80,1024]{2,1,0:T(8,128)(2,1)S(1)}, bf16[8,80,1024]{2,1,0:T(8,128)(2,1)}, u32[]{:S(2)}, u32[]{:S(2)}) collective-permute-start(bf16[8,80,1024]{2,1,0:T(8,128)(2,1)S(1)} %collective-permute-done.1.refs_2_), channel_id=1, source_target_pairs={{0,16},{16,0},{1,17},{17,1},{2,18},{18,2},{3,19},{19,3},{4,20},{20... | collective-permute-start | bytes 3932168 | tf_op jit(solution)/shard_map/ppermute | solution.py:165
  57.0 1.3 copy-start
  58.3 0.9 copy-start.2
  59.2 0.9 copy-start.4
  60.2 0.9 copy-start.6
  62.8 9.1 %collective-permute-start.13 = (bf16[160,768]{1,0:T(8,128)(2,1)S(1)}, bf16[160,768]{1,0:T(8,128)(2,1)S(1)}, u32[]{:S(2)}, u32[]{:S(2)}) collective-permute-start(bf16[160,768]{1,0:T(8,128)(2,1)S(1)} %get-tuple-element.24), channel_id=1, source_target_pairs={{0,7},{1,0},{2,1},{3,2},{4,3},{5,4},{6,5},{7,6},{8,15},{9,8},{10,9... | collective-permute-start | bytes 737288 | tf_op jit(solution)/shard_map/ppermute | solution.py:121
  66.9 10.3 %collective-permute-start.9 = (bf16[160,768]{1,0:T(8,128)(2,1)S(1)}, bf16[160,768]{1,0:T(8,128)(2,1)S(1)}, u32[]{:S(2)}, u32[]{:S(2)}) collective-permute-start(bf16[160,768]{1,0:T(8,128)(2,1)S(1)} %get-tuple-element.20), channel_id=1, source_target_pairs={{0,1},{1,2},{2,3},{3,4},{4,5},{5,6},{6,7},{7,0},{8,9},{9,10},{10,1... | collective-permute-start | bytes 737288 | tf_op jit(solution)/shard_map/ppermute | solution.py:120
  72.0 14.6 %collective-permute-start.14 = (bf16[320,768]{1,0:T(8,128)(2,1)S(1)}, bf16[320,768]{1,0:T(8,128)(2,1)S(1)}, u32[]{:S(2)}, u32[]{:S(2)}) collective-permute-start(bf16[320,768]{1,0:T(8,128)(2,1)S(1)} %shard_map.44), channel_id=1, source_target_pairs={{0,7},{1,0},{2,1},{3,2},{4,3},{5,4},{6,5},{7,6},{8,15},{9,8},{10,9... | collective-permute-start | bytes 1474568 | tf_op jit(solution)/shard_map/ppermute | solution.py:128
  77.4 14.7 %collective-permute-start.10 = (bf16[320,768]{1,0:T(8,128)(2,1)S(1)}, bf16[320,768]{1,0:T(8,128)(2,1)S(1)}, u32[]{:S(2)}, u32[]{:S(2)}) collective-permute-start(bf16[320,768]{1,0:T(8,128)(2,1)S(1)} %shard_map.41), channel_id=1, source_target_pairs={{0,1},{1,2},{2,3},{3,4},{4,5},{5,6},{6,7},{7,0},{8,9},{9,10},{10,1... | collective-permute-start | bytes 1474568 | tf_op jit(solution)/shard_map/ppermute | solution.py:127
  86.7 13.7 %collective-permute-start.15 = (bf16[320,768]{1,0:T(8,128)(2,1)S(1)}, bf16[320,768]{1,0:T(8,128)(2,1)S(1)}, u32[]{:S(2)}, u32[]{:S(2)}) collective-permute-start(bf16[320,768]{1,0:T(8,128)(2,1)S(1)} %shard_map.45), channel_id=1, source_target_pairs={{0,7},{1,0},{2,1},{3,2},{4,3},{5,4},{6,5},{7,6},{8,15},{9,8},{10,9... | collective-permute-start | bytes 1474568 | tf_op jit(solution)/shard_map/ppermute | solution.py:128
  92.1 13.7 %collective-permute-start.11 = (bf16[320,768]{1,0:T(8,128)(2,1)S(1)}, bf16[320,768]{1,0:T(8,128)(2,1)S(1)}, u32[]{:S(2)}, u32[]{:S(2)}) collective-permute-start(bf16[320,768]{1,0:T(8,128)(2,1)S(1)} %shard_map.42), channel_id=1, source_target_pairs={{0,1},{1,2},{2,3},{3,4},{4,5},{5,6},{6,7},{7,0},{8,9},{9,10},{10,1... | collective-permute-start | bytes 1474568 | tf_op jit(solution)/shard_map/ppermute | solution.py:127
  100.5 12.8 %collective-permute-start.16 = (bf16[320,768]{1,0:T(8,128)(2,1)S(1)}, bf16[320,768]{1,0:T(8,128)(2,1)S(1)}, u32[]{:S(2)}, u32[]{:S(2)}) collective-permute-start(bf16[320,768]{1,0:T(8,128)(2,1)S(1)} %shard_map.46), channel_id=1, source_target_pairs={{0,7},{1,0},{2,1},{3,2},{4,3},{5,4},{6,5},{7,6},{8,15},{9,8},{10,9... | collective-permute-start | bytes 1474568 | tf_op jit(solution)/shard_map/ppermute | solution.py:128
  106.0 12.5 %collective-permute-start.12 = (bf16[320,768]{1,0:T(8,128)(2,1)S(1)}, bf16[320,768]{1,0:T(8,128)(2,1)S(1)}, u32[]{:S(2)}, u32[]{:S(2)}) collective-permute-start(bf16[320,768]{1,0:T(8,128)(2,1)S(1)} %shard_map.43), channel_id=1, source_target_pairs={{0,1},{1,2},{2,3},{3,4},{4,5},{5,6},{6,7},{7,0},{8,9},{9,10},{10,1... | collective-permute-start | bytes 1474568 | tf_op jit(solution)/shard_map/ppermute | solution.py:127
  118.4 19.3 %copy-start.7 = (s32[128,2]{0,1:T(2,128)S(1)}, s32[128,2]{0,1:T(2,128)}, u32[]{:S(2)}) copy-start(s32[128,2]{0,1:T(2,128)} %param.3) | copy-start | bytes 3076
  119.4 36.6 %all-to-all-start = ((bf16[8,40,768]{2,1,0:T(8,128)(2,1)}), bf16[8,40,768]{2,1,0:T(8,128)(2,1)S(1)}, u32[]{:S(2)}, u32[]{:S(2)}) async-start(bf16[8,40,768]{2,1,0:T(8,128)(2,1)} %bitcast.31), calls=%async_computation | async-start | bytes 983040 | tf_op jit(solution)/shard_map/all_to_all | solution.py:137

commit v12 on v11

--- a/solution.py
+++ b/solution.py
@@ -111,6 +111,19 @@
     )(base, *came)
 
 
+def after(value, *others):
+    anywhere = pl.BlockSpec(memory_space=pl.ANY)
+    return pl.pallas_call(
+        lambda *refs: None,
+        out_shape=jax.ShapeDtypeStruct(value.shape, value.dtype),
+        in_specs=[anywhere] * (1 + len(others)),
+        out_specs=anywhere,
+        input_output_aliases={0: 0},
+        cost_estimate=pl.CostEstimate(flops=0, bytes_accessed=0, transcendentals=0),
+        compiler_params=pltpu.CompilerParams(vmem_limit_bytes=1024 * 1024),
+    )(value, *others)
+
+
 def sum_by_arms(partial, n):
     mid = n // 2
     up = [(i, (i + 1) % n) for i in range(n)]
@@ -161,7 +174,7 @@
     x_rows = lax.ppermute(own, "xp", SWAP)
     c_rows = lax.ppermute(own, "c", SWAP)
     column, other = gather_columns(slab)
-    x_rows, *_ = lax.optimization_barrier((x_rows, *column, *other))
+    x_rows = after(x_rows, *column, *other)
     pieces = (own, c_rows, x_rows, lax.ppermute(x_rows, "c", SWAP))
 
     places = [lax.axis_index("t"), lax.axis_index("xp") * SIZES["c"] + lax.axis_index("c")]

time: 159 us -> 158 us (level)
  local copies, waits for them, and re-layouts: 6.87 us -> 4.16 us
    unnamed x16, local copies, waits for them, and re-layouts: 6.27 us -> 3.55 us
where the time goes in v12:
time: 158 us; the launch traced here: 157 us
  starting transfers between devices  88.1 us (56%)
  waiting for transfers between devices  49.2 us (31%)
  Pallas kernels  13.9 us (9%)
  local copies, waits for them, and re-layouts  4.16 us (3%)
    all_to_all x1, starting transfers between devices, give_back(): lax.all_to_all(summed.reshape(-1, capacity, features), ('xp', 'c', 'e'),...  18.3 us
    all_to_all x1, waiting for transfers between devices, give_back(): lax.all_to_all(summed.reshape(-1, capacity, features), ('xp', 'c', 'e'),...  17.4 us
    ppermute x3, starting transfers between devices, sum_by_arms(): from_above = lax.ppermute(going_down, 't', down)  16 us
    ppermute x3, waiting for transfers between devices, sum_by_arms(): from_above = lax.ppermute(going_down, 't', down)  12.8 us
    ppermute x3, starting transfers between devices, gather_columns(): opposite = lambda value: lax.ppermute(value, ('xh', 'xp'), WEIGHT_SWAP)  10.5 us
    pallas_call x4, Pallas kernels, product(): pl.pallas_call(functools.partial(product_kernel, pieces=len(pieces), outs...  10.5 us
    ppermute x1, starting transfers between devices, gather_columns(): pair = jnp.stack([slab, lax.ppermute(slab, 'h', SWAP)])  7.62 us
    ppermute x1, starting transfers between devices, gather_columns(): lax.ppermute(pair, 'm', turn(1))  6.84 us
  transfers between devices with their start and end apart: 18, of which 10 were waited for; matrix products, arithmetic and copies ran while one was open for 1% of the time, Pallas kernels for 6%

profile of v12, /device:TPU:1, one launch (start us, length us, event | category | flops | bytes accessed | tf_op | source)
XLA Modules:
  0.0 156.8 jit_solution(6818723209728112325)
XLA Ops:
  0.0 3.9 %collective-permute-start.1 = (bf16[8,80,1024]{2,1,0:T(8,128)(2,1)}, bf16[8,80,1024]{2,1,0:T(8,128)(2,1)S(1)}, u32[]{:S(2)}, u32[]{:S(2)}) collective-permute-start(bf16[8,80,1024]{2,1,0:T(8,128)(2,1)} %bitcast.33), channel_id=1, source_target_pairs={{0,192},{192,0},{1,193},{193,1},{2,194},{194,2},{3,195},{195,3},{4... | collective-permute-start | bytes 3932168 | tf_op jit(solution)/shard_map/ppermute | solution.py:174
  3.9 7.6 %collective-permute-start.2 = (bf16[64,1024]{1,0:T(8,128)(2,1)}, bf16[64,1024]{1,0:T(8,128)(2,1)S(1)}, u32[]{:S(2)}, u32[]{:S(2)}) collective-permute-start(bf16[64,1024]{1,0:T(8,128)(2,1)} %bitcast.41), channel_id=1, source_target_pairs={{0,96},{96,0},{1,97},{97,1},{2,98},{98,2},{3,99},{99,3},{4,100},{1... | collective-permute-start | bytes 393224 | tf_op jit(solution)/shard_map/ppermute | solution.py:22
  11.6 2.6 %collective-permute-done.2 = bf16[64,1024]{1,0:T(8,128)(2,1)S(1)} collective-permute-done((bf16[64,1024]{1,0:T(8,128)(2,1)}, bf16[64,1024]{1,0:T(8,128)(2,1)S(1)}, u32[]{:S(2)}, u32[]{:S(2)}) %collective-permute-start.2) | collective-permute-done | bytes 131104 | tf_op jit(solution)/shard_map/ppermute | solution.py:22
  14.1 0.9 pad_maximum_fusion.refs_1_.refs_4_
  15.1 0.0 copy-start
  15.1 6.8 %collective-permute-start.3 = (bf16[2,64,1024]{2,1,0:T(8,128)(2,1)S(1)}, bf16[2,64,1024]{2,1,0:T(8,128)(2,1)S(1)}, u32[]{:S(2)}, u32[]{:S(2)}) collective-permute-start(bf16[2,64,1024]{2,1,0:T(8,128)(2,1)S(1)} %pad_maximum_fusion.refs_1_.refs_4_), channel_id=1, source_target_pairs={{0,32},{32,64},{64,0},{1,33},{33,65},{65,1},{2,34},{34,66},{66,2},... | collective-permute-start | bytes 786440 | tf_op jit(solution)/shard_map/ppermute | solution.py:23
  21.9 6.5 %collective-permute-start.4 = (bf16[2,64,1024]{2,1,0:T(8,128)(2,1)S(1)}, bf16[2,64,1024]{2,1,0:T(8,128)(2,1)S(1)}, u32[]{:S(2)}, u32[]{:S(2)}) collective-permute-start(bf16[2,64,1024]{2,1,0:T(8,128)(2,1)S(1)} %pad_maximum_fusion.refs_1_.refs_4_), channel_id=1, source_target_pairs={{0,64},{32,0},{64,32},{1,65},{33,1},{65,33},{2,66},{34,2},{66,34},... | collective-permute-start | bytes 786440 | tf_op jit(solution)/shard_map/ppermute | solution.py:23
  28.4 3.0 %collective-permute-start.5 = (bf16[2,64,1024]{2,1,0:T(8,128)(2,1)S(1)}, bf16[2,64,1024]{2,1,0:T(8,128)(2,1)S(1)}, u32[]{:S(2)}, u32[]{:S(2)}) collective-permute-start(bf16[2,64,1024]{2,1,0:T(8,128)(2,1)S(1)} %pad_maximum_fusion.refs_1_.refs_4_), channel_id=1, source_target_pairs={{0,576},{192,384},{384,192},{576,0},{1,577},{193,385},{385,193},{5... | collective-permute-start | bytes 786440 | tf_op jit(solution)/shard_map/ppermute | solution.py:21
  31.4 0.0 collective-permute-done.3.refs_2_.refs_5_
  31.5 4.3 %collective-permute-start.6 = (bf16[2,64,1024]{2,1,0:T(8,128)(2,1)S(1)}, bf16[2,64,1024]{2,1,0:T(8,128)(2,1)S(1)}, u32[]{:S(2)}, u32[]{:S(2)}) collective-permute-start(bf16[2,64,1024]{2,1,0:T(8,128)(2,1)S(1)} %collective-permute-done.3.refs_2_.refs_5_), channel_id=1, source_target_pairs={{0,576},{192,384},{384,192},{576,0},{1,577},{193,385},{385,193},{5... | collective-permute-start | bytes 786440 | tf_op jit(solution)/shard_map/ppermute | solution.py:21
  35.8 2.9 %collective-permute-done.4.refs_3_.refs_6_ = bf16[2,64,1024]{2,1,0:T(8,128)(2,1)S(1)} collective-permute-done((bf16[2,64,1024]{2,1,0:T(8,128)(2,1)S(1)}, bf16[2,64,1024]{2,1,0:T(8,128)(2,1)S(1)}, u32[]{:S(2)}, u32[]{:S(2)}) %collective-permute-start.4) | collective-permute-done | bytes 262176 | tf_op jit(solution)/shard_map/ppermute | solution.py:23
  38.7 3.2 %collective-permute-start.7 = (bf16[2,64,1024]{2,1,0:T(8,128)(2,1)S(1)}, bf16[2,64,1024]{2,1,0:T(8,128)(2,1)S(1)}, u32[]{:S(2)}, u32[]{:S(2)}) collective-permute-start(bf16[2,64,1024]{2,1,0:T(8,128)(2,1)S(1)} %collective-permute-done.4.refs_3_.refs_6_), channel_id=1, source_target_pairs={{0,576},{192,384},{384,192},{576,0},{1,577},{193,385},{385,193},{5... | collective-permute-start | bytes 786440 | tf_op jit(solution)/shard_map/ppermute | solution.py:21
  41.9 3.1 %collective-permute-start = (bf16[8,80,1024]{2,1,0:T(8,128)(2,1)}, bf16[8,80,1024]{2,1,0:T(8,128)(2,1)}, u32[]{:S(2)}, u32[]{:S(2)}) collective-permute-start(bf16[8,80,1024]{2,1,0:T(8,128)(2,1)} %bitcast.34), channel_id=1, source_target_pairs={{0,16},{16,0},{1,17},{17,1},{2,18},{18,2},{3,19},{19,3},{4,20},{20... | collective-permute-start | bytes 3932168 | tf_op jit(solution)/shard_map/ppermute | solution.py:175
  45.0 0.0 collective-permute-done.5.refs_4_.refs_7_
  45.0 0.0 copy-start.1
  45.1 0.0 collective-permute-done.6.refs_5_.refs_8_
  45.1 0.0 copy-start.3
  45.1 5.1 %collective-permute-done.7.refs_6_.refs_9_ = bf16[2,64,1024]{2,1,0:T(8,128)(2,1)S(1)} collective-permute-done((bf16[2,64,1024]{2,1,0:T(8,128)(2,1)S(1)}, bf16[2,64,1024]{2,1,0:T(8,128)(2,1)S(1)}, u32[]{:S(2)}, u32[]{:S(2)}) %collective-permute-start.7) | collective-permute-done | bytes 262176 | tf_op jit(solution)/shard_map/ppermute | solution.py:21
  50.2 0.0 collective-permute-done.1.refs_0_
  50.2 0.7 copy-done.5
  50.9 3.4 %collective-permute-start.8 = (bf16[8,80,1024]{2,1,0:T(8,128)(2,1)S(1)}, bf16[8,80,1024]{2,1,0:T(8,128)(2,1)}, u32[]{:S(2)}, u32[]{:S(2)}) collective-permute-start(bf16[8,80,1024]{2,1,0:T(8,128)(2,1)S(1)} %shard_map.37.refs_2_), channel_id=1, source_target_pairs={{0,16},{16,0},{1,17},{17,1},{2,18},{18,2},{3,19},{19,3},{4,20},{20... | collective-permute-start | bytes 3932168 | tf_op jit(solution)/shard_map/ppermute | solution.py:178
  54.3 0.0 collective-permute-done.refs_1_
  54.3 2.8 %collective-permute-done.8.refs_3_ = bf16[8,80,1024]{2,1,0:T(8,128)(2,1)} collective-permute-done((bf16[8,80,1024]{2,1,0:T(8,128)(2,1)S(1)}, bf16[8,80,1024]{2,1,0:T(8,128)(2,1)}, u32[]{:S(2)}, u32[]{:S(2)}) %collective-permute-start.8) | collective-permute-done | bytes 1310752 | tf_op jit(solution)/shard_map/ppermute | solution.py:178
  57.1 0.9 copy-done.2
  58.0 0.9 copy-done.4
  59.0 0.9 copy-done.6
  59.9 1.7 %shard_map.41 = (bf16[160,768]{1,0:T(8,128)(2,1)S(1)}, bf16[160,768]{1,0:T(8,128)(2,1)S(1)}) custom-call(s32[1]{0:T(128)} %bitcast.26.here, s32[1]{0:T(128)} %bitcast.27.place, bf16[8,80,1024]{2,1,0:T(8,128)(2,1)S(1)} %bitcast.35, bf16[8,80,1024]{2,1,0:T(8,128)(2,1)} %collective-permute-done.refs_1_, bf16[8,80,1024]{2,1,0:T(8,128)(2,1)S(1)} %shard_map.37.refs_2_, ...), custom_call_target="tpu_custom_call" | custom-call | flops 503316480 | bytes 2719744 | tf_op jit(solution)/shard_map/pallas_call | solution.py:73
  61.7 4.2 %collective-permute-start.13 = (bf16[160,768]{1,0:T(8,128)(2,1)S(1)}, bf16[160,768]{1,0:T(8,128)(2,1)S(1)}, u32[]{:S(2)}, u32[]{:S(2)}) collective-permute-start(bf16[160,768]{1,0:T(8,128)(2,1)S(1)} %get-tuple-element.22), channel_id=1, source_target_pairs={{0,7},{1,0},{2,1},{3,2},{4,3},{5,4},{6,5},{7,6},{8,15},{9,8},{10,9... | collective-permute-start | bytes 737288 | tf_op jit(solution)/shard_map/ppermute | solution.py:134
  65.8 1.9 %collective-permute-start.9 = (bf16[160,768]{1,0:T(8,128)(2,1)S(1)}, bf16[160,768]{1,0:T(8,128)(2,1)S(1)}, u32[]{:S(2)}, u32[]{:S(2)}) collective-permute-start(bf16[160,768]{1,0:T(8,128)(2,1)S(1)} %get-tuple-element.18), channel_id=1, source_target_pairs={{0,1},{1,2},{2,3},{3,4},{4,5},{5,6},{6,7},{7,0},{8,9},{9,10},{10,1... | collective-permute-start | bytes 737288 | tf_op jit(solution)/shard_map/ppermute | solution.py:133
  67.8 2.6 %shard_map.40 = (bf16[320,768]{1,0:T(8,128)(2,1)S(1)}, bf16[320,768]{1,0:T(8,128)(2,1)S(1)}) custom-call(s32[1]{0:T(128)} %bitcast.26.here, s32[1]{0:T(128)} %bitcast.27.place, bf16[8,80,1024]{2,1,0:T(8,128)(2,1)S(1)} %bitcast.36, bf16[8,80,1024]{2,1,0:T(8,128)(2,1)} %collective-permute-done.refs_1_, bf16[8,80,1024]{2,1,0:T(8,128)(2,1)S(1)} %shard_map.37.refs_2_, ...), custom_call_target="tpu_custom_call" | custom-call | flops 1006632960 | bytes 3866624 | tf_op jit(solution)/shard_map/pallas_call | solution.py:73
  70.4 0.4 collective-permute-done.13.refs_1_
  70.8 0.1 shard_map.45
  70.9 5.3 %collective-permute-start.14 = (bf16[320,768]{1,0:T(8,128)(2,1)S(1)}, bf16[320,768]{1,0:T(8,128)(2,1)S(1)}, u32[]{:S(2)}, u32[]{:S(2)}) collective-permute-start(bf16[320,768]{1,0:T(8,128)(2,1)S(1)} %shard_map.45), channel_id=1, source_target_pairs={{0,7},{1,0},{2,1},{3,2},{4,3},{5,4},{6,5},{7,6},{8,15},{9,8},{10,9... | collective-permute-start | bytes 1474568 | tf_op jit(solution)/shard_map/ppermute | solution.py:141
  76.2 0.0 collective-permute-done.9.refs_1_
  76.2 0.1 shard_map.42
  76.3 1.9 %collective-permute-start.10 = (bf16[320,768]{1,0:T(8,128)(2,1)S(1)}, bf16[320,768]{1,0:T(8,128)(2,1)S(1)}, u32[]{:S(2)}, u32[]{:S(2)}) collective-permute-start(bf16[320,768]{1,0:T(8,128)(2,1)S(1)} %shard_map.42), channel_id=1, source_target_pairs={{0,1},{1,2},{2,3},{3,4},{4,5},{5,6},{6,7},{7,0},{8,9},{9,10},{10,1... | collective-permute-start | bytes 1474568 | tf_op jit(solution)/shard_map/ppermute | solution.py:140
  78.2 2.6 %shard_map.39 = (bf16[320,768]{1,0:T(8,128)(2,1)S(1)}, bf16[320,768]{1,0:T(8,128)(2,1)S(1)}) custom-call(s32[1]{0:T(128)} %bitcast.26.here, s32[1]{0:T(128)} %bitcast.27.place, bf16[8,80,1024]{2,1,0:T(8,128)(2,1)S(1)} %bitcast.37, bf16[8,80,1024]{2,1,0:T(8,128)(2,1)} %collective-permute-done.refs_1_, bf16[8,80,1024]{2,1,0:T(8,128)(2,1)S(1)} %shard_map.37.refs_2_, ...), custom_call_target="tpu_custom_call" | custom-call | flops 1006632960 | bytes 3866624 | tf_op jit(solution)/shard_map/pallas_call | solution.py:73
  80.8 3.6 %shard_map.38 = (bf16[320,768]{1,0:T(8,128)(2,1)S(1)}, bf16[320,768]{1,0:T(8,128)(2,1)S(1)}, bf16[320,768]{1,0:T(8,128)(2,1)S(1)}) custom-call(s32[1]{0:T(128)} %bitcast.26.here, s32[1]{0:T(128)} %bitcast.27.place, bf16[8,80,1024]{2,1,0:T(8,128)(2,1)S(1)} %bitcast.38, bf16[8,80,1024]{2,1,0:T(8,128)(2,1)} %collective-permute-done.refs_1_, ...), custom_call_target="tpu_custom_call" | custom-call | flops 1509949440 | bytes 5013504 | tf_op jit(solution)/shard_map/pallas_call | solution.py:73
  84.4 1.1 collective-permute-done.14.refs_1_
  85.5 0.1 shard_map.46
  85.6 5.3 %collective-permute-start.15 = (bf16[320,768]{1,0:T(8,128)(2,1)S(1)}, bf16[320,768]{1,0:T(8,128)(2,1)S(1)}, u32[]{:S(2)}, u32[]{:S(2)}) collective-permute-start(bf16[320,768]{1,0:T(8,128)(2,1)S(1)} %shard_map.46), channel_id=1, source_target_pairs={{0,7},{1,0},{2,1},{3,2},{4,3},{5,4},{6,5},{7,6},{8,15},{9,8},{10,9... | collective-permute-start | bytes 1474568 | tf_op jit(solution)/shard_map/ppermute | solution.py:141
  90.9 0.0 collective-permute-done.10.refs_1_
  90.9 0.1 shard_map.43
  91.1 1.9 %collective-permute-start.11 = (bf16[320,768]{1,0:T(8,128)(2,1)S(1)}, bf16[320,768]{1,0:T(8,128)(2,1)S(1)}, u32[]{:S(2)}, u32[]{:S(2)}) collective-permute-start(bf16[320,768]{1,0:T(8,128)(2,1)S(1)} %shard_map.43), channel_id=1, source_target_pairs={{0,1},{1,2},{2,3},{3,4},{4,5},{5,6},{6,7},{7,0},{8,9},{9,10},{10,1... | collective-permute-start | bytes 1474568 | tf_op jit(solution)/shard_map/ppermute | solution.py:140
  93.0 6.3 %collective-permute-done.15.refs_1_ = bf16[320,768]{1,0:T(8,128)(2,1)S(1)} collective-permute-done((bf16[320,768]{1,0:T(8,128)(2,1)S(1)}, bf16[320,768]{1,0:T(8,128)(2,1)S(1)}, u32[]{:S(2)}, u32[]{:S(2)}) %collective-permute-start.15) | collective-permute-done | bytes 491552 | tf_op jit(solution)/shard_map/ppermute | solution.py:141
  99.3 0.1 shard_map.47
  99.4 5.3 %collective-permute-start.16 = (bf16[320,768]{1,0:T(8,128)(2,1)S(1)}, bf16[320,768]{1,0:T(8,128)(2,1)S(1)}, u32[]{:S(2)}, u32[]{:S(2)}) collective-permute-start(bf16[320,768]{1,0:T(8,128)(2,1)S(1)} %shard_map.47), channel_id=1, source_target_pairs={{0,7},{1,0},{2,1},{3,2},{4,3},{5,4},{6,5},{7,6},{8,15},{9,8},{10,9... | collective-permute-start | bytes 1474568 | tf_op jit(solution)/shard_map/ppermute | solution.py:141
  104.7 0.0 collective-permute-done.11.refs_1_
  104.7 0.1 shard_map.44
  104.9 1.9 %collective-permute-start.12 = (bf16[320,768]{1,0:T(8,128)(2,1)S(1)}, bf16[320,768]{1,0:T(8,128)(2,1)S(1)}, u32[]{:S(2)}, u32[]{:S(2)}) collective-permute-start(bf16[320,768]{1,0:T(8,128)(2,1)S(1)} %shard_map.44), channel_id=1, source_target_pairs={{0,1},{1,2},{2,3},{3,4},{4,5},{5,6},{6,7},{7,0},{8,9},{9,10},{10,1... | collective-permute-start | bytes 1474568 | tf_op jit(solution)/shard_map/ppermute | solution.py:140
  106.8 5.4 %collective-permute-done.16.refs_2_ = bf16[320,768]{1,0:T(8,128)(2,1)S(1)} collective-permute-done((bf16[320,768]{1,0:T(8,128)(2,1)S(1)}, bf16[320,768]{1,0:T(8,128)(2,1)S(1)}, u32[]{:S(2)}, u32[]{:S(2)}) %collective-permute-start.16) | collective-permute-done | bytes 491552 | tf_op jit(solution)/shard_map/ppermute | solution.py:141
  112.2 5.2 %collective-permute-done.12.refs_1_ = bf16[320,768]{1,0:T(8,128)(2,1)S(1)} collective-permute-done((bf16[320,768]{1,0:T(8,128)(2,1)S(1)}, bf16[320,768]{1,0:T(8,128)(2,1)S(1)}, u32[]{:S(2)}, u32[]{:S(2)}) %collective-permute-start.12) | collective-permute-done | bytes 491552 | tf_op jit(solution)/shard_map/ppermute | solution.py:140
  117.4 1.0 shard_map.48
  118.3 18.3 %all-to-all-start = ((bf16[8,40,768]{2,1,0:T(8,128)(2,1)}), bf16[8,40,768]{2,1,0:T(8,128)(2,1)S(1)}, u32[]{:S(2)}, u32[]{:S(2)}) async-start(bf16[8,40,768]{2,1,0:T(8,128)(2,1)} %bitcast.31), calls=%async_computation | async-start | bytes 983040 | tf_op jit(solution)/shard_map/all_to_all | solution.py:150
  136.7 0.0 copy-done.7
  136.7 0.1 copy.15
  136.8 0.2 reduce_window_sum.11
  137.0 0.1 copy.16
  137.0 0.1 copy.17
  137.2 0.1 copy.19
  137.3 0.1 eq.43
  137.4 0.1 stack.105.refs_0_
  137.5 17.4 %all-to-all-done = bf16[8,40,768]{2,1,0:T(8,128)(2,1)S(1)} async-done(((bf16[8,40,768]{2,1,0:T(8,128)(2,1)}), bf16[8,40,768]{2,1,0:T(8,128)(2,1)S(1)}, u32[]{:S(2)}, u32[]{:S(2)}) %all-to-all-start) | async-done | bytes 491552 | tf_op jit(solution)/shard_map/all_to_all | solution.py:150
  154.9 1.9 %shard_map.49 = bf16[128,3072]{1,0:T(8,128)(2,1)} custom-call(s32[24]{0:T(128)S(1)} %stack.105.refs_0_, bf16[128,80]{1,0:T(8,128)(2,1)S(1)} %and_convert_fusion.refs_1_, bf16[4,80,768]{2,1,0:T(8,128)(2,1)S(1)} %bitcast.39), custom_call_target="tpu_custom_call" | custom-call | tf_op jit(solution)/shard_map/pallas_call | solution.py:200
  (16 shorter events, 0.1 us)
Async XLA Ops:
  0.0 50.2 %collective-permute-start.1 = (bf16[8,80,1024]{2,1,0:T(8,128)(2,1)}, bf16[8,80,1024]{2,1,0:T(8,128)(2,1)S(1)}, u32[]{:S(2)}, u32[]{:S(2)}) collective-permute-start(bf16[8,80,1024]{2,1,0:T(8,128)(2,1)} %bitcast.33), channel_id=1, source_target_pairs={{0,192},{192,0},{1,193},{193,1},{2,194},{194,2},{3,195},{195,3},{4... | collective-permute-start | bytes 3932168 | tf_op jit(solution)/shard_map/ppermute | solution.py:174
  3.9 10.2 %collective-permute-start.2 = (bf16[64,1024]{1,0:T(8,128)(2,1)}, bf16[64,1024]{1,0:T(8,128)(2,1)S(1)}, u32[]{:S(2)}, u32[]{:S(2)}) collective-permute-start(bf16[64,1024]{1,0:T(8,128)(2,1)} %bitcast.41), channel_id=1, source_target_pairs={{0,96},{96,0},{1,97},{97,1},{2,98},{98,2},{3,99},{99,3},{4,100},{1... | collective-permute-start | bytes 393224 | tf_op jit(solution)/shard_map/ppermute | solution.py:22
  15.1 42.0 %copy-start = (bf16[1,1,8,2,40,1024]{5,4,3,2,1,0:T(8,128)(2,1)S(1)}, bf16[1,1,8,2,40,1024]{5,4,3,2,1,0:T(8,128)(2,1)}, u32[]{:S(2)}) copy-start(bf16[1,1,8,2,40,1024]{5,4,3,2,1,0:T(8,128)(2,1)} %param.4) | copy-start | bytes 3932164
  15.1 16.4 %collective-permute-start.3 = (bf16[2,64,1024]{2,1,0:T(8,128)(2,1)S(1)}, bf16[2,64,1024]{2,1,0:T(8,128)(2,1)S(1)}, u32[]{:S(2)}, u32[]{:S(2)}) collective-permute-start(bf16[2,64,1024]{2,1,0:T(8,128)(2,1)S(1)} %pad_maximum_fusion.refs_1_.refs_4_), channel_id=1, source_target_pairs={{0,32},{32,64},{64,0},{1,33},{33,65},{65,1},{2,34},{34,66},{66,2},... | collective-permute-start | bytes 786440 | tf_op jit(solution)/shard_map/ppermute | solution.py:23
  21.9 16.8 %collective-permute-start.4 = (bf16[2,64,1024]{2,1,0:T(8,128)(2,1)S(1)}, bf16[2,64,1024]{2,1,0:T(8,128)(2,1)S(1)}, u32[]{:S(2)}, u32[]{:S(2)}) collective-permute-start(bf16[2,64,1024]{2,1,0:T(8,128)(2,1)S(1)} %pad_maximum_fusion.refs_1_.refs_4_), channel_id=1, source_target_pairs={{0,64},{32,0},{64,32},{1,65},{33,1},{65,33},{2,66},{34,2},{66,34},... | collective-permute-start | bytes 786440 | tf_op jit(solution)/shard_map/ppermute | solution.py:23
  28.4 16.6 %collective-permute-start.5 = (bf16[2,64,1024]{2,1,0:T(8,128)(2,1)S(1)}, bf16[2,64,1024]{2,1,0:T(8,128)(2,1)S(1)}, u32[]{:S(2)}, u32[]{:S(2)}) collective-permute-start(bf16[2,64,1024]{2,1,0:T(8,128)(2,1)S(1)} %pad_maximum_fusion.refs_1_.refs_4_), channel_id=1, source_target_pairs={{0,576},{192,384},{384,192},{576,0},{1,577},{193,385},{385,193},{5... | collective-permute-start | bytes 786440 | tf_op jit(solution)/shard_map/ppermute | solution.py:21
  31.5 13.6 %collective-permute-start.6 = (bf16[2,64,1024]{2,1,0:T(8,128)(2,1)S(1)}, bf16[2,64,1024]{2,1,0:T(8,128)(2,1)S(1)}, u32[]{:S(2)}, u32[]{:S(2)}) collective-permute-start(bf16[2,64,1024]{2,1,0:T(8,128)(2,1)S(1)} %collective-permute-done.3.refs_2_.refs_5_), channel_id=1, source_target_pairs={{0,576},{192,384},{384,192},{576,0},{1,577},{193,385},{385,193},{5... | collective-permute-start | bytes 786440 | tf_op jit(solution)/shard_map/ppermute | solution.py:21
  38.7 11.5 %collective-permute-start.7 = (bf16[2,64,1024]{2,1,0:T(8,128)(2,1)S(1)}, bf16[2,64,1024]{2,1,0:T(8,128)(2,1)S(1)}, u32[]{:S(2)}, u32[]{:S(2)}) collective-permute-start(bf16[2,64,1024]{2,1,0:T(8,128)(2,1)S(1)} %collective-permute-done.4.refs_3_.refs_6_), channel_id=1, source_target_pairs={{0,576},{192,384},{384,192},{576,0},{1,577},{193,385},{385,193},{5... | collective-permute-start | bytes 786440 | tf_op jit(solution)/shard_map/ppermute | solution.py:21
  41.9 12.5 %collective-permute-start = (bf16[8,80,1024]{2,1,0:T(8,128)(2,1)}, bf16[8,80,1024]{2,1,0:T(8,128)(2,1)}, u32[]{:S(2)}, u32[]{:S(2)}) collective-permute-start(bf16[8,80,1024]{2,1,0:T(8,128)(2,1)} %bitcast.34), channel_id=1, source_target_pairs={{0,16},{16,0},{1,17},{17,1},{2,18},{18,2},{3,19},{19,3},{4,20},{20... | collective-permute-start | bytes 3932168 | tf_op jit(solution)/shard_map/ppermute | solution.py:175
  45.0 5.2 %copy-start.1 = (bf16[2,64,1024]{2,1,0:T(8,128)(2,1)}, bf16[2,64,1024]{2,1,0:T(8,128)(2,1)S(1)}, u32[]{:S(2)}) copy-start(bf16[2,64,1024]{2,1,0:T(8,128)(2,1)S(1)} %collective-permute-done.5.refs_4_.refs_7_) | copy-start | bytes 786436
  45.1 5.2 %copy-start.3 = (bf16[2,64,1024]{2,1,0:T(8,128)(2,1)}, bf16[2,64,1024]{2,1,0:T(8,128)(2,1)S(1)}, u32[]{:S(2)}) copy-start(bf16[2,64,1024]{2,1,0:T(8,128)(2,1)S(1)} %collective-permute-done.6.refs_5_.refs_8_) | copy-start | bytes 786436
  50.2 0.7 copy-start.5
  50.9 6.2 %collective-permute-start.8 = (bf16[8,80,1024]{2,1,0:T(8,128)(2,1)S(1)}, bf16[8,80,1024]{2,1,0:T(8,128)(2,1)}, u32[]{:S(2)}, u32[]{:S(2)}) collective-permute-start(bf16[8,80,1024]{2,1,0:T(8,128)(2,1)S(1)} %shard_map.37.refs_2_), channel_id=1, source_target_pairs={{0,16},{16,0},{1,17},{17,1},{2,18},{18,2},{3,19},{19,3},{4,20},{20... | collective-permute-start | bytes 3932168 | tf_op jit(solution)/shard_map/ppermute | solution.py:178
  57.1 1.0 copy-start.2
  58.0 0.9 copy-start.4
  59.0 0.9 copy-start.6
  61.7 9.1 %collective-permute-start.13 = (bf16[160,768]{1,0:T(8,128)(2,1)S(1)}, bf16[160,768]{1,0:T(8,128)(2,1)S(1)}, u32[]{:S(2)}, u32[]{:S(2)}) collective-permute-start(bf16[160,768]{1,0:T(8,128)(2,1)S(1)} %get-tuple-element.22), channel_id=1, source_target_pairs={{0,7},{1,0},{2,1},{3,2},{4,3},{5,4},{6,5},{7,6},{8,15},{9,8},{10,9... | collective-permute-start | bytes 737288 | tf_op jit(solution)/shard_map/ppermute | solution.py:134
  65.8 10.3 %collective-permute-start.9 = (bf16[160,768]{1,0:T(8,128)(2,1)S(1)}, bf16[160,768]{1,0:T(8,128)(2,1)S(1)}, u32[]{:S(2)}, u32[]{:S(2)}) collective-permute-start(bf16[160,768]{1,0:T(8,128)(2,1)S(1)} %get-tuple-element.18), channel_id=1, source_target_pairs={{0,1},{1,2},{2,3},{3,4},{4,5},{5,6},{6,7},{7,0},{8,9},{9,10},{10,1... | collective-permute-start | bytes 737288 | tf_op jit(solution)/shard_map/ppermute | solution.py:133
  70.9 14.6 %collective-permute-start.14 = (bf16[320,768]{1,0:T(8,128)(2,1)S(1)}, bf16[320,768]{1,0:T(8,128)(2,1)S(1)}, u32[]{:S(2)}, u32[]{:S(2)}) collective-permute-start(bf16[320,768]{1,0:T(8,128)(2,1)S(1)} %shard_map.45), channel_id=1, source_target_pairs={{0,7},{1,0},{2,1},{3,2},{4,3},{5,4},{6,5},{7,6},{8,15},{9,8},{10,9... | collective-permute-start | bytes 1474568 | tf_op jit(solution)/shard_map/ppermute | solution.py:141
  76.3 14.6 %collective-permute-start.10 = (bf16[320,768]{1,0:T(8,128)(2,1)S(1)}, bf16[320,768]{1,0:T(8,128)(2,1)S(1)}, u32[]{:S(2)}, u32[]{:S(2)}) collective-permute-start(bf16[320,768]{1,0:T(8,128)(2,1)S(1)} %shard_map.42), channel_id=1, source_target_pairs={{0,1},{1,2},{2,3},{3,4},{4,5},{5,6},{6,7},{7,0},{8,9},{9,10},{10,1... | collective-permute-start | bytes 1474568 | tf_op jit(solution)/shard_map/ppermute | solution.py:140
  85.6 13.7 %collective-permute-start.15 = (bf16[320,768]{1,0:T(8,128)(2,1)S(1)}, bf16[320,768]{1,0:T(8,128)(2,1)S(1)}, u32[]{:S(2)}, u32[]{:S(2)}) collective-permute-start(bf16[320,768]{1,0:T(8,128)(2,1)S(1)} %shard_map.46), channel_id=1, source_target_pairs={{0,7},{1,0},{2,1},{3,2},{4,3},{5,4},{6,5},{7,6},{8,15},{9,8},{10,9... | collective-permute-start | bytes 1474568 | tf_op jit(solution)/shard_map/ppermute | solution.py:141
  91.1 13.7 %collective-permute-start.11 = (bf16[320,768]{1,0:T(8,128)(2,1)S(1)}, bf16[320,768]{1,0:T(8,128)(2,1)S(1)}, u32[]{:S(2)}, u32[]{:S(2)}) collective-permute-start(bf16[320,768]{1,0:T(8,128)(2,1)S(1)} %shard_map.43), channel_id=1, source_target_pairs={{0,1},{1,2},{2,3},{3,4},{4,5},{5,6},{6,7},{7,0},{8,9},{9,10},{10,1... | collective-permute-start | bytes 1474568 | tf_op jit(solution)/shard_map/ppermute | solution.py:140
  99.4 12.8 %collective-permute-start.16 = (bf16[320,768]{1,0:T(8,128)(2,1)S(1)}, bf16[320,768]{1,0:T(8,128)(2,1)S(1)}, u32[]{:S(2)}, u32[]{:S(2)}) collective-permute-start(bf16[320,768]{1,0:T(8,128)(2,1)S(1)} %shard_map.47), channel_id=1, source_target_pairs={{0,7},{1,0},{2,1},{3,2},{4,3},{5,4},{6,5},{7,6},{8,15},{9,8},{10,9... | collective-permute-start | bytes 1474568 | tf_op jit(solution)/shard_map/ppermute | solution.py:141
  104.9 12.5 %collective-permute-start.12 = (bf16[320,768]{1,0:T(8,128)(2,1)S(1)}, bf16[320,768]{1,0:T(8,128)(2,1)S(1)}, u32[]{:S(2)}, u32[]{:S(2)}) collective-permute-start(bf16[320,768]{1,0:T(8,128)(2,1)S(1)} %shard_map.44), channel_id=1, source_target_pairs={{0,1},{1,2},{2,3},{3,4},{4,5},{5,6},{6,7},{7,0},{8,9},{9,10},{10,1... | collective-permute-start | bytes 1474568 | tf_op jit(solution)/shard_map/ppermute | solution.py:140
  117.3 19.3 %copy-start.7 = (s32[128,2]{0,1:T(2,128)S(1)}, s32[128,2]{0,1:T(2,128)}, u32[]{:S(2)}) copy-start(s32[128,2]{0,1:T(2,128)} %param.3) | copy-start | bytes 3076
  118.3 36.6 %all-to-all-start = ((bf16[8,40,768]{2,1,0:T(8,128)(2,1)}), bf16[8,40,768]{2,1,0:T(8,128)(2,1)S(1)}, u32[]{:S(2)}, u32[]{:S(2)}) async-start(bf16[8,40,768]{2,1,0:T(8,128)(2,1)} %bitcast.31), calls=%async_computation | async-start | bytes 983040 | tf_op jit(solution)/shard_map/all_to_all | solution.py:150

commit v13 on v12

--- a/solution.py
+++ b/solution.py
@@ -175,7 +175,7 @@
     c_rows = lax.ppermute(own, "c", SWAP)
     column, other = gather_columns(slab)
     x_rows = after(x_rows, *column, *other)
-    pieces = (own, c_rows, x_rows, lax.ppermute(x_rows, "c", SWAP))
+    pieces = (after(own, column[0]), c_rows, x_rows, lax.ppermute(x_rows, "c", SWAP))
 
     places = [lax.axis_index("t"), lax.axis_index("xp") * SIZES["c"] + lax.axis_index("c")]
     where = [place.astype(jnp.int32).reshape(1) for place in places]

time: 158 us -> 155 us (0.981)
    unnamed x16 -> x17, local copies, waits for them, and re-layouts: 3.55 us -> 2.07 us
where the time goes in v13:
time: 155 us; the launch traced here: 154 us
  starting transfers between devices  88.5 us (57%)
  waiting for transfers between devices  48.3 us (31%)
  Pallas kernels  13.9 us (9%)
  local copies, waits for them, and re-layouts  2.68 us (2%)
    all_to_all x1, starting transfers between devices, give_back(): lax.all_to_all(summed.reshape(-1, capacity, features), ('xp', 'c', 'e'),...  18.5 us
    all_to_all x1, waiting for transfers between devices, give_back(): lax.all_to_all(summed.reshape(-1, capacity, features), ('xp', 'c', 'e'),...  17.4 us
    ppermute x3, starting transfers between devices, sum_by_arms(): from_above = lax.ppermute(going_down, 't', down)  16 us
    ppermute x3, waiting for transfers between devices, sum_by_arms(): from_above = lax.ppermute(going_down, 't', down)  12.7 us
    ppermute x3, starting transfers between devices, gather_columns(): opposite = lambda value: lax.ppermute(value, ('xh', 'xp'), WEIGHT_SWAP)  10.7 us
    pallas_call x4, Pallas kernels, product(): pl.pallas_call(functools.partial(product_kernel, pieces=len(pieces), outs...  10.5 us
    ppermute x1, starting transfers between devices, gather_columns(): pair = jnp.stack([slab, lax.ppermute(slab, 'h', SWAP)])  7.62 us
    ppermute x1, starting transfers between devices, gather_columns(): lax.ppermute(pair, 'm', turn(1))  6.6 us
  transfers between devices with their start and end apart: 18, of which 10 were waited for; matrix products, arithmetic and copies ran while one was open for 1% of the time, Pallas kernels for 6%

profile of v13, /device:TPU:1, one launch (start us, length us, event | category | flops | bytes accessed | tf_op | source)
XLA Modules:
  0.0 154.0 jit_solution(14030599205563375398)
XLA Ops:
  0.0 1.4 copy.24
  1.4 3.9 %collective-permute-start.2 = (bf16[8,80,1024]{2,1,0:T(8,128)(2,1)S(1)}, bf16[8,80,1024]{2,1,0:T(8,128)(2,1)S(1)}, u32[]{:S(2)}, u32[]{:S(2)}) collective-permute-start(bf16[8,80,1024]{2,1,0:T(8,128)(2,1)S(1)} %bitcast.33), channel_id=1, source_target_pairs={{0,192},{192,0},{1,193},{193,1},{2,194},{194,2},{3,195},{195,3},{4... | collective-permute-start | bytes 3932168 | tf_op jit(solution)/shard_map/ppermute | solution.py:174
  5.3 0.0 copy-done.6
  5.3 7.6 %collective-permute-start = (bf16[64,1024]{1,0:T(8,128)(2,1)S(1)}, bf16[64,1024]{1,0:T(8,128)(2,1)S(1)}, u32[]{:S(2)}, u32[]{:S(2)}) collective-permute-start(bf16[64,1024]{1,0:T(8,128)(2,1)S(1)} %bitcast.38), channel_id=1, source_target_pairs={{0,96},{96,0},{1,97},{97,1},{2,98},{98,2},{3,99},{99,3},{4,100},{1... | collective-permute-start | bytes 393224 | tf_op jit(solution)/shard_map/ppermute | solution.py:22
  12.9 2.3 %collective-permute-done = bf16[64,1024]{1,0:T(8,128)(2,1)S(1)} collective-permute-done((bf16[64,1024]{1,0:T(8,128)(2,1)S(1)}, bf16[64,1024]{1,0:T(8,128)(2,1)S(1)}, u32[]{:S(2)}, u32[]{:S(2)}) %collective-permute-start) | collective-permute-done | bytes 131104 | tf_op jit(solution)/shard_map/ppermute | solution.py:22
  15.3 6.6 %collective-permute-start.3 = (bf16[2,64,1024]{2,1,0:T(8,128)(2,1)S(1)}, bf16[2,64,1024]{2,1,0:T(8,128)(2,1)S(1)}, u32[]{:S(2)}, u32[]{:S(2)}) collective-permute-start(bf16[2,64,1024]{2,1,0:T(8,128)(2,1)S(1)} %pad_maximum_fusion.refs_1_.refs_4_), channel_id=1, source_target_pairs={{0,32},{32,64},{64,0},{1,33},{33,65},{65,1},{2,34},{34,66},{66,2},... | collective-permute-start | bytes 786440 | tf_op jit(solution)/shard_map/ppermute | solution.py:23
  21.9 6.5 %collective-permute-start.4 = (bf16[2,64,1024]{2,1,0:T(8,128)(2,1)S(1)}, bf16[2,64,1024]{2,1,0:T(8,128)(2,1)S(1)}, u32[]{:S(2)}, u32[]{:S(2)}) collective-permute-start(bf16[2,64,1024]{2,1,0:T(8,128)(2,1)S(1)} %pad_maximum_fusion.refs_1_.refs_4_), channel_id=1, source_target_pairs={{0,64},{32,0},{64,32},{1,65},{33,1},{65,33},{2,66},{34,2},{66,34},... | collective-permute-start | bytes 786440 | tf_op jit(solution)/shard_map/ppermute | solution.py:23
  28.4 3.0 %collective-permute-start.5 = (bf16[2,64,1024]{2,1,0:T(8,128)(2,1)S(1)}, bf16[2,64,1024]{2,1,0:T(8,128)(2,1)S(1)}, u32[]{:S(2)}, u32[]{:S(2)}) collective-permute-start(bf16[2,64,1024]{2,1,0:T(8,128)(2,1)S(1)} %pad_maximum_fusion.refs_1_.refs_4_), channel_id=1, source_target_pairs={{0,576},{192,384},{384,192},{576,0},{1,577},{193,385},{385,193},{5... | collective-permute-start | bytes 786440 | tf_op jit(solution)/shard_map/ppermute | solution.py:21
  31.4 0.0 collective-permute-done.3.refs_2_.refs_5_
  31.5 4.3 %collective-permute-start.6 = (bf16[2,64,1024]{2,1,0:T(8,128)(2,1)S(1)}, bf16[2,64,1024]{2,1,0:T(8,128)(2,1)S(1)}, u32[]{:S(2)}, u32[]{:S(2)}) collective-permute-start(bf16[2,64,1024]{2,1,0:T(8,128)(2,1)S(1)} %collective-permute-done.3.refs_2_.refs_5_), channel_id=1, source_target_pairs={{0,576},{192,384},{384,192},{576,0},{1,577},{193,385},{385,193},{5... | collective-permute-start | bytes 786440 | tf_op jit(solution)/shard_map/ppermute | solution.py:21
  35.8 2.8 %collective-permute-done.4.refs_3_.refs_6_ = bf16[2,64,1024]{2,1,0:T(8,128)(2,1)S(1)} collective-permute-done((bf16[2,64,1024]{2,1,0:T(8,128)(2,1)S(1)}, bf16[2,64,1024]{2,1,0:T(8,128)(2,1)S(1)}, u32[]{:S(2)}, u32[]{:S(2)}) %collective-permute-start.4) | collective-permute-done | bytes 262176 | tf_op jit(solution)/shard_map/ppermute | solution.py:23
  38.5 3.3 %collective-permute-start.7 = (bf16[2,64,1024]{2,1,0:T(8,128)(2,1)S(1)}, bf16[2,64,1024]{2,1,0:T(8,128)(2,1)S(1)}, u32[]{:S(2)}, u32[]{:S(2)}) collective-permute-start(bf16[2,64,1024]{2,1,0:T(8,128)(2,1)S(1)} %collective-permute-done.4.refs_3_.refs_6_), channel_id=1, source_target_pairs={{0,576},{192,384},{384,192},{576,0},{1,577},{193,385},{385,193},{5... | collective-permute-start | bytes 786440 | tf_op jit(solution)/shard_map/ppermute | solution.py:21
  41.9 3.3 %collective-permute-start.1 = (bf16[8,80,1024]{2,1,0:T(8,128)(2,1)S(1)}, bf16[8,80,1024]{2,1,0:T(8,128)(2,1)}, u32[]{:S(2)}, u32[]{:S(2)}) collective-permute-start(bf16[8,80,1024]{2,1,0:T(8,128)(2,1)S(1)} %bitcast.34), channel_id=1, source_target_pairs={{0,16},{16,0},{1,17},{17,1},{2,18},{18,2},{3,19},{19,3},{4,20},{20... | collective-permute-start | bytes 3932168 | tf_op jit(solution)/shard_map/ppermute | solution.py:175
  45.2 0.0 collective-permute-done.5.refs_4_.refs_7_
  45.2 0.0 copy-start
  45.2 0.0 collective-permute-done.6.refs_5_.refs_8_
  45.2 0.0 copy-start.2
  45.2 4.8 %collective-permute-done.7.refs_6_.refs_9_ = bf16[2,64,1024]{2,1,0:T(8,128)(2,1)S(1)} collective-permute-done((bf16[2,64,1024]{2,1,0:T(8,128)(2,1)S(1)}, bf16[2,64,1024]{2,1,0:T(8,128)(2,1)S(1)}, u32[]{:S(2)}, u32[]{:S(2)}) %collective-permute-start.7) | collective-permute-done | bytes 262176 | tf_op jit(solution)/shard_map/ppermute | solution.py:21
  50.0 0.0 collective-permute-done.2.refs_0_
  50.0 0.0 copy-done
  50.0 0.0 copy-done.2
  50.0 0.7 copy-done.4
  50.7 3.6 %collective-permute-start.8 = (bf16[8,80,1024]{2,1,0:T(8,128)(2,1)S(1)}, bf16[8,80,1024]{2,1,0:T(8,128)(2,1)}, u32[]{:S(2)}, u32[]{:S(2)}) collective-permute-start(bf16[8,80,1024]{2,1,0:T(8,128)(2,1)S(1)} %shard_map.38.refs_2_), channel_id=1, source_target_pairs={{0,16},{16,0},{1,17},{17,1},{2,18},{18,2},{3,19},{19,3},{4,20},{20... | collective-permute-start | bytes 3932168 | tf_op jit(solution)/shard_map/ppermute | solution.py:178
  54.3 0.0 copy-start.1
  54.4 0.0 collective-permute-done.1.refs_1_
  54.4 2.7 %collective-permute-done.8.refs_3_ = bf16[8,80,1024]{2,1,0:T(8,128)(2,1)} collective-permute-done((bf16[8,80,1024]{2,1,0:T(8,128)(2,1)S(1)}, bf16[8,80,1024]{2,1,0:T(8,128)(2,1)}, u32[]{:S(2)}, u32[]{:S(2)}) %collective-permute-start.8) | collective-permute-done | bytes 1310752 | tf_op jit(solution)/shard_map/ppermute | solution.py:178
  57.1 0.0 copy-done.3
  57.1 1.7 %shard_map.42 = (bf16[160,768]{1,0:T(8,128)(2,1)S(1)}, bf16[160,768]{1,0:T(8,128)(2,1)S(1)}) custom-call(s32[1]{0:T(128)} %bitcast.26.here, s32[1]{0:T(128)} %bitcast.27.place, bf16[8,80,1024]{2,1,0:T(8,128)(2,1)S(1)} %shard_map.37.refs_0_, bf16[8,80,1024]{2,1,0:T(8,128)(2,1)} %collective-permute-done.1.refs_1_, bf16[8,80,1024]{2,1,0:T(8,128)(2,1)S(1)} %shard_map.38.refs_2_, ...), custom_call_target="tpu_custom_call" | custom-call | flops 503316480 | bytes 2719744 | tf_op jit(solution)/shard_map/pallas_call | solution.py:73
  58.8 4.2 %collective-permute-start.13 = (bf16[160,768]{1,0:T(8,128)(2,1)S(1)}, bf16[160,768]{1,0:T(8,128)(2,1)S(1)}, u32[]{:S(2)}, u32[]{:S(2)}) collective-permute-start(bf16[160,768]{1,0:T(8,128)(2,1)S(1)} %get-tuple-element.22), channel_id=1, source_target_pairs={{0,7},{1,0},{2,1},{3,2},{4,3},{5,4},{6,5},{7,6},{8,15},{9,8},{10,9... | collective-permute-start | bytes 737288 | tf_op jit(solution)/shard_map/ppermute | solution.py:134
  63.0 1.9 %collective-permute-start.9 = (bf16[160,768]{1,0:T(8,128)(2,1)S(1)}, bf16[160,768]{1,0:T(8,128)(2,1)S(1)}, u32[]{:S(2)}, u32[]{:S(2)}) collective-permute-start(bf16[160,768]{1,0:T(8,128)(2,1)S(1)} %get-tuple-element.18), channel_id=1, source_target_pairs={{0,1},{1,2},{2,3},{3,4},{4,5},{5,6},{6,7},{7,0},{8,9},{9,10},{10,1... | collective-permute-start | bytes 737288 | tf_op jit(solution)/shard_map/ppermute | solution.py:133
  64.9 2.6 %shard_map.41 = (bf16[320,768]{1,0:T(8,128)(2,1)S(1)}, bf16[320,768]{1,0:T(8,128)(2,1)S(1)}) custom-call(s32[1]{0:T(128)} %bitcast.26.here, s32[1]{0:T(128)} %bitcast.27.place, bf16[8,80,1024]{2,1,0:T(8,128)(2,1)S(1)} %shard_map.37.refs_0_, bf16[8,80,1024]{2,1,0:T(8,128)(2,1)} %collective-permute-done.1.refs_1_, bf16[8,80,1024]{2,1,0:T(8,128)(2,1)S(1)} %shard_map.38.refs_2_, ...), custom_call_target="tpu_custom_call" | custom-call | flops 1006632960 | bytes 3866624 | tf_op jit(solution)/shard_map/pallas_call | solution.py:73
  67.5 0.4 collective-permute-done.13.refs_1_
  67.9 0.1 shard_map.46
  68.0 5.3 %collective-permute-start.14 = (bf16[320,768]{1,0:T(8,128)(2,1)S(1)}, bf16[320,768]{1,0:T(8,128)(2,1)S(1)}, u32[]{:S(2)}, u32[]{:S(2)}) collective-permute-start(bf16[320,768]{1,0:T(8,128)(2,1)S(1)} %shard_map.46), channel_id=1, source_target_pairs={{0,7},{1,0},{2,1},{3,2},{4,3},{5,4},{6,5},{7,6},{8,15},{9,8},{10,9... | collective-permute-start | bytes 1474568 | tf_op jit(solution)/shard_map/ppermute | solution.py:141
  73.3 0.0 collective-permute-done.9.refs_1_
  73.3 0.1 shard_map.43
  73.4 1.9 %collective-permute-start.10 = (bf16[320,768]{1,0:T(8,128)(2,1)S(1)}, bf16[320,768]{1,0:T(8,128)(2,1)S(1)}, u32[]{:S(2)}, u32[]{:S(2)}) collective-permute-start(bf16[320,768]{1,0:T(8,128)(2,1)S(1)} %shard_map.43), channel_id=1, source_target_pairs={{0,1},{1,2},{2,3},{3,4},{4,5},{5,6},{6,7},{7,0},{8,9},{9,10},{10,1... | collective-permute-start | bytes 1474568 | tf_op jit(solution)/shard_map/ppermute | solution.py:140
  75.3 2.6 %shard_map.40 = (bf16[320,768]{1,0:T(8,128)(2,1)S(1)}, bf16[320,768]{1,0:T(8,128)(2,1)S(1)}) custom-call(s32[1]{0:T(128)} %bitcast.26.here, s32[1]{0:T(128)} %bitcast.27.place, bf16[8,80,1024]{2,1,0:T(8,128)(2,1)S(1)} %shard_map.37.refs_0_, bf16[8,80,1024]{2,1,0:T(8,128)(2,1)} %collective-permute-done.1.refs_1_, bf16[8,80,1024]{2,1,0:T(8,128)(2,1)S(1)} %shard_map.38.refs_2_, ...), custom_call_target="tpu_custom_call" | custom-call | flops 1006632960 | bytes 3866624 | tf_op jit(solution)/shard_map/pallas_call | solution.py:73
  77.9 3.6 %shard_map.39 = (bf16[320,768]{1,0:T(8,128)(2,1)S(1)}, bf16[320,768]{1,0:T(8,128)(2,1)S(1)}, bf16[320,768]{1,0:T(8,128)(2,1)S(1)}) custom-call(s32[1]{0:T(128)} %bitcast.26.here, s32[1]{0:T(128)} %bitcast.27.place, bf16[8,80,1024]{2,1,0:T(8,128)(2,1)S(1)} %shard_map.37.refs_0_, bf16[8,80,1024]{2,1,0:T(8,128)(2,1)} %collective-permute-done.1.refs_1_, ...), custom_call_target="tpu_custom_call" | custom-call | flops 1509949440 | bytes 5013504 | tf_op jit(solution)/shard_map/pallas_call | solution.py:73
  81.5 1.1 collective-permute-done.14.refs_1_
  82.6 0.1 shard_map.47
  82.7 5.3 %collective-permute-start.15 = (bf16[320,768]{1,0:T(8,128)(2,1)S(1)}, bf16[320,768]{1,0:T(8,128)(2,1)S(1)}, u32[]{:S(2)}, u32[]{:S(2)}) collective-permute-start(bf16[320,768]{1,0:T(8,128)(2,1)S(1)} %shard_map.47), channel_id=1, source_target_pairs={{0,7},{1,0},{2,1},{3,2},{4,3},{5,4},{6,5},{7,6},{8,15},{9,8},{10,9... | collective-permute-start | bytes 1474568 | tf_op jit(solution)/shard_map/ppermute | solution.py:141
  88.0 0.0 collective-permute-done.10.refs_1_
  88.0 0.1 shard_map.44
  88.2 1.9 %collective-permute-start.11 = (bf16[320,768]{1,0:T(8,128)(2,1)S(1)}, bf16[320,768]{1,0:T(8,128)(2,1)S(1)}, u32[]{:S(2)}, u32[]{:S(2)}) collective-permute-start(bf16[320,768]{1,0:T(8,128)(2,1)S(1)} %shard_map.44), channel_id=1, source_target_pairs={{0,1},{1,2},{2,3},{3,4},{4,5},{5,6},{6,7},{7,0},{8,9},{9,10},{10,1... | collective-permute-start | bytes 1474568 | tf_op jit(solution)/shard_map/ppermute | solution.py:140
  90.1 6.3 %collective-permute-done.15.refs_1_ = bf16[320,768]{1,0:T(8,128)(2,1)S(1)} collective-permute-done((bf16[320,768]{1,0:T(8,128)(2,1)S(1)}, bf16[320,768]{1,0:T(8,128)(2,1)S(1)}, u32[]{:S(2)}, u32[]{:S(2)}) %collective-permute-start.15) | collective-permute-done | bytes 491552 | tf_op jit(solution)/shard_map/ppermute | solution.py:141
  96.4 0.1 shard_map.48
  96.5 5.3 %collective-permute-start.16 = (bf16[320,768]{1,0:T(8,128)(2,1)S(1)}, bf16[320,768]{1,0:T(8,128)(2,1)S(1)}, u32[]{:S(2)}, u32[]{:S(2)}) collective-permute-start(bf16[320,768]{1,0:T(8,128)(2,1)S(1)} %shard_map.48), channel_id=1, source_target_pairs={{0,7},{1,0},{2,1},{3,2},{4,3},{5,4},{6,5},{7,6},{8,15},{9,8},{10,9... | collective-permute-start | bytes 1474568 | tf_op jit(solution)/shard_map/ppermute | solution.py:141
  101.8 0.0 collective-permute-done.11.refs_1_
  101.8 0.1 shard_map.45
  102.0 1.9 %collective-permute-start.12 = (bf16[320,768]{1,0:T(8,128)(2,1)S(1)}, bf16[320,768]{1,0:T(8,128)(2,1)S(1)}, u32[]{:S(2)}, u32[]{:S(2)}) collective-permute-start(bf16[320,768]{1,0:T(8,128)(2,1)S(1)} %shard_map.45), channel_id=1, source_target_pairs={{0,1},{1,2},{2,3},{3,4},{4,5},{5,6},{6,7},{7,0},{8,9},{9,10},{10,1... | collective-permute-start | bytes 1474568 | tf_op jit(solution)/shard_map/ppermute | solution.py:140
  103.9 5.4 %collective-permute-done.16.refs_2_ = bf16[320,768]{1,0:T(8,128)(2,1)S(1)} collective-permute-done((bf16[320,768]{1,0:T(8,128)(2,1)S(1)}, bf16[320,768]{1,0:T(8,128)(2,1)S(1)}, u32[]{:S(2)}, u32[]{:S(2)}) %collective-permute-start.16) | collective-permute-done | bytes 491552 | tf_op jit(solution)/shard_map/ppermute | solution.py:141
  109.2 5.2 %collective-permute-done.12.refs_1_ = bf16[320,768]{1,0:T(8,128)(2,1)S(1)} collective-permute-done((bf16[320,768]{1,0:T(8,128)(2,1)S(1)}, bf16[320,768]{1,0:T(8,128)(2,1)S(1)}, u32[]{:S(2)}, u32[]{:S(2)}) %collective-permute-start.12) | collective-permute-done | bytes 491552 | tf_op jit(solution)/shard_map/ppermute | solution.py:140
  114.4 1.0 shard_map.49
  115.4 18.5 %all-to-all-start = ((bf16[8,40,768]{2,1,0:T(8,128)(2,1)}), bf16[8,40,768]{2,1,0:T(8,128)(2,1)S(1)}, u32[]{:S(2)}, u32[]{:S(2)}) async-start(bf16[8,40,768]{2,1,0:T(8,128)(2,1)} %bitcast.31), calls=%async_computation | async-start | bytes 983040 | tf_op jit(solution)/shard_map/all_to_all | solution.py:150
  133.9 0.1 copy.16
  134.0 0.2 reduce_window_sum.11
  134.2 0.1 copy.17
  134.2 0.1 copy.18
  134.4 0.1 copy.20
  134.5 0.1 eq.43
  134.6 0.1 stack.105.refs_0_
  134.7 17.4 %all-to-all-done = bf16[8,40,768]{2,1,0:T(8,128)(2,1)S(1)} async-done(((bf16[8,40,768]{2,1,0:T(8,128)(2,1)}), bf16[8,40,768]{2,1,0:T(8,128)(2,1)S(1)}, u32[]{:S(2)}, u32[]{:S(2)}) %all-to-all-start) | async-done | bytes 491552 | tf_op jit(solution)/shard_map/all_to_all | solution.py:150
  152.1 1.9 %shard_map.50 = bf16[128,3072]{1,0:T(8,128)(2,1)} custom-call(s32[24]{0:T(128)S(1)} %stack.105.refs_0_, bf16[128,80]{1,0:T(8,128)(2,1)S(1)} %and_convert_fusion.refs_1_, bf16[4,80,768]{2,1,0:T(8,128)(2,1)S(1)} %bitcast.36), custom_call_target="tpu_custom_call" | custom-call | tf_op jit(solution)/shard_map/pallas_call | solution.py:200
  (18 shorter events, 0.1 us)
Async XLA Ops:
  0.0 5.3 %copy-start.6 = (bf16[1,64,1024]{2,1,0:T(8,128)(2,1)S(1)}, bf16[1,64,1024]{2,1,0:T(8,128)(2,1)}, u32[]{:S(2)}) copy-start(bf16[1,64,1024]{2,1,0:T(8,128)(2,1)} %param.5) | copy-start | bytes 393220
  1.4 48.7 %collective-permute-start.2 = (bf16[8,80,1024]{2,1,0:T(8,128)(2,1)S(1)}, bf16[8,80,1024]{2,1,0:T(8,128)(2,1)S(1)}, u32[]{:S(2)}, u32[]{:S(2)}) collective-permute-start(bf16[8,80,1024]{2,1,0:T(8,128)(2,1)S(1)} %bitcast.33), channel_id=1, source_target_pairs={{0,192},{192,0},{1,193},{193,1},{2,194},{194,2},{3,195},{195,3},{4... | collective-permute-start | bytes 3932168 | tf_op jit(solution)/shard_map/ppermute | solution.py:174
  5.3 10.0 %collective-permute-start = (bf16[64,1024]{1,0:T(8,128)(2,1)S(1)}, bf16[64,1024]{1,0:T(8,128)(2,1)S(1)}, u32[]{:S(2)}, u32[]{:S(2)}) collective-permute-start(bf16[64,1024]{1,0:T(8,128)(2,1)S(1)} %bitcast.38), channel_id=1, source_target_pairs={{0,96},{96,0},{1,97},{97,1},{2,98},{98,2},{3,99},{99,3},{4,100},{1... | collective-permute-start | bytes 393224 | tf_op jit(solution)/shard_map/ppermute | solution.py:22
  15.3 16.1 %collective-permute-start.3 = (bf16[2,64,1024]{2,1,0:T(8,128)(2,1)S(1)}, bf16[2,64,1024]{2,1,0:T(8,128)(2,1)S(1)}, u32[]{:S(2)}, u32[]{:S(2)}) collective-permute-start(bf16[2,64,1024]{2,1,0:T(8,128)(2,1)S(1)} %pad_maximum_fusion.refs_1_.refs_4_), channel_id=1, source_target_pairs={{0,32},{32,64},{64,0},{1,33},{33,65},{65,1},{2,34},{34,66},{66,2},... | collective-permute-start | bytes 786440 | tf_op jit(solution)/shard_map/ppermute | solution.py:23
  21.9 16.6 %collective-permute-start.4 = (bf16[2,64,1024]{2,1,0:T(8,128)(2,1)S(1)}, bf16[2,64,1024]{2,1,0:T(8,128)(2,1)S(1)}, u32[]{:S(2)}, u32[]{:S(2)}) collective-permute-start(bf16[2,64,1024]{2,1,0:T(8,128)(2,1)S(1)} %pad_maximum_fusion.refs_1_.refs_4_), channel_id=1, source_target_pairs={{0,64},{32,0},{64,32},{1,65},{33,1},{65,33},{2,66},{34,2},{66,34},... | collective-permute-start | bytes 786440 | tf_op jit(solution)/shard_map/ppermute | solution.py:23
  28.4 16.7 %collective-permute-start.5 = (bf16[2,64,1024]{2,1,0:T(8,128)(2,1)S(1)}, bf16[2,64,1024]{2,1,0:T(8,128)(2,1)S(1)}, u32[]{:S(2)}, u32[]{:S(2)}) collective-permute-start(bf16[2,64,1024]{2,1,0:T(8,128)(2,1)S(1)} %pad_maximum_fusion.refs_1_.refs_4_), channel_id=1, source_target_pairs={{0,576},{192,384},{384,192},{576,0},{1,577},{193,385},{385,193},{5... | collective-permute-start | bytes 786440 | tf_op jit(solution)/shard_map/ppermute | solution.py:21
  31.5 13.7 %collective-permute-start.6 = (bf16[2,64,1024]{2,1,0:T(8,128)(2,1)S(1)}, bf16[2,64,1024]{2,1,0:T(8,128)(2,1)S(1)}, u32[]{:S(2)}, u32[]{:S(2)}) collective-permute-start(bf16[2,64,1024]{2,1,0:T(8,128)(2,1)S(1)} %collective-permute-done.3.refs_2_.refs_5_), channel_id=1, source_target_pairs={{0,576},{192,384},{384,192},{576,0},{1,577},{193,385},{385,193},{5... | collective-permute-start | bytes 786440 | tf_op jit(solution)/shard_map/ppermute | solution.py:21
  38.5 11.5 %collective-permute-start.7 = (bf16[2,64,1024]{2,1,0:T(8,128)(2,1)S(1)}, bf16[2,64,1024]{2,1,0:T(8,128)(2,1)S(1)}, u32[]{:S(2)}, u32[]{:S(2)}) collective-permute-start(bf16[2,64,1024]{2,1,0:T(8,128)(2,1)S(1)} %collective-permute-done.4.refs_3_.refs_6_), channel_id=1, source_target_pairs={{0,576},{192,384},{384,192},{576,0},{1,577},{193,385},{385,193},{5... | collective-permute-start | bytes 786440 | tf_op jit(solution)/shard_map/ppermute | solution.py:21
  41.9 12.5 %collective-permute-start.1 = (bf16[8,80,1024]{2,1,0:T(8,128)(2,1)S(1)}, bf16[8,80,1024]{2,1,0:T(8,128)(2,1)}, u32[]{:S(2)}, u32[]{:S(2)}) collective-permute-start(bf16[8,80,1024]{2,1,0:T(8,128)(2,1)S(1)} %bitcast.34), channel_id=1, source_target_pairs={{0,16},{16,0},{1,17},{17,1},{2,18},{18,2},{3,19},{19,3},{4,20},{20... | collective-permute-start | bytes 3932168 | tf_op jit(solution)/shard_map/ppermute | solution.py:175
  45.2 4.8 %copy-start = (bf16[2,64,1024]{2,1,0:T(8,128)(2,1)}, bf16[2,64,1024]{2,1,0:T(8,128)(2,1)S(1)}, u32[]{:S(2)}) copy-start(bf16[2,64,1024]{2,1,0:T(8,128)(2,1)S(1)} %collective-permute-done.5.refs_4_.refs_7_) | copy-start | bytes 786436
  45.2 4.8 %copy-start.2 = (bf16[2,64,1024]{2,1,0:T(8,128)(2,1)}, bf16[2,64,1024]{2,1,0:T(8,128)(2,1)S(1)}, u32[]{:S(2)}) copy-start(bf16[2,64,1024]{2,1,0:T(8,128)(2,1)S(1)} %collective-permute-done.6.refs_5_.refs_8_) | copy-start | bytes 786436
  50.0 0.7 copy-start.4
  50.7 6.4 %collective-permute-start.8 = (bf16[8,80,1024]{2,1,0:T(8,128)(2,1)S(1)}, bf16[8,80,1024]{2,1,0:T(8,128)(2,1)}, u32[]{:S(2)}, u32[]{:S(2)}) collective-permute-start(bf16[8,80,1024]{2,1,0:T(8,128)(2,1)S(1)} %shard_map.38.refs_2_), channel_id=1, source_target_pairs={{0,16},{16,0},{1,17},{17,1},{2,18},{18,2},{3,19},{19,3},{4,20},{20... | collective-permute-start | bytes 3932168 | tf_op jit(solution)/shard_map/ppermute | solution.py:178
  54.3 2.8 %copy-start.1 = (bf16[2,64,1024]{2,1,0:T(8,128)(2,1)S(1)}, bf16[2,64,1024]{2,1,0:T(8,128)(2,1)}, u32[]{:S(2)}) copy-start(bf16[2,64,1024]{2,1,0:T(8,128)(2,1)} %copy-done) | copy-start | bytes 786436
  54.3 2.8 %copy-start.3 = (bf16[2,64,1024]{2,1,0:T(8,128)(2,1)S(1)}, bf16[2,64,1024]{2,1,0:T(8,128)(2,1)}, u32[]{:S(2)}) copy-start(bf16[2,64,1024]{2,1,0:T(8,128)(2,1)} %copy-done.2) | copy-start | bytes 786436
  54.4 2.7 %copy-start.5 = (bf16[2,64,1024]{2,1,0:T(8,128)(2,1)S(1)}, bf16[2,64,1024]{2,1,0:T(8,128)(2,1)}, u32[]{:S(2)}) copy-start(bf16[2,64,1024]{2,1,0:T(8,128)(2,1)} %copy-done.4) | copy-start | bytes 786436
  58.8 9.1 %collective-permute-start.13 = (bf16[160,768]{1,0:T(8,128)(2,1)S(1)}, bf16[160,768]{1,0:T(8,128)(2,1)S(1)}, u32[]{:S(2)}, u32[]{:S(2)}) collective-permute-start(bf16[160,768]{1,0:T(8,128)(2,1)S(1)} %get-tuple-element.22), channel_id=1, source_target_pairs={{0,7},{1,0},{2,1},{3,2},{4,3},{5,4},{6,5},{7,6},{8,15},{9,8},{10,9... | collective-permute-start | bytes 737288 | tf_op jit(solution)/shard_map/ppermute | solution.py:134
  63.0 10.3 %collective-permute-start.9 = (bf16[160,768]{1,0:T(8,128)(2,1)S(1)}, bf16[160,768]{1,0:T(8,128)(2,1)S(1)}, u32[]{:S(2)}, u32[]{:S(2)}) collective-permute-start(bf16[160,768]{1,0:T(8,128)(2,1)S(1)} %get-tuple-element.18), channel_id=1, source_target_pairs={{0,1},{1,2},{2,3},{3,4},{4,5},{5,6},{6,7},{7,0},{8,9},{9,10},{10,1... | collective-permute-start | bytes 737288 | tf_op jit(solution)/shard_map/ppermute | solution.py:133
  68.0 14.6 %collective-permute-start.14 = (bf16[320,768]{1,0:T(8,128)(2,1)S(1)}, bf16[320,768]{1,0:T(8,128)(2,1)S(1)}, u32[]{:S(2)}, u32[]{:S(2)}) collective-permute-start(bf16[320,768]{1,0:T(8,128)(2,1)S(1)} %shard_map.46), channel_id=1, source_target_pairs={{0,7},{1,0},{2,1},{3,2},{4,3},{5,4},{6,5},{7,6},{8,15},{9,8},{10,9... | collective-permute-start | bytes 1474568 | tf_op jit(solution)/shard_map/ppermute | solution.py:141
  73.4 14.6 %collective-permute-start.10 = (bf16[320,768]{1,0:T(8,128)(2,1)S(1)}, bf16[320,768]{1,0:T(8,128)(2,1)S(1)}, u32[]{:S(2)}, u32[]{:S(2)}) collective-permute-start(bf16[320,768]{1,0:T(8,128)(2,1)S(1)} %shard_map.43), channel_id=1, source_target_pairs={{0,1},{1,2},{2,3},{3,4},{4,5},{5,6},{6,7},{7,0},{8,9},{9,10},{10,1... | collective-permute-start | bytes 1474568 | tf_op jit(solution)/shard_map/ppermute | solution.py:140
  82.7 13.7 %collective-permute-start.15 = (bf16[320,768]{1,0:T(8,128)(2,1)S(1)}, bf16[320,768]{1,0:T(8,128)(2,1)S(1)}, u32[]{:S(2)}, u32[]{:S(2)}) collective-permute-start(bf16[320,768]{1,0:T(8,128)(2,1)S(1)} %shard_map.47), channel_id=1, source_target_pairs={{0,7},{1,0},{2,1},{3,2},{4,3},{5,4},{6,5},{7,6},{8,15},{9,8},{10,9... | collective-permute-start | bytes 1474568 | tf_op jit(solution)/shard_map/ppermute | solution.py:141
  88.2 13.7 %collective-permute-start.11 = (bf16[320,768]{1,0:T(8,128)(2,1)S(1)}, bf16[320,768]{1,0:T(8,128)(2,1)S(1)}, u32[]{:S(2)}, u32[]{:S(2)}) collective-permute-start(bf16[320,768]{1,0:T(8,128)(2,1)S(1)} %shard_map.44), channel_id=1, source_target_pairs={{0,1},{1,2},{2,3},{3,4},{4,5},{5,6},{6,7},{7,0},{8,9},{9,10},{10,1... | collective-permute-start | bytes 1474568 | tf_op jit(solution)/shard_map/ppermute | solution.py:140
  96.5 12.8 %collective-permute-start.16 = (bf16[320,768]{1,0:T(8,128)(2,1)S(1)}, bf16[320,768]{1,0:T(8,128)(2,1)S(1)}, u32[]{:S(2)}, u32[]{:S(2)}) collective-permute-start(bf16[320,768]{1,0:T(8,128)(2,1)S(1)} %shard_map.48), channel_id=1, source_target_pairs={{0,7},{1,0},{2,1},{3,2},{4,3},{5,4},{6,5},{7,6},{8,15},{9,8},{10,9... | collective-permute-start | bytes 1474568 | tf_op jit(solution)/shard_map/ppermute | solution.py:141
  102.0 12.5 %collective-permute-start.12 = (bf16[320,768]{1,0:T(8,128)(2,1)S(1)}, bf16[320,768]{1,0:T(8,128)(2,1)S(1)}, u32[]{:S(2)}, u32[]{:S(2)}) collective-permute-start(bf16[320,768]{1,0:T(8,128)(2,1)S(1)} %shard_map.45), channel_id=1, source_target_pairs={{0,1},{1,2},{2,3},{3,4},{4,5},{5,6},{6,7},{7,0},{8,9},{9,10},{10,1... | collective-permute-start | bytes 1474568 | tf_op jit(solution)/shard_map/ppermute | solution.py:140
  114.4 19.4 %copy-start.7 = (s32[128,2]{0,1:T(2,128)S(1)}, s32[128,2]{0,1:T(2,128)}, u32[]{:S(2)}) copy-start(s32[128,2]{0,1:T(2,128)} %param.3) | copy-start | bytes 3076
  115.4 36.7 %all-to-all-start = ((bf16[8,40,768]{2,1,0:T(8,128)(2,1)}), bf16[8,40,768]{2,1,0:T(8,128)(2,1)S(1)}, u32[]{:S(2)}, u32[]{:S(2)}) async-start(bf16[8,40,768]{2,1,0:T(8,128)(2,1)} %bitcast.31), calls=%async_computation | async-start | bytes 983040 | tf_op jit(solution)/shard_map/all_to_all | solution.py:150
